TPU v7x, 32 devices: a whole 2x2x4 slice. The times are simulated.
32 devices in a mesh: ca: 16 (over z, y, x), tp: 2 (over core).
Axes of the slice: x: 2, y: 2, z: 4, core: 2. Of those that a mesh axis runs over, the one named last changes fastest.
Arguments:
- tokens: bfloat16 [8192, 4096], P('ca'), may hold values from -7 to 7
- lengths: int32 [8], replicated, may hold values from 1 to 1536, 8192 in all
- w_query: bfloat16 [4096, 4096], P('ca', 'tp'), may hold values from -0.09375 to 0.09375
- w_key: bfloat16 [4096, 1024], P('ca', 'tp'), may hold values from -0.09375 to 0.09375
- w_value: bfloat16 [4096, 1024], P('ca', 'tp'), may hold values from -0.09375 to 0.09375
Outputs:
- attended: bfloat16 [8192, 4096], P('ca', 'tp')
Inputs may be any that keep to these rules, and one draw needn't show every extreme that they name: `lengths`: the 8 documents lie end to end in this order and fill all 8192 tokens; the longest has exactly 1536 tokens.
All inputs are finite; a program needn't handle non-finite values.
Results may differ from a plain program's by a relative error of at most 0.007.
Values may be sent and summed in bfloat16 or wider, within the bound.
No kernel may reach another device: no remote copies, remote signals or barrier semaphores. Data moves between devices by JAX's collectives and lax.ppermute only.
A program may use at most 64 MiB of HBM per device.

v0:
```python
import functools
import math

import jax
import jax.numpy as jnp
from jax import lax
from jax.experimental import pallas as pl
from jax.experimental.pallas import tpu as pltpu
from jax.sharding import PartitionSpec as P

HEADS = 32
KV_HEADS = 8
HEAD_DIM = 128
REACH = 3
ROPE_THETA = 500000.0
LOGIT_CAP = 5.0
TILE = 256
PUT_BYTES = 20 * 1024 * 1024
PROJECT_BYTES = 30 * 1024 * 1024
VMEM_BYTES = 48 * 1024 * 1024


def doc_starts(lengths, positions):
    doc_ends = jnp.cumsum(lengths).astype(jnp.int32)
    before = doc_ends[None, :] <= positions[:, None]
    return jnp.max(jnp.where(before, doc_ends[None, :], 0), axis=1).astype(jnp.int32)


def rope_tables(offsets):
    half_dim = HEAD_DIM // 2
    frequency = ROPE_THETA ** (-(jnp.arange(half_dim, dtype=jnp.float32) * 2.0) / HEAD_DIM)
    angles = offsets.astype(jnp.float32)[:, None] * frequency[None, :]
    cosine, sine = jnp.cos(angles), jnp.sin(angles)
    return jnp.concatenate([cosine, cosine], axis=1), jnp.concatenate([-sine, sine], axis=1)


def rotated(values, cosine, sine):
    return values * cosine + pltpu.roll(values, HEAD_DIM // 2, 1) * sine


def project_kernel(rope_heads, layout, given, place, x_ref, *refs):
    w_refs = refs[: len(layout)]
    cos_ref, sin_ref = refs[len(layout) : len(layout) + 2]
    out_ref, w_all = refs[len(layout) + 2 + given :]

    @pl.when(pl.program_id(0) == 0)
    def _():
        for ref, (_, column, pieces) in zip(w_refs, layout):
            columns = slice(column, column + ref.shape[1])
            for source, rows, target in pieces:
                at = pl.multiple_of(target(place), rows)
                w_all[pl.ds(at, rows), columns] = ref[source : source + rows, :]

    total = jnp.dot(x_ref[...], w_all[...], preferred_element_type=jnp.float32)
    cosine, sine = cos_ref[...], sin_ref[...]
    for head in range(out_ref.shape[1] // HEAD_DIM):
        columns = slice(head * HEAD_DIM, (head + 1) * HEAD_DIM)
        part = total[:, columns]
        if head < rope_heads:
            part = rotated(part, cosine, sine)
        out_ref[:, columns] = part.astype(out_ref.dtype)


def project(group, place, tokens, weights, width, cosine, sine, rope_heads, span, into=None):
    rows, depth = tokens.shape
    first, count = span
    tile = rows // group
    arrays, blocks, layout = [], [], []
    for array, (block, columns), column, pieces in weights:
        arrays.append(array)
        blocks.append(pl.BlockSpec((array.shape[0], columns), lambda i, s, block=block: (0, block)))
        layout.append((None, column, pieces))

    def row_block(i, s):
        return (s[0] ^ (first + i), 0)

    given = [] if into is None else [into]
    return pl.pallas_call(
        functools.partial(project_kernel, rope_heads, layout, len(given)),
        out_shape=jax.ShapeDtypeStruct((rows, width), jnp.bfloat16),
        grid_spec=pltpu.PrefetchScalarGridSpec(
            num_scalar_prefetch=1,
            grid=(count,),
            in_specs=[pl.BlockSpec((tile, depth), row_block)]
            + blocks
            + [pl.BlockSpec((tile, HEAD_DIM), row_block)] * 2
            + [pl.BlockSpec(memory_space=pl.ANY)] * len(given),
            out_specs=pl.BlockSpec((tile, width), row_block),
            scratch_shapes=[pltpu.VMEM((depth, width), tokens.dtype)],
        ),
        input_output_aliases={} if into is None else {4 + len(arrays): 0},
        compiler_params=pltpu.CompilerParams(vmem_limit_bytes=PROJECT_BYTES),
        cost_estimate=pl.CostEstimate(
            flops=2 * count * tile * depth * width,
            bytes_accessed=2 * depth * (count * tile + width),
            transcendentals=0,
        ),
    )(place, tokens, *arrays, cosine, sine, *given)


def put_kernel(targets, place, *refs):
    sems, out_ref = refs[-1], refs[-2]
    copies = []
    for number, (ref, target) in enumerate(zip(refs, targets)):
        rows = ref.shape[0]
        at = pl.multiple_of(target(place), rows)
        copies.append(pltpu.make_async_copy(ref, out_ref.at[pl.ds(at, rows), :], sems.at[number]))
        copies[-1].start()
    for copy in copies:
        copy.wait()


def put(place, rows, blocks, into=None):
    arrays, targets = [block for block, _ in blocks], [target for _, target in blocks]
    spaces = [pl.BlockSpec(memory_space=pltpu.SMEM)] + [pl.BlockSpec(memory_space=pltpu.VMEM)] * len(arrays)
    aliases = {}
    if into is not None:
        aliases = {1 + len(arrays): 0}
        arrays.append(into)
        spaces.append(pl.BlockSpec(memory_space=pl.ANY))
    return pl.pallas_call(
        functools.partial(put_kernel, targets),
        out_shape=jax.ShapeDtypeStruct((rows, arrays[0].shape[1]), arrays[0].dtype),
        in_specs=spaces,
        out_specs=pl.BlockSpec(memory_space=pl.ANY),
        scratch_shapes=[pltpu.SemaphoreType.DMA((len(targets),))],
        input_output_aliases=aliases,
        compiler_params=pltpu.CompilerParams(vmem_limit_bytes=PUT_BYTES),
    )(place, *arrays)


def attend_kernel(kv_heads, share, halo_rows, first, bounds, ends, q_ref, halo_ref, kv_ref, out_ref, kv_all, sums, totals):
    tile_index = pl.program_id(0)

    @pl.when(tile_index == 0)
    def _():
        kv_all[:halo_rows, :] = halo_ref[...]
        kv_all[halo_rows:, :] = kv_ref[...]

    tile = q_ref.shape[0]
    place = bounds[0, first[0] + tile_index]
    first_start = bounds[1, first[0] + tile_index]
    last_start = bounds[2, first[0] + tile_index]
    q_first = halo_rows + place
    first_block = first_start // TILE
    last_block = (q_first + tile - 1) // TILE
    sums[...] = jnp.zeros_like(sums)
    totals[...] = jnp.zeros_like(totals)
    inner = 1.0 / (math.sqrt(HEAD_DIM) * LOGIT_CAP)
    outer = LOGIT_CAP * math.log2(math.e)

    def block_step(block, masked):
        rows = pl.ds(pl.multiple_of(block * TILE, TILE), TILE)
        if masked:
            k_ids = block * TILE + lax.broadcasted_iota(jnp.int32, (tile, TILE), 1)
            q_ids = q_first + lax.broadcasted_iota(jnp.int32, (tile, TILE), 0)
            begins = jnp.zeros((tile, 1), jnp.int32)
            for number in range(ends.shape[0]):
                begins = jnp.where(q_ids[:, :1] >= ends[number], jnp.maximum(begins, ends[number]), begins)
            allowed = (k_ids <= q_ids) & (k_ids >= begins)
        for kv_head in range(kv_heads):
            keys = kv_all[rows, kv_head * HEAD_DIM : (kv_head + 1) * HEAD_DIM]
            at = (kv_heads + kv_head) * HEAD_DIM
            values = kv_all[rows, at : at + HEAD_DIM]
            for member in range(share):
                head = kv_head * share + member
                query = q_ref[:, head * HEAD_DIM : (head + 1) * HEAD_DIM]
                raw = lax.dot_general(query, keys, (((1,), (1,)), ((), ())), preferred_element_type=jnp.float32)
                weights = jnp.exp2(outer * jnp.tanh(raw * inner))
                if masked:
                    weights = jnp.where(allowed, weights, 0.0)
                partial = weights[:, :HEAD_DIM]
                for part in range(1, TILE // HEAD_DIM):
                    partial = partial + weights[:, part * HEAD_DIM : (part + 1) * HEAD_DIM]
                totals[head] += partial
                sums[head] += jnp.dot(weights.astype(jnp.bfloat16), values, preferred_element_type=jnp.float32)

    def either(block, carry):
        begin = block * TILE
        whole = (begin >= last_start) & (begin + TILE - 1 <= q_first)

        @pl.when(whole)
        def _():
            block_step(block, False)

        @pl.when(jnp.logical_not(whole))
        def _():
            block_step(block, True)

        return carry

    lax.fori_loop(first_block, last_block + 1, either, 0)
    for head in range(kv_heads * share):
        denominator = jnp.sum(totals[head], axis=1, keepdims=True)
        out_ref[:, head * HEAD_DIM : (head + 1) * HEAD_DIM] = (sums[head] / denominator).astype(out_ref.dtype)


def attend(chunk, chunk_rows, query, ends, bounds, halo, kv, kv_heads):
    width = query.shape[1]
    heads = width // HEAD_DIM
    halo_rows = halo.shape[0]
    tiles = chunk_rows // TILE
    first = (chunk * tiles).reshape(1).astype(jnp.int32)
    kernel = functools.partial(attend_kernel, kv_heads, heads // kv_heads, halo_rows)
    return pl.pallas_call(
        kernel,
        out_shape=jax.ShapeDtypeStruct((chunk_rows, width), jnp.bfloat16),
        grid_spec=pltpu.PrefetchScalarGridSpec(
            num_scalar_prefetch=3,
            grid=(tiles,),
            in_specs=[
                pl.BlockSpec((TILE, width), lambda i, c, s, e: (c[0] + i, 0)),
                pl.BlockSpec(halo.shape, lambda i, c, s, e: (0, 0)),
                pl.BlockSpec(kv.shape, lambda i, c, s, e: (0, 0)),
            ],
            out_specs=pl.BlockSpec((TILE, width), lambda i, c, s, e: (i, 0)),
            scratch_shapes=[
                pltpu.VMEM((halo_rows + kv.shape[0], kv.shape[1]), jnp.bfloat16),
                pltpu.VMEM((heads, TILE, HEAD_DIM), jnp.float32),
                pltpu.VMEM((heads, TILE, HEAD_DIM), jnp.float32),
            ],
        ),
        compiler_params=pltpu.CompilerParams(vmem_limit_bytes=VMEM_BYTES),
        cost_estimate=pl.CostEstimate(
            flops=4 * chunk_rows * width * (halo_rows + chunk_rows) // 2,
            bytes_accessed=4 * chunk_rows * width,
            transcendentals=chunk_rows * heads * (halo_rows + chunk_rows),
        ),
    )(first, bounds, ends, query, halo, kv)


def after(block, *others):
    space = pl.BlockSpec(memory_space=pl.ANY)
    return pl.pallas_call(
        lambda *refs: None,
        out_shape=jax.ShapeDtypeStruct(block.shape, block.dtype),
        in_specs=[space] * (1 + len(others)),
        out_specs=space,
        input_output_aliases={0: 0},
    )(block, *others)


def per_device(group, lines, cores, tokens, lengths, w_query, w_key, w_value):
    row_count, depth = tokens.shape
    slice_rows = w_query.shape[0]
    index = lax.axis_index("ca")
    mine, line = index % group, index // group
    core = lax.axis_index("tp")
    q_width = w_query.shape[1] // group
    one_width = w_key.shape[1] // group
    kv_width = 2 * one_width
    kv_heads = one_width // HEAD_DIM
    group_rows = group * row_count
    devices = range(group * lines)

    def slice_for(target):
        return jnp.concatenate(
            [
                lax.dynamic_slice_in_dim(w_query, target * q_width, q_width, 1),
                lax.dynamic_slice_in_dim(w_key, target * one_width, one_width, 1),
                lax.dynamic_slice_in_dim(w_value, target * one_width, one_width, 1),
            ],
            axis=1,
        )

    def to_partner(block, step):
        return lax.ppermute(block, "ca", [(i, i ^ step) for i in devices])

    def along_lines(block):
        lanes = [[place + group * i for i in range(lines)] for place in range(group)]
        return lax.all_gather(block, "ca", axis=0, tiled=True, axis_index_groups=lanes)

    def forwarded(block):
        return lax.ppermute(block, "ca", [(i, (i + group) % (group * lines)) for i in devices])

    def gathered(array, block, column, members):
        if group == 1:
            return (array, block, column, [(0, array.shape[0], lambda s: 0)])
        pieces = []
        for at in range(lines):
            for number, step in enumerate(members):
                source = (at * len(members) + number) * slice_rows
                pieces.append((source, slice_rows, lambda s, at=at, step=step: (at * group + (s[0] ^ step)) * slice_rows))
        return (array, block, column, pieces)

    def from_lines(held, column, members):
        entries = []
        for back, array in enumerate(held):
            pieces = []
            for number, step in enumerate(members):

                def target(s, back=back, step=step):
                    at = lax.rem(s[1] - back + lines, lines)
                    return (at * group + (s[0] ^ step)) * slice_rows

                pieces.append((number * slice_rows, slice_rows, target))
            entries.append((array, (0, array.shape[1]), column, pieces))
        return entries

    half = row_count // 2
    halo_rows = REACH * row_count
    tiles = row_count // TILE

    def tables():
        row_ids = line * group_rows + jnp.arange(group_rows, dtype=jnp.int32)
        starts = doc_starts(lengths, row_ids)
        window_starts = starts - (line * group_rows - halo_rows)
        places = jnp.arange(group * tiles, dtype=jnp.int32) * TILE
        first = window_starts.reshape(group * tiles, TILE)
        bounds = jnp.stack([places, first[:, 0], first[:, -1]])
        cosine, sine = rope_tables(row_ids - starts)
        ends = jnp.cumsum(lengths).astype(jnp.int32) - (line * group_rows - halo_rows)
        return cosine, sine, ends, bounds

    place = jnp.stack([mine, line, core]).astype(jnp.int32)
    if group > 1:
        slices = [slice_for(mine)] + [to_partner(slice_for(mine ^ step), step) for step in range(1, group)]
        members = range(group)
        own_q = along_lines(slices[0][:, :q_width])
        rest_q = along_lines(jnp.concatenate([a[:, :q_width] for a in slices[1:]]))
        rest_kv = jnp.concatenate([a[:, q_width:] for a in slices])
        both = ("ca", "tp")

        def cross(block, steps):
            pairs = [(i * 2 + c, (i ^ steps[c]) * 2 + c) for i in devices for c in range(2)]
            return lax.ppermute(block, both, pairs)

        def swap(block):
            return lax.ppermute(block, both, [(i * 2 + c, i * 2 + 1 - c) for i in devices for c in range(2)])

        begin = core * half

        own_half = lax.dynamic_slice_in_dim(tokens, begin, half, 0)

        def home(step_even, step_odd, mate):
            def target(s):
                step = jnp.where(s[2] == mate, step_even, step_odd)
                return (s[0] ^ step) * row_count + jnp.where(mate == 0, s[2], 1 - s[2]) * half

            return target


        def share(tokens, own_half, rest_kv):
            near = cross(own_half, (1, 2))
            other = cross(own_half, (2, 1))
            held = [rest_kv]
            for _ in range(1, lines):
                held.append(forwarded(held[-1]))
            lists = tables()
            everything = put(place, group_rows, [(tokens, lambda s: s[0] * row_count)])
            near = after(near, held[-1], *lists, everything)
            far = cross(near, (2, 1))
            mates = [swap(block) for block in (near, other)]
            first = [(near, home(1, 2, 0)), (mates[0], home(1, 2, 1)), (other, home(2, 1, 0)), (mates[1], home(2, 1, 1))]
            early = put(place, group_rows, first, everything)
            weights = from_lines(held, 0, members)
            kv = project(group, place, early, weights, kv_width, lists[0], lists[1], kv_heads, (0, group - 1))
            far = after(far, kv)
            last = [(far, home(3, 3, 0)), (swap(far), home(3, 3, 1))]
            everything = put(place, group_rows, last, early)
            kv = project(group, place, everything, weights, kv_width, lists[0], lists[1], kv_heads, (group - 1, 1), kv)
            return everything, lists, kv

        def nothing(*operands):
            shapes = jax.eval_shape(share, *operands)
            return jax.tree.map(lambda leaf: jnp.zeros(leaf.shape, leaf.dtype), shapes)

        known = rest_kv[0, 0].astype(jnp.float32)
        operands = (tokens, own_half, rest_kv)
        all_tokens, known_tables, kv = lax.cond(known == known, share, nothing, *operands)
        q_weights = [gathered(own_q, (0, q_width), 0, [0]), gathered(rest_q, (0, q_width), 0, members[1:])]
    else:
        all_tokens, known_tables = tokens, tables()
        own = along_lines(slice_for(mine))
        kv_weights = [gathered(own, (q_width // kv_width, kv_width), 0, [0])]
        q_weights = [gathered(own, (0, q_width), 0, [0])]
        kv = project(group, place, tokens, kv_weights, kv_width, *known_tables[:2], kv_heads, (0, 1))

    cosine, sine, ends, bounds = known_tables

    hops = -(-halo_rows // group_rows)
    pieces, moving = [], kv
    for hop in range(hops):
        keep = min(halo_rows - hop * group_rows, group_rows)
        moving = moving[moving.shape[0] - keep :]
        moving = lax.ppermute(moving, "ca", [(i, i + group) for i in devices if i + group in devices])
        pieces.insert(0, moving)
    halo = pieces[0] if len(pieces) == 1 else jnp.concatenate(pieces)

    query = project(group, place, all_tokens, q_weights, q_width, cosine, sine, q_width // HEAD_DIM, (0, group))
    result = jnp.zeros((row_count, w_query.shape[1]), jnp.bfloat16)
    for step in reversed(range(group)):
        part = attend(mine ^ step, row_count, query, ends, bounds, halo, kv, kv_heads)
        if step > 0:
            part = to_partner(part, step)
        elif group == 1:
            return part
        result = lax.dynamic_update_slice_in_dim(result, part, (mine ^ step) * q_width, 1)
    return result


def solution(mesh):
    size, cores = mesh.shape["ca"], mesh.shape["tp"]
    local_kv = KV_HEADS // cores
    group = 4 if cores == 2 and local_kv == 4 and size % 4 == 0 else 1
    placed = (P("ca", None), P(), P("ca", "tp"), P("ca", "tp"), P("ca", "tp"))
    body = functools.partial(per_device, group, size // group, cores)
    return jax.shard_map(body, mesh=mesh, in_specs=placed, out_specs=P("ca", "tp"), check_vma=False)
```

profile of v0, /device:TPU:22, one launch (start us, length us, event | category | flops | bytes accessed | tf_op | source)
XLA Modules:
  0.0 245.1 jit_solution(8683666531501435552)
XLA Ops:
  6.5 2.0 constant_dynamic-slice_fusion.2
  10.1 2.5 %collective-permute-start.11 = (bf16[256,768]{1,0:T(8,128)(2,1)S(1)}, bf16[256,768]{1,0:T(8,128)(2,1)S(1)}, u32[]{:S(2)}, u32[]{:S(2)}) collective-permute-start(bf16[256,768]{1,0:T(8,128)(2,1)S(1)} %pad_maximum_fusion.6), channel_id=1, source_target_pairs={{0,6},{2,4},{4,2},{6,0},{8,14},{10,12},{12,10},{14,8},{16,22},{18,... | collective-permute-start | bytes 1179656 | tf_op jit(solution)/shard_map/ppermute | solution.py:267
  12.6 8.3 %collective-permute-done.9 = bf16[256,768]{1,0:T(8,128)(2,1)S(1)} collective-permute-done((bf16[256,768]{1,0:T(8,128)(2,1)S(1)}, bf16[256,768]{1,0:T(8,128)(2,1)S(1)}, u32[]{:S(2)}, u32[]{:S(2)}) %collective-permute-start.9) | collective-permute-done | bytes 393248 | tf_op jit(solution)/shard_map/ppermute | solution.py:267
  21.0 7.6 %collective-permute-done.10 = bf16[256,768]{1,0:T(8,128)(2,1)S(1)} collective-permute-done((bf16[256,768]{1,0:T(8,128)(2,1)S(1)}, bf16[256,768]{1,0:T(8,128)(2,1)S(1)}, u32[]{:S(2)}, u32[]{:S(2)}) %collective-permute-start.10) | collective-permute-done | bytes 393248 | tf_op jit(solution)/shard_map/ppermute | solution.py:267
  31.0 133.5 %conditional.1 = (bf16[2048,4096]{1,0:T(8,128)(2,1)}, f32[2048,128]{1,0:T(8,128)}, f32[2048,128]{1,0:T(8,128)}, s32[8]{0:T(128)S(1)}, s32[3,8]{1,0:T(4,128)S(1)}, /*index=5*/bf16[2048,256]{1,0:T(8,128)(2,1)}) conditional(s32[]{:T(128)} %bitcast.3, () %tuple.13, (s32[]{:T(128)}, bf16[512,4096]{1,0:T(8,128)(2,1)}, bf16[1024,256]{1,0:T(8,128)(2,1)S(1)}, ...), branch_computations={%region_0.1_spmd, %region_1.4_spmd} | conditional | flops 4295811072 | bytes 137440208 | solution.py:370
  31.1 3.3 %constant_dynamic-slice_fusion = bf16[256,4096]{1,0:T(8,128)(2,1)} fusion(bf16[512,4096]{1,0:T(8,128)(2,1)} %get-tuple-element.49.refs_0_, s32[]{:T(128)S(6)} %select_n.13), kind=kLoop, calls=%fused_computation.15 | loop fusion | bytes 4194308 | tf_op jit(solution)/shard_map/dynamic_slice | solution.py:333
  38.5 9.9 %collective-permute-done.1.refs_1_ = bf16[1024,256]{1,0:T(8,128)(2,1)S(1)} collective-permute-done((bf16[1024,256]{1,0:T(8,128)(2,1)S(1)}, bf16[1024,256]{1,0:T(8,128)(2,1)S(1)}, u32[]{:S(2)}, u32[]{:S(2)}) %collective-permute-start.1) | collective-permute-done | bytes 524320 | tf_op jit(solution)/shard_map/cond/branch_1_fun/ppermute | solution.py:274
  50.0 3.7 %fusion = (f32[2048,64]{1,0:T(8,128)S(1)}, f32[2048,64]{1,0:T(8,128)S(1)}, f32[2048,64]{1,0:T(8,128)S(1)}) fusion(f32[64]{0:T(128)S(1)} %multiply_power_fusion, f32[2048]{0:T(1024)S(1)} %get-tuple-element.57), kind=kLoop, calls=%fused_computation.4 | loop fusion | flops 262144 | bytes 1581312 | tf_op jit(solution)/shard_map/cond/branch_1_fun/neg | solution.py:34
  53.7 31.6 %collective-permute-done.2.refs_2_ = bf16[1024,256]{1,0:T(8,128)(2,1)S(1)} collective-permute-done((bf16[1024,256]{1,0:T(8,128)(2,1)S(1)}, bf16[1024,256]{1,0:T(8,128)(2,1)S(1)}, u32[]{:S(2)}, u32[]{:S(2)}) %collective-permute-start.2) | collective-permute-done | bytes 524320 | tf_op jit(solution)/shard_map/cond/branch_1_fun/ppermute | solution.py:274
  85.2 4.4 %collective-permute-start.3 = (bf16[1024,256]{1,0:T(8,128)(2,1)S(1)}, bf16[1024,256]{1,0:T(8,128)(2,1)S(1)}, u32[]{:S(2)}, u32[]{:S(2)}) collective-permute-start(bf16[1024,256]{1,0:T(8,128)(2,1)S(1)} %collective-permute-done.2.refs_2_), channel_id=1, source_target_pairs={{0,8},{2,10},{4,12},{6,14},{8,16},{10,18},{12,20},{14,22},{16,24},... | collective-permute-start | bytes 1572872 | tf_op jit(solution)/shard_map/cond/branch_1_fun/ppermute | solution.py:274
  89.7 4.2 %branch_1_fun.7.refs_6_.refs_4_ = bf16[2048,4096]{1,0:T(8,128)(2,1)} custom-call(s32[3]{0:T(128)S(1)} %get-tuple-element.27.place, bf16[512,4096]{1,0:T(8,128)(2,1)} %get-tuple-element.49.refs_0_), custom_call_target="tpu_custom_call" | custom-call | tf_op jit(solution)/shard_map/cond/branch_1_fun/pallas_call | solution.py:121
  93.9 2.0 pad_maximum_fusion
  95.8 25.6 %collective-permute-done.3.refs_1_.refs_3_ = bf16[1024,256]{1,0:T(8,128)(2,1)S(1)} collective-permute-done((bf16[1024,256]{1,0:T(8,128)(2,1)S(1)}, bf16[1024,256]{1,0:T(8,128)(2,1)S(1)}, u32[]{:S(2)}, u32[]{:S(2)}) %collective-permute-start.3) | collective-permute-done | bytes 524320 | tf_op jit(solution)/shard_map/cond/branch_1_fun/ppermute | solution.py:274
  124.0 3.3 %collective-permute-done.5.refs_1_ = bf16[256,4096]{1,0:T(8,128)(2,1)S(1)} collective-permute-done((bf16[256,4096]{1,0:T(8,128)(2,1)}, bf16[256,4096]{1,0:T(8,128)(2,1)S(1)}, u32[]{:S(2)}, u32[]{:S(2)}) %collective-permute-start.5) | collective-permute-done | bytes 2097184 | tf_op jit(solution)/shard_map/cond/branch_1_fun/ppermute | solution.py:329
  127.3 3.0 %collective-permute-done.7.refs_3_ = bf16[256,4096]{1,0:T(8,128)(2,1)S(1)} collective-permute-done((bf16[256,4096]{1,0:T(8,128)(2,1)}, bf16[256,4096]{1,0:T(8,128)(2,1)S(1)}, u32[]{:S(2)}, u32[]{:S(2)}) %collective-permute-start.7) | collective-permute-done | bytes 2097184 | tf_op jit(solution)/shard_map/cond/branch_1_fun/ppermute | solution.py:329
  130.3 1.6 copy-done.3
  131.9 5.1 %branch_1_fun.9.x_ref.refs_2_ = bf16[2048,4096]{1,0:T(8,128)(2,1)} custom-call(s32[3]{0:T(128)S(1)} %get-tuple-element.27.place, bf16[256,4096]{1,0:T(8,128)(2,1)S(1)} %copy-done.3, bf16[256,4096]{1,0:T(8,128)(2,1)S(1)} %collective-permute-done.5.refs_1_, bf16[256,4096]{1,0:T(8,128)(2,1)} %collective-permute-done.6.refs_2_, ...), custom_call_target="tpu_custom_call", output_to_operand_aliasing={{}: (5, {})} | custom-call | tf_op jit(solution)/shard_map/cond/branch_1_fun/pallas_call | solution.py:121
  137.0 8.8 %branch_1_fun.10.refs_1_.refs_6_ = bf16[2048,256]{1,0:T(8,128)(2,1)} custom-call(s32[3]{0:T(128)S(1)} %get-tuple-element.27.place, bf16[2048,4096]{1,0:T(8,128)(2,1)} %branch_1_fun.9.x_ref.refs_2_, bf16[1024,256]{1,0:T(8,128)(2,1)S(1)} %copy-done.16, bf16[1024,256]{1,0:T(8,128)(2,1)S(1)} %collective-permute-done.1.refs_1_, bf16[1024,256]{1,0:T(8,128)(2,1)S(1)} %copy-done.7, ...), custom_call_target="tpu_custom_call" | custom-call | flops 3221225472 | bytes 14680064 | tf_op jit(solution)/shard_map/cond/branch_1_fun/pallas_call | solution.py:78
  145.8 3.9 %collective-permute-done.4.refs_0_ = bf16[256,4096]{1,0:T(8,128)(2,1)S(1)} collective-permute-done((bf16[256,4096]{1,0:T(8,128)(2,1)}, bf16[256,4096]{1,0:T(8,128)(2,1)S(1)}, u32[]{:S(2)}, u32[]{:S(2)}) %collective-permute-start.4) | collective-permute-done | bytes 2097184 | tf_op jit(solution)/shard_map/cond/branch_1_fun/ppermute | solution.py:326
  151.0 4.4 %collective-permute-done.8.refs_1_ = bf16[256,4096]{1,0:T(8,128)(2,1)S(1)} collective-permute-done((bf16[256,4096]{1,0:T(8,128)(2,1)}, bf16[256,4096]{1,0:T(8,128)(2,1)S(1)}, u32[]{:S(2)}, u32[]{:S(2)}) %collective-permute-start.8) | collective-permute-done | bytes 2097184 | tf_op jit(solution)/shard_map/cond/branch_1_fun/ppermute | solution.py:329
  155.4 1.6 copy-done.1
  157.0 2.5 %branch_1_fun.12.x_ref = bf16[2048,4096]{1,0:T(8,128)(2,1)} custom-call(s32[3]{0:T(128)S(1)} %get-tuple-element.27.place, bf16[256,4096]{1,0:T(8,128)(2,1)S(1)} %copy-done.1, bf16[256,4096]{1,0:T(8,128)(2,1)S(1)} %collective-permute-done.8.refs_1_, bf16[2048,4096]{1,0:T(8,128)(2,1)} %branch_1_fun.9.x_ref.refs_2_), custom_call_target="tpu_custom_call", output_to_operand_aliasing={{}: (3, {})} | custom-call | tf_op jit(solution)/shard_map/cond/branch_1_fun/pallas_call | solution.py:121
  159.6 5.0 %branch_1_fun.13 = bf16[2048,256]{1,0:T(8,128)(2,1)} custom-call(s32[3]{0:T(128)S(1)} %get-tuple-element.27.place, bf16[2048,4096]{1,0:T(8,128)(2,1)} %branch_1_fun.12.x_ref, bf16[1024,256]{1,0:T(8,128)(2,1)S(1)} %copy-done.17, bf16[1024,256]{1,0:T(8,128)(2,1)S(1)} %collective-permute-done.1.refs_1_, ...), custom_call_target="tpu_custom_call", output_to_operand_aliasing={{}: (8, {})} | custom-call | flops 1073741824 | bytes 6291456 | tf_op jit(solution)/shard_map/cond/branch_1_fun/pallas_call | solution.py:78
  165.8 3.7 %collective-permute-start.12 = (bf16[1536,256]{1,0:T(8,128)(2,1)S(1)}, bf16[1536,256]{1,0:T(8,128)(2,1)S(1)}, u32[]{:S(2)}, u32[]{:S(2)}) collective-permute-start(bf16[1536,256]{1,0:T(8,128)(2,1)S(1)} %slice.37), channel_id=1, source_target_pairs={{0,8},{2,10},{4,12},{6,14},{8,16},{10,18},{12,20},{14,22},{16,24},... | collective-permute-start | bytes 2359304 | tf_op jit(solution)/shard_map/ppermute | solution.py:386
  169.5 1.9 copy-done.9
  172.6 13.4 %shard_map.57.q_ref = bf16[2048,512]{1,0:T(8,128)(2,1)S(1)} custom-call(s32[3]{0:T(128)S(1)} %pad_add_fusion.1.place, bf16[2048,4096]{1,0:T(8,128)(2,1)} %get-tuple-element.41.x_ref, bf16[1024,512]{1,0:T(8,128)(2,1)S(1)} %copy-done.10, bf16[3072,512]{1,0:T(8,128)(2,1)S(1)} %copy-done.9, f32[2048,128]{1,0:T(8,128)} %get-tuple-element.42.refs_2_, ...), custom_call_target="tpu_custom_call" | custom-call | flops 8589934592 | bytes 20971520 | tf_op jit(solution)/shard_map/pallas_call | solution.py:78
  187.3 9.7 %shard_map.58 = bf16[512,512]{1,0:T(8,128)(2,1)S(1)} custom-call(s32[1]{0:T(128)} %bitcast.2.first, s32[3,8]{1,0:T(4,128)S(1)} %get-tuple-element.39.bounds, s32[8]{0:T(128)S(1)} %get-tuple-element.40.ends, bf16[2048,512]{1,0:T(8,128)(2,1)S(1)} %shard_map.57.q_ref, bf16[1536,256]{1,0:T(8,128)(2,1)S(1)} %collective-permute-done.12.halo_ref, ...), custom_call_target="tpu_custom_call" | custom-call | flops 1073741824 | bytes 1048576 | tf_op jit(solution)/shard_map/pallas_call | solution.py:205
  197.1 2.3 collective-permute-start.13
  201.0 6.5 %shard_map.59 = bf16[512,512]{1,0:T(8,128)(2,1)S(1)} custom-call(s32[1]{0:T(128)} %bitcast.7.first, s32[3,8]{1,0:T(4,128)S(1)} %get-tuple-element.39.bounds, s32[8]{0:T(128)S(1)} %get-tuple-element.40.ends, bf16[2048,512]{1,0:T(8,128)(2,1)S(1)} %copy-done.12, bf16[1536,256]{1,0:T(8,128)(2,1)S(1)} %collective-permute-done.12.halo_ref, ...), custom_call_target="tpu_custom_call" | custom-call | flops 1073741824 | bytes 1048576 | tf_op jit(solution)/shard_map/pallas_call | solution.py:205
  210.7 7.8 %shard_map.60 = bf16[512,512]{1,0:T(8,128)(2,1)S(1)} custom-call(s32[1]{0:T(128)} %bitcast.8.first, s32[3,8]{1,0:T(4,128)S(1)} %get-tuple-element.39.bounds, s32[8]{0:T(128)S(1)} %get-tuple-element.40.ends, bf16[2048,512]{1,0:T(8,128)(2,1)S(1)} %copy-done.13, bf16[1536,256]{1,0:T(8,128)(2,1)S(1)} %collective-permute-done.12.halo_ref, ...), custom_call_target="tpu_custom_call" | custom-call | flops 1073741824 | bytes 1048576 | tf_op jit(solution)/shard_map/pallas_call | solution.py:205
  218.5 3.9 %collective-permute-start.15 = (bf16[512,512]{1,0:T(8,128)(2,1)S(1)}, bf16[512,512]{1,0:T(8,128)(2,1)}, u32[]{:S(2)}, u32[]{:S(2)}) collective-permute-start(bf16[512,512]{1,0:T(8,128)(2,1)S(1)} %shard_map.60), channel_id=1, source_target_pairs={{0,2},{2,0},{4,6},{6,4},{8,10},{10,8},{12,14},{14,12},{16,18},{18,... | collective-permute-start | bytes 1572872 | tf_op jit(solution)/shard_map/ppermute | solution.py:267
  224.0 10.6 %shard_map.61 = bf16[512,512]{1,0:T(8,128)(2,1)S(1)} custom-call(s32[1]{0:T(128)} %bitcast.9.first, s32[3,8]{1,0:T(4,128)S(1)} %get-tuple-element.39.bounds, s32[8]{0:T(128)S(1)} %get-tuple-element.40.ends, bf16[2048,512]{1,0:T(8,128)(2,1)S(1)} %copy-done.14, bf16[1536,256]{1,0:T(8,128)(2,1)S(1)} %collective-permute-done.12.halo_ref, ...), custom_call_target="tpu_custom_call" | custom-call | flops 1073741824 | bytes 1048576 | tf_op jit(solution)/shard_map/pallas_call | solution.py:205
  (105 shorter events, 26.5 us)
Async XLA Ops:
  6.5 2.2 copy-start.19
  6.5 162.9 %all-gather.3.cloned.1.call-start = ((), (), s32[]{:S(2)}) async-start(), calls=%async_computation | async-start | bytes 1310720 | tf_op jit(solution)/shard_map/all_gather | solution.py:271
  8.6 160.9 %all-gather.5.cloned.1.call-start = ((), (), s32[]{:S(2)}) async-start(), calls=%async_computation.1 | async-start | bytes 3932160 | tf_op jit(solution)/shard_map/all_gather | solution.py:271
  8.9 12.1 %collective-permute-start.9 = (bf16[256,768]{1,0:T(8,128)(2,1)S(1)}, bf16[256,768]{1,0:T(8,128)(2,1)S(1)}, u32[]{:S(2)}, u32[]{:S(2)}) collective-permute-start(bf16[256,768]{1,0:T(8,128)(2,1)S(1)} %pad_maximum_fusion.4), channel_id=1, source_target_pairs={{0,2},{2,0},{4,6},{6,4},{8,10},{10,8},{12,14},{14,12},{16,18},{18,... | collective-permute-start | bytes 1179656 | tf_op jit(solution)/shard_map/ppermute | solution.py:267
  9.5 19.1 %collective-permute-start.10 = (bf16[256,768]{1,0:T(8,128)(2,1)S(1)}, bf16[256,768]{1,0:T(8,128)(2,1)S(1)}, u32[]{:S(2)}, u32[]{:S(2)}) collective-permute-start(bf16[256,768]{1,0:T(8,128)(2,1)S(1)} %pad_maximum_fusion.5), channel_id=1, source_target_pairs={{0,4},{2,6},{4,0},{6,2},{8,12},{10,14},{12,8},{14,10},{16,20},{18,... | collective-permute-start | bytes 1179656 | tf_op jit(solution)/shard_map/ppermute | solution.py:267
  10.1 18.5 %collective-permute-start.11 = (bf16[256,768]{1,0:T(8,128)(2,1)S(1)}, bf16[256,768]{1,0:T(8,128)(2,1)S(1)}, u32[]{:S(2)}, u32[]{:S(2)}) collective-permute-start(bf16[256,768]{1,0:T(8,128)(2,1)S(1)} %pad_maximum_fusion.6), channel_id=1, source_target_pairs={{0,6},{2,4},{4,2},{6,0},{8,14},{10,12},{12,10},{14,8},{16,22},{18,... | collective-permute-start | bytes 1179656 | tf_op jit(solution)/shard_map/ppermute | solution.py:267
  28.6 2.4 copy-start.25
  31.1 5.3 %copy-start.15 = (bf16[1024,256]{1,0:T(8,128)(2,1)}, bf16[1024,256]{1,0:T(8,128)(2,1)S(1)}, u32[]{:S(2)}) copy-start(bf16[1024,256]{1,0:T(8,128)(2,1)S(1)} %get-tuple-element.30.refs_0_) | copy-start | bytes 1572868 | tf_op jit(solution)/shard_map/cond
  34.4 87.0 %collective-permute-start = (bf16[256,4096]{1,0:T(8,128)(2,1)}, bf16[256,4096]{1,0:T(8,128)(2,1)S(1)}, u32[]{:S(2)}, u32[]{:S(2)}) collective-permute-start(bf16[256,4096]{1,0:T(8,128)(2,1)} %constant_dynamic-slice_fusion), channel_id=1, source_target_pairs={{0,2},{1,5},{2,0},{3,7},{4,6},{5,1},{6,4},{7,3},{8,10},{9,13},{10,... | collective-permute-start | bytes 6291464 | tf_op jit(solution)/shard_map/cond/branch_1_fun/ppermute | solution.py:326
  35.9 87.0 %collective-permute-start.6 = (bf16[256,4096]{1,0:T(8,128)(2,1)}, bf16[256,4096]{1,0:T(8,128)(2,1)}, u32[]{:S(2)}, u32[]{:S(2)}) collective-permute-start(bf16[256,4096]{1,0:T(8,128)(2,1)} %constant_dynamic-slice_fusion), channel_id=1, source_target_pairs={{0,4},{1,3},{2,6},{3,1},{4,0},{5,7},{6,2},{7,5},{8,12},{9,11},{10,... | collective-permute-start | bytes 6291464 | tf_op jit(solution)/shard_map/cond/branch_1_fun/ppermute | solution.py:326
  36.4 12.0 %collective-permute-start.1 = (bf16[1024,256]{1,0:T(8,128)(2,1)S(1)}, bf16[1024,256]{1,0:T(8,128)(2,1)S(1)}, u32[]{:S(2)}, u32[]{:S(2)}) collective-permute-start(bf16[1024,256]{1,0:T(8,128)(2,1)S(1)} %get-tuple-element.30.refs_0_), channel_id=1, source_target_pairs={{0,8},{2,10},{4,12},{6,14},{8,16},{10,18},{12,20},{14,22},{16,24},... | collective-permute-start | bytes 1572872 | tf_op jit(solution)/shard_map/cond/branch_1_fun/ppermute | solution.py:274
  48.4 36.9 %collective-permute-start.2 = (bf16[1024,256]{1,0:T(8,128)(2,1)S(1)}, bf16[1024,256]{1,0:T(8,128)(2,1)S(1)}, u32[]{:S(2)}, u32[]{:S(2)}) collective-permute-start(bf16[1024,256]{1,0:T(8,128)(2,1)S(1)} %collective-permute-done.1.refs_1_), channel_id=1, source_target_pairs={{0,8},{2,10},{4,12},{6,14},{8,16},{10,18},{12,20},{14,22},{16,24},... | collective-permute-start | bytes 1572872 | tf_op jit(solution)/shard_map/cond/branch_1_fun/ppermute | solution.py:274
  85.2 8.6 %copy-start.6 = (bf16[1024,256]{1,0:T(8,128)(2,1)}, bf16[1024,256]{1,0:T(8,128)(2,1)S(1)}, u32[]{:S(2)}) copy-start(bf16[1024,256]{1,0:T(8,128)(2,1)S(1)} %collective-permute-done.2.refs_2_) | copy-start | bytes 1572868 | tf_op jit(solution)/shard_map/cond
  85.2 36.2 %collective-permute-start.3 = (bf16[1024,256]{1,0:T(8,128)(2,1)S(1)}, bf16[1024,256]{1,0:T(8,128)(2,1)S(1)}, u32[]{:S(2)}, u32[]{:S(2)}) collective-permute-start(bf16[1024,256]{1,0:T(8,128)(2,1)S(1)} %collective-permute-done.2.refs_2_), channel_id=1, source_target_pairs={{0,8},{2,10},{4,12},{6,14},{8,16},{10,18},{12,20},{14,22},{16,24},... | collective-permute-start | bytes 1572872 | tf_op jit(solution)/shard_map/cond/branch_1_fun/ppermute | solution.py:274
  89.6 31.8 %copy-start.21 = (s32[3,8]{1,0:T(4,128)}, s32[3,8]{1,0:T(4,128)S(1)}, u32[]{:S(2)}) copy-start(s32[3,8]{1,0:T(4,128)S(1)} %pad_add_fusion.refs_5_) | copy-start | bytes 292 | tf_op jit(solution)/shard_map/cond
  93.8 27.6 %copy-start.23 = (s32[8]{0:T(128)}, s32[8]{0:T(128)S(1)}, u32[]{:S(2)}) copy-start(s32[8]{0:T(128)S(1)} %broadcast_subtract_fusion.1.refs_4_) | copy-start | bytes 100 | tf_op jit(solution)/shard_map/cond
  122.9 4.4 %collective-permute-start.5 = (bf16[256,4096]{1,0:T(8,128)(2,1)}, bf16[256,4096]{1,0:T(8,128)(2,1)S(1)}, u32[]{:S(2)}, u32[]{:S(2)}) collective-permute-start(bf16[256,4096]{1,0:T(8,128)(2,1)} %branch_1_fun.8.refs_0_), channel_id=1, source_target_pairs={{0,1},{1,0},{2,3},{3,2},{4,5},{5,4},{6,7},{7,6},{8,9},{9,8},{10,11... | collective-permute-start | bytes 6291464 | tf_op jit(solution)/shard_map/cond/branch_1_fun/ppermute | solution.py:329
  122.9 7.4 %collective-permute-start.7 = (bf16[256,4096]{1,0:T(8,128)(2,1)}, bf16[256,4096]{1,0:T(8,128)(2,1)S(1)}, u32[]{:S(2)}, u32[]{:S(2)}) collective-permute-start(bf16[256,4096]{1,0:T(8,128)(2,1)} %collective-permute-done.6.refs_2_), channel_id=1, source_target_pairs={{0,1},{1,0},{2,3},{3,2},{4,5},{5,4},{6,7},{7,6},{8,9},{9,8},{10,11... | collective-permute-start | bytes 6291464 | tf_op jit(solution)/shard_map/cond/branch_1_fun/ppermute | solution.py:329
  123.4 26.2 %collective-permute-start.4 = (bf16[256,4096]{1,0:T(8,128)(2,1)}, bf16[256,4096]{1,0:T(8,128)(2,1)S(1)}, u32[]{:S(2)}, u32[]{:S(2)}) collective-permute-start(bf16[256,4096]{1,0:T(8,128)(2,1)} %branch_1_fun.8.refs_0_), channel_id=1, source_target_pairs={{0,4},{1,3},{2,6},{3,1},{4,0},{5,7},{6,2},{7,5},{8,12},{9,11},{10,... | collective-permute-start | bytes 6291464 | tf_op jit(solution)/shard_map/cond/branch_1_fun/ppermute | solution.py:326
  131.9 5.1 %copy-start.5 = (bf16[1024,256]{1,0:T(8,128)(2,1)S(1)}, bf16[1024,256]{1,0:T(8,128)(2,1)}, u32[]{:S(2)}) copy-start(bf16[1024,256]{1,0:T(8,128)(2,1)} %copy-done.4) | copy-start | bytes 1572868 | tf_op jit(solution)/shard_map/cond
  131.9 5.1 %copy-start.7 = (bf16[1024,256]{1,0:T(8,128)(2,1)S(1)}, bf16[1024,256]{1,0:T(8,128)(2,1)}, u32[]{:S(2)}) copy-start(bf16[1024,256]{1,0:T(8,128)(2,1)} %copy-done.6) | copy-start | bytes 1572868 | tf_op jit(solution)/shard_map/cond
  131.9 5.1 %copy-start.16 = (bf16[1024,256]{1,0:T(8,128)(2,1)S(1)}, bf16[1024,256]{1,0:T(8,128)(2,1)}, u32[]{:S(2)}) copy-start(bf16[1024,256]{1,0:T(8,128)(2,1)} %copy-done.15) | copy-start | bytes 1572868 | tf_op jit(solution)/shard_map/cond
  151.0 4.4 %collective-permute-start.8 = (bf16[256,4096]{1,0:T(8,128)(2,1)}, bf16[256,4096]{1,0:T(8,128)(2,1)S(1)}, u32[]{:S(2)}, u32[]{:S(2)}) collective-permute-start(bf16[256,4096]{1,0:T(8,128)(2,1)} %branch_1_fun.11.refs_0_), channel_id=1, source_target_pairs={{0,1},{1,0},{2,3},{3,2},{4,5},{5,4},{6,7},{7,6},{8,9},{9,8},{10,11... | collective-permute-start | bytes 6291464 | tf_op jit(solution)/shard_map/cond/branch_1_fun/ppermute | solution.py:329
  157.0 2.5 %copy-start.8 = (bf16[1024,256]{1,0:T(8,128)(2,1)S(1)}, bf16[1024,256]{1,0:T(8,128)(2,1)}, u32[]{:S(2)}) copy-start(bf16[1024,256]{1,0:T(8,128)(2,1)} %copy-done.6) | copy-start | bytes 1572868 | tf_op jit(solution)/shard_map/cond
  157.0 2.6 %copy-start.17 = (bf16[1024,256]{1,0:T(8,128)(2,1)S(1)}, bf16[1024,256]{1,0:T(8,128)(2,1)}, u32[]{:S(2)}) copy-start(bf16[1024,256]{1,0:T(8,128)(2,1)} %copy-done.15) | copy-start | bytes 1572868 | tf_op jit(solution)/shard_map/cond
  159.5 5.0 %copy-start.22 = (s32[3,8]{1,0:T(4,128)S(1)}, s32[3,8]{1,0:T(4,128)}, u32[]{:S(2)}) copy-start(s32[3,8]{1,0:T(4,128)} %copy-done.21) | copy-start | bytes 292 | tf_op jit(solution)/shard_map/cond
  159.5 5.0 %copy-start.24 = (s32[8]{0:T(128)S(1)}, s32[8]{0:T(128)}, u32[]{:S(2)}) copy-start(s32[8]{0:T(128)} %copy-done.23) | copy-start | bytes 100 | tf_op jit(solution)/shard_map/cond
  165.8 21.6 %collective-permute-start.12 = (bf16[1536,256]{1,0:T(8,128)(2,1)S(1)}, bf16[1536,256]{1,0:T(8,128)(2,1)S(1)}, u32[]{:S(2)}, u32[]{:S(2)}) collective-permute-start(bf16[1536,256]{1,0:T(8,128)(2,1)S(1)} %slice.37), channel_id=1, source_target_pairs={{0,8},{2,10},{4,12},{6,14},{8,16},{10,18},{12,20},{14,22},{16,24},... | collective-permute-start | bytes 2359304 | tf_op jit(solution)/shard_map/ppermute | solution.py:386
  186.0 11.0 %copy-start.11 = (bf16[2048,512]{1,0:T(8,128)(2,1)}, bf16[2048,512]{1,0:T(8,128)(2,1)S(1)}, u32[]{:S(2)}) copy-start(bf16[2048,512]{1,0:T(8,128)(2,1)S(1)} %shard_map.57.q_ref) | copy-start | bytes 6291460
  197.1 37.5 %collective-permute-start.13 = (bf16[512,512]{1,0:T(8,128)(2,1)S(1)}, bf16[512,512]{1,0:T(8,128)(2,1)S(1)}, u32[]{:S(2)}, u32[]{:S(2)}) collective-permute-start(bf16[512,512]{1,0:T(8,128)(2,1)S(1)} %shard_map.58), channel_id=1, source_target_pairs={{0,6},{2,4},{4,2},{6,0},{8,14},{10,12},{12,10},{14,8},{16,22},{18,... | collective-permute-start | bytes 1572872 | tf_op jit(solution)/shard_map/ppermute | solution.py:267
  207.5 27.4 %collective-permute-start.14 = (bf16[512,512]{1,0:T(8,128)(2,1)S(1)}, bf16[512,512]{1,0:T(8,128)(2,1)S(1)}, u32[]{:S(2)}, u32[]{:S(2)}) collective-permute-start(bf16[512,512]{1,0:T(8,128)(2,1)S(1)} %shard_map.59), channel_id=1, source_target_pairs={{0,4},{2,6},{4,0},{6,2},{8,12},{10,14},{12,8},{14,10},{16,20},{18,... | collective-permute-start | bytes 1572872 | tf_op jit(solution)/shard_map/ppermute | solution.py:267
  218.5 16.5 %collective-permute-start.15 = (bf16[512,512]{1,0:T(8,128)(2,1)S(1)}, bf16[512,512]{1,0:T(8,128)(2,1)}, u32[]{:S(2)}, u32[]{:S(2)}) collective-permute-start(bf16[512,512]{1,0:T(8,128)(2,1)S(1)} %shard_map.60), channel_id=1, source_target_pairs={{0,2},{2,0},{4,6},{6,4},{8,10},{10,8},{12,14},{14,12},{16,18},{18,... | collective-permute-start | bytes 1572872 | tf_op jit(solution)/shard_map/ppermute | solution.py:267
  (12 other events, 18.2 us)
Sparse Core Ops, SparseCore 0:
  8.9 28.4 all-gather.2
  39.0 84.2 all-gather.4
where the time goes:
time: 249 us; the launch traced here: 245 us
  waiting for transfers between devices  98.9 us (40%)
  Pallas kernels  73.6 us (30%)
  starting transfers between devices  25.8 us (10%)
  local copies, waits for them, and re-layouts  24.5 us (10%)
  between operations  14.4 us (6%)
  other arithmetic  7.73 us (3%)
    ppermute x3, waiting for transfers between devices, forwarded(): lax.ppermute(block, 'ca', [(i, (i + group) % (group * lines)) for i in de...  67.1 us
    pallas_call x4, Pallas kernels, attend(): pl.pallas_call(kernel, out_shape=jax.ShapeDtypeStruct((chunk_rows, width)...  34.7 us
    pallas_call x3, Pallas kernels, project(): pl.pallas_call(functools.partial(project_kernel, rope_heads, layout, len(...  27.2 us
    ppermute x6, waiting for transfers between devices, to_partner(): return lax.ppermute(block, 'ca', [(i, i ^ step) for i in devices])  15.9 us
    pallas_call x3, Pallas kernels, put(): pl.pallas_call(functools.partial(put_kernel, targets), out_shape=jax.Shap...  11.7 us
    ppermute x6, starting transfers between devices, to_partner(): return lax.ppermute(block, 'ca', [(i, i ^ step) for i in devices])  11.5 us
    ppermute x3, waiting for transfers between devices, swap(): lax.ppermute(block, both, [(i * 2 + c, i * 2 + 1 - c) for i in devices fo...  10.7 us
    unnamed x20, local copies, waits for them, and re-layouts  9.22 us
  transfers between devices with their start and end apart: 18, of which 10 were waited for; matrix products, arithmetic and copies ran while one was open for 5% of the time, Pallas kernels for 26%

commit v1 on v0

--- a/solution.py
+++ b/solution.py
@@ -16,8 +16,8 @@
 LOGIT_CAP = 5.0
 TILE = 256
 PUT_BYTES = 20 * 1024 * 1024
-PROJECT_BYTES = 30 * 1024 * 1024
-VMEM_BYTES = 48 * 1024 * 1024
+PROJECT_BYTES = 58 * 1024 * 1024
+VMEM_BYTES = 58 * 1024 * 1024
 
 
 def doc_starts(lengths, positions):
@@ -129,7 +129,7 @@
     )(place, *arrays)
 
 
-def attend_kernel(kv_heads, share, halo_rows, first, bounds, ends, q_ref, halo_ref, kv_ref, out_ref, kv_all, sums, totals):
+def attend_kernel(kv_heads, share, halo_rows, first, bounds, ends, q_ref, halo_ref, kv_ref, out_ref, kv_all, q_all, sums, totals):
     tile_index = pl.program_id(0)
 
     @pl.when(tile_index == 0)
@@ -138,6 +138,8 @@
         kv_all[halo_rows:, :] = kv_ref[...]
 
     tile = q_ref.shape[0]
+    for head in range(kv_heads * share):
+        q_all[head * tile : (head + 1) * tile, :] = q_ref[:, head * HEAD_DIM : (head + 1) * HEAD_DIM]
     place = bounds[0, first[0] + tile_index]
     first_start = bounds[1, first[0] + tile_index]
     last_start = bounds[2, first[0] + tile_index]
@@ -162,18 +164,19 @@
             keys = kv_all[rows, kv_head * HEAD_DIM : (kv_head + 1) * HEAD_DIM]
             at = (kv_heads + kv_head) * HEAD_DIM
             values = kv_all[rows, at : at + HEAD_DIM]
-            for member in range(share):
-                head = kv_head * share + member
-                query = q_ref[:, head * HEAD_DIM : (head + 1) * HEAD_DIM]
-                raw = lax.dot_general(query, keys, (((1,), (1,)), ((), ())), preferred_element_type=jnp.float32)
-                weights = jnp.exp2(outer * jnp.tanh(raw * inner))
-                if masked:
-                    weights = jnp.where(allowed, weights, 0.0)
-                partial = weights[:, :HEAD_DIM]
-                for part in range(1, TILE // HEAD_DIM):
-                    partial = partial + weights[:, part * HEAD_DIM : (part + 1) * HEAD_DIM]
-                totals[head] += partial
-                sums[head] += jnp.dot(weights.astype(jnp.bfloat16), values, preferred_element_type=jnp.float32)
+            members = slice(kv_head * share * tile, (kv_head + 1) * share * tile)
+            raw = lax.dot_general(
+                q_all[members, :], keys, (((1,), (1,)), ((), ())), preferred_element_type=jnp.float32
+            )
+            weights = jnp.exp2(outer * jnp.tanh(raw * inner))
+            if masked:
+                weights = weights.reshape(share, tile, TILE)
+                weights = jnp.where(allowed[None], weights, 0.0).reshape(share * tile, TILE)
+            partial = weights[:, :HEAD_DIM]
+            for part in range(1, TILE // HEAD_DIM):
+                partial = partial + weights[:, part * HEAD_DIM : (part + 1) * HEAD_DIM]
+            totals[members, :] += partial
+            sums[members, :] += jnp.dot(weights.astype(jnp.bfloat16), values, preferred_element_type=jnp.float32)
 
     def either(block, carry):
         begin = block * TILE
@@ -191,8 +194,9 @@
 
     lax.fori_loop(first_block, last_block + 1, either, 0)
     for head in range(kv_heads * share):
-        denominator = jnp.sum(totals[head], axis=1, keepdims=True)
-        out_ref[:, head * HEAD_DIM : (head + 1) * HEAD_DIM] = (sums[head] / denominator).astype(out_ref.dtype)
+        rows = slice(head * tile, (head + 1) * tile)
+        denominator = jnp.sum(totals[rows, :], axis=1, keepdims=True)
+        out_ref[:, head * HEAD_DIM : (head + 1) * HEAD_DIM] = (sums[rows, :] / denominator).astype(out_ref.dtype)
 
 
 def attend(chunk, chunk_rows, query, ends, bounds, halo, kv, kv_heads):
@@ -216,8 +220,9 @@
             out_specs=pl.BlockSpec((TILE, width), lambda i, c, s, e: (i, 0)),
             scratch_shapes=[
                 pltpu.VMEM((halo_rows + kv.shape[0], kv.shape[1]), jnp.bfloat16),
-                pltpu.VMEM((heads, TILE, HEAD_DIM), jnp.float32),
-                pltpu.VMEM((heads, TILE, HEAD_DIM), jnp.float32),
+                pltpu.VMEM((heads * TILE, HEAD_DIM), jnp.bfloat16),
+                pltpu.VMEM((heads * TILE, HEAD_DIM), jnp.float32),
+                pltpu.VMEM((heads * TILE, HEAD_DIM), jnp.float32),
             ],
         ),
         compiler_params=pltpu.CompilerParams(vmem_limit_bytes=VMEM_BYTES),
@@ -315,10 +320,9 @@
     place = jnp.stack([mine, line, core]).astype(jnp.int32)
     if group > 1:
         slices = [slice_for(mine)] + [to_partner(slice_for(mine ^ step), step) for step in range(1, group)]
-        members = range(group)
-        own_q = along_lines(slices[0][:, :q_width])
+        own_slices = along_lines(slices[0])
         rest_q = along_lines(jnp.concatenate([a[:, :q_width] for a in slices[1:]]))
-        rest_kv = jnp.concatenate([a[:, q_width:] for a in slices])
+        rest_kv = jnp.concatenate([a[:, q_width:] for a in slices[1:]])
         both = ("ca", "tp")
 
         def cross(block, steps):
@@ -353,13 +357,9 @@
             mates = [swap(block) for block in (near, other)]
             first = [(near, home(1, 2, 0)), (mates[0], home(1, 2, 1)), (other, home(2, 1, 0)), (mates[1], home(2, 1, 1))]
             early = put(place, group_rows, first, everything)
-            weights = from_lines(held, 0, members)
-            kv = project(group, place, early, weights, kv_width, lists[0], lists[1], kv_heads, (0, group - 1))
-            far = after(far, kv)
             last = [(far, home(3, 3, 0)), (swap(far), home(3, 3, 1))]
             everything = put(place, group_rows, last, early)
-            kv = project(group, place, everything, weights, kv_width, lists[0], lists[1], kv_heads, (group - 1, 1), kv)
-            return everything, lists, kv
+            return everything, lists, tuple(held[1:])
 
         def nothing(*operands):
             shapes = jax.eval_shape(share, *operands)
@@ -367,17 +367,19 @@
 
         known = rest_kv[0, 0].astype(jnp.float32)
         operands = (tokens, own_half, rest_kv)
-        all_tokens, known_tables, kv = lax.cond(known == known, share, nothing, *operands)
-        q_weights = [gathered(own_q, (0, q_width), 0, [0]), gathered(rest_q, (0, q_width), 0, members[1:])]
+        all_tokens, known_tables, held = lax.cond(known == known, share, nothing, *operands)
+        others = range(1, group)
+        kv_weights = [gathered(own_slices, (q_width // kv_width, kv_width), 0, [0])]
+        kv_weights += from_lines((rest_kv, *held), 0, others)
+        q_weights = [gathered(own_slices, (0, q_width), 0, [0]), gathered(rest_q, (0, q_width), 0, others)]
     else:
         all_tokens, known_tables = tokens, tables()
         own = along_lines(slice_for(mine))
         kv_weights = [gathered(own, (q_width // kv_width, kv_width), 0, [0])]
         q_weights = [gathered(own, (0, q_width), 0, [0])]
-        kv = project(group, place, tokens, kv_weights, kv_width, *known_tables[:2], kv_heads, (0, 1))
-
     cosine, sine, ends, bounds = known_tables
 
+    kv = project(group, place, all_tokens, kv_weights, kv_width, cosine, sine, kv_heads, (0, group))
     hops = -(-halo_rows // group_rows)
     pieces, moving = [], kv
     for hop in range(hops):

time: 249 us -> 222 us (0.89)
  the two profiles are of different devices: /device:TPU:22 before, /device:TPU:16 now
where the time goes in v1:
time: 222 us; the launch traced here: 223 us
  waiting for transfers between devices  83.5 us (38%)
  Pallas kernels  75.2 us (34%)
  starting transfers between devices  27.3 us (12%)
  between operations  14.9 us (7%)
  local copies, waits for them, and re-layouts  13.8 us (6%)
  other arithmetic  7.54 us (3%)
    pallas_call x4, Pallas kernels, attend(): pl.pallas_call(kernel, out_shape=jax.ShapeDtypeStruct((chunk_rows, width)...  37.6 us
    ppermute x3, waiting for transfers between devices, forwarded(): lax.ppermute(block, 'ca', [(i, (i + group) % (group * lines)) for i in de...  36.3 us
    pallas_call x2, Pallas kernels, project(): pl.pallas_call(functools.partial(project_kernel, rope_heads, layout, len(...  26 us
    ppermute x3, waiting for transfers between devices, cross(): return lax.ppermute(block, both, pairs)  24.5 us
    ppermute x6, waiting for transfers between devices, to_partner(): return lax.ppermute(block, 'ca', [(i, i ^ step) for i in devices])  20.8 us
    pallas_call x3, Pallas kernels, put(): pl.pallas_call(functools.partial(put_kernel, targets), out_shape=jax.Shap...  11.6 us
    ppermute x6, starting transfers between devices, to_partner(): return lax.ppermute(block, 'ca', [(i, i ^ step) for i in devices])  9.83 us
    ppermute x3, starting transfers between devices, forwarded(): lax.ppermute(block, 'ca', [(i, (i + group) % (group * lines)) for i in de...  7.49 us
  transfers between devices with their start and end apart: 18, of which 8 were waited for; matrix products, arithmetic and copies ran while one was open for 5% of the time, Pallas kernels for 30%

profile of v1, /device:TPU:16, one launch (start us, length us, event | category | flops | bytes accessed | tf_op | source)
XLA Modules:
  0.0 222.6 jit_solution(13729162238233739806)
XLA Ops:
  6.5 1.3 constant_dynamic-slice_fusion.3
  8.9 1.6 collective-permute-start.10
  10.5 1.5 collective-permute-start.11
  12.7 15.6 %collective-permute-done.10 = bf16[256,768]{1,0:T(8,128)(2,1)S(1)} collective-permute-done((bf16[256,768]{1,0:T(8,128)(2,1)S(1)}, bf16[256,768]{1,0:T(8,128)(2,1)S(1)}, u32[]{:S(2)}, u32[]{:S(2)}) %collective-permute-start.10) | collective-permute-done | bytes 393248 | tf_op jit(solution)/shard_map/ppermute | solution.py:272
  33.4 96.9 %conditional.1 = (bf16[2048,4096]{1,0:T(8,128)(2,1)}, f32[2048,128]{1,0:T(8,128)S(1)}, f32[2048,128]{1,0:T(8,128)}, s32[8]{0:T(128)S(1)}, s32[3,8]{1,0:T(4,128)S...) conditional(s32[]{:T(128)} %bitcast.3, () %tuple.13, ...), branch_computations={%region_0.1_spmd, %region_1.4_spmd} | conditional | flops 844094 | bytes 99167160 | solution.py:370
  33.4 3.2 %constant_dynamic-slice_fusion = bf16[256,4096]{1,0:T(8,128)(2,1)} fusion(bf16[512,4096]{1,0:T(8,128)(2,1)} %get-tuple-element.53.refs_0_, s32[]{:T(128)S(6)} %select_n.13), kind=kLoop, calls=%fused_computation.15 | loop fusion | bytes 4194308 | tf_op jit(solution)/shard_map/dynamic_slice | solution.py:337
  36.5 1.5 collective-permute-start
  38.0 1.5 collective-permute-start.7
  39.5 1.6 collective-permute-start.1
  41.6 11.3 %collective-permute-done.1 = bf16[768,256]{1,0:T(8,128)(2,1)S(1)} collective-permute-done((bf16[768,256]{1,0:T(8,128)(2,1)S(1)}, bf16[768,256]{1,0:T(8,128)(2,1)S(1)}, u32[]{:S(2)}, u32[]{:S(2)}) %collective-permute-start.1) | collective-permute-done | bytes 393248 | tf_op jit(solution)/shard_map/cond/branch_1_fun/ppermute | solution.py:279
  52.9 1.7 collective-permute-start.2
  54.6 3.7 %fusion = (f32[2048,64]{1,0:T(8,128)S(1)}, f32[2048,64]{1,0:T(8,128)S(1)}, f32[2048,64]{1,0:T(8,128)S(1)}) fusion(f32[64]{0:T(128)S(1)} %multiply_power_fusion, f32[2048]{0:T(1024)S(1)} %get-tuple-element.61), kind=kLoop, calls=%fused_computation.4 | loop fusion | flops 262144 | bytes 1581312 | tf_op jit(solution)/shard_map/cond/branch_1_fun/neg | solution.py:34
  58.3 5.2 %collective-permute-done.2 = bf16[768,256]{1,0:T(8,128)(2,1)S(1)} collective-permute-done((bf16[768,256]{1,0:T(8,128)(2,1)S(1)}, bf16[768,256]{1,0:T(8,128)(2,1)S(1)}, u32[]{:S(2)}, u32[]{:S(2)}) %collective-permute-start.2) | collective-permute-done | bytes 393248 | tf_op jit(solution)/shard_map/cond/branch_1_fun/ppermute | solution.py:279
  63.5 4.2 %collective-permute-start.3 = (bf16[768,256]{1,0:T(8,128)(2,1)S(1)}, bf16[768,256]{1,0:T(8,128)(2,1)S(1)}, u32[]{:S(2)}, u32[]{:S(2)}) collective-permute-start(bf16[768,256]{1,0:T(8,128)(2,1)S(1)} %collective-permute-done.2), channel_id=1, source_target_pairs={{0,8},{2,10},{4,12},{6,14},{8,16},{10,18},{12,20},{14,22},{16,24},... | collective-permute-start | bytes 1179656 | tf_op jit(solution)/shard_map/cond/branch_1_fun/ppermute | solution.py:279
  67.8 4.2 %branch_1_fun.4.refs_6_.refs_4_ = bf16[2048,4096]{1,0:T(8,128)(2,1)} custom-call(s32[3]{0:T(128)S(1)} %get-tuple-element.27.place, bf16[512,4096]{1,0:T(8,128)(2,1)} %get-tuple-element.53.refs_0_), custom_call_target="tpu_custom_call" | custom-call | tf_op jit(solution)/shard_map/cond/branch_1_fun/pallas_call | solution.py:121
  72.0 1.6 pad_maximum_fusion
  73.6 19.8 %collective-permute-done.3.refs_1_ = bf16[768,256]{1,0:T(8,128)(2,1)S(1)} collective-permute-done((bf16[768,256]{1,0:T(8,128)(2,1)S(1)}, bf16[768,256]{1,0:T(8,128)(2,1)S(1)}, u32[]{:S(2)}, u32[]{:S(2)}) %collective-permute-start.3) | collective-permute-done | bytes 393248 | tf_op jit(solution)/shard_map/cond/branch_1_fun/ppermute | solution.py:279
  96.6 24.5 %collective-permute-done.4.refs_0_ = bf16[256,4096]{1,0:T(8,128)(2,1)S(1)} collective-permute-done((bf16[256,4096]{1,0:T(8,128)(2,1)}, bf16[256,4096]{1,0:T(8,128)(2,1)S(1)}, u32[]{:S(2)}, u32[]{:S(2)}) %collective-permute-start.4) | collective-permute-done | bytes 2097184 | tf_op jit(solution)/shard_map/cond/branch_1_fun/ppermute | solution.py:330
  121.1 1.6 copy-done.1
  122.7 4.9 %branch_1_fun.6.refs_2_ = bf16[2048,4096]{1,0:T(8,128)(2,1)} custom-call(s32[3]{0:T(128)S(1)} %get-tuple-element.27.place, bf16[256,4096]{1,0:T(8,128)(2,1)S(1)} %copy-done.1, bf16[256,4096]{1,0:T(8,128)(2,1)S(1)} %collective-permute-done.6.refs_1_, bf16[256,4096]{1,0:T(8,128)(2,1)} %collective-permute-done.7.refs_2_, ...), custom_call_target="tpu_custom_call", output_to_operand_aliasing={{}: (5, {})} | custom-call | tf_op jit(solution)/shard_map/cond/branch_1_fun/pallas_call | solution.py:121
  127.7 2.5 %branch_1_fun.7 = bf16[2048,4096]{1,0:T(8,128)(2,1)} custom-call(s32[3]{0:T(128)S(1)} %get-tuple-element.27.place, bf16[256,4096]{1,0:T(8,128)(2,1)S(1)} %collective-permute-done.4.refs_0_, bf16[256,4096]{1,0:T(8,128)(2,1)S(1)} %collective-permute-done.5.refs_1_, bf16[2048,4096]{1,0:T(8,128)(2,1)} %branch_1_fun.6.refs_2_), custom_call_target="tpu_custom_call", output_to_operand_aliasing={{}: (3, {})} | custom-call | tf_op jit(solution)/shard_map/cond/branch_1_fun/pallas_call | solution.py:121
  130.3 10.5 %shard_map.58.kv_ref = bf16[2048,256]{1,0:T(8,128)(2,1)} custom-call(s32[3]{0:T(128)S(1)} %pad_add_fusion.1.place, bf16[2048,4096]{1,0:T(8,128)(2,1)} %get-tuple-element.43.x_ref, bf16[1024,768]{1,0:T(8,128)(2,1)} %all-gather.3.cloned.1.call-done.refs_0_, bf16[768,256]{1,0:T(8,128)(2,1)} %copy-done.7, bf16[768,256]{1,0:T(8,128)(2,1)S(1)} %get-tuple-element.46.refs_2_, ...), custom_call_target="tpu_custom_call" | custom-call | flops 4294967296 | bytes 18874368 | tf_op jit(solution)/shard_map/pallas_call | solution.py:78
  142.0 5.1 %collective-permute-start.12 = (bf16[1536,256]{1,0:T(8,128)(2,1)S(1)}, bf16[1536,256]{1,0:T(8,128)(2,1)S(1)}, u32[]{:S(2)}, u32[]{:S(2)}) collective-permute-start(bf16[1536,256]{1,0:T(8,128)(2,1)S(1)} %slice.48), channel_id=1, source_target_pairs={{0,8},{2,10},{4,12},{6,14},{8,16},{10,18},{12,20},{14,22},{16,24},... | collective-permute-start | bytes 2359304 | tf_op jit(solution)/shard_map/ppermute | solution.py:388
  147.2 15.5 %shard_map.57.q_ref = bf16[2048,512]{1,0:T(8,128)(2,1)} custom-call(s32[3]{0:T(128)S(1)} %pad_add_fusion.1.place, bf16[2048,4096]{1,0:T(8,128)(2,1)} %get-tuple-element.43.x_ref, bf16[1024,768]{1,0:T(8,128)(2,1)} %all-gather.3.cloned.1.call-done.refs_0_, bf16[3072,512]{1,0:T(8,128)(2,1)} %all-gather.5.cloned.1.call-done.refs_1_, ...), custom_call_target="tpu_custom_call" | custom-call | flops 8589934592 | bytes 20971520 | tf_op jit(solution)/shard_map/pallas_call | solution.py:78
  162.7 1.9 collective-permute-done.12.halo_ref
  165.4 9.5 %shard_map.59 = bf16[512,512]{1,0:T(8,128)(2,1)} custom-call(s32[1]{0:T(128)} %bitcast.2.first, s32[3,8]{1,0:T(4,128)S(1)} %get-tuple-element.41.bounds, s32[8]{0:T(128)S(1)} %get-tuple-element.42.ends, bf16[2048,512]{1,0:T(8,128)(2,1)} %shard_map.57.q_ref, bf16[1536,256]{1,0:T(8,128)(2,1)} %copy-done.19, bf16[2048,256]{1,0:T(8,128)(2,1)} %shard_map.58.kv_ref), custom_call_target="tpu_custom_call" | custom-call | flops 1073741824 | bytes 1048576 | tf_op jit(solution)/shard_map/pallas_call | solution.py:209
  174.9 2.3 %collective-permute-start.13 = (bf16[512,512]{1,0:T(8,128)(2,1)}, bf16[512,512]{1,0:T(8,128)(2,1)S(1)}, u32[]{:S(2)}, u32[]{:S(2)}) collective-permute-start(bf16[512,512]{1,0:T(8,128)(2,1)} %shard_map.59), channel_id=1, source_target_pairs={{0,6},{2,4},{4,2},{6,0},{8,14},{10,12},{12,10},{14,8},{16,22},{18,... | collective-permute-start | bytes 1572872 | tf_op jit(solution)/shard_map/ppermute | solution.py:272
  177.2 6.9 %shard_map.60 = bf16[512,512]{1,0:T(8,128)(2,1)} custom-call(s32[1]{0:T(128)} %bitcast.7.first, s32[3,8]{1,0:T(4,128)S(1)} %get-tuple-element.41.bounds, s32[8]{0:T(128)S(1)} %get-tuple-element.42.ends, bf16[2048,512]{1,0:T(8,128)(2,1)} %shard_map.57.q_ref, bf16[1536,256]{1,0:T(8,128)(2,1)} %copy-done.19, bf16[2048,256]{1,0:T(8,128)(2,1)} %shard_map.58.kv_ref), custom_call_target="tpu_custom_call" | custom-call | flops 1073741824 | bytes 1048576 | tf_op jit(solution)/shard_map/pallas_call | solution.py:209
  184.1 3.9 %collective-permute-start.14 = (bf16[512,512]{1,0:T(8,128)(2,1)}, bf16[512,512]{1,0:T(8,128)(2,1)S(1)}, u32[]{:S(2)}, u32[]{:S(2)}) collective-permute-start(bf16[512,512]{1,0:T(8,128)(2,1)} %shard_map.60), channel_id=1, source_target_pairs={{0,4},{2,6},{4,0},{6,2},{8,12},{10,14},{12,8},{14,10},{16,20},{18,... | collective-permute-start | bytes 1572872 | tf_op jit(solution)/shard_map/ppermute | solution.py:272
  188.0 12.0 %shard_map.61 = bf16[512,512]{1,0:T(8,128)(2,1)} custom-call(s32[1]{0:T(128)} %bitcast.8.first, s32[3,8]{1,0:T(4,128)S(1)} %get-tuple-element.41.bounds, s32[8]{0:T(128)S(1)} %get-tuple-element.42.ends, bf16[2048,512]{1,0:T(8,128)(2,1)} %shard_map.57.q_ref, bf16[1536,256]{1,0:T(8,128)(2,1)} %copy-done.19, bf16[2048,256]{1,0:T(8,128)(2,1)} %shard_map.58.kv_ref), custom_call_target="tpu_custom_call" | custom-call | flops 1073741824 | bytes 1048576 | tf_op jit(solution)/shard_map/pallas_call | solution.py:209
  200.0 9.2 %shard_map.62 = bf16[512,512]{1,0:T(8,128)(2,1)} custom-call(s32[1]{0:T(128)} %bitcast.9.first, s32[3,8]{1,0:T(4,128)S(1)} %get-tuple-element.41.bounds, s32[8]{0:T(128)S(1)} %get-tuple-element.42.ends, bf16[2048,512]{1,0:T(8,128)(2,1)} %shard_map.57.q_ref, bf16[1536,256]{1,0:T(8,128)(2,1)} %copy-done.19, bf16[2048,256]{1,0:T(8,128)(2,1)} %shard_map.58.kv_ref), custom_call_target="tpu_custom_call" | custom-call | flops 1073741824 | bytes 1048576 | tf_op jit(solution)/shard_map/pallas_call | solution.py:209
  209.6 3.9 %collective-permute-done.15 = bf16[512,512]{1,0:T(8,128)(2,1)S(1)} collective-permute-done((bf16[512,512]{1,0:T(8,128)(2,1)}, bf16[512,512]{1,0:T(8,128)(2,1)S(1)}, u32[]{:S(2)}, u32[]{:S(2)}) %collective-permute-start.15) | collective-permute-done | bytes 524320 | tf_op jit(solution)/shard_map/ppermute | solution.py:272
  (94 shorter events, 13.7 us)
Async XLA Ops:
  6.5 123.7 %all-gather.3.cloned.1.call-start = ((), (), s32[]{:S(2)}) async-start(), calls=%async_computation | async-start | bytes 1966080 | tf_op jit(solution)/shard_map/all_gather | solution.py:276
  8.8 138.4 %all-gather.5.cloned.1.call-start = ((), (), s32[]{:S(2)}) async-start(), calls=%async_computation.1 | async-start | bytes 3932160 | tf_op jit(solution)/shard_map/all_gather | solution.py:276
  8.9 19.3 %collective-permute-start.10 = (bf16[256,768]{1,0:T(8,128)(2,1)S(1)}, bf16[256,768]{1,0:T(8,128)(2,1)S(1)}, u32[]{:S(2)}, u32[]{:S(2)}) collective-permute-start(bf16[256,768]{1,0:T(8,128)(2,1)S(1)} %pad_maximum_fusion.4), channel_id=1, source_target_pairs={{0,4},{2,6},{4,0},{6,2},{8,12},{10,14},{12,8},{14,10},{16,20},{18,... | collective-permute-start | bytes 1179656 | tf_op jit(solution)/shard_map/ppermute | solution.py:272
  10.5 17.8 %collective-permute-start.11 = (bf16[256,768]{1,0:T(8,128)(2,1)S(1)}, bf16[256,768]{1,0:T(8,128)(2,1)S(1)}, u32[]{:S(2)}, u32[]{:S(2)}) collective-permute-start(bf16[256,768]{1,0:T(8,128)(2,1)S(1)} %pad_maximum_fusion.5), channel_id=1, source_target_pairs={{0,6},{2,4},{4,2},{6,0},{8,14},{10,12},{12,10},{14,8},{16,22},{18,... | collective-permute-start | bytes 1179656 | tf_op jit(solution)/shard_map/ppermute | solution.py:272
  12.1 17.5 %collective-permute-start.9 = (bf16[256,768]{1,0:T(8,128)(2,1)S(1)}, bf16[256,768]{1,0:T(8,128)(2,1)S(1)}, u32[]{:S(2)}, u32[]{:S(2)}) collective-permute-start(bf16[256,768]{1,0:T(8,128)(2,1)S(1)} %pad_maximum_fusion.3), channel_id=1, source_target_pairs={{0,2},{2,0},{4,6},{6,4},{8,10},{10,8},{12,14},{14,12},{16,18},{18,... | collective-permute-start | bytes 1179656 | tf_op jit(solution)/shard_map/ppermute | solution.py:272
  29.6 3.0 %copy-start.20 = (s32[8]{0:T(128)S(1)}, s32[8]{0:T(128)}, u32[]{:S(2)}) copy-start(s32[8]{0:T(128)} %param.8) | copy-start | bytes 100
  36.5 56.9 %collective-permute-start = (bf16[256,4096]{1,0:T(8,128)(2,1)}, bf16[256,4096]{1,0:T(8,128)(2,1)S(1)}, u32[]{:S(2)}, u32[]{:S(2)}) collective-permute-start(bf16[256,4096]{1,0:T(8,128)(2,1)} %constant_dynamic-slice_fusion), channel_id=1, source_target_pairs={{0,2},{1,5},{2,0},{3,7},{4,6},{5,1},{6,4},{7,3},{8,10},{9,13},{10,... | collective-permute-start | bytes 6291464 | tf_op jit(solution)/shard_map/cond/branch_1_fun/ppermute | solution.py:330
  38.0 58.1 %collective-permute-start.7 = (bf16[256,4096]{1,0:T(8,128)(2,1)}, bf16[256,4096]{1,0:T(8,128)(2,1)}, u32[]{:S(2)}, u32[]{:S(2)}) collective-permute-start(bf16[256,4096]{1,0:T(8,128)(2,1)} %constant_dynamic-slice_fusion), channel_id=1, source_target_pairs={{0,4},{1,3},{2,6},{3,1},{4,0},{5,7},{6,2},{7,5},{8,12},{9,11},{10,... | collective-permute-start | bytes 6291464 | tf_op jit(solution)/shard_map/cond/branch_1_fun/ppermute | solution.py:330
  39.5 13.4 %collective-permute-start.1 = (bf16[768,256]{1,0:T(8,128)(2,1)S(1)}, bf16[768,256]{1,0:T(8,128)(2,1)S(1)}, u32[]{:S(2)}, u32[]{:S(2)}) collective-permute-start(bf16[768,256]{1,0:T(8,128)(2,1)S(1)} %get-tuple-element.30), channel_id=1, source_target_pairs={{0,8},{2,10},{4,12},{6,14},{8,16},{10,18},{12,20},{14,22},{16,24},... | collective-permute-start | bytes 1179656 | tf_op jit(solution)/shard_map/cond/branch_1_fun/ppermute | solution.py:279
  41.6 51.8 %copy-start.17 = (s32[8]{0:T(128)}, s32[8]{0:T(128)S(1)}, u32[]{:S(2)}) copy-start(s32[8]{0:T(128)S(1)} %broadcast_subtract_fusion.1.refs_4_) | copy-start | bytes 100 | tf_op jit(solution)/shard_map/cond
  52.9 19.1 %copy-start.8 = (bf16[768,256]{1,0:T(8,128)(2,1)}, bf16[768,256]{1,0:T(8,128)(2,1)S(1)}, u32[]{:S(2)}) copy-start(bf16[768,256]{1,0:T(8,128)(2,1)S(1)} %collective-permute-done.1) | copy-start | bytes 1179652 | tf_op jit(solution)/shard_map/cond
  52.9 10.7 %collective-permute-start.2 = (bf16[768,256]{1,0:T(8,128)(2,1)S(1)}, bf16[768,256]{1,0:T(8,128)(2,1)S(1)}, u32[]{:S(2)}, u32[]{:S(2)}) collective-permute-start(bf16[768,256]{1,0:T(8,128)(2,1)S(1)} %collective-permute-done.1), channel_id=1, source_target_pairs={{0,8},{2,10},{4,12},{6,14},{8,16},{10,18},{12,20},{14,22},{16,24},... | collective-permute-start | bytes 1179656 | tf_op jit(solution)/shard_map/cond/branch_1_fun/ppermute | solution.py:279
  63.5 8.5 %copy-start.10 = (bf16[768,256]{1,0:T(8,128)(2,1)}, bf16[768,256]{1,0:T(8,128)(2,1)S(1)}, u32[]{:S(2)}) copy-start(bf16[768,256]{1,0:T(8,128)(2,1)S(1)} %collective-permute-done.2) | copy-start | bytes 1179652 | tf_op jit(solution)/shard_map/cond
  63.5 29.9 %collective-permute-start.3 = (bf16[768,256]{1,0:T(8,128)(2,1)S(1)}, bf16[768,256]{1,0:T(8,128)(2,1)S(1)}, u32[]{:S(2)}, u32[]{:S(2)}) collective-permute-start(bf16[768,256]{1,0:T(8,128)(2,1)S(1)} %collective-permute-done.2), channel_id=1, source_target_pairs={{0,8},{2,10},{4,12},{6,14},{8,16},{10,18},{12,20},{14,22},{16,24},... | collective-permute-start | bytes 1179656 | tf_op jit(solution)/shard_map/cond/branch_1_fun/ppermute | solution.py:279
  72.0 21.4 %copy-start.15 = (s32[3,8]{1,0:T(4,128)}, s32[3,8]{1,0:T(4,128)S(1)}, u32[]{:S(2)}) copy-start(s32[3,8]{1,0:T(4,128)S(1)} %pad_add_fusion.refs_5_) | copy-start | bytes 292 | tf_op jit(solution)/shard_map/cond
  73.6 21.1 %copy-start.2 = (f32[2048,128]{1,0:T(8,128)}, f32[2048,128]{1,0:T(8,128)S(1)}, u32[]{:S(2)}) copy-start(f32[2048,128]{1,0:T(8,128)S(1)} %get-tuple-element.89.refs_2_) | copy-start | bytes 3145732 | tf_op jit(solution)/shard_map/cond
  94.8 26.2 %collective-permute-start.4 = (bf16[256,4096]{1,0:T(8,128)(2,1)}, bf16[256,4096]{1,0:T(8,128)(2,1)S(1)}, u32[]{:S(2)}, u32[]{:S(2)}) collective-permute-start(bf16[256,4096]{1,0:T(8,128)(2,1)} %branch_1_fun.5.refs_0_), channel_id=1, source_target_pairs={{0,4},{1,3},{2,6},{3,1},{4,0},{5,7},{6,2},{7,5},{8,12},{9,11},{10,... | collective-permute-start | bytes 6291464 | tf_op jit(solution)/shard_map/cond/branch_1_fun/ppermute | solution.py:330
  96.1 25.0 %collective-permute-start.6 = (bf16[256,4096]{1,0:T(8,128)(2,1)}, bf16[256,4096]{1,0:T(8,128)(2,1)S(1)}, u32[]{:S(2)}, u32[]{:S(2)}) collective-permute-start(bf16[256,4096]{1,0:T(8,128)(2,1)} %branch_1_fun.5.refs_0_), channel_id=1, source_target_pairs={{0,1},{1,0},{2,3},{3,2},{4,5},{5,4},{6,7},{7,6},{8,9},{9,8},{10,11... | collective-permute-start | bytes 6291464 | tf_op jit(solution)/shard_map/cond/branch_1_fun/ppermute | solution.py:333
  96.1 25.0 %collective-permute-start.8 = (bf16[256,4096]{1,0:T(8,128)(2,1)}, bf16[256,4096]{1,0:T(8,128)(2,1)S(1)}, u32[]{:S(2)}, u32[]{:S(2)}) collective-permute-start(bf16[256,4096]{1,0:T(8,128)(2,1)} %collective-permute-done.7.refs_2_), channel_id=1, source_target_pairs={{0,1},{1,0},{2,3},{3,2},{4,5},{5,4},{6,7},{7,6},{8,9},{9,8},{10,11... | collective-permute-start | bytes 6291464 | tf_op jit(solution)/shard_map/cond/branch_1_fun/ppermute | solution.py:333
  121.1 6.6 %collective-permute-start.5 = (bf16[256,4096]{1,0:T(8,128)(2,1)S(1)}, bf16[256,4096]{1,0:T(8,128)(2,1)S(1)}, u32[]{:S(2)}, u32[]{:S(2)}) collective-permute-start(bf16[256,4096]{1,0:T(8,128)(2,1)S(1)} %collective-permute-done.4.refs_0_), channel_id=1, source_target_pairs={{0,1},{1,0},{2,3},{3,2},{4,5},{5,4},{6,7},{7,6},{8,9},{9,8},{10,11... | collective-permute-start | bytes 6291464 | tf_op jit(solution)/shard_map/cond/branch_1_fun/ppermute | solution.py:333
  121.1 1.6 copy-start.1
  127.6 2.6 %copy-start.3 = (f32[2048,128]{1,0:T(8,128)S(1)}, f32[2048,128]{1,0:T(8,128)}, u32[]{:S(2)}) copy-start(f32[2048,128]{1,0:T(8,128)} %copy-done.2) | copy-start | bytes 3145732 | tf_op jit(solution)/shard_map/cond
  127.6 2.6 %copy-start.5 = (bf16[768,256]{1,0:T(8,128)(2,1)S(1)}, bf16[768,256]{1,0:T(8,128)(2,1)}, u32[]{:S(2)}) copy-start(bf16[768,256]{1,0:T(8,128)(2,1)} %copy-done.4) | copy-start | bytes 1179652 | tf_op jit(solution)/shard_map/cond
  127.7 2.6 %copy-start.9 = (bf16[768,256]{1,0:T(8,128)(2,1)S(1)}, bf16[768,256]{1,0:T(8,128)(2,1)}, u32[]{:S(2)}) copy-start(bf16[768,256]{1,0:T(8,128)(2,1)} %copy-done.8) | copy-start | bytes 1179652 | tf_op jit(solution)/shard_map/cond
  127.7 2.6 %copy-start.11 = (bf16[768,256]{1,0:T(8,128)(2,1)S(1)}, bf16[768,256]{1,0:T(8,128)(2,1)}, u32[]{:S(2)}) copy-start(bf16[768,256]{1,0:T(8,128)(2,1)} %copy-done.10) | copy-start | bytes 1179652 | tf_op jit(solution)/shard_map/cond
  127.7 2.6 %copy-start.16 = (s32[3,8]{1,0:T(4,128)S(1)}, s32[3,8]{1,0:T(4,128)}, u32[]{:S(2)}) copy-start(s32[3,8]{1,0:T(4,128)} %copy-done.15) | copy-start | bytes 292 | tf_op jit(solution)/shard_map/cond
  127.7 2.6 %copy-start.18 = (s32[8]{0:T(128)S(1)}, s32[8]{0:T(128)}, u32[]{:S(2)}) copy-start(s32[8]{0:T(128)} %copy-done.17) | copy-start | bytes 100 | tf_op jit(solution)/shard_map/cond
  142.0 22.5 %collective-permute-start.12 = (bf16[1536,256]{1,0:T(8,128)(2,1)S(1)}, bf16[1536,256]{1,0:T(8,128)(2,1)S(1)}, u32[]{:S(2)}, u32[]{:S(2)}) collective-permute-start(bf16[1536,256]{1,0:T(8,128)(2,1)S(1)} %slice.48), channel_id=1, source_target_pairs={{0,8},{2,10},{4,12},{6,14},{8,16},{10,18},{12,20},{14,22},{16,24},... | collective-permute-start | bytes 2359304 | tf_op jit(solution)/shard_map/ppermute | solution.py:388
  174.9 34.2 %collective-permute-start.13 = (bf16[512,512]{1,0:T(8,128)(2,1)}, bf16[512,512]{1,0:T(8,128)(2,1)S(1)}, u32[]{:S(2)}, u32[]{:S(2)}) collective-permute-start(bf16[512,512]{1,0:T(8,128)(2,1)} %shard_map.59), channel_id=1, source_target_pairs={{0,6},{2,4},{4,2},{6,0},{8,14},{10,12},{12,10},{14,8},{16,22},{18,... | collective-permute-start | bytes 1572872 | tf_op jit(solution)/shard_map/ppermute | solution.py:272
  184.1 25.4 %collective-permute-start.14 = (bf16[512,512]{1,0:T(8,128)(2,1)}, bf16[512,512]{1,0:T(8,128)(2,1)S(1)}, u32[]{:S(2)}, u32[]{:S(2)}) collective-permute-start(bf16[512,512]{1,0:T(8,128)(2,1)} %shard_map.60), channel_id=1, source_target_pairs={{0,4},{2,6},{4,0},{6,2},{8,12},{10,14},{12,8},{14,10},{16,20},{18,... | collective-permute-start | bytes 1572872 | tf_op jit(solution)/shard_map/ppermute | solution.py:272
  200.0 13.5 %collective-permute-start.15 = (bf16[512,512]{1,0:T(8,128)(2,1)}, bf16[512,512]{1,0:T(8,128)(2,1)S(1)}, u32[]{:S(2)}, u32[]{:S(2)}) collective-permute-start(bf16[512,512]{1,0:T(8,128)(2,1)} %shard_map.61), channel_id=1, source_target_pairs={{0,2},{2,0},{4,6},{6,4},{8,10},{10,8},{12,14},{14,12},{16,18},{18,... | collective-permute-start | bytes 1572872 | tf_op jit(solution)/shard_map/ppermute | solution.py:272
  209.4 5.5 %copy-start.12 = (bf16[512,512]{1,0:T(8,128)(2,1)S(1)}, bf16[512,512]{1,0:T(8,128)(2,1)}, u32[]{:S(2)}) copy-start(bf16[512,512]{1,0:T(8,128)(2,1)} %shard_map.62) | copy-start | bytes 1572868
  (7 other events, 8.5 us)
Sparse Core Ops, SparseCore 0:
  9.0 41.8 all-gather.2
  52.4 73.4 all-gather.4

commit v2 on v1

--- a/solution.py
+++ b/solution.py
@@ -16,7 +16,7 @@
 LOGIT_CAP = 5.0
 TILE = 256
 PUT_BYTES = 20 * 1024 * 1024
-PROJECT_BYTES = 58 * 1024 * 1024
+PROJECT_BYTES = 30 * 1024 * 1024
 VMEM_BYTES = 58 * 1024 * 1024
 
 
@@ -344,30 +344,36 @@
             return target
 
 
-        def share(tokens, own_half, rest_kv):
-            near = cross(own_half, (1, 2))
-            other = cross(own_half, (2, 1))
+        near = cross(own_half, (1, 2))
+        other = cross(own_half, (2, 1))
+
+        def prepare(tokens, rest_kv):
             held = [rest_kv]
-            for _ in range(1, lines):
+            for _ in range(1, lines - 1):
                 held.append(forwarded(held[-1]))
-            lists = tables()
-            everything = put(place, group_rows, [(tokens, lambda s: s[0] * row_count)])
-            near = after(near, held[-1], *lists, everything)
+            return put(place, group_rows, [(tokens, lambda s: s[0] * row_count)]), tables(), tuple(held[1:])
+
+        def share(everything, near, other, block):
             far = cross(near, (2, 1))
+            block = forwarded(block)
             mates = [swap(block) for block in (near, other)]
             first = [(near, home(1, 2, 0)), (mates[0], home(1, 2, 1)), (other, home(2, 1, 0)), (mates[1], home(2, 1, 1))]
-            early = put(place, group_rows, first, everything)
+            everything = put(place, group_rows, first, after(everything, block))
+            far = after(far, everything)
             last = [(far, home(3, 3, 0)), (swap(far), home(3, 3, 1))]
-            everything = put(place, group_rows, last, early)
-            return everything, lists, tuple(held[1:])
-
-        def nothing(*operands):
-            shapes = jax.eval_shape(share, *operands)
-            return jax.tree.map(lambda leaf: jnp.zeros(leaf.shape, leaf.dtype), shapes)
-
-        known = rest_kv[0, 0].astype(jnp.float32)
-        operands = (tokens, own_half, rest_kv)
-        all_tokens, known_tables, held = lax.cond(known == known, share, nothing, *operands)
+            return put(place, group_rows, last, everything), block
+
+        def region(body, flag, *operands):
+            def nothing(*operands):
+                shapes = jax.eval_shape(body, *operands)
+                return jax.tree.map(lambda leaf: jnp.zeros(leaf.shape, leaf.dtype), shapes)
+
+            known = flag.reshape(-1)[0].astype(jnp.float32)
+            return lax.cond(known == known, body, nothing, *operands)
+
+        all_tokens, known_tables, held = region(prepare, rest_kv[:1, :1], tokens, rest_kv)
+        all_tokens, furthest = region(share, held[-1][:1, :1], all_tokens, near, other, held[-1])
+        held = (*held, furthest)
         others = range(1, group)
         kv_weights = [gathered(own_slices, (q_width // kv_width, kv_width), 0, [0])]
         kv_weights += from_lines((rest_kv, *held), 0, others)

time: 222 us -> 216 us (0.973)
  starting transfers between devices: 27.3 us -> 19.4 us
  local copies, waits for them, and re-layouts: 13.8 us -> 17.5 us
    ppermute x3, waiting for transfers between devices: 24.5 us -> 15.3 us  [cross(): return lax.ppermute(block, both, pairs)]
    ppermute x3, waiting for transfers between devices: 0.01 us -> 4.3 us  [swap(): lax.ppermute(block, both, [(i * 2 + c, i * 2 + 1 - c) for i in devices fo...]
    ppermute x3, waiting for transfers between devices: 36.3 us -> 40.1 us  [forwarded(): lax.ppermute(block, 'ca', [(i, (i + group) % (group * lines)) for i in de...]
    ppermute x6, starting transfers between devices: 9.83 us -> 6.3 us  [to_partner(): return lax.ppermute(block, 'ca', [(i, i ^ step) for i in devices])]
    unnamed x14 -> x24, local copies, waits for them, and re-layouts: 2.98 us -> 5.95 us
    pallas_call x2, Pallas kernels: 26 us -> 23.4 us  [project(): pl.pallas_call(functools.partial(project_kernel, rope_heads, layout, len(...]
    ppermute x3, starting transfers between devices: 7.49 us -> 4.97 us  [forwarded(): lax.ppermute(block, 'ca', [(i, (i + group) % (group * lines)) for i in de...]
  transfers between devices with their start and end apart: 18 -> 18, of which waited for: 8 -> 9; matrix products, arithmetic and copies ran while one was open for 5% -> 5% of each run, Pallas kernels for 30% -> 30%
where the time goes in v2:
time: 216 us; the launch traced here: 215 us
  waiting for transfers between devices  82.1 us (38%)
  Pallas kernels  73 us (34%)
  starting transfers between devices  19.4 us (9%)
  local copies, waits for them, and re-layouts  17.5 us (8%)
  between operations  16.2 us (8%)
  other arithmetic  6.62 us (3%)
    ppermute x3, waiting for transfers between devices, forwarded(): lax.ppermute(block, 'ca', [(i, (i + group) % (group * lines)) for i in de...  40.1 us
    pallas_call x4, Pallas kernels, attend(): pl.pallas_call(kernel, out_shape=jax.ShapeDtypeStruct((chunk_rows, width)...  36.2 us
    pallas_call x2, Pallas kernels, project(): pl.pallas_call(functools.partial(project_kernel, rope_heads, layout, len(...  23.4 us
    ppermute x6, waiting for transfers between devices, to_partner(): return lax.ppermute(block, 'ca', [(i, i ^ step) for i in devices])  21.3 us
    ppermute x3, waiting for transfers between devices, cross(): return lax.ppermute(block, both, pairs)  15.3 us
    pallas_call x3, Pallas kernels, put(): pl.pallas_call(functools.partial(put_kernel, targets), out_shape=jax.Shap...  13.5 us
    ppermute x6, starting transfers between devices, to_partner(): return lax.ppermute(block, 'ca', [(i, i ^ step) for i in devices])  6.3 us
    unnamed x24, local copies, waits for them, and re-layouts  5.95 us
  transfers between devices with their start and end apart: 18, of which 9 were waited for; matrix products, arithmetic and copies ran while one was open for 5% of the time, Pallas kernels for 30%

profile of v2, /device:TPU:16, one launch (start us, length us, event | category | flops | bytes accessed | tf_op | source)
XLA Modules:
  0.0 214.9 jit_solution(7315636006040925353)
XLA Ops:
  8.9 1.6 collective-permute-start.8
  10.6 1.5 collective-permute-start.9
  12.7 15.6 %collective-permute-done.8 = bf16[256,768]{1,0:T(8,128)(2,1)S(1)} collective-permute-done((bf16[256,768]{1,0:T(8,128)(2,1)S(1)}, bf16[256,768]{1,0:T(8,128)(2,1)S(1)}, u32[]{:S(2)}, u32[]{:S(2)}) %collective-permute-start.8) | collective-permute-done | bytes 393248 | tf_op jit(solution)/shard_map/ppermute | solution.py:272
  30.6 3.1 %constant_dynamic-slice_fusion.3 = bf16[256,4096]{1,0:T(8,128)(2,1)} fusion(bf16[512,4096]{1,0:T(8,128)(2,1)} %param.9, s32[]{:T(128)S(6)} %select_n.58), kind=kLoop, calls=%fused_computation.28 | loop fusion | bytes 4194308 | tf_op jit(solution)/shard_map/dynamic_slice | solution.py:337
  33.8 1.5 collective-permute-start.10
  35.3 1.5 collective-permute-start.11
  38.7 25.2 %conditional.2 = (bf16[2048,4096]{1,0:T(8,128)(2,1)}, f32[2048,128]{1,0:T(8,128)S(1)}, f32[2048,128]{1,0:T(8,128)S(1)}, s32[8]{0:T(128)S(1)}, s32[3,8]{1,0:T(4,1...) conditional(s32[]{:T(128)} %bitcast.3, () %tuple.21, (s32[3]{0:T(128)S(1)}, ...), branch_computations={%region_0.1_spmd, %region_1.4_spmd} | conditional | flops 844090 | bytes 19661006 | solution.py:372
  38.8 1.7 collective-permute-start.5
  40.9 3.7 %fusion = (f32[2048,64]{1,0:T(8,128)S(1)}, f32[2048,64]{1,0:T(8,128)S(1)}, f32[2048,64]{1,0:T(8,128)S(1)}) fusion(f32[64]{0:T(128)S(1)} %multiply_power_fusion, f32[2048]{0:T(1024)S(1)} %get-tuple-element.61), kind=kLoop, calls=%fused_computation.4 | loop fusion | flops 262144 | bytes 1581312 | tf_op jit(solution)/shard_map/cond/branch_1_fun/neg | solution.py:34
  44.7 8.3 %collective-permute-done.5 = bf16[768,256]{1,0:T(8,128)(2,1)} collective-permute-done((bf16[768,256]{1,0:T(8,128)(2,1)S(1)}, bf16[768,256]{1,0:T(8,128)(2,1)}, u32[]{:S(2)}, u32[]{:S(2)}) %collective-permute-start.5) | collective-permute-done | bytes 393248 | tf_op jit(solution)/shard_map/cond/branch_1_fun/ppermute | solution.py:279
  53.0 1.7 collective-permute-start.6
  54.7 4.2 %branch_1_fun.5 = bf16[2048,4096]{1,0:T(8,128)(2,1)} custom-call(s32[3]{0:T(128)S(1)} %get-tuple-element.25.place, bf16[512,4096]{1,0:T(8,128)(2,1)} %get-tuple-element.26.refs_0_), custom_call_target="tpu_custom_call" | custom-call | tf_op jit(solution)/shard_map/cond/branch_1_fun/pallas_call | solution.py:121
  59.5 4.3 %collective-permute-done.6 = bf16[768,256]{1,0:T(8,128)(2,1)} collective-permute-done((bf16[768,256]{1,0:T(8,128)(2,1)}, bf16[768,256]{1,0:T(8,128)(2,1)}, u32[]{:S(2)}, u32[]{:S(2)}) %collective-permute-start.6) | collective-permute-done | bytes 393248 | tf_op jit(solution)/shard_map/cond/branch_1_fun/ppermute | solution.py:279
  66.4 15.3 %collective-permute-done.10 = bf16[256,4096]{1,0:T(8,128)(2,1)} collective-permute-done((bf16[256,4096]{1,0:T(8,128)(2,1)}, bf16[256,4096]{1,0:T(8,128)(2,1)}, u32[]{:S(2)}, u32[]{:S(2)}) %collective-permute-start.10) | collective-permute-done | bytes 2097184 | tf_op jit(solution)/shard_map/ppermute | solution.py:330
  81.7 47.4 %conditional.3 = (bf16[2048,4096]{1,0:T(8,128)(2,1)}, bf16[768,256]{1,0:T(8,128)(2,1)S(1)}) conditional(s32[]{:T(128)} %bitcast.7, () %tuple.23, (bf16[256,4096]{1,0:T(8,128)(2,1)}, bf16[256,4096]{1,0:T(8,128)(2,1)}, bf16[768,256]{1,0:T(8,128)(2,1)}, bf16[2048,4096]{1,0:T(8,128)(2,1)}, s32[3]{0:T(128)S(1)}) %tuple.24), branch_computations={%region_4.5_spmd, %region_5.6_spmd} | conditional | bytes 55050568 | solution.py:372
  82.8 1.6 collective-permute-start.3
  84.4 27.4 %collective-permute-done.3.refs_1_ = bf16[768,256]{1,0:T(8,128)(2,1)S(1)} collective-permute-done((bf16[768,256]{1,0:T(8,128)(2,1)}, bf16[768,256]{1,0:T(8,128)(2,1)S(1)}, u32[]{:S(2)}, u32[]{:S(2)}) %collective-permute-start.3) | collective-permute-done | bytes 393248 | tf_op jit(solution)/shard_map/cond/branch_1_fun/ppermute | solution.py:279
  112.5 6.8 %branch_1_fun.7.refs_1_.refs_2_ = bf16[2048,4096]{1,0:T(8,128)(2,1)} custom-call(s32[3]{0:T(128)S(1)} %get-tuple-element.30.place, bf16[256,4096]{1,0:T(8,128)(2,1)} %get-tuple-element.31.refs_0_, bf16[256,4096]{1,0:T(8,128)(2,1)} %collective-permute-done.1.refs_1_, bf16[256,4096]{1,0:T(8,128)(2,1)} %get-tuple-element.32.refs_2_, ...), custom_call_target="tpu_custom_call", output_to_operand_aliasing={{}: (5, {})} | custom-call | tf_op jit(solution)/shard_map/cond/branch_1_fun/pallas_call | solution.py:121
  120.7 4.3 %collective-permute-done.4.refs_1_ = bf16[256,4096]{1,0:T(8,128)(2,1)S(1)} collective-permute-done((bf16[256,4096]{1,0:T(8,128)(2,1)}, bf16[256,4096]{1,0:T(8,128)(2,1)S(1)}, u32[]{:S(2)}, u32[]{:S(2)}) %collective-permute-start.4) | collective-permute-done | bytes 2097184 | tf_op jit(solution)/shard_map/cond/branch_1_fun/ppermute | solution.py:333
  125.0 1.6 copy-done.1
  126.6 2.5 %branch_1_fun.9 = bf16[2048,4096]{1,0:T(8,128)(2,1)} custom-call(s32[3]{0:T(128)S(1)} %get-tuple-element.30.place, bf16[256,4096]{1,0:T(8,128)(2,1)S(1)} %copy-done.1, bf16[256,4096]{1,0:T(8,128)(2,1)S(1)} %collective-permute-done.4.refs_1_, bf16[2048,4096]{1,0:T(8,128)(2,1)} %branch_1_fun.7.refs_1_.refs_2_), custom_call_target="tpu_custom_call", output_to_operand_aliasing={{}: (3, {})} | custom-call | tf_op jit(solution)/shard_map/cond/branch_1_fun/pallas_call | solution.py:121
  129.2 1.4 copy-done.3
  130.6 9.9 %shard_map.57.kv_ref = bf16[2048,256]{1,0:T(8,128)(2,1)S(1)} custom-call(s32[3]{0:T(128)S(1)} %pad_add_fusion.1.place, bf16[2048,4096]{1,0:T(8,128)(2,1)} %get-tuple-element.48.x_ref, bf16[1024,768]{1,0:T(8,128)(2,1)S(1)} %copy-done.3, bf16[768,256]{1,0:T(8,128)(2,1)S(1)} %pad_maximum_fusion.6.refs_1_, bf16[768,256]{1,0:T(8,128)(2,1)} %get-tuple-element.51.refs_2_, ...), custom_call_target="tpu_custom_call" | custom-call | flops 4294967296 | bytes 18874368 | tf_op jit(solution)/shard_map/pallas_call | solution.py:78
  140.5 3.9 %collective-permute-start.12 = (bf16[1536,256]{1,0:T(8,128)(2,1)S(1)}, bf16[1536,256]{1,0:T(8,128)(2,1)}, u32[]{:S(2)}, u32[]{:S(2)}) collective-permute-start(bf16[1536,256]{1,0:T(8,128)(2,1)S(1)} %slice.52), channel_id=1, source_target_pairs={{0,8},{2,10},{4,12},{6,14},{8,16},{10,18},{12,20},{14,22},{16,24},... | collective-permute-start | bytes 2359304 | tf_op jit(solution)/shard_map/ppermute | solution.py:394
  144.5 1.9 copy-done.5
  146.4 13.5 %shard_map.56.q_ref = bf16[2048,512]{1,0:T(8,128)(2,1)S(1)} custom-call(s32[3]{0:T(128)S(1)} %pad_add_fusion.1.place, bf16[2048,4096]{1,0:T(8,128)(2,1)} %get-tuple-element.48.x_ref, bf16[1024,768]{1,0:T(8,128)(2,1)S(1)} %copy-done.4, bf16[3072,512]{1,0:T(8,128)(2,1)S(1)} %copy-done.5, f32[2048,128]{1,0:T(8,128)} %copy-done.7, f32[2048,128]{1,0:T(8,128)} %copy-done.8), custom_call_target="tpu_custom_call" | custom-call | flops 8589934592 | bytes 20971520 | tf_op jit(solution)/shard_map/pallas_call | solution.py:78
  162.2 8.1 %shard_map.58 = bf16[512,512]{1,0:T(8,128)(2,1)} custom-call(s32[1]{0:T(128)} %bitcast.2.first, s32[3,8]{1,0:T(4,128)S(1)} %get-tuple-element.44.bounds, s32[8]{0:T(128)S(1)} %get-tuple-element.45.ends, bf16[2048,512]{1,0:T(8,128)(2,1)} %copy-done.6, bf16[1536,256]{1,0:T(8,128)(2,1)} %collective-permute-done.12.halo_ref, bf16[2048,256]{1,0:T(8,128)(2,1)} %copy-done.2), custom_call_target="tpu_custom_call" | custom-call | flops 1073741824 | bytes 1048576 | tf_op jit(solution)/shard_map/pallas_call | solution.py:209
  170.2 2.1 collective-permute-start.13
  172.3 9.8 %shard_map.59 = bf16[512,512]{1,0:T(8,128)(2,1)} custom-call(s32[1]{0:T(128)} %bitcast.8.first, s32[3,8]{1,0:T(4,128)S(1)} %get-tuple-element.44.bounds, s32[8]{0:T(128)S(1)} %get-tuple-element.45.ends, bf16[2048,512]{1,0:T(8,128)(2,1)} %copy-done.6, bf16[1536,256]{1,0:T(8,128)(2,1)} %collective-permute-done.12.halo_ref, bf16[2048,256]{1,0:T(8,128)(2,1)} %copy-done.2), custom_call_target="tpu_custom_call" | custom-call | flops 1073741824 | bytes 1048576 | tf_op jit(solution)/shard_map/pallas_call | solution.py:209
  182.6 10.3 %shard_map.60 = bf16[512,512]{1,0:T(8,128)(2,1)} custom-call(s32[1]{0:T(128)} %bitcast.9.first, s32[3,8]{1,0:T(4,128)S(1)} %get-tuple-element.44.bounds, s32[8]{0:T(128)S(1)} %get-tuple-element.45.ends, bf16[2048,512]{1,0:T(8,128)(2,1)} %copy-done.6, bf16[1536,256]{1,0:T(8,128)(2,1)} %collective-permute-done.12.halo_ref, bf16[2048,256]{1,0:T(8,128)(2,1)} %copy-done.2), custom_call_target="tpu_custom_call" | custom-call | flops 1073741824 | bytes 1048576 | tf_op jit(solution)/shard_map/pallas_call | solution.py:209
  192.9 8.0 %shard_map.61 = bf16[512,512]{1,0:T(8,128)(2,1)} custom-call(s32[1]{0:T(128)} %bitcast.10.first, s32[3,8]{1,0:T(4,128)S(1)} %get-tuple-element.44.bounds, s32[8]{0:T(128)S(1)} %get-tuple-element.45.ends, bf16[2048,512]{1,0:T(8,128)(2,1)} %copy-done.6, bf16[1536,256]{1,0:T(8,128)(2,1)} %collective-permute-done.12.halo_ref, bf16[2048,256]{1,0:T(8,128)(2,1)} %copy-done.2), custom_call_target="tpu_custom_call" | custom-call | flops 1073741824 | bytes 1048576 | tf_op jit(solution)/shard_map/pallas_call | solution.py:209
  201.3 4.5 %collective-permute-done.15 = bf16[512,512]{1,0:T(8,128)(2,1)S(1)} collective-permute-done((bf16[512,512]{1,0:T(8,128)(2,1)}, bf16[512,512]{1,0:T(8,128)(2,1)S(1)}, u32[]{:S(2)}, u32[]{:S(2)}) %collective-permute-start.15) | collective-permute-done | bytes 524320 | tf_op jit(solution)/shard_map/ppermute | solution.py:272
  (87 shorter events, 17.1 us)
Async XLA Ops:
  6.5 1.4 copy-start.14
  6.5 1.4 copy-start.13
  6.5 122.6 %all-gather.3.cloned.1.call-start = ((), (), s32[]{:S(2)}) async-start(), calls=%async_computation | async-start | bytes 1966080 | tf_op jit(solution)/shard_map/all_gather | solution.py:276
  8.9 135.6 %all-gather.5.cloned.1.call-start = ((), (), s32[]{:S(2)}) async-start(), calls=%async_computation.1 | async-start | bytes 3932160 | tf_op jit(solution)/shard_map/all_gather | solution.py:276
  8.9 19.3 %collective-permute-start.8 = (bf16[256,768]{1,0:T(8,128)(2,1)S(1)}, bf16[256,768]{1,0:T(8,128)(2,1)S(1)}, u32[]{:S(2)}, u32[]{:S(2)}) collective-permute-start(bf16[256,768]{1,0:T(8,128)(2,1)S(1)} %pad_maximum_fusion.4), channel_id=1, source_target_pairs={{0,4},{2,6},{4,0},{6,2},{8,12},{10,14},{12,8},{14,10},{16,20},{18,... | collective-permute-start | bytes 1179656 | tf_op jit(solution)/shard_map/ppermute | solution.py:272
  10.6 17.8 %collective-permute-start.9 = (bf16[256,768]{1,0:T(8,128)(2,1)S(1)}, bf16[256,768]{1,0:T(8,128)(2,1)S(1)}, u32[]{:S(2)}, u32[]{:S(2)}) collective-permute-start(bf16[256,768]{1,0:T(8,128)(2,1)S(1)} %pad_maximum_fusion.5), channel_id=1, source_target_pairs={{0,6},{2,4},{4,2},{6,0},{8,14},{10,12},{12,10},{14,8},{16,22},{18,... | collective-permute-start | bytes 1179656 | tf_op jit(solution)/shard_map/ppermute | solution.py:272
  12.1 17.5 %collective-permute-start.7 = (bf16[256,768]{1,0:T(8,128)(2,1)S(1)}, bf16[256,768]{1,0:T(8,128)(2,1)S(1)}, u32[]{:S(2)}, u32[]{:S(2)}) collective-permute-start(bf16[256,768]{1,0:T(8,128)(2,1)S(1)} %pad_maximum_fusion.3), channel_id=1, source_target_pairs={{0,2},{2,0},{4,6},{6,4},{8,10},{10,8},{12,14},{14,12},{16,18},{18,... | collective-permute-start | bytes 1179656 | tf_op jit(solution)/shard_map/ppermute | solution.py:272
  30.6 8.1 %copy-start.15 = (s32[8]{0:T(128)S(1)}, s32[8]{0:T(128)}, u32[]{:S(2)}) copy-start(s32[8]{0:T(128)} %param.10) | copy-start | bytes 100
  33.8 47.9 %collective-permute-start.10 = (bf16[256,4096]{1,0:T(8,128)(2,1)}, bf16[256,4096]{1,0:T(8,128)(2,1)}, u32[]{:S(2)}, u32[]{:S(2)}) collective-permute-start(bf16[256,4096]{1,0:T(8,128)(2,1)} %constant_dynamic-slice_fusion.3), channel_id=1, source_target_pairs={{0,2},{1,5},{2,0},{3,7},{4,6},{5,1},{6,4},{7,3},{8,10},{9,13},{10,... | collective-permute-start | bytes 6291464 | tf_op jit(solution)/shard_map/ppermute | solution.py:330
  35.3 46.4 %collective-permute-start.11 = (bf16[256,4096]{1,0:T(8,128)(2,1)}, bf16[256,4096]{1,0:T(8,128)(2,1)}, u32[]{:S(2)}, u32[]{:S(2)}) collective-permute-start(bf16[256,4096]{1,0:T(8,128)(2,1)} %constant_dynamic-slice_fusion.3), channel_id=1, source_target_pairs={{0,4},{1,3},{2,6},{3,1},{4,0},{5,7},{6,2},{7,5},{8,12},{9,11},{10,... | collective-permute-start | bytes 6291464 | tf_op jit(solution)/shard_map/ppermute | solution.py:330
  38.8 14.2 %collective-permute-start.5 = (bf16[768,256]{1,0:T(8,128)(2,1)S(1)}, bf16[768,256]{1,0:T(8,128)(2,1)}, u32[]{:S(2)}, u32[]{:S(2)}) collective-permute-start(bf16[768,256]{1,0:T(8,128)(2,1)S(1)} %get-tuple-element.29), channel_id=1, source_target_pairs={{0,8},{2,10},{4,12},{6,14},{8,16},{10,18},{12,20},{14,22},{16,24},... | collective-permute-start | bytes 1179656 | tf_op jit(solution)/shard_map/cond/branch_1_fun/ppermute | solution.py:279
  53.0 10.9 %collective-permute-start.6 = (bf16[768,256]{1,0:T(8,128)(2,1)}, bf16[768,256]{1,0:T(8,128)(2,1)}, u32[]{:S(2)}, u32[]{:S(2)}) collective-permute-start(bf16[768,256]{1,0:T(8,128)(2,1)} %collective-permute-done.5), channel_id=1, source_target_pairs={{0,8},{2,10},{4,12},{6,14},{8,16},{10,18},{12,20},{14,22},{16,24},... | collective-permute-start | bytes 1179656 | tf_op jit(solution)/shard_map/cond/branch_1_fun/ppermute | solution.py:279
  63.9 17.8 %copy-start.7 = (f32[2048,128]{1,0:T(8,128)}, f32[2048,128]{1,0:T(8,128)S(1)}, u32[]{:S(2)}) copy-start(f32[2048,128]{1,0:T(8,128)S(1)} %get-tuple-element.49.refs_2_.refs_5_) | copy-start | bytes 3145732
  63.9 17.8 %copy-start.8 = (f32[2048,128]{1,0:T(8,128)}, f32[2048,128]{1,0:T(8,128)S(1)}, u32[]{:S(2)}) copy-start(f32[2048,128]{1,0:T(8,128)S(1)} %get-tuple-element.50.refs_3_.refs_6_) | copy-start | bytes 3145732
  81.7 30.8 %collective-permute-start.1 = (bf16[256,4096]{1,0:T(8,128)(2,1)}, bf16[256,4096]{1,0:T(8,128)(2,1)}, u32[]{:S(2)}, u32[]{:S(2)}) collective-permute-start(bf16[256,4096]{1,0:T(8,128)(2,1)} %get-tuple-element.31.refs_0_), channel_id=1, source_target_pairs={{0,1},{1,0},{2,3},{3,2},{4,5},{5,4},{6,7},{7,6},{8,9},{9,8},{10,11... | collective-permute-start | bytes 6291464 | tf_op jit(solution)/shard_map/cond/branch_1_fun/ppermute | solution.py:333
  81.8 30.7 %collective-permute-start.2 = (bf16[256,4096]{1,0:T(8,128)(2,1)}, bf16[256,4096]{1,0:T(8,128)(2,1)}, u32[]{:S(2)}, u32[]{:S(2)}) collective-permute-start(bf16[256,4096]{1,0:T(8,128)(2,1)} %get-tuple-element.32.refs_2_), channel_id=1, source_target_pairs={{0,1},{1,0},{2,3},{3,2},{4,5},{5,4},{6,7},{7,6},{8,9},{9,8},{10,11... | collective-permute-start | bytes 6291464 | tf_op jit(solution)/shard_map/cond/branch_1_fun/ppermute | solution.py:333
  82.3 37.0 %collective-permute-start = (bf16[256,4096]{1,0:T(8,128)(2,1)}, bf16[256,4096]{1,0:T(8,128)(2,1)S(1)}, u32[]{:S(2)}, u32[]{:S(2)}) collective-permute-start(bf16[256,4096]{1,0:T(8,128)(2,1)} %get-tuple-element.31.refs_0_), channel_id=1, source_target_pairs={{0,4},{1,3},{2,6},{3,1},{4,0},{5,7},{6,2},{7,5},{8,12},{9,11},{10,... | collective-permute-start | bytes 6291464 | tf_op jit(solution)/shard_map/cond/branch_1_fun/ppermute | solution.py:330
  82.8 29.0 %collective-permute-start.3 = (bf16[768,256]{1,0:T(8,128)(2,1)}, bf16[768,256]{1,0:T(8,128)(2,1)S(1)}, u32[]{:S(2)}, u32[]{:S(2)}) collective-permute-start(bf16[768,256]{1,0:T(8,128)(2,1)} %get-tuple-element.34), channel_id=1, source_target_pairs={{0,8},{2,10},{4,12},{6,14},{8,16},{10,18},{12,20},{14,22},{16,24},... | collective-permute-start | bytes 1179656 | tf_op jit(solution)/shard_map/cond/branch_1_fun/ppermute | solution.py:279
  119.3 1.3 copy-start
  120.7 8.5 %copy-start.10 = (bf16[768,256]{1,0:T(8,128)(2,1)S(1)}, bf16[768,256]{1,0:T(8,128)(2,1)}, u32[]{:S(2)}) copy-start(bf16[768,256]{1,0:T(8,128)(2,1)} %copy-done.9) | copy-start | bytes 1179652 | tf_op jit(solution)/shard_map/cond
  120.7 4.4 %collective-permute-start.4 = (bf16[256,4096]{1,0:T(8,128)(2,1)}, bf16[256,4096]{1,0:T(8,128)(2,1)S(1)}, u32[]{:S(2)}, u32[]{:S(2)}) collective-permute-start(bf16[256,4096]{1,0:T(8,128)(2,1)} %branch_1_fun.8.refs_0_), channel_id=1, source_target_pairs={{0,1},{1,0},{2,3},{3,2},{4,5},{5,4},{6,7},{7,6},{8,9},{9,8},{10,11... | collective-permute-start | bytes 6291464 | tf_op jit(solution)/shard_map/cond/branch_1_fun/ppermute | solution.py:333
  125.0 1.6 copy-start.1
  129.2 1.4 copy-start.3
  130.6 13.9 %copy-start.4 = (bf16[1024,768]{1,0:T(8,128)(2,1)S(1)}, bf16[1024,768]{1,0:T(8,128)(2,1)}, u32[]{:S(2)}) copy-start(bf16[1024,768]{1,0:T(8,128)(2,1)} %all-gather.3.cloned.1.call-done.refs_0_) | copy-start | bytes 4718596
  140.5 19.3 %copy-start.2 = (bf16[2048,256]{1,0:T(8,128)(2,1)}, bf16[2048,256]{1,0:T(8,128)(2,1)S(1)}, u32[]{:S(2)}) copy-start(bf16[2048,256]{1,0:T(8,128)(2,1)S(1)} %shard_map.57.kv_ref) | copy-start | bytes 3145732
  140.5 21.6 %collective-permute-start.12 = (bf16[1536,256]{1,0:T(8,128)(2,1)S(1)}, bf16[1536,256]{1,0:T(8,128)(2,1)}, u32[]{:S(2)}, u32[]{:S(2)}) collective-permute-start(bf16[1536,256]{1,0:T(8,128)(2,1)S(1)} %slice.52), channel_id=1, source_target_pairs={{0,8},{2,10},{4,12},{6,14},{8,16},{10,18},{12,20},{14,22},{16,24},... | collective-permute-start | bytes 2359304 | tf_op jit(solution)/shard_map/ppermute | solution.py:394
  144.5 1.9 copy-start.5
  170.2 30.7 %collective-permute-start.13 = (bf16[512,512]{1,0:T(8,128)(2,1)}, bf16[512,512]{1,0:T(8,128)(2,1)S(1)}, u32[]{:S(2)}, u32[]{:S(2)}) collective-permute-start(bf16[512,512]{1,0:T(8,128)(2,1)} %shard_map.58), channel_id=1, source_target_pairs={{0,6},{2,4},{4,2},{6,0},{8,14},{10,12},{12,10},{14,8},{16,22},{18,... | collective-permute-start | bytes 1572872 | tf_op jit(solution)/shard_map/ppermute | solution.py:272
  182.1 19.2 %collective-permute-start.14 = (bf16[512,512]{1,0:T(8,128)(2,1)}, bf16[512,512]{1,0:T(8,128)(2,1)S(1)}, u32[]{:S(2)}, u32[]{:S(2)}) collective-permute-start(bf16[512,512]{1,0:T(8,128)(2,1)} %shard_map.59), channel_id=1, source_target_pairs={{0,4},{2,6},{4,0},{6,2},{8,12},{10,14},{12,8},{14,10},{16,20},{18,... | collective-permute-start | bytes 1572872 | tf_op jit(solution)/shard_map/ppermute | solution.py:272
  192.9 12.9 %collective-permute-start.15 = (bf16[512,512]{1,0:T(8,128)(2,1)}, bf16[512,512]{1,0:T(8,128)(2,1)S(1)}, u32[]{:S(2)}, u32[]{:S(2)}) collective-permute-start(bf16[512,512]{1,0:T(8,128)(2,1)} %shard_map.60), channel_id=1, source_target_pairs={{0,2},{2,0},{4,6},{6,4},{8,10},{10,8},{12,14},{14,12},{16,18},{18,... | collective-permute-start | bytes 1572872 | tf_op jit(solution)/shard_map/ppermute | solution.py:272
  201.2 6.0 %copy-start.12 = (bf16[512,512]{1,0:T(8,128)(2,1)S(1)}, bf16[512,512]{1,0:T(8,128)(2,1)}, u32[]{:S(2)}) copy-start(bf16[512,512]{1,0:T(8,128)(2,1)} %shard_map.61) | copy-start | bytes 1572868
  205.9 1.3 copy-start.11
  (2 other events, 2.1 us)
Sparse Core Ops, SparseCore 0:
  9.0 42.5 all-gather.2
  53.2 73.1 all-gather.4

commit v3 on v2

--- a/solution.py
+++ b/solution.py
@@ -14,7 +14,7 @@
 REACH = 3
 ROPE_THETA = 500000.0
 LOGIT_CAP = 5.0
-TILE = 256
+TILE = 128
 PUT_BYTES = 20 * 1024 * 1024
 PROJECT_BYTES = 30 * 1024 * 1024
 VMEM_BYTES = 58 * 1024 * 1024
@@ -144,18 +144,18 @@
     first_start = bounds[1, first[0] + tile_index]
     last_start = bounds[2, first[0] + tile_index]
     q_first = halo_rows + place
-    first_block = first_start // TILE
-    last_block = (q_first + tile - 1) // TILE
+    lowest = first_start // TILE * TILE
+    units = (q_first + tile - lowest) // TILE
     sums[...] = jnp.zeros_like(sums)
     totals[...] = jnp.zeros_like(totals)
     inner = 1.0 / (math.sqrt(HEAD_DIM) * LOGIT_CAP)
     outer = LOGIT_CAP * math.log2(math.e)
 
-    def block_step(block, masked):
-        rows = pl.ds(pl.multiple_of(block * TILE, TILE), TILE)
+    def block_step(begin, size, masked):
+        rows = pl.ds(pl.multiple_of(begin, TILE), size)
         if masked:
-            k_ids = block * TILE + lax.broadcasted_iota(jnp.int32, (tile, TILE), 1)
-            q_ids = q_first + lax.broadcasted_iota(jnp.int32, (tile, TILE), 0)
+            k_ids = begin + lax.broadcasted_iota(jnp.int32, (tile, size), 1)
+            q_ids = q_first + lax.broadcasted_iota(jnp.int32, (tile, size), 0)
             begins = jnp.zeros((tile, 1), jnp.int32)
             for number in range(ends.shape[0]):
                 begins = jnp.where(q_ids[:, :1] >= ends[number], jnp.maximum(begins, ends[number]), begins)
@@ -170,29 +170,35 @@
             )
             weights = jnp.exp2(outer * jnp.tanh(raw * inner))
             if masked:
-                weights = weights.reshape(share, tile, TILE)
-                weights = jnp.where(allowed[None], weights, 0.0).reshape(share * tile, TILE)
+                weights = weights.reshape(share, tile, size)
+                weights = jnp.where(allowed[None], weights, 0.0).reshape(share * tile, size)
             partial = weights[:, :HEAD_DIM]
-            for part in range(1, TILE // HEAD_DIM):
+            for part in range(1, size // HEAD_DIM):
                 partial = partial + weights[:, part * HEAD_DIM : (part + 1) * HEAD_DIM]
             totals[members, :] += partial
             sums[members, :] += jnp.dot(weights.astype(jnp.bfloat16), values, preferred_element_type=jnp.float32)
 
-    def either(block, carry):
-        begin = block * TILE
-        whole = (begin >= last_start) & (begin + TILE - 1 <= q_first)
+    def either(begin, size):
+        whole = (begin >= last_start) & (begin + size - 1 <= q_first)
 
         @pl.when(whole)
         def _():
-            block_step(block, False)
+            block_step(begin, size, False)
 
         @pl.when(jnp.logical_not(whole))
         def _():
-            block_step(block, True)
-
+            block_step(begin, size, True)
+
+    def pair(number, carry):
+        either(q_first + tile - 2 * TILE * (number + 1), 2 * TILE)
         return carry
 
-    lax.fori_loop(first_block, last_block + 1, either, 0)
+    lax.fori_loop(0, units // 2, pair, 0)
+
+    @pl.when(lax.rem(units, 2) == 1)
+    def _():
+        either(lowest, TILE)
+
     for head in range(kv_heads * share):
         rows = slice(head * tile, (head + 1) * tile)
         denominator = jnp.sum(totals[rows, :], axis=1, keepdims=True)
@@ -353,15 +359,14 @@
                 held.append(forwarded(held[-1]))
             return put(place, group_rows, [(tokens, lambda s: s[0] * row_count)]), tables(), tuple(held[1:])
 
-        def share(everything, near, other, block):
+        def share(everything, near, other):
             far = cross(near, (2, 1))
-            block = forwarded(block)
             mates = [swap(block) for block in (near, other)]
             first = [(near, home(1, 2, 0)), (mates[0], home(1, 2, 1)), (other, home(2, 1, 0)), (mates[1], home(2, 1, 1))]
-            everything = put(place, group_rows, first, after(everything, block))
+            everything = put(place, group_rows, first, everything)
             far = after(far, everything)
             last = [(far, home(3, 3, 0)), (swap(far), home(3, 3, 1))]
-            return put(place, group_rows, last, everything), block
+            return put(place, group_rows, last, everything)
 
         def region(body, flag, *operands):
             def nothing(*operands):
@@ -372,8 +377,8 @@
             return lax.cond(known == known, body, nothing, *operands)
 
         all_tokens, known_tables, held = region(prepare, rest_kv[:1, :1], tokens, rest_kv)
-        all_tokens, furthest = region(share, held[-1][:1, :1], all_tokens, near, other, held[-1])
-        held = (*held, furthest)
+        held = (*held, forwarded(held[-1]))
+        all_tokens = region(share, near[:1, :1], all_tokens, near, other)
         others = range(1, group)
         kv_weights = [gathered(own_slices, (q_width // kv_width, kv_width), 0, [0])]
         kv_weights += from_lines((rest_kv, *held), 0, others)

time: 216 us -> 216 us (level)
  the two profiles are of different devices: /device:TPU:16 before, /device:TPU:30 now
where the time goes in v3:
time: 216 us; the launch traced here: 214 us
  Pallas kernels  74.3 us (34%)
  waiting for transfers between devices  70.2 us (32%)
  starting transfers between devices  28.3 us (13%)
  local copies, waits for them, and re-layouts  18.7 us (9%)
  between operations  16.2 us (8%)
  other arithmetic  6.59 us (3%)
    pallas_call x4, Pallas kernels, attend(): pl.pallas_call(kernel, out_shape=jax.ShapeDtypeStruct((chunk_rows, width)...  38.7 us
    pallas_call x2, Pallas kernels, project(): pl.pallas_call(functools.partial(project_kernel, rope_heads, layout, len(...  23.3 us
    ppermute x3, waiting for transfers between devices, cross(): return lax.ppermute(block, both, pairs)  23.1 us
    ppermute x6, waiting for transfers between devices, to_partner(): return lax.ppermute(block, 'ca', [(i, i ^ step) for i in devices])  16.9 us
    ppermute x3, waiting for transfers between devices, forwarded(): lax.ppermute(block, 'ca', [(i, (i + group) % (group * lines)) for i in de...  16.8 us
    ppermute x6, starting transfers between devices, to_partner(): return lax.ppermute(block, 'ca', [(i, i ^ step) for i in devices])  16 us
    pallas_call x3, Pallas kernels, put(): pl.pallas_call(functools.partial(put_kernel, targets), out_shape=jax.Shap...  12.3 us
    ppermute x3, waiting for transfers between devices, swap(): lax.ppermute(block, both, [(i * 2 + c, i * 2 + 1 - c) for i in devices fo...  9.71 us
  transfers between devices with their start and end apart: 18, of which 10 were waited for; matrix products, arithmetic and copies ran while one was open for 6% of the time, Pallas kernels for 31%

profile of v3, /device:TPU:30, one launch (start us, length us, event | category | flops | bytes accessed | tf_op | source)
XLA Modules:
  0.0 214.4 jit_solution(12736536623443707336)
XLA Ops:
  9.5 1.6 collective-permute-start.8
  11.1 1.6 collective-permute-start.6
  12.7 15.6 %collective-permute-done.7 = bf16[256,768]{1,0:T(8,128)(2,1)S(1)} collective-permute-done((bf16[256,768]{1,0:T(8,128)(2,1)S(1)}, bf16[256,768]{1,0:T(8,128)(2,1)S(1)}, u32[]{:S(2)}, u32[]{:S(2)}) %collective-permute-start.7) | collective-permute-done | bytes 393248 | tf_op jit(solution)/shard_map/ppermute | solution.py:278
  30.6 3.2 %constant_dynamic-slice_fusion.3 = bf16[256,4096]{1,0:T(8,128)(2,1)} fusion(bf16[512,4096]{1,0:T(8,128)(2,1)} %param.9, s32[]{:T(128)S(6)} %select_n.58), kind=kLoop, calls=%fused_computation.28 | loop fusion | bytes 4194308 | tf_op jit(solution)/shard_map/dynamic_slice | solution.py:343
  36.8 29.2 %conditional.2 = (bf16[2048,4096]{1,0:T(8,128)(2,1)}, f32[2048,128]{1,0:T(8,128)S(1)}, f32[2048,128]{1,0:T(8,128)S(1)}, s32[8]{0:T(128)S(1)}, s32[3,16]{1,0:T(4,...) conditional(s32[]{:T(128)} %bitcast.4, () %tuple.19, (s32[3]{0:T(128)S(1)}, ...), branch_computations={%region_0.1_spmd, %region_1.4_spmd} | conditional | flops 844146 | bytes 19661102 | solution.py:377
  37.4 3.7 %fusion = (f32[2048,64]{1,0:T(8,128)S(1)}, f32[2048,64]{1,0:T(8,128)S(1)}, f32[2048,64]{1,0:T(8,128)S(1)}) fusion(f32[64]{0:T(128)S(1)} %multiply_power_fusion, f32[2048]{0:T(1024)S(1)} %get-tuple-element.57), kind=kLoop, calls=%fused_computation.4 | loop fusion | flops 262144 | bytes 1581312 | tf_op jit(solution)/shard_map/cond/branch_1_fun/neg | solution.py:34
  41.2 11.9 %collective-permute-done.4 = bf16[768,256]{1,0:T(8,128)(2,1)} collective-permute-done((bf16[768,256]{1,0:T(8,128)(2,1)S(1)}, bf16[768,256]{1,0:T(8,128)(2,1)}, u32[]{:S(2)}, u32[]{:S(2)}) %collective-permute-start.4) | collective-permute-done | bytes 393248 | tf_op jit(solution)/shard_map/cond/branch_1_fun/ppermute | solution.py:285
  53.1 3.3 %collective-permute-start.5 = (bf16[768,256]{1,0:T(8,128)(2,1)}, bf16[768,256]{1,0:T(8,128)(2,1)}, u32[]{:S(2)}, u32[]{:S(2)}) collective-permute-start(bf16[768,256]{1,0:T(8,128)(2,1)} %collective-permute-done.4), channel_id=1, source_target_pairs={{0,8},{2,10},{4,12},{6,14},{8,16},{10,18},{12,20},{14,22},{16,24},... | collective-permute-start | bytes 1179656 | tf_op jit(solution)/shard_map/cond/branch_1_fun/ppermute | solution.py:285
  56.4 4.1 %branch_1_fun.4 = bf16[2048,4096]{1,0:T(8,128)(2,1)} custom-call(s32[3]{0:T(128)S(1)} %get-tuple-element.26.place, bf16[512,4096]{1,0:T(8,128)(2,1)} %get-tuple-element.27.refs_0_), custom_call_target="tpu_custom_call" | custom-call | tf_op jit(solution)/shard_map/cond/branch_1_fun/pallas_call | solution.py:121
  61.2 4.9 %collective-permute-done.5 = bf16[768,256]{1,0:T(8,128)(2,1)} collective-permute-done((bf16[768,256]{1,0:T(8,128)(2,1)}, bf16[768,256]{1,0:T(8,128)(2,1)}, u32[]{:S(2)}, u32[]{:S(2)}) %collective-permute-start.5) | collective-permute-done | bytes 393248 | tf_op jit(solution)/shard_map/cond/branch_1_fun/ppermute | solution.py:285
  67.0 4.3 %collective-permute-start.11 = (bf16[768,256]{1,0:T(8,128)(2,1)}, bf16[768,256]{1,0:T(8,128)(2,1)S(1)}, u32[]{:S(2)}, u32[]{:S(2)}) collective-permute-start(bf16[768,256]{1,0:T(8,128)(2,1)} %get-tuple-element.48.refs_3_), channel_id=1, source_target_pairs={{0,8},{2,10},{4,12},{6,14},{8,16},{10,18},{12,20},{14,22},{16,24},... | collective-permute-start | bytes 1179656 | tf_op jit(solution)/shard_map/ppermute | solution.py:285
  71.3 9.3 %collective-permute-done.9 = bf16[256,4096]{1,0:T(8,128)(2,1)} collective-permute-done((bf16[256,4096]{1,0:T(8,128)(2,1)}, bf16[256,4096]{1,0:T(8,128)(2,1)}, u32[]{:S(2)}, u32[]{:S(2)}) %collective-permute-start.9) | collective-permute-done | bytes 2097184 | tf_op jit(solution)/shard_map/ppermute | solution.py:336
  83.0 36.6 %conditional.3 = (bf16[2048,4096]{1,0:T(8,128)(2,1)}) conditional(s32[]{:T(128)} %bitcast.8, () %tuple.21, (bf16[256,4096]{1,0:T(8,128)(2,1)}, bf16[256,4096]{1,0:T(8,128)(2,1)}, s32[3]{0:T(128)S(1)}, bf16[2048,4096]{1,0:T(8,128)(2,1)}) %tuple.22), branch_computations={%region_4.5_spmd, %region_5.6_spmd} | conditional | bytes 50331872 | solution.py:377
  83.6 1.5 collective-permute-start
  85.1 2.3 %collective-permute-done.1.refs_1_ = bf16[256,4096]{1,0:T(8,128)(2,1)S(1)} collective-permute-done((bf16[256,4096]{1,0:T(8,128)(2,1)}, bf16[256,4096]{1,0:T(8,128)(2,1)S(1)}, u32[]{:S(2)}, u32[]{:S(2)}) %collective-permute-start.1) | collective-permute-done | bytes 2097184 | tf_op jit(solution)/shard_map/cond/branch_1_fun/ppermute | solution.py:339
  87.4 3.0 %collective-permute-done.2.refs_3_ = bf16[256,4096]{1,0:T(8,128)(2,1)S(1)} collective-permute-done((bf16[256,4096]{1,0:T(8,128)(2,1)}, bf16[256,4096]{1,0:T(8,128)(2,1)S(1)}, u32[]{:S(2)}, u32[]{:S(2)}) %collective-permute-start.2) | collective-permute-done | bytes 2097184 | tf_op jit(solution)/shard_map/cond/branch_1_fun/ppermute | solution.py:339
  90.4 5.6 %branch_1_fun.5.refs_1_.refs_2_ = bf16[2048,4096]{1,0:T(8,128)(2,1)} custom-call(s32[3]{0:T(128)S(1)} %get-tuple-element.31.place, bf16[256,4096]{1,0:T(8,128)(2,1)} %get-tuple-element.32.refs_0_, bf16[256,4096]{1,0:T(8,128)(2,1)S(1)} %collective-permute-done.1.refs_1_, bf16[256,4096]{1,0:T(8,128)(2,1)} %get-tuple-element.33.refs_2_, ...), custom_call_target="tpu_custom_call", output_to_operand_aliasing={{}: (5, {})} | custom-call | tf_op jit(solution)/shard_map/cond/branch_1_fun/pallas_call | solution.py:121
  96.1 13.8 %collective-permute-done.refs_0_ = bf16[256,4096]{1,0:T(8,128)(2,1)S(1)} collective-permute-done((bf16[256,4096]{1,0:T(8,128)(2,1)}, bf16[256,4096]{1,0:T(8,128)(2,1)S(1)}, u32[]{:S(2)}, u32[]{:S(2)}) %collective-permute-start) | collective-permute-done | bytes 2097184 | tf_op jit(solution)/shard_map/cond/branch_1_fun/ppermute | solution.py:336
  111.2 4.4 %collective-permute-done.3.refs_1_ = bf16[256,4096]{1,0:T(8,128)(2,1)S(1)} collective-permute-done((bf16[256,4096]{1,0:T(8,128)(2,1)}, bf16[256,4096]{1,0:T(8,128)(2,1)S(1)}, u32[]{:S(2)}, u32[]{:S(2)}) %collective-permute-start.3) | collective-permute-done | bytes 2097184 | tf_op jit(solution)/shard_map/cond/branch_1_fun/ppermute | solution.py:339
  115.5 1.6 copy-done.1
  117.1 2.5 %branch_1_fun.7 = bf16[2048,4096]{1,0:T(8,128)(2,1)} custom-call(s32[3]{0:T(128)S(1)} %get-tuple-element.31.place, bf16[256,4096]{1,0:T(8,128)(2,1)S(1)} %copy-done.1, bf16[256,4096]{1,0:T(8,128)(2,1)S(1)} %collective-permute-done.3.refs_1_, bf16[2048,4096]{1,0:T(8,128)(2,1)} %branch_1_fun.5.refs_1_.refs_2_), custom_call_target="tpu_custom_call", output_to_operand_aliasing={{}: (3, {})} | custom-call | tf_op jit(solution)/shard_map/cond/branch_1_fun/pallas_call | solution.py:121
  121.1 9.9 %shard_map.57.kv_ref = bf16[2048,256]{1,0:T(8,128)(2,1)S(1)} custom-call(s32[3]{0:T(128)S(1)} %pad_add_fusion.1.place, bf16[2048,4096]{1,0:T(8,128)(2,1)} %get-tuple-element.90.x_ref, bf16[1024,768]{1,0:T(8,128)(2,1)S(1)} %copy-done.3, bf16[768,256]{1,0:T(8,128)(2,1)S(1)} %pad_maximum_fusion.6.refs_1_, bf16[768,256]{1,0:T(8,128)(2,1)} %get-tuple-element.47.refs_2_, ...), custom_call_target="tpu_custom_call" | custom-call | flops 4294967296 | bytes 18874368 | tf_op jit(solution)/shard_map/pallas_call | solution.py:78
  133.6 1.9 copy-done.5
  135.4 13.5 %shard_map.56.q_ref = bf16[2048,512]{1,0:T(8,128)(2,1)S(1)} custom-call(s32[3]{0:T(128)S(1)} %pad_add_fusion.1.place, bf16[2048,4096]{1,0:T(8,128)(2,1)} %get-tuple-element.90.x_ref, bf16[1024,768]{1,0:T(8,128)(2,1)S(1)} %copy-done.4, bf16[3072,512]{1,0:T(8,128)(2,1)S(1)} %copy-done.5, f32[2048,128]{1,0:T(8,128)} %copy-done.7, f32[2048,128]{1,0:T(8,128)} %copy-done.8), custom_call_target="tpu_custom_call" | custom-call | flops 8589934592 | bytes 20971520 | tf_op jit(solution)/shard_map/pallas_call | solution.py:78
  150.2 3.6 %collective-permute-done.12.halo_ref = bf16[1536,256]{1,0:T(8,128)(2,1)} collective-permute-done((bf16[1536,256]{1,0:T(8,128)(2,1)}, bf16[1536,256]{1,0:T(8,128)(2,1)}, u32[]{:S(2)}, u32[]{:S(2)}) %collective-permute-start.12) | collective-permute-done | bytes 786464 | tf_op jit(solution)/shard_map/ppermute | solution.py:399
  153.9 8.0 %shard_map.58 = bf16[512,512]{1,0:T(8,128)(2,1)} custom-call(s32[1]{0:T(128)} %bitcast.3.first, s32[3,16]{1,0:T(4,128)S(1)} %get-tuple-element.42.bounds, s32[8]{0:T(128)S(1)} %get-tuple-element.43.ends, bf16[2048,512]{1,0:T(8,128)(2,1)} %copy-done.6, bf16[1536,256]{1,0:T(8,128)(2,1)} %collective-permute-done.12.halo_ref, bf16[2048,256]{1,0:T(8,128)(2,1)} %copy-done.2), custom_call_target="tpu_custom_call" | custom-call | flops 1073741824 | bytes 1048576 | tf_op jit(solution)/shard_map/pallas_call | solution.py:215
  161.9 6.5 %collective-permute-start.13 = (bf16[512,512]{1,0:T(8,128)(2,1)}, bf16[512,512]{1,0:T(8,128)(2,1)S(1)}, u32[]{:S(2)}, u32[]{:S(2)}) collective-permute-start(bf16[512,512]{1,0:T(8,128)(2,1)} %shard_map.58), channel_id=1, source_target_pairs={{0,6},{2,4},{4,2},{6,0},{8,14},{10,12},{12,10},{14,8},{16,22},{18,... | collective-permute-start | bytes 1572872 | tf_op jit(solution)/shard_map/ppermute | solution.py:278
  168.4 7.9 %shard_map.59 = bf16[512,512]{1,0:T(8,128)(2,1)} custom-call(s32[1]{0:T(128)} %bitcast.9.first, s32[3,16]{1,0:T(4,128)S(1)} %get-tuple-element.42.bounds, s32[8]{0:T(128)S(1)} %get-tuple-element.43.ends, bf16[2048,512]{1,0:T(8,128)(2,1)} %copy-done.6, bf16[1536,256]{1,0:T(8,128)(2,1)} %collective-permute-done.12.halo_ref, bf16[2048,256]{1,0:T(8,128)(2,1)} %copy-done.2), custom_call_target="tpu_custom_call" | custom-call | flops 1073741824 | bytes 1048576 | tf_op jit(solution)/shard_map/pallas_call | solution.py:215
  176.3 1.9 collective-permute-start.14
  178.2 9.7 %shard_map.60 = bf16[512,512]{1,0:T(8,128)(2,1)} custom-call(s32[1]{0:T(128)} %bitcast.10.first, s32[3,16]{1,0:T(4,128)S(1)} %get-tuple-element.42.bounds, s32[8]{0:T(128)S(1)} %get-tuple-element.43.ends, bf16[2048,512]{1,0:T(8,128)(2,1)} %copy-done.6, bf16[1536,256]{1,0:T(8,128)(2,1)} %collective-permute-done.12.halo_ref, bf16[2048,256]{1,0:T(8,128)(2,1)} %copy-done.2), custom_call_target="tpu_custom_call" | custom-call | flops 1073741824 | bytes 1048576 | tf_op jit(solution)/shard_map/pallas_call | solution.py:215
  187.9 3.9 %collective-permute-start.15 = (bf16[512,512]{1,0:T(8,128)(2,1)}, bf16[512,512]{1,0:T(8,128)(2,1)S(1)}, u32[]{:S(2)}, u32[]{:S(2)}) collective-permute-start(bf16[512,512]{1,0:T(8,128)(2,1)} %shard_map.60), channel_id=1, source_target_pairs={{0,2},{2,0},{4,6},{6,4},{8,10},{10,8},{12,14},{14,12},{16,18},{18,... | collective-permute-start | bytes 1572872 | tf_op jit(solution)/shard_map/ppermute | solution.py:278
  191.8 13.1 %shard_map.61 = bf16[512,512]{1,0:T(8,128)(2,1)} custom-call(s32[1]{0:T(128)} %bitcast.11.first, s32[3,16]{1,0:T(4,128)S(1)} %get-tuple-element.42.bounds, s32[8]{0:T(128)S(1)} %get-tuple-element.43.ends, bf16[2048,512]{1,0:T(8,128)(2,1)} %copy-done.6, bf16[1536,256]{1,0:T(8,128)(2,1)} %collective-permute-done.12.halo_ref, bf16[2048,256]{1,0:T(8,128)(2,1)} %copy-done.2), custom_call_target="tpu_custom_call" | custom-call | flops 1073741824 | bytes 1048576 | tf_op jit(solution)/shard_map/pallas_call | solution.py:215
  (81 shorter events, 20.0 us)
Async XLA Ops:
  6.5 1.4 copy-start.12
  6.5 1.4 copy-start.11
  6.5 113.1 %all-gather.3.cloned.1.call-start = ((), (), s32[]{:S(2)}) async-start(), calls=%async_computation | async-start | bytes 1966080 | tf_op jit(solution)/shard_map/all_gather | solution.py:282
  8.8 124.7 %all-gather.5.cloned.1.call-start = ((), (), s32[]{:S(2)}) async-start(), calls=%async_computation.1 | async-start | bytes 3932160 | tf_op jit(solution)/shard_map/all_gather | solution.py:282
  8.9 19.3 %collective-permute-start.7 = (bf16[256,768]{1,0:T(8,128)(2,1)S(1)}, bf16[256,768]{1,0:T(8,128)(2,1)S(1)}, u32[]{:S(2)}, u32[]{:S(2)}) collective-permute-start(bf16[256,768]{1,0:T(8,128)(2,1)S(1)} %pad_maximum_fusion.4), channel_id=1, source_target_pairs={{0,4},{2,6},{4,0},{6,2},{8,12},{10,14},{12,8},{14,10},{16,20},{18,... | collective-permute-start | bytes 1179656 | tf_op jit(solution)/shard_map/ppermute | solution.py:278
  9.5 18.8 %collective-permute-start.8 = (bf16[256,768]{1,0:T(8,128)(2,1)S(1)}, bf16[256,768]{1,0:T(8,128)(2,1)S(1)}, u32[]{:S(2)}, u32[]{:S(2)}) collective-permute-start(bf16[256,768]{1,0:T(8,128)(2,1)S(1)} %pad_maximum_fusion.5), channel_id=1, source_target_pairs={{0,6},{2,4},{4,2},{6,0},{8,14},{10,12},{12,10},{14,8},{16,22},{18,... | collective-permute-start | bytes 1179656 | tf_op jit(solution)/shard_map/ppermute | solution.py:278
  11.1 18.5 %collective-permute-start.6 = (bf16[256,768]{1,0:T(8,128)(2,1)S(1)}, bf16[256,768]{1,0:T(8,128)(2,1)S(1)}, u32[]{:S(2)}, u32[]{:S(2)}) collective-permute-start(bf16[256,768]{1,0:T(8,128)(2,1)S(1)} %pad_maximum_fusion.3), channel_id=1, source_target_pairs={{0,2},{2,0},{4,6},{6,4},{8,10},{10,8},{12,14},{14,12},{16,18},{18,... | collective-permute-start | bytes 1179656 | tf_op jit(solution)/shard_map/ppermute | solution.py:278
  30.6 6.2 %copy-start.13 = (s32[8]{0:T(128)S(1)}, s32[8]{0:T(128)}, u32[]{:S(2)}) copy-start(s32[8]{0:T(128)} %param.10) | copy-start | bytes 100
  33.8 46.9 %collective-permute-start.9 = (bf16[256,4096]{1,0:T(8,128)(2,1)}, bf16[256,4096]{1,0:T(8,128)(2,1)}, u32[]{:S(2)}, u32[]{:S(2)}) collective-permute-start(bf16[256,4096]{1,0:T(8,128)(2,1)} %constant_dynamic-slice_fusion.3), channel_id=1, source_target_pairs={{0,2},{1,5},{2,0},{3,7},{4,6},{5,1},{6,4},{7,3},{8,10},{9,13},{10,... | collective-permute-start | bytes 6291464 | tf_op jit(solution)/shard_map/ppermute | solution.py:336
  34.3 48.7 %collective-permute-start.10 = (bf16[256,4096]{1,0:T(8,128)(2,1)}, bf16[256,4096]{1,0:T(8,128)(2,1)}, u32[]{:S(2)}, u32[]{:S(2)}) collective-permute-start(bf16[256,4096]{1,0:T(8,128)(2,1)} %constant_dynamic-slice_fusion.3), channel_id=1, source_target_pairs={{0,4},{1,3},{2,6},{3,1},{4,0},{5,7},{6,2},{7,5},{8,12},{9,11},{10,... | collective-permute-start | bytes 6291464 | tf_op jit(solution)/shard_map/ppermute | solution.py:336
  36.8 16.3 %collective-permute-start.4 = (bf16[768,256]{1,0:T(8,128)(2,1)S(1)}, bf16[768,256]{1,0:T(8,128)(2,1)}, u32[]{:S(2)}, u32[]{:S(2)}) collective-permute-start(bf16[768,256]{1,0:T(8,128)(2,1)S(1)} %get-tuple-element.30), channel_id=1, source_target_pairs={{0,8},{2,10},{4,12},{6,14},{8,16},{10,18},{12,20},{14,22},{16,24},... | collective-permute-start | bytes 1179656 | tf_op jit(solution)/shard_map/cond/branch_1_fun/ppermute | solution.py:285
  53.1 12.9 %collective-permute-start.5 = (bf16[768,256]{1,0:T(8,128)(2,1)}, bf16[768,256]{1,0:T(8,128)(2,1)}, u32[]{:S(2)}, u32[]{:S(2)}) collective-permute-start(bf16[768,256]{1,0:T(8,128)(2,1)} %collective-permute-done.4), channel_id=1, source_target_pairs={{0,8},{2,10},{4,12},{6,14},{8,16},{10,18},{12,20},{14,22},{16,24},... | collective-permute-start | bytes 1179656 | tf_op jit(solution)/shard_map/cond/branch_1_fun/ppermute | solution.py:285
  66.0 1.0 copy-start.7
  67.0 16.0 %copy-start.8 = (f32[2048,128]{1,0:T(8,128)}, f32[2048,128]{1,0:T(8,128)S(1)}, u32[]{:S(2)}) copy-start(f32[2048,128]{1,0:T(8,128)S(1)} %get-tuple-element.46.refs_3_.refs_6_) | copy-start | bytes 3145732
  67.0 52.7 %collective-permute-start.11 = (bf16[768,256]{1,0:T(8,128)(2,1)}, bf16[768,256]{1,0:T(8,128)(2,1)S(1)}, u32[]{:S(2)}, u32[]{:S(2)}) collective-permute-start(bf16[768,256]{1,0:T(8,128)(2,1)} %get-tuple-element.48.refs_3_), channel_id=1, source_target_pairs={{0,8},{2,10},{4,12},{6,14},{8,16},{10,18},{12,20},{14,22},{16,24},... | collective-permute-start | bytes 1179656 | tf_op jit(solution)/shard_map/ppermute | solution.py:285
  83.0 4.4 %collective-permute-start.1 = (bf16[256,4096]{1,0:T(8,128)(2,1)}, bf16[256,4096]{1,0:T(8,128)(2,1)S(1)}, u32[]{:S(2)}, u32[]{:S(2)}) collective-permute-start(bf16[256,4096]{1,0:T(8,128)(2,1)} %get-tuple-element.32.refs_0_), channel_id=1, source_target_pairs={{0,1},{1,0},{2,3},{3,2},{4,5},{5,4},{6,7},{7,6},{8,9},{9,8},{10,11... | collective-permute-start | bytes 6291464 | tf_op jit(solution)/shard_map/cond/branch_1_fun/ppermute | solution.py:339
  83.1 7.4 %collective-permute-start.2 = (bf16[256,4096]{1,0:T(8,128)(2,1)}, bf16[256,4096]{1,0:T(8,128)(2,1)S(1)}, u32[]{:S(2)}, u32[]{:S(2)}) collective-permute-start(bf16[256,4096]{1,0:T(8,128)(2,1)} %get-tuple-element.33.refs_2_), channel_id=1, source_target_pairs={{0,1},{1,0},{2,3},{3,2},{4,5},{5,4},{6,7},{7,6},{8,9},{9,8},{10,11... | collective-permute-start | bytes 6291464 | tf_op jit(solution)/shard_map/cond/branch_1_fun/ppermute | solution.py:339
  83.6 26.2 %collective-permute-start = (bf16[256,4096]{1,0:T(8,128)(2,1)}, bf16[256,4096]{1,0:T(8,128)(2,1)S(1)}, u32[]{:S(2)}, u32[]{:S(2)}) collective-permute-start(bf16[256,4096]{1,0:T(8,128)(2,1)} %get-tuple-element.32.refs_0_), channel_id=1, source_target_pairs={{0,4},{1,3},{2,6},{3,1},{4,0},{5,7},{6,2},{7,5},{8,12},{9,11},{10,... | collective-permute-start | bytes 6291464 | tf_op jit(solution)/shard_map/cond/branch_1_fun/ppermute | solution.py:336
  109.8 1.3 copy-start
  111.1 4.4 %collective-permute-start.3 = (bf16[256,4096]{1,0:T(8,128)(2,1)}, bf16[256,4096]{1,0:T(8,128)(2,1)S(1)}, u32[]{:S(2)}, u32[]{:S(2)}) collective-permute-start(bf16[256,4096]{1,0:T(8,128)(2,1)} %branch_1_fun.6.refs_0_), channel_id=1, source_target_pairs={{0,1},{1,0},{2,3},{3,2},{4,5},{5,4},{6,7},{7,6},{8,9},{9,8},{10,11... | collective-permute-start | bytes 6291464 | tf_op jit(solution)/shard_map/cond/branch_1_fun/ppermute | solution.py:339
  115.5 1.6 copy-start.1
  119.7 1.4 copy-start.3
  121.1 12.5 %copy-start.4 = (bf16[1024,768]{1,0:T(8,128)(2,1)S(1)}, bf16[1024,768]{1,0:T(8,128)(2,1)}, u32[]{:S(2)}) copy-start(bf16[1024,768]{1,0:T(8,128)(2,1)} %all-gather.3.cloned.1.call-done.refs_0_) | copy-start | bytes 4718596
  131.0 17.9 %copy-start.2 = (bf16[2048,256]{1,0:T(8,128)(2,1)}, bf16[2048,256]{1,0:T(8,128)(2,1)S(1)}, u32[]{:S(2)}) copy-start(bf16[2048,256]{1,0:T(8,128)(2,1)S(1)} %shard_map.57.kv_ref) | copy-start | bytes 3145732
  132.0 21.8 %collective-permute-start.12 = (bf16[1536,256]{1,0:T(8,128)(2,1)}, bf16[1536,256]{1,0:T(8,128)(2,1)}, u32[]{:S(2)}, u32[]{:S(2)}) collective-permute-start(bf16[1536,256]{1,0:T(8,128)(2,1)} %slice.53), channel_id=1, source_target_pairs={{0,8},{2,10},{4,12},{6,14},{8,16},{10,18},{12,20},{14,22},{16,24},... | collective-permute-start | bytes 2359304 | tf_op jit(solution)/shard_map/ppermute | solution.py:399
  133.5 1.9 copy-start.5
  148.9 1.3 copy-start.6
  161.9 43.0 %collective-permute-start.13 = (bf16[512,512]{1,0:T(8,128)(2,1)}, bf16[512,512]{1,0:T(8,128)(2,1)S(1)}, u32[]{:S(2)}, u32[]{:S(2)}) collective-permute-start(bf16[512,512]{1,0:T(8,128)(2,1)} %shard_map.58), channel_id=1, source_target_pairs={{0,6},{2,4},{4,2},{6,0},{8,14},{10,12},{12,10},{14,8},{16,22},{18,... | collective-permute-start | bytes 1572872 | tf_op jit(solution)/shard_map/ppermute | solution.py:278
  176.3 28.9 %collective-permute-start.14 = (bf16[512,512]{1,0:T(8,128)(2,1)}, bf16[512,512]{1,0:T(8,128)(2,1)S(1)}, u32[]{:S(2)}, u32[]{:S(2)}) collective-permute-start(bf16[512,512]{1,0:T(8,128)(2,1)} %shard_map.59), channel_id=1, source_target_pairs={{0,4},{2,6},{4,0},{6,2},{8,12},{10,14},{12,8},{14,10},{16,20},{18,... | collective-permute-start | bytes 1572872 | tf_op jit(solution)/shard_map/ppermute | solution.py:278
  187.9 17.4 %collective-permute-start.15 = (bf16[512,512]{1,0:T(8,128)(2,1)}, bf16[512,512]{1,0:T(8,128)(2,1)S(1)}, u32[]{:S(2)}, u32[]{:S(2)}) collective-permute-start(bf16[512,512]{1,0:T(8,128)(2,1)} %shard_map.60), channel_id=1, source_target_pairs={{0,2},{2,0},{4,6},{6,4},{8,10},{10,8},{12,14},{14,12},{16,18},{18,... | collective-permute-start | bytes 1572872 | tf_op jit(solution)/shard_map/ppermute | solution.py:278
  205.1 1.6 copy-start.10
  205.4 1.3 copy-start.9
Sparse Core Ops, SparseCore 0:
  9.0 42.1 all-gather.2
  52.7 71.7 all-gather.4

commit v4 on v3

--- a/solution.py
+++ b/solution.py
@@ -14,7 +14,8 @@
 REACH = 3
 ROPE_THETA = 500000.0
 LOGIT_CAP = 5.0
-TILE = 128
+TILE = 256
+UNIT = 128
 PUT_BYTES = 20 * 1024 * 1024
 PROJECT_BYTES = 30 * 1024 * 1024
 VMEM_BYTES = 58 * 1024 * 1024
@@ -144,15 +145,15 @@
     first_start = bounds[1, first[0] + tile_index]
     last_start = bounds[2, first[0] + tile_index]
     q_first = halo_rows + place
-    lowest = first_start // TILE * TILE
-    units = (q_first + tile - lowest) // TILE
+    lowest = first_start // UNIT * UNIT
+    units = (q_first - lowest) // UNIT
     sums[...] = jnp.zeros_like(sums)
     totals[...] = jnp.zeros_like(totals)
     inner = 1.0 / (math.sqrt(HEAD_DIM) * LOGIT_CAP)
     outer = LOGIT_CAP * math.log2(math.e)
 
     def block_step(begin, size, masked):
-        rows = pl.ds(pl.multiple_of(begin, TILE), size)
+        rows = pl.ds(pl.multiple_of(begin, UNIT), size)
         if masked:
             k_ids = begin + lax.broadcasted_iota(jnp.int32, (tile, size), 1)
             q_ids = q_first + lax.broadcasted_iota(jnp.int32, (tile, size), 0)
@@ -189,15 +190,21 @@
         def _():
             block_step(begin, size, True)
 
-    def pair(number, carry):
-        either(q_first + tile - 2 * TILE * (number + 1), 2 * TILE)
+    def long_step(number, carry):
+        either(q_first - 4 * UNIT * (number + 1), 4 * UNIT)
         return carry
 
-    lax.fori_loop(0, units // 2, pair, 0)
-
-    @pl.when(lax.rem(units, 2) == 1)
+    block_step(q_first, tile, True)
+    lax.fori_loop(0, units // 4, long_step, 0)
+    rest = lax.rem(units, 4)
+
+    @pl.when(rest >= 2)
     def _():
-        either(lowest, TILE)
+        either(lowest + lax.rem(rest, 2) * UNIT, 2 * UNIT)
+
+    @pl.when(lax.rem(rest, 2) == 1)
+    def _():
+        either(lowest, UNIT)
 
     for head in range(kv_heads * share):
         rows = slice(head * tile, (head + 1) * tile)
@@ -376,8 +383,9 @@
             known = flag.reshape(-1)[0].astype(jnp.float32)
             return lax.cond(known == known, body, nothing, *operands)
 
-        all_tokens, known_tables, held = region(prepare, rest_kv[:1, :1], tokens, rest_kv)
+        all_tokens, known_tables, held = prepare(tokens, rest_kv)
         held = (*held, forwarded(held[-1]))
+        near = after(near, held[1], *known_tables)
         all_tokens = region(share, near[:1, :1], all_tokens, near, other)
         others = range(1, group)
         kv_weights = [gathered(own_slices, (q_width // kv_width, kv_width), 0, [0])]

time: 216 us -> 209 us (0.968)
  the two profiles are of different devices: /device:TPU:30 before, /device:TPU:16 now
where the time goes in v4:
time: 209 us
  waiting for transfers between devices  70 us (33%)
  Pallas kernels  68.5 us (33%)
  starting transfers between devices  23 us (11%)
  local copies, waits for them, and re-layouts  21.4 us (10%)
  between operations  15.1 us (7%)
  other arithmetic  10.8 us (5%)
    pallas_call x4, Pallas kernels, attend(): pl.pallas_call(kernel, out_shape=jax.ShapeDtypeStruct((chunk_rows, width)...  34.2 us
    pallas_call x2, Pallas kernels, project(): pl.pallas_call(functools.partial(project_kernel, rope_heads, layout, len(...  22.6 us
    ppermute x6, waiting for transfers between devices, to_partner(): return lax.ppermute(block, 'ca', [(i, i ^ step) for i in devices])  21.6 us
    ppermute x3, waiting for transfers between devices, cross(): return lax.ppermute(block, both, pairs)  21.5 us
    ppermute x3, waiting for transfers between devices, forwarded(): lax.ppermute(block, 'ca', [(i, (i + group) % (group * lines)) for i in de...  17 us
    unnamed x36, local copies, waits for them, and re-layouts  13.1 us
    pallas_call x3, Pallas kernels, put(): pl.pallas_call(functools.partial(put_kernel, targets), out_shape=jax.Shap...  11.7 us
    ppermute x6, starting transfers between devices, to_partner(): return lax.ppermute(block, 'ca', [(i, i ^ step) for i in devices])  9.68 us
  transfers between devices with their start and end apart: 18, of which 11 were waited for; matrix products, arithmetic and copies ran while one was open for 8% of the time, Pallas kernels for 29%

profile of v4, /device:TPU:16, one launch (start us, length us, event | category | flops | bytes accessed | tf_op | source)
XLA Modules:
  0.0 208.8 jit_solution(13978054604431339106)
XLA Ops:
  12.7 8.3 %collective-permute-done.5 = bf16[256,768]{1,0:T(8,128)(2,1)S(1)} collective-permute-done((bf16[256,768]{1,0:T(8,128)(2,1)S(1)}, bf16[256,768]{1,0:T(8,128)(2,1)S(1)}, u32[]{:S(2)}, u32[]{:S(2)}) %collective-permute-start.5) | collective-permute-done | bytes 393248 | tf_op jit(solution)/shard_map/ppermute | solution.py:285
  21.0 8.6 %collective-permute-done.6 = bf16[256,768]{1,0:T(8,128)(2,1)S(1)} collective-permute-done((bf16[256,768]{1,0:T(8,128)(2,1)S(1)}, bf16[256,768]{1,0:T(8,128)(2,1)S(1)}, u32[]{:S(2)}, u32[]{:S(2)}) %collective-permute-start.6) | collective-permute-done | bytes 393248 | tf_op jit(solution)/shard_map/ppermute | solution.py:285
  30.6 3.1 %constant_dynamic-slice_fusion.12 = bf16[256,4096]{1,0:T(8,128)(2,1)} fusion(bf16[512,4096]{1,0:T(8,128)(2,1)} %refs_0_.1, s32[]{:T(128)S(6)} %select_n.53), kind=kLoop, calls=%fused_computation.30 | loop fusion | bytes 4194308 | tf_op jit(solution)/shard_map/dynamic_slice | solution.py:350
  36.3 1.6 collective-permute-start.8
  38.6 14.2 %collective-permute-done.8.refs_2_ = bf16[768,256]{1,0:T(8,128)(2,1)S(1)} collective-permute-done((bf16[768,256]{1,0:T(8,128)(2,1)S(1)}, bf16[768,256]{1,0:T(8,128)(2,1)S(1)}, u32[]{:S(2)}, u32[]{:S(2)}) %collective-permute-start.8) | collective-permute-done | bytes 393248 | tf_op jit(solution)/shard_map/ppermute | solution.py:292
  52.9 1.7 collective-permute-start.9
  55.4 5.4 %fusion = (f32[2048,64]{1,0:T(8,128)S(1)}, f32[2048,64]{1,0:T(8,128)S(1)}, f32[2048,64]{1,0:T(8,128)}) fusion(f32[64]{0:T(128)S(1)} %multiply_power_fusion, f32[2048]{0:T(1024)S(1)} %get-tuple-element.37), kind=kLoop, calls=%fused_computation.10 | loop fusion | flops 262144 | bytes 1581312 | tf_op jit(solution)/shard_map/neg | solution.py:35
  60.8 2.8 %collective-permute-done.9.refs_1_.refs_3_ = bf16[768,256]{1,0:T(8,128)(2,1)} collective-permute-done((bf16[768,256]{1,0:T(8,128)(2,1)S(1)}, bf16[768,256]{1,0:T(8,128)(2,1)}, u32[]{:S(2)}, u32[]{:S(2)}) %collective-permute-start.9) | collective-permute-done | bytes 393248 | tf_op jit(solution)/shard_map/ppermute | solution.py:292
  63.5 1.9 collective-permute-start.11
  65.5 2.2 %copy-done.2 = bf16[512,4096]{1,0:T(8,128)(2,1)S(1)} copy-done((bf16[512,4096]{1,0:T(8,128)(2,1)S(1)}, bf16[512,4096]{1,0:T(8,128)(2,1)}, u32[]{:S(2)}) %copy-start.2) | copy-done | bytes 4194328
  67.7 2.5 %shard_map.56 = bf16[2048,4096]{1,0:T(8,128)(2,1)} custom-call(s32[3]{0:T(128)S(1)} %pad_add_fusion.1.place, bf16[512,4096]{1,0:T(8,128)(2,1)S(1)} %copy-done.2), custom_call_target="tpu_custom_call" | custom-call | tf_op jit(solution)/shard_map/pallas_call | solution.py:122
  70.8 2.0 pad_maximum_fusion
  72.8 7.7 %collective-permute-done.4.refs_0_ = bf16[256,4096]{1,0:T(8,128)(2,1)} collective-permute-done((bf16[256,4096]{1,0:T(8,128)(2,1)}, bf16[256,4096]{1,0:T(8,128)(2,1)}, u32[]{:S(2)}, u32[]{:S(2)}) %collective-permute-start.4) | collective-permute-done | bytes 2097184 | tf_op jit(solution)/shard_map/ppermute | solution.py:343
  83.1 34.9 %conditional.1 = (bf16[2048,4096]{1,0:T(8,128)(2,1)}) conditional(s32[]{:T(128)} %bitcast.6, () %tuple.11, (bf16[256,4096]{1,0:T(8,128)(2,1)}, bf16[256,4096]{1,0:T(8,128)(2,1)}, s32[3]{0:T(128)S(1)}, bf16[2048,4096]{1,0:T(8,128)(2,1)}) %tuple.12), branch_computations={%region_2.3_spmd, %region_3.4_spmd} | conditional | bytes 33554600 | solution.py:384
  83.7 1.6 collective-permute-start
  85.3 2.3 %collective-permute-done.1.refs_1_ = bf16[256,4096]{1,0:T(8,128)(2,1)S(1)} collective-permute-done((bf16[256,4096]{1,0:T(8,128)(2,1)}, bf16[256,4096]{1,0:T(8,128)(2,1)S(1)}, u32[]{:S(2)}, u32[]{:S(2)}) %collective-permute-start.1) | collective-permute-done | bytes 2097184 | tf_op jit(solution)/shard_map/cond/branch_1_fun/ppermute | solution.py:346
  87.6 3.0 %collective-permute-done.2.refs_3_ = bf16[256,4096]{1,0:T(8,128)(2,1)S(1)} collective-permute-done((bf16[256,4096]{1,0:T(8,128)(2,1)}, bf16[256,4096]{1,0:T(8,128)(2,1)S(1)}, u32[]{:S(2)}, u32[]{:S(2)}) %collective-permute-start.2) | collective-permute-done | bytes 2097184 | tf_op jit(solution)/shard_map/cond/branch_1_fun/ppermute | solution.py:346
  90.6 5.6 %branch_1_fun.3.refs_1_.refs_2_ = bf16[2048,4096]{1,0:T(8,128)(2,1)} custom-call(s32[3]{0:T(128)S(1)} %get-tuple-element.16.place, bf16[256,4096]{1,0:T(8,128)(2,1)} %get-tuple-element.17.refs_0_, bf16[256,4096]{1,0:T(8,128)(2,1)S(1)} %collective-permute-done.1.refs_1_, bf16[256,4096]{1,0:T(8,128)(2,1)} %get-tuple-element.18.refs_2_, ...), custom_call_target="tpu_custom_call", output_to_operand_aliasing={{}: (5, {})} | custom-call | tf_op jit(solution)/shard_map/cond/branch_1_fun/pallas_call | solution.py:122
  96.2 13.9 %collective-permute-done.refs_0_ = bf16[256,4096]{1,0:T(8,128)(2,1)} collective-permute-done((bf16[256,4096]{1,0:T(8,128)(2,1)}, bf16[256,4096]{1,0:T(8,128)(2,1)}, u32[]{:S(2)}, u32[]{:S(2)}) %collective-permute-start) | collective-permute-done | bytes 2097184 | tf_op jit(solution)/shard_map/cond/branch_1_fun/ppermute | solution.py:343
  110.1 4.4 %collective-permute-done.3.refs_1_ = bf16[256,4096]{1,0:T(8,128)(2,1)S(1)} collective-permute-done((bf16[256,4096]{1,0:T(8,128)(2,1)}, bf16[256,4096]{1,0:T(8,128)(2,1)S(1)}, u32[]{:S(2)}, u32[]{:S(2)}) %collective-permute-start.3) | collective-permute-done | bytes 2097184 | tf_op jit(solution)/shard_map/cond/branch_1_fun/ppermute | solution.py:346
  114.5 3.6 %branch_1_fun.5 = bf16[2048,4096]{1,0:T(8,128)(2,1)} custom-call(s32[3]{0:T(128)S(1)} %get-tuple-element.16.place, bf16[256,4096]{1,0:T(8,128)(2,1)} %branch_1_fun.4.refs_0_, bf16[256,4096]{1,0:T(8,128)(2,1)S(1)} %collective-permute-done.3.refs_1_, bf16[2048,4096]{1,0:T(8,128)(2,1)} %branch_1_fun.3.refs_1_.refs_2_), custom_call_target="tpu_custom_call", output_to_operand_aliasing={{}: (3, {})} | custom-call | tf_op jit(solution)/shard_map/cond/branch_1_fun/pallas_call | solution.py:122
  122.2 9.4 %shard_map.58.kv_ref = bf16[2048,256]{1,0:T(8,128)(2,1)S(1)} custom-call(s32[3]{0:T(128)S(1)} %pad_add_fusion.1.place, bf16[2048,4096]{1,0:T(8,128)(2,1)} %get-tuple-element.45.x_ref, bf16[1024,768]{1,0:T(8,128)(2,1)S(1)} %copy-done.4, bf16[768,256]{1,0:T(8,128)(2,1)S(1)} %pad_maximum_fusion.6.refs_1_, bf16[768,256]{1,0:T(8,128)(2,1)S(1)} %copy-done.7, ...), custom_call_target="tpu_custom_call" | custom-call | flops 4294967296 | bytes 18874368 | tf_op jit(solution)/shard_map/pallas_call | solution.py:79
  132.6 3.7 %collective-permute-start.12 = (bf16[1536,256]{1,0:T(8,128)(2,1)}, bf16[1536,256]{1,0:T(8,128)(2,1)}, u32[]{:S(2)}, u32[]{:S(2)}) collective-permute-start(bf16[1536,256]{1,0:T(8,128)(2,1)} %slice.49), channel_id=1, source_target_pairs={{0,8},{2,10},{4,12},{6,14},{8,16},{10,18},{12,20},{14,22},{16,24},... | collective-permute-start | bytes 2359304 | tf_op jit(solution)/shard_map/ppermute | solution.py:407
  137.8 1.9 copy-done.10
  139.7 13.2 %shard_map.57.q_ref = bf16[2048,512]{1,0:T(8,128)(2,1)S(1)} custom-call(s32[3]{0:T(128)S(1)} %pad_add_fusion.1.place, bf16[2048,4096]{1,0:T(8,128)(2,1)} %get-tuple-element.45.x_ref, bf16[1024,768]{1,0:T(8,128)(2,1)S(1)} %copy-done.5, bf16[3072,512]{1,0:T(8,128)(2,1)S(1)} %copy-done.10, f32[2048,128]{1,0:T(8,128)S(1)} %copy-done, f32[2048,128]{1,0:T(8,128)S(1)} %copy-done.1), custom_call_target="tpu_custom_call" | custom-call | flops 8589934592 | bytes 20971520 | tf_op jit(solution)/shard_map/pallas_call | solution.py:79
  154.4 8.3 %shard_map.59 = bf16[512,512]{1,0:T(8,128)(2,1)} custom-call(s32[1]{0:T(128)} %bitcast.first, s32[3,8]{1,0:T(4,128)} %pad_add_fusion.refs_5_.bounds, s32[8]{0:T(128)} %broadcast_subtract_fusion.1.refs_4_.ends, bf16[2048,512]{1,0:T(8,128)(2,1)} %copy-done.11, bf16[1536,256]{1,0:T(8,128)(2,1)} %collective-permute-done.12.halo_ref, bf16[2048,256]{1,0:T(8,128)(2,1)} %copy-done.3), custom_call_target="tpu_custom_call" | custom-call | flops 1073741824 | bytes 1048576 | tf_op jit(solution)/shard_map/pallas_call | solution.py:222
  162.7 2.4 %collective-permute-start.13 = (bf16[512,512]{1,0:T(8,128)(2,1)}, bf16[512,512]{1,0:T(8,128)(2,1)S(1)}, u32[]{:S(2)}, u32[]{:S(2)}) collective-permute-start(bf16[512,512]{1,0:T(8,128)(2,1)} %shard_map.59), channel_id=1, source_target_pairs={{0,6},{2,4},{4,2},{6,0},{8,14},{10,12},{12,10},{14,8},{16,22},{18,... | collective-permute-start | bytes 1572872 | tf_op jit(solution)/shard_map/ppermute | solution.py:285
  165.1 6.5 %shard_map.60 = bf16[512,512]{1,0:T(8,128)(2,1)} custom-call(s32[1]{0:T(128)} %bitcast.7.first, s32[3,8]{1,0:T(4,128)} %pad_add_fusion.refs_5_.bounds, s32[8]{0:T(128)} %broadcast_subtract_fusion.1.refs_4_.ends, bf16[2048,512]{1,0:T(8,128)(2,1)} %copy-done.11, bf16[1536,256]{1,0:T(8,128)(2,1)} %collective-permute-done.12.halo_ref, bf16[2048,256]{1,0:T(8,128)(2,1)} %copy-done.3), custom_call_target="tpu_custom_call" | custom-call | flops 1073741824 | bytes 1048576 | tf_op jit(solution)/shard_map/pallas_call | solution.py:222
  171.7 3.6 %collective-permute-start.14 = (bf16[512,512]{1,0:T(8,128)(2,1)}, bf16[512,512]{1,0:T(8,128)(2,1)S(1)}, u32[]{:S(2)}, u32[]{:S(2)}) collective-permute-start(bf16[512,512]{1,0:T(8,128)(2,1)} %shard_map.60), channel_id=1, source_target_pairs={{0,4},{2,6},{4,0},{6,2},{8,12},{10,14},{12,8},{14,10},{16,20},{18,... | collective-permute-start | bytes 1572872 | tf_op jit(solution)/shard_map/ppermute | solution.py:285
  175.2 11.1 %shard_map.61 = bf16[512,512]{1,0:T(8,128)(2,1)} custom-call(s32[1]{0:T(128)} %bitcast.8.first, s32[3,8]{1,0:T(4,128)} %pad_add_fusion.refs_5_.bounds, s32[8]{0:T(128)} %broadcast_subtract_fusion.1.refs_4_.ends, bf16[2048,512]{1,0:T(8,128)(2,1)} %copy-done.11, bf16[1536,256]{1,0:T(8,128)(2,1)} %collective-permute-done.12.halo_ref, bf16[2048,256]{1,0:T(8,128)(2,1)} %copy-done.3), custom_call_target="tpu_custom_call" | custom-call | flops 1073741824 | bytes 1048576 | tf_op jit(solution)/shard_map/pallas_call | solution.py:222
  186.3 8.3 %shard_map.62 = bf16[512,512]{1,0:T(8,128)(2,1)} custom-call(s32[1]{0:T(128)} %bitcast.9.first, s32[3,8]{1,0:T(4,128)} %pad_add_fusion.refs_5_.bounds, s32[8]{0:T(128)} %broadcast_subtract_fusion.1.refs_4_.ends, bf16[2048,512]{1,0:T(8,128)(2,1)} %copy-done.11, bf16[1536,256]{1,0:T(8,128)(2,1)} %collective-permute-done.12.halo_ref, bf16[2048,256]{1,0:T(8,128)(2,1)} %copy-done.3), custom_call_target="tpu_custom_call" | custom-call | flops 1073741824 | bytes 1048576 | tf_op jit(solution)/shard_map/pallas_call | solution.py:222
  195.0 4.7 %collective-permute-done.15 = bf16[512,512]{1,0:T(8,128)(2,1)S(1)} collective-permute-done((bf16[512,512]{1,0:T(8,128)(2,1)}, bf16[512,512]{1,0:T(8,128)(2,1)S(1)}, u32[]{:S(2)}, u32[]{:S(2)}) %collective-permute-start.15) | collective-permute-done | bytes 524320 | tf_op jit(solution)/shard_map/ppermute | solution.py:285
  (89 shorter events, 24.2 us)
Async XLA Ops:
  6.5 1.4 copy-start.16
  6.5 1.4 copy-start.15
  6.5 112.2 %all-gather.3.cloned.1.call-start = ((), (), s32[]{:S(2)}) async-start(), calls=%async_computation | async-start | bytes 1966080 | tf_op jit(solution)/shard_map/all_gather | solution.py:289
  8.8 127.5 %all-gather.5.cloned.1.call-start = ((), (), s32[]{:S(2)}) async-start(), calls=%async_computation.1 | async-start | bytes 3932160 | tf_op jit(solution)/shard_map/all_gather | solution.py:289
  8.9 12.1 %collective-permute-start.5 = (bf16[256,768]{1,0:T(8,128)(2,1)S(1)}, bf16[256,768]{1,0:T(8,128)(2,1)S(1)}, u32[]{:S(2)}, u32[]{:S(2)}) collective-permute-start(bf16[256,768]{1,0:T(8,128)(2,1)S(1)} %pad_maximum_fusion.3), channel_id=1, source_target_pairs={{0,2},{2,0},{4,6},{6,4},{8,10},{10,8},{12,14},{14,12},{16,18},{18,... | collective-permute-start | bytes 1179656 | tf_op jit(solution)/shard_map/ppermute | solution.py:285
  10.5 19.1 %collective-permute-start.6 = (bf16[256,768]{1,0:T(8,128)(2,1)S(1)}, bf16[256,768]{1,0:T(8,128)(2,1)S(1)}, u32[]{:S(2)}, u32[]{:S(2)}) collective-permute-start(bf16[256,768]{1,0:T(8,128)(2,1)S(1)} %pad_maximum_fusion.4), channel_id=1, source_target_pairs={{0,4},{2,6},{4,0},{6,2},{8,12},{10,14},{12,8},{14,10},{16,20},{18,... | collective-permute-start | bytes 1179656 | tf_op jit(solution)/shard_map/ppermute | solution.py:285
  12.1 17.5 %collective-permute-start.7 = (bf16[256,768]{1,0:T(8,128)(2,1)S(1)}, bf16[256,768]{1,0:T(8,128)(2,1)S(1)}, u32[]{:S(2)}, u32[]{:S(2)}) collective-permute-start(bf16[256,768]{1,0:T(8,128)(2,1)S(1)} %pad_maximum_fusion.5), channel_id=1, source_target_pairs={{0,6},{2,4},{4,2},{6,0},{8,14},{10,12},{12,10},{14,8},{16,22},{18,... | collective-permute-start | bytes 1179656 | tf_op jit(solution)/shard_map/ppermute | solution.py:285
  30.6 5.2 %copy-start.17 = (s32[8]{0:T(128)S(1)}, s32[8]{0:T(128)}, u32[]{:S(2)}) copy-start(s32[8]{0:T(128)} %param.8) | copy-start | bytes 100
  33.8 46.7 %collective-permute-start.4 = (bf16[256,4096]{1,0:T(8,128)(2,1)}, bf16[256,4096]{1,0:T(8,128)(2,1)}, u32[]{:S(2)}, u32[]{:S(2)}) collective-permute-start(bf16[256,4096]{1,0:T(8,128)(2,1)} %constant_dynamic-slice_fusion.12), channel_id=1, source_target_pairs={{0,2},{1,5},{2,0},{3,7},{4,6},{5,1},{6,4},{7,3},{8,10},{9,13},{10,... | collective-permute-start | bytes 6291464 | tf_op jit(solution)/shard_map/ppermute | solution.py:343
  34.9 48.2 %collective-permute-start.10 = (bf16[256,4096]{1,0:T(8,128)(2,1)}, bf16[256,4096]{1,0:T(8,128)(2,1)}, u32[]{:S(2)}, u32[]{:S(2)}) collective-permute-start(bf16[256,4096]{1,0:T(8,128)(2,1)} %constant_dynamic-slice_fusion.12), channel_id=1, source_target_pairs={{0,4},{1,3},{2,6},{3,1},{4,0},{5,7},{6,2},{7,5},{8,12},{9,11},{10,... | collective-permute-start | bytes 6291464 | tf_op jit(solution)/shard_map/ppermute | solution.py:343
  36.3 16.6 %collective-permute-start.8 = (bf16[768,256]{1,0:T(8,128)(2,1)S(1)}, bf16[768,256]{1,0:T(8,128)(2,1)S(1)}, u32[]{:S(2)}, u32[]{:S(2)}) collective-permute-start(bf16[768,256]{1,0:T(8,128)(2,1)S(1)} %pad_maximum_fusion.6.refs_1_), channel_id=1, source_target_pairs={{0,8},{2,10},{4,12},{6,14},{8,16},{10,18},{12,20},{14,22},{16,24},... | collective-permute-start | bytes 1179656 | tf_op jit(solution)/shard_map/ppermute | solution.py:292
  52.9 10.7 %collective-permute-start.9 = (bf16[768,256]{1,0:T(8,128)(2,1)S(1)}, bf16[768,256]{1,0:T(8,128)(2,1)}, u32[]{:S(2)}, u32[]{:S(2)}) collective-permute-start(bf16[768,256]{1,0:T(8,128)(2,1)S(1)} %collective-permute-done.8.refs_2_), channel_id=1, source_target_pairs={{0,8},{2,10},{4,12},{6,14},{8,16},{10,18},{12,20},{14,22},{16,24},... | collective-permute-start | bytes 1179656 | tf_op jit(solution)/shard_map/ppermute | solution.py:292
  63.5 54.5 %collective-permute-start.11 = (bf16[768,256]{1,0:T(8,128)(2,1)}, bf16[768,256]{1,0:T(8,128)(2,1)S(1)}, u32[]{:S(2)}, u32[]{:S(2)}) collective-permute-start(bf16[768,256]{1,0:T(8,128)(2,1)} %collective-permute-done.9.refs_1_.refs_3_), channel_id=1, source_target_pairs={{0,8},{2,10},{4,12},{6,14},{8,16},{10,18},{12,20},{14,22},{16,24},... | collective-permute-start | bytes 1179656 | tf_op jit(solution)/shard_map/ppermute | solution.py:292
  65.5 2.2 %copy-start.2 = (bf16[512,4096]{1,0:T(8,128)(2,1)S(1)}, bf16[512,4096]{1,0:T(8,128)(2,1)}, u32[]{:S(2)}) copy-start(bf16[512,4096]{1,0:T(8,128)(2,1)} %refs_0_.1) | copy-start | bytes 12582916
  67.7 3.1 %copy-start.12 = (f32[2048,64]{1,0:T(8,128)S(1)}, f32[2048,64]{1,0:T(8,128)}, u32[]{:S(2)}) copy-start(f32[2048,64]{1,0:T(8,128)} %get-tuple-element.36) | copy-start | bytes 1572868
  83.1 35.7 %copy-start = (f32[2048,128]{1,0:T(8,128)S(1)}, f32[2048,128]{1,0:T(8,128)}, u32[]{:S(2)}) copy-start(f32[2048,128]{1,0:T(8,128)} %get-tuple-element.43.refs_2_.refs_5_) | copy-start | bytes 3145732
  83.1 35.7 %copy-start.1 = (f32[2048,128]{1,0:T(8,128)S(1)}, f32[2048,128]{1,0:T(8,128)}, u32[]{:S(2)}) copy-start(f32[2048,128]{1,0:T(8,128)} %get-tuple-element.44.refs_3_.refs_6_) | copy-start | bytes 3145732
  83.2 4.4 %collective-permute-start.1 = (bf16[256,4096]{1,0:T(8,128)(2,1)}, bf16[256,4096]{1,0:T(8,128)(2,1)S(1)}, u32[]{:S(2)}, u32[]{:S(2)}) collective-permute-start(bf16[256,4096]{1,0:T(8,128)(2,1)} %get-tuple-element.17.refs_0_), channel_id=1, source_target_pairs={{0,1},{1,0},{2,3},{3,2},{4,5},{5,4},{6,7},{7,6},{8,9},{9,8},{10,11... | collective-permute-start | bytes 6291464 | tf_op jit(solution)/shard_map/cond/branch_1_fun/ppermute | solution.py:346
  83.2 7.4 %collective-permute-start.2 = (bf16[256,4096]{1,0:T(8,128)(2,1)}, bf16[256,4096]{1,0:T(8,128)(2,1)S(1)}, u32[]{:S(2)}, u32[]{:S(2)}) collective-permute-start(bf16[256,4096]{1,0:T(8,128)(2,1)} %get-tuple-element.18.refs_2_), channel_id=1, source_target_pairs={{0,1},{1,0},{2,3},{3,2},{4,5},{5,4},{6,7},{7,6},{8,9},{9,8},{10,11... | collective-permute-start | bytes 6291464 | tf_op jit(solution)/shard_map/cond/branch_1_fun/ppermute | solution.py:346
  83.7 26.4 %collective-permute-start = (bf16[256,4096]{1,0:T(8,128)(2,1)}, bf16[256,4096]{1,0:T(8,128)(2,1)}, u32[]{:S(2)}, u32[]{:S(2)}) collective-permute-start(bf16[256,4096]{1,0:T(8,128)(2,1)} %get-tuple-element.17.refs_0_), channel_id=1, source_target_pairs={{0,4},{1,3},{2,6},{3,1},{4,0},{5,7},{6,2},{7,5},{8,12},{9,11},{10,... | collective-permute-start | bytes 6291464 | tf_op jit(solution)/shard_map/cond/branch_1_fun/ppermute | solution.py:343
  110.1 4.4 %collective-permute-start.3 = (bf16[256,4096]{1,0:T(8,128)(2,1)}, bf16[256,4096]{1,0:T(8,128)(2,1)S(1)}, u32[]{:S(2)}, u32[]{:S(2)}) collective-permute-start(bf16[256,4096]{1,0:T(8,128)(2,1)} %branch_1_fun.4.refs_0_), channel_id=1, source_target_pairs={{0,1},{1,0},{2,3},{3,2},{4,5},{5,4},{6,7},{7,6},{8,9},{9,8},{10,11... | collective-permute-start | bytes 6291464 | tf_op jit(solution)/shard_map/cond/branch_1_fun/ppermute | solution.py:346
  118.8 1.4 copy-start.4
  131.6 21.4 %copy-start.3 = (bf16[2048,256]{1,0:T(8,128)(2,1)}, bf16[2048,256]{1,0:T(8,128)(2,1)S(1)}, u32[]{:S(2)}) copy-start(bf16[2048,256]{1,0:T(8,128)(2,1)S(1)} %shard_map.58.kv_ref) | copy-start | bytes 3145732
  132.6 21.8 %collective-permute-start.12 = (bf16[1536,256]{1,0:T(8,128)(2,1)}, bf16[1536,256]{1,0:T(8,128)(2,1)}, u32[]{:S(2)}, u32[]{:S(2)}) collective-permute-start(bf16[1536,256]{1,0:T(8,128)(2,1)} %slice.49), channel_id=1, source_target_pairs={{0,8},{2,10},{4,12},{6,14},{8,16},{10,18},{12,20},{14,22},{16,24},... | collective-permute-start | bytes 2359304 | tf_op jit(solution)/shard_map/ppermute | solution.py:407
  136.4 1.4 copy-start.5
  137.8 1.9 copy-start.10
  152.9 1.3 copy-start.11
  162.7 31.9 %collective-permute-start.13 = (bf16[512,512]{1,0:T(8,128)(2,1)}, bf16[512,512]{1,0:T(8,128)(2,1)S(1)}, u32[]{:S(2)}, u32[]{:S(2)}) collective-permute-start(bf16[512,512]{1,0:T(8,128)(2,1)} %shard_map.59), channel_id=1, source_target_pairs={{0,6},{2,4},{4,2},{6,0},{8,14},{10,12},{12,10},{14,8},{16,22},{18,... | collective-permute-start | bytes 1572872 | tf_op jit(solution)/shard_map/ppermute | solution.py:285
  171.7 23.3 %collective-permute-start.14 = (bf16[512,512]{1,0:T(8,128)(2,1)}, bf16[512,512]{1,0:T(8,128)(2,1)S(1)}, u32[]{:S(2)}, u32[]{:S(2)}) collective-permute-start(bf16[512,512]{1,0:T(8,128)(2,1)} %shard_map.60), channel_id=1, source_target_pairs={{0,4},{2,6},{4,0},{6,2},{8,12},{10,14},{12,8},{14,10},{16,20},{18,... | collective-permute-start | bytes 1572872 | tf_op jit(solution)/shard_map/ppermute | solution.py:285
  186.3 13.4 %collective-permute-start.15 = (bf16[512,512]{1,0:T(8,128)(2,1)}, bf16[512,512]{1,0:T(8,128)(2,1)S(1)}, u32[]{:S(2)}, u32[]{:S(2)}) collective-permute-start(bf16[512,512]{1,0:T(8,128)(2,1)} %shard_map.61), channel_id=1, source_target_pairs={{0,2},{2,0},{4,6},{6,4},{8,10},{10,8},{12,14},{14,12},{16,18},{18,... | collective-permute-start | bytes 1572872 | tf_op jit(solution)/shard_map/ppermute | solution.py:285
  194.9 6.2 %copy-start.14 = (bf16[512,512]{1,0:T(8,128)(2,1)S(1)}, bf16[512,512]{1,0:T(8,128)(2,1)}, u32[]{:S(2)}) copy-start(bf16[512,512]{1,0:T(8,128)(2,1)} %shard_map.62) | copy-start | bytes 1572868
  199.8 1.3 copy-start.13
  (4 other events, 3.5 us)
Sparse Core Ops, SparseCore 0:
  9.0 44.8 all-gather.2
  55.4 70.9 all-gather.4

commit v5 on v4

--- a/solution.py
+++ b/solution.py
@@ -357,6 +357,7 @@
             return target
 
 
+        others = range(1, group)
         near = cross(own_half, (1, 2))
         other = cross(own_half, (2, 1))
 
@@ -366,14 +367,18 @@
                 held.append(forwarded(held[-1]))
             return put(place, group_rows, [(tokens, lambda s: s[0] * row_count)]), tables(), tuple(held[1:])
 
-        def share(everything, near, other):
+        def share(everything, near, other, own_slices, held, cosine, sine):
             far = cross(near, (2, 1))
             mates = [swap(block) for block in (near, other)]
             first = [(near, home(1, 2, 0)), (mates[0], home(1, 2, 1)), (other, home(2, 1, 0)), (mates[1], home(2, 1, 1))]
             everything = put(place, group_rows, first, everything)
-            far = after(far, everything)
+            weights = [gathered(own_slices, (q_width // kv_width, kv_width), 0, [0])] + from_lines(held, 0, others)
+            kv = project(group, place, everything, weights, kv_width, cosine, sine, kv_heads, (0, group - 1))
+            far = after(far, kv)
             last = [(far, home(3, 3, 0)), (swap(far), home(3, 3, 1))]
-            return put(place, group_rows, last, everything)
+            everything = put(place, group_rows, last, everything)
+            span = (group - 1, 1)
+            return everything, project(group, place, everything, weights, kv_width, cosine, sine, kv_heads, span, kv)
 
         def region(body, flag, *operands):
             def nothing(*operands):
@@ -384,21 +389,19 @@
             return lax.cond(known == known, body, nothing, *operands)
 
         all_tokens, known_tables, held = prepare(tokens, rest_kv)
-        held = (*held, forwarded(held[-1]))
-        near = after(near, held[1], *known_tables)
-        all_tokens = region(share, near[:1, :1], all_tokens, near, other)
-        others = range(1, group)
-        kv_weights = [gathered(own_slices, (q_width // kv_width, kv_width), 0, [0])]
-        kv_weights += from_lines((rest_kv, *held), 0, others)
+        held = (rest_kv, *held, forwarded(held[-1]))
+        near = after(near, held[2], *known_tables)
+        operands = (all_tokens, near, other, own_slices, held, *known_tables[:2])
+        all_tokens, kv = region(share, near[:1, :1], *operands)
         q_weights = [gathered(own_slices, (0, q_width), 0, [0]), gathered(rest_q, (0, q_width), 0, others)]
     else:
         all_tokens, known_tables = tokens, tables()
         own = along_lines(slice_for(mine))
         kv_weights = [gathered(own, (q_width // kv_width, kv_width), 0, [0])]
         q_weights = [gathered(own, (0, q_width), 0, [0])]
+        kv = project(group, place, tokens, kv_weights, kv_width, *known_tables[:2], kv_heads, (0, group))
     cosine, sine, ends, bounds = known_tables
 
-    kv = project(group, place, all_tokens, kv_weights, kv_width, cosine, sine, kv_heads, (0, group))
     hops = -(-halo_rows // group_rows)
     pieces, moving = [], kv
     for hop in range(hops):

time: 209 us -> 211 us (level)
  Pallas kernels: 68.5 us -> 73.3 us
    ppermute x3, waiting for transfers between devices: 17 us -> 25.9 us  [forwarded(): lax.ppermute(block, 'ca', [(i, (i + group) % (group * lines)) for i in de...]
    ppermute x3, waiting for transfers between devices: 21.5 us -> 14.3 us  [cross(): return lax.ppermute(block, both, pairs)]
    unnamed x36 -> x28, local copies, waits for them, and re-layouts: 13.1 us -> 7.68 us
    pallas_call x2 -> x3, Pallas kernels: 22.6 us -> 27.4 us  [project(): pl.pallas_call(functools.partial(project_kernel, rope_heads, layout, len(...]
    cond x0 -> x22, local copies, waits for them, and re-layouts: none -> 4.3 us
    ppermute x6, waiting for transfers between devices: 21.6 us -> 19 us  [to_partner(): return lax.ppermute(block, 'ca', [(i, i ^ step) for i in devices])]
  transfers between devices with their start and end apart: 18 -> 18, of which waited for: 11 -> 11; matrix products, arithmetic and copies ran while one was open for 8% -> 7% of each run, Pallas kernels for 29% -> 31%
where the time goes in v5:
time: 211 us; the launch traced here: 210 us
  Pallas kernels  73.3 us (35%)
  waiting for transfers between devices  68.5 us (32%)
  starting transfers between devices  22.7 us (11%)
  local copies, waits for them, and re-layouts  20.5 us (10%)
  between operations  15 us (7%)
  other arithmetic  9.61 us (5%)
    pallas_call x4, Pallas kernels, attend(): pl.pallas_call(kernel, out_shape=jax.ShapeDtypeStruct((chunk_rows, width)...  35 us
    pallas_call x3, Pallas kernels, project(): pl.pallas_call(functools.partial(project_kernel, rope_heads, layout, len(...  27.4 us
    ppermute x3, waiting for transfers between devices, forwarded(): lax.ppermute(block, 'ca', [(i, (i + group) % (group * lines)) for i in de...  25.9 us
    ppermute x6, waiting for transfers between devices, to_partner(): return lax.ppermute(block, 'ca', [(i, i ^ step) for i in devices])  19 us
    ppermute x3, waiting for transfers between devices, cross(): return lax.ppermute(block, both, pairs)  14.3 us
    pallas_call x3, Pallas kernels, put(): pl.pallas_call(functools.partial(put_kernel, targets), out_shape=jax.Shap...  10.8 us
    ppermute x3, waiting for transfers between devices, swap(): lax.ppermute(block, both, [(i * 2 + c, i * 2 + 1 - c) for i in devices fo...  9.16 us
    ppermute x6, starting transfers between devices, to_partner(): return lax.ppermute(block, 'ca', [(i, i ^ step) for i in devices])  8.94 us
  transfers between devices with their start and end apart: 18, of which 11 were waited for; matrix products, arithmetic and copies ran while one was open for 7% of the time, Pallas kernels for 31%

profile of v5, /device:TPU:16, one launch (start us, length us, event | category | flops | bytes accessed | tf_op | source)
XLA Modules:
  0.0 209.6 jit_solution(5778640829458980507)
XLA Ops:
  12.7 8.3 %collective-permute-done.5 = bf16[256,768]{1,0:T(8,128)(2,1)S(1)} collective-permute-done((bf16[256,768]{1,0:T(8,128)(2,1)S(1)}, bf16[256,768]{1,0:T(8,128)(2,1)S(1)}, u32[]{:S(2)}, u32[]{:S(2)}) %collective-permute-start.5) | collective-permute-done | bytes 393248 | tf_op jit(solution)/shard_map/ppermute | solution.py:285
  21.0 8.6 %collective-permute-done.6 = bf16[256,768]{1,0:T(8,128)(2,1)S(1)} collective-permute-done((bf16[256,768]{1,0:T(8,128)(2,1)S(1)}, bf16[256,768]{1,0:T(8,128)(2,1)S(1)}, u32[]{:S(2)}, u32[]{:S(2)}) %collective-permute-start.6) | collective-permute-done | bytes 393248 | tf_op jit(solution)/shard_map/ppermute | solution.py:285
  30.7 3.1 %constant_dynamic-slice_fusion.12 = bf16[256,4096]{1,0:T(8,128)(2,1)} fusion(bf16[512,4096]{1,0:T(8,128)(2,1)} %refs_0_.1, s32[]{:T(128)S(6)} %select_n.53), kind=kLoop, calls=%fused_computation.30 | loop fusion | bytes 4194308 | tf_op jit(solution)/shard_map/dynamic_slice | solution.py:350
  38.7 14.2 %collective-permute-done.8 = bf16[768,256]{1,0:T(8,128)(2,1)S(1)} collective-permute-done((bf16[768,256]{1,0:T(8,128)(2,1)S(1)}, bf16[768,256]{1,0:T(8,128)(2,1)S(1)}, u32[]{:S(2)}, u32[]{:S(2)}) %collective-permute-start.8) | collective-permute-done | bytes 393248 | tf_op jit(solution)/shard_map/ppermute | solution.py:292
  52.9 1.7 collective-permute-start.9
  54.6 5.5 %fusion = (f32[2048,64]{1,0:T(8,128)S(1)}, f32[2048,64]{1,0:T(8,128)}, f32[2048,64]{1,0:T(8,128)}) fusion(f32[64]{0:T(128)S(1)} %multiply_power_fusion, f32[2048]{0:T(1024)S(1)} %get-tuple-element.59), kind=kLoop, calls=%fused_computation.10 | loop fusion | flops 262144 | bytes 1581312 | tf_op jit(solution)/shard_map/neg | solution.py:35
  60.2 3.3 %collective-permute-done.9.refs_1_ = bf16[768,256]{1,0:T(8,128)(2,1)S(1)} collective-permute-done((bf16[768,256]{1,0:T(8,128)(2,1)S(1)}, bf16[768,256]{1,0:T(8,128)(2,1)S(1)}, u32[]{:S(2)}, u32[]{:S(2)}) %collective-permute-start.9) | collective-permute-done | bytes 393248 | tf_op jit(solution)/shard_map/ppermute | solution.py:292
  63.4 1.9 collective-permute-start.11
  65.4 2.2 %copy-done = bf16[512,4096]{1,0:T(8,128)(2,1)S(1)} copy-done((bf16[512,4096]{1,0:T(8,128)(2,1)S(1)}, bf16[512,4096]{1,0:T(8,128)(2,1)}, u32[]{:S(2)}) %copy-start) | copy-done | bytes 4194328
  67.7 2.5 %shard_map.56 = bf16[2048,4096]{1,0:T(8,128)(2,1)} custom-call(s32[3]{0:T(128)S(1)} %pad_add_fusion.1.place, bf16[512,4096]{1,0:T(8,128)(2,1)S(1)} %copy-done), custom_call_target="tpu_custom_call" | custom-call | tf_op jit(solution)/shard_map/pallas_call | solution.py:122
  71.4 9.1 %collective-permute-done.4.refs_0_ = bf16[256,4096]{1,0:T(8,128)(2,1)} collective-permute-done((bf16[256,4096]{1,0:T(8,128)(2,1)}, bf16[256,4096]{1,0:T(8,128)(2,1)}, u32[]{:S(2)}, u32[]{:S(2)}) %collective-permute-start.4) | collective-permute-done | bytes 2097184 | tf_op jit(solution)/shard_map/ppermute | solution.py:343
  83.0 8.5 %collective-permute-done.11 = bf16[768,256]{1,0:T(8,128)(2,1)} collective-permute-done((bf16[768,256]{1,0:T(8,128)(2,1)S(1)}, bf16[768,256]{1,0:T(8,128)(2,1)}, u32[]{:S(2)}, u32[]{:S(2)}) %collective-permute-start.11) | collective-permute-done | bytes 393248 | tf_op jit(solution)/shard_map/ppermute | solution.py:292
  91.5 42.5 %conditional.1 = (bf16[2048,4096]{1,0:T(8,128)(2,1)}, bf16[2048,256]{1,0:T(8,128)(2,1)}) conditional(s32[]{:T(128)} %bitcast.6, () %tuple.13, (bf16[256,4096]{1,0:T(8,128)(2,1)}, bf16[256,4096]{1,0:T(8,128)(2,1)}, s32[3]{0:T(128)S(1)}, bf16[2048,4096]{1,0:T(8,128)(2,1)}, bf16[1024,768]{1,0:T(8,128)(2,1)}, /*index=5*/bf16[768,256]{1,0:T(8,128)(2,1)}, ...), branch_computations={%region_2.3_spmd, %region_3.4_spmd} | conditional | flops 4294967296 | bytes 102760936 | solution.py:389
  92.5 1.7 collective-permute-start
  94.2 1.8 collective-permute-done.1.refs_1_
  96.0 3.0 %collective-permute-done.2.refs_3_ = bf16[256,4096]{1,0:T(8,128)(2,1)S(1)} collective-permute-done((bf16[256,4096]{1,0:T(8,128)(2,1)}, bf16[256,4096]{1,0:T(8,128)(2,1)S(1)}, u32[]{:S(2)}, u32[]{:S(2)}) %collective-permute-start.2) | collective-permute-done | bytes 2097184 | tf_op jit(solution)/shard_map/cond/branch_1_fun/ppermute | solution.py:346
  99.0 5.8 %branch_1_fun.5.x_ref.refs_2_ = bf16[2048,4096]{1,0:T(8,128)(2,1)} custom-call(s32[3]{0:T(128)S(1)} %get-tuple-element.27.place, bf16[256,4096]{1,0:T(8,128)(2,1)} %get-tuple-element.28.refs_0_, bf16[256,4096]{1,0:T(8,128)(2,1)S(1)} %collective-permute-done.1.refs_1_, bf16[256,4096]{1,0:T(8,128)(2,1)} %get-tuple-element.29.refs_2_, ...), custom_call_target="tpu_custom_call", output_to_operand_aliasing={{}: (5, {})} | custom-call | tf_op jit(solution)/shard_map/cond/branch_1_fun/pallas_call | solution.py:122
  104.8 8.8 %branch_1_fun.6.refs_1_.refs_7_ = bf16[2048,256]{1,0:T(8,128)(2,1)} custom-call(s32[3]{0:T(128)S(1)} %get-tuple-element.27.place, bf16[2048,4096]{1,0:T(8,128)(2,1)} %branch_1_fun.5.x_ref.refs_2_, bf16[1024,768]{1,0:T(8,128)(2,1)S(1)} %copy-done.9, bf16[768,256]{1,0:T(8,128)(2,1)S(1)} %copy-done.14, bf16[768,256]{1,0:T(8,128)(2,1)S(1)} %copy-done.18, ...), custom_call_target="tpu_custom_call" | custom-call | flops 3221225472 | bytes 14680064 | tf_op jit(solution)/shard_map/cond/branch_1_fun/pallas_call | solution.py:79
  113.6 5.2 %collective-permute-done.refs_0_ = bf16[256,4096]{1,0:T(8,128)(2,1)S(1)} collective-permute-done((bf16[256,4096]{1,0:T(8,128)(2,1)}, bf16[256,4096]{1,0:T(8,128)(2,1)S(1)}, u32[]{:S(2)}, u32[]{:S(2)}) %collective-permute-start) | collective-permute-done | bytes 2097184 | tf_op jit(solution)/shard_map/cond/branch_1_fun/ppermute | solution.py:343
  120.1 4.4 %collective-permute-done.3.refs_1_ = bf16[256,4096]{1,0:T(8,128)(2,1)S(1)} collective-permute-done((bf16[256,4096]{1,0:T(8,128)(2,1)}, bf16[256,4096]{1,0:T(8,128)(2,1)S(1)}, u32[]{:S(2)}, u32[]{:S(2)}) %collective-permute-start.3) | collective-permute-done | bytes 2097184 | tf_op jit(solution)/shard_map/cond/branch_1_fun/ppermute | solution.py:346
  126.1 2.5 %branch_1_fun.8.x_ref = bf16[2048,4096]{1,0:T(8,128)(2,1)} custom-call(s32[3]{0:T(128)S(1)} %get-tuple-element.27.place, bf16[256,4096]{1,0:T(8,128)(2,1)S(1)} %copy-done.2, bf16[256,4096]{1,0:T(8,128)(2,1)S(1)} %collective-permute-done.3.refs_1_, bf16[2048,4096]{1,0:T(8,128)(2,1)} %branch_1_fun.5.x_ref.refs_2_), custom_call_target="tpu_custom_call", output_to_operand_aliasing={{}: (3, {})} | custom-call | tf_op jit(solution)/shard_map/cond/branch_1_fun/pallas_call | solution.py:122
  129.1 5.0 %branch_1_fun.9 = bf16[2048,256]{1,0:T(8,128)(2,1)} custom-call(s32[3]{0:T(128)S(1)} %get-tuple-element.27.place, bf16[2048,4096]{1,0:T(8,128)(2,1)} %branch_1_fun.8.x_ref, bf16[1024,768]{1,0:T(8,128)(2,1)S(1)} %copy-done.10, bf16[768,256]{1,0:T(8,128)(2,1)S(1)} %copy-done.15, bf16[768,256]{1,0:T(8,128)(2,1)S(1)} %copy-done.19, ...), custom_call_target="tpu_custom_call", output_to_operand_aliasing={{}: (9, {})} | custom-call | flops 1073741824 | bytes 6291456 | tf_op jit(solution)/shard_map/cond/branch_1_fun/pallas_call | solution.py:79
  135.2 4.7 %collective-permute-start.12 = (bf16[1536,256]{1,0:T(8,128)(2,1)S(1)}, bf16[1536,256]{1,0:T(8,128)(2,1)S(1)}, u32[]{:S(2)}, u32[]{:S(2)}) collective-permute-start(bf16[1536,256]{1,0:T(8,128)(2,1)S(1)} %slice.39), channel_id=1, source_target_pairs={{0,8},{2,10},{4,12},{6,14},{8,16},{10,18},{12,20},{14,22},{16,24},... | collective-permute-start | bytes 2359304 | tf_op jit(solution)/shard_map/ppermute | solution.py:410
  140.0 1.9 copy-done.3
  141.8 13.7 %shard_map.57.q_ref = bf16[2048,512]{1,0:T(8,128)(2,1)S(1)} custom-call(s32[3]{0:T(128)S(1)} %pad_add_fusion.1.place, bf16[2048,4096]{1,0:T(8,128)(2,1)} %get-tuple-element.40.x_ref, bf16[1024,768]{1,0:T(8,128)(2,1)} %all-gather.3.cloned.1.call-done.refs_0_, bf16[3072,512]{1,0:T(8,128)(2,1)S(1)} %copy-done.3, f32[2048,128]{1,0:T(8,128)S(1)} %get-tuple-element.65.refs_2_, ...), custom_call_target="tpu_custom_call" | custom-call | flops 8589934592 | bytes 20971520 | tf_op jit(solution)/shard_map/pallas_call | solution.py:79
  157.7 9.2 %shard_map.58 = bf16[512,512]{1,0:T(8,128)(2,1)} custom-call(s32[1]{0:T(128)} %bitcast.first, s32[3,8]{1,0:T(4,128)} %pad_add_fusion.refs_5_.bounds, s32[8]{0:T(128)} %broadcast_subtract_fusion.1.refs_4_.ends, bf16[2048,512]{1,0:T(8,128)(2,1)} %copy-done.4, bf16[1536,256]{1,0:T(8,128)(2,1)} %copy-done.23, bf16[2048,256]{1,0:T(8,128)(2,1)} %get-tuple-element.41.kv_ref), custom_call_target="tpu_custom_call" | custom-call | flops 1073741824 | bytes 1048576 | tf_op jit(solution)/shard_map/pallas_call | solution.py:222
  168.4 7.4 %shard_map.59 = bf16[512,512]{1,0:T(8,128)(2,1)} custom-call(s32[1]{0:T(128)} %bitcast.7.first, s32[3,8]{1,0:T(4,128)} %pad_add_fusion.refs_5_.bounds, s32[8]{0:T(128)} %broadcast_subtract_fusion.1.refs_4_.ends, bf16[2048,512]{1,0:T(8,128)(2,1)} %copy-done.4, bf16[1536,256]{1,0:T(8,128)(2,1)} %copy-done.23, bf16[2048,256]{1,0:T(8,128)(2,1)} %get-tuple-element.41.kv_ref), custom_call_target="tpu_custom_call" | custom-call | flops 1073741824 | bytes 1048576 | tf_op jit(solution)/shard_map/pallas_call | solution.py:222
  175.8 1.9 collective-permute-start.14
  177.6 9.3 %shard_map.60 = bf16[512,512]{1,0:T(8,128)(2,1)} custom-call(s32[1]{0:T(128)} %bitcast.8.first, s32[3,8]{1,0:T(4,128)} %pad_add_fusion.refs_5_.bounds, s32[8]{0:T(128)} %broadcast_subtract_fusion.1.refs_4_.ends, bf16[2048,512]{1,0:T(8,128)(2,1)} %copy-done.4, bf16[1536,256]{1,0:T(8,128)(2,1)} %copy-done.23, bf16[2048,256]{1,0:T(8,128)(2,1)} %get-tuple-element.41.kv_ref), custom_call_target="tpu_custom_call" | custom-call | flops 1073741824 | bytes 1048576 | tf_op jit(solution)/shard_map/pallas_call | solution.py:222
  186.9 1.9 collective-permute-start.15
  188.9 9.2 %shard_map.61 = bf16[512,512]{1,0:T(8,128)(2,1)} custom-call(s32[1]{0:T(128)} %bitcast.9.first, s32[3,8]{1,0:T(4,128)} %pad_add_fusion.refs_5_.bounds, s32[8]{0:T(128)} %broadcast_subtract_fusion.1.refs_4_.ends, bf16[2048,512]{1,0:T(8,128)(2,1)} %copy-done.4, bf16[1536,256]{1,0:T(8,128)(2,1)} %copy-done.23, bf16[2048,256]{1,0:T(8,128)(2,1)} %get-tuple-element.41.kv_ref), custom_call_target="tpu_custom_call" | custom-call | flops 1073741824 | bytes 1048576 | tf_op jit(solution)/shard_map/pallas_call | solution.py:222
  198.4 2.1 %collective-permute-done.15 = bf16[512,512]{1,0:T(8,128)(2,1)S(1)} collective-permute-done((bf16[512,512]{1,0:T(8,128)(2,1)}, bf16[512,512]{1,0:T(8,128)(2,1)S(1)}, u32[]{:S(2)}, u32[]{:S(2)}) %collective-permute-start.15) | collective-permute-done | bytes 524320 | tf_op jit(solution)/shard_map/ppermute | solution.py:285
  (104 shorter events, 26.3 us)
Async XLA Ops:
  6.5 85.0 %all-gather.3.cloned.1.call-start = ((), (), s32[]{:S(2)}) async-start(), calls=%async_computation | async-start | bytes 1966080 | tf_op jit(solution)/shard_map/all_gather | solution.py:289
  8.8 131.1 %all-gather.5.cloned.1.call-start = ((), (), s32[]{:S(2)}) async-start(), calls=%async_computation.1 | async-start | bytes 3932160 | tf_op jit(solution)/shard_map/all_gather | solution.py:289
  8.9 12.1 %collective-permute-start.5 = (bf16[256,768]{1,0:T(8,128)(2,1)S(1)}, bf16[256,768]{1,0:T(8,128)(2,1)S(1)}, u32[]{:S(2)}, u32[]{:S(2)}) collective-permute-start(bf16[256,768]{1,0:T(8,128)(2,1)S(1)} %pad_maximum_fusion.3), channel_id=1, source_target_pairs={{0,2},{2,0},{4,6},{6,4},{8,10},{10,8},{12,14},{14,12},{16,18},{18,... | collective-permute-start | bytes 1179656 | tf_op jit(solution)/shard_map/ppermute | solution.py:285
  10.5 19.1 %collective-permute-start.6 = (bf16[256,768]{1,0:T(8,128)(2,1)S(1)}, bf16[256,768]{1,0:T(8,128)(2,1)S(1)}, u32[]{:S(2)}, u32[]{:S(2)}) collective-permute-start(bf16[256,768]{1,0:T(8,128)(2,1)S(1)} %pad_maximum_fusion.4), channel_id=1, source_target_pairs={{0,4},{2,6},{4,0},{6,2},{8,12},{10,14},{12,8},{14,10},{16,20},{18,... | collective-permute-start | bytes 1179656 | tf_op jit(solution)/shard_map/ppermute | solution.py:285
  12.1 17.5 %collective-permute-start.7 = (bf16[256,768]{1,0:T(8,128)(2,1)S(1)}, bf16[256,768]{1,0:T(8,128)(2,1)S(1)}, u32[]{:S(2)}, u32[]{:S(2)}) collective-permute-start(bf16[256,768]{1,0:T(8,128)(2,1)S(1)} %pad_maximum_fusion.5), channel_id=1, source_target_pairs={{0,6},{2,4},{4,2},{6,0},{8,14},{10,12},{12,10},{14,8},{16,22},{18,... | collective-permute-start | bytes 1179656 | tf_op jit(solution)/shard_map/ppermute | solution.py:285
  30.7 5.2 %copy-start.24 = (s32[8]{0:T(128)S(1)}, s32[8]{0:T(128)}, u32[]{:S(2)}) copy-start(s32[8]{0:T(128)} %param.8) | copy-start | bytes 100
  33.8 46.7 %collective-permute-start.4 = (bf16[256,4096]{1,0:T(8,128)(2,1)}, bf16[256,4096]{1,0:T(8,128)(2,1)}, u32[]{:S(2)}, u32[]{:S(2)}) collective-permute-start(bf16[256,4096]{1,0:T(8,128)(2,1)} %constant_dynamic-slice_fusion.12), channel_id=1, source_target_pairs={{0,2},{1,5},{2,0},{3,7},{4,6},{5,1},{6,4},{7,3},{8,10},{9,13},{10,... | collective-permute-start | bytes 6291464 | tf_op jit(solution)/shard_map/ppermute | solution.py:343
  34.9 56.6 %collective-permute-start.10 = (bf16[256,4096]{1,0:T(8,128)(2,1)}, bf16[256,4096]{1,0:T(8,128)(2,1)}, u32[]{:S(2)}, u32[]{:S(2)}) collective-permute-start(bf16[256,4096]{1,0:T(8,128)(2,1)} %constant_dynamic-slice_fusion.12), channel_id=1, source_target_pairs={{0,4},{1,3},{2,6},{3,1},{4,0},{5,7},{6,2},{7,5},{8,12},{9,11},{10,... | collective-permute-start | bytes 6291464 | tf_op jit(solution)/shard_map/ppermute | solution.py:343
  36.3 27.1 %copy-start.13 = (bf16[768,256]{1,0:T(8,128)(2,1)}, bf16[768,256]{1,0:T(8,128)(2,1)S(1)}, u32[]{:S(2)}) copy-start(bf16[768,256]{1,0:T(8,128)(2,1)S(1)} %pad_maximum_fusion.6) | copy-start | bytes 1179652
  36.3 16.6 %collective-permute-start.8 = (bf16[768,256]{1,0:T(8,128)(2,1)S(1)}, bf16[768,256]{1,0:T(8,128)(2,1)S(1)}, u32[]{:S(2)}, u32[]{:S(2)}) collective-permute-start(bf16[768,256]{1,0:T(8,128)(2,1)S(1)} %pad_maximum_fusion.6), channel_id=1, source_target_pairs={{0,8},{2,10},{4,12},{6,14},{8,16},{10,18},{12,20},{14,22},{16,24},... | collective-permute-start | bytes 1179656 | tf_op jit(solution)/shard_map/ppermute | solution.py:292
  52.9 12.5 %copy-start.17 = (bf16[768,256]{1,0:T(8,128)(2,1)}, bf16[768,256]{1,0:T(8,128)(2,1)S(1)}, u32[]{:S(2)}) copy-start(bf16[768,256]{1,0:T(8,128)(2,1)S(1)} %collective-permute-done.8) | copy-start | bytes 1179652
  52.9 10.6 %collective-permute-start.9 = (bf16[768,256]{1,0:T(8,128)(2,1)S(1)}, bf16[768,256]{1,0:T(8,128)(2,1)S(1)}, u32[]{:S(2)}, u32[]{:S(2)}) collective-permute-start(bf16[768,256]{1,0:T(8,128)(2,1)S(1)} %collective-permute-done.8), channel_id=1, source_target_pairs={{0,8},{2,10},{4,12},{6,14},{8,16},{10,18},{12,20},{14,22},{16,24},... | collective-permute-start | bytes 1179656 | tf_op jit(solution)/shard_map/ppermute | solution.py:292
  63.4 28.1 %collective-permute-start.11 = (bf16[768,256]{1,0:T(8,128)(2,1)S(1)}, bf16[768,256]{1,0:T(8,128)(2,1)}, u32[]{:S(2)}, u32[]{:S(2)}) collective-permute-start(bf16[768,256]{1,0:T(8,128)(2,1)S(1)} %collective-permute-done.9.refs_1_), channel_id=1, source_target_pairs={{0,8},{2,10},{4,12},{6,14},{8,16},{10,18},{12,20},{14,22},{16,24},... | collective-permute-start | bytes 1179656 | tf_op jit(solution)/shard_map/ppermute | solution.py:292
  67.7 3.1 %copy-start.11 = (f32[2048,64]{1,0:T(8,128)S(1)}, f32[2048,64]{1,0:T(8,128)}, u32[]{:S(2)}) copy-start(f32[2048,64]{1,0:T(8,128)} %get-tuple-element.57) | copy-start | bytes 1572868
  67.7 3.1 %copy-start.12 = (f32[2048,64]{1,0:T(8,128)S(1)}, f32[2048,64]{1,0:T(8,128)}, u32[]{:S(2)}) copy-start(f32[2048,64]{1,0:T(8,128)} %get-tuple-element.58) | copy-start | bytes 1572868
  71.4 20.1 %copy-start.5 = (f32[2048,128]{1,0:T(8,128)}, f32[2048,128]{1,0:T(8,128)S(1)}, u32[]{:S(2)}) copy-start(f32[2048,128]{1,0:T(8,128)S(1)} %get-tuple-element.66.refs_3_) | copy-start | bytes 3145732
  91.5 4.4 %collective-permute-start.1 = (bf16[256,4096]{1,0:T(8,128)(2,1)}, bf16[256,4096]{1,0:T(8,128)(2,1)S(1)}, u32[]{:S(2)}, u32[]{:S(2)}) collective-permute-start(bf16[256,4096]{1,0:T(8,128)(2,1)} %get-tuple-element.28.refs_0_), channel_id=1, source_target_pairs={{0,1},{1,0},{2,3},{3,2},{4,5},{5,4},{6,7},{7,6},{8,9},{9,8},{10,11... | collective-permute-start | bytes 6291464 | tf_op jit(solution)/shard_map/cond/branch_1_fun/ppermute | solution.py:346
  92.5 6.5 %collective-permute-start.2 = (bf16[256,4096]{1,0:T(8,128)(2,1)}, bf16[256,4096]{1,0:T(8,128)(2,1)S(1)}, u32[]{:S(2)}, u32[]{:S(2)}) collective-permute-start(bf16[256,4096]{1,0:T(8,128)(2,1)} %get-tuple-element.29.refs_2_), channel_id=1, source_target_pairs={{0,1},{1,0},{2,3},{3,2},{4,5},{5,4},{6,7},{7,6},{8,9},{9,8},{10,11... | collective-permute-start | bytes 6291464 | tf_op jit(solution)/shard_map/cond/branch_1_fun/ppermute | solution.py:346
  92.5 26.2 %collective-permute-start = (bf16[256,4096]{1,0:T(8,128)(2,1)}, bf16[256,4096]{1,0:T(8,128)(2,1)S(1)}, u32[]{:S(2)}, u32[]{:S(2)}) collective-permute-start(bf16[256,4096]{1,0:T(8,128)(2,1)} %get-tuple-element.28.refs_0_), channel_id=1, source_target_pairs={{0,4},{1,3},{2,6},{3,1},{4,0},{5,7},{6,2},{7,5},{8,12},{9,11},{10,... | collective-permute-start | bytes 6291464 | tf_op jit(solution)/shard_map/cond/branch_1_fun/ppermute | solution.py:343
  99.0 5.8 %copy-start.7 = (f32[2048,128]{1,0:T(8,128)S(1)}, f32[2048,128]{1,0:T(8,128)}, u32[]{:S(2)}) copy-start(f32[2048,128]{1,0:T(8,128)} %copy-done.6) | copy-start | bytes 3145732 | tf_op jit(solution)/shard_map/cond
  99.0 5.8 %copy-start.9 = (bf16[1024,768]{1,0:T(8,128)(2,1)S(1)}, bf16[1024,768]{1,0:T(8,128)(2,1)}, u32[]{:S(2)}) copy-start(bf16[1024,768]{1,0:T(8,128)(2,1)} %get-tuple-element.31.refs_0_) | copy-start | bytes 4718596 | tf_op jit(solution)/shard_map/cond
  99.0 5.8 %copy-start.14 = (bf16[768,256]{1,0:T(8,128)(2,1)S(1)}, bf16[768,256]{1,0:T(8,128)(2,1)}, u32[]{:S(2)}) copy-start(bf16[768,256]{1,0:T(8,128)(2,1)} %get-tuple-element.32.refs_1_) | copy-start | bytes 1179652 | tf_op jit(solution)/shard_map/cond
  99.0 5.8 %copy-start.18 = (bf16[768,256]{1,0:T(8,128)(2,1)S(1)}, bf16[768,256]{1,0:T(8,128)(2,1)}, u32[]{:S(2)}) copy-start(bf16[768,256]{1,0:T(8,128)(2,1)} %get-tuple-element.33.refs_2_) | copy-start | bytes 1179652 | tf_op jit(solution)/shard_map/cond
  120.1 4.4 %collective-permute-start.3 = (bf16[256,4096]{1,0:T(8,128)(2,1)}, bf16[256,4096]{1,0:T(8,128)(2,1)S(1)}, u32[]{:S(2)}, u32[]{:S(2)}) collective-permute-start(bf16[256,4096]{1,0:T(8,128)(2,1)} %branch_1_fun.7.refs_0_), channel_id=1, source_target_pairs={{0,1},{1,0},{2,3},{3,2},{4,5},{5,4},{6,7},{7,6},{8,9},{9,8},{10,11... | collective-permute-start | bytes 6291464 | tf_op jit(solution)/shard_map/cond/branch_1_fun/ppermute | solution.py:346
  126.0 2.5 %copy-start.10 = (bf16[1024,768]{1,0:T(8,128)(2,1)S(1)}, bf16[1024,768]{1,0:T(8,128)(2,1)}, u32[]{:S(2)}) copy-start(bf16[1024,768]{1,0:T(8,128)(2,1)} %get-tuple-element.31.refs_0_) | copy-start | bytes 4718596 | tf_op jit(solution)/shard_map/cond
  126.0 2.6 %copy-start.15 = (bf16[768,256]{1,0:T(8,128)(2,1)S(1)}, bf16[768,256]{1,0:T(8,128)(2,1)}, u32[]{:S(2)}) copy-start(bf16[768,256]{1,0:T(8,128)(2,1)} %get-tuple-element.32.refs_1_) | copy-start | bytes 1179652 | tf_op jit(solution)/shard_map/cond
  126.0 3.0 %copy-start.19 = (bf16[768,256]{1,0:T(8,128)(2,1)S(1)}, bf16[768,256]{1,0:T(8,128)(2,1)}, u32[]{:S(2)}) copy-start(bf16[768,256]{1,0:T(8,128)(2,1)} %get-tuple-element.33.refs_2_) | copy-start | bytes 1179652 | tf_op jit(solution)/shard_map/cond
  135.2 21.6 %collective-permute-start.12 = (bf16[1536,256]{1,0:T(8,128)(2,1)S(1)}, bf16[1536,256]{1,0:T(8,128)(2,1)S(1)}, u32[]{:S(2)}, u32[]{:S(2)}) collective-permute-start(bf16[1536,256]{1,0:T(8,128)(2,1)S(1)} %slice.39), channel_id=1, source_target_pairs={{0,8},{2,10},{4,12},{6,14},{8,16},{10,18},{12,20},{14,22},{16,24},... | collective-permute-start | bytes 2359304 | tf_op jit(solution)/shard_map/ppermute | solution.py:410
  166.9 31.1 %collective-permute-start.13 = (bf16[512,512]{1,0:T(8,128)(2,1)}, bf16[512,512]{1,0:T(8,128)(2,1)S(1)}, u32[]{:S(2)}, u32[]{:S(2)}) collective-permute-start(bf16[512,512]{1,0:T(8,128)(2,1)} %shard_map.58), channel_id=1, source_target_pairs={{0,6},{2,4},{4,2},{6,0},{8,14},{10,12},{12,10},{14,8},{16,22},{18,... | collective-permute-start | bytes 1572872 | tf_op jit(solution)/shard_map/ppermute | solution.py:285
  175.8 22.6 %collective-permute-start.14 = (bf16[512,512]{1,0:T(8,128)(2,1)}, bf16[512,512]{1,0:T(8,128)(2,1)S(1)}, u32[]{:S(2)}, u32[]{:S(2)}) collective-permute-start(bf16[512,512]{1,0:T(8,128)(2,1)} %shard_map.59), channel_id=1, source_target_pairs={{0,4},{2,6},{4,0},{6,2},{8,12},{10,14},{12,8},{14,10},{16,20},{18,... | collective-permute-start | bytes 1572872 | tf_op jit(solution)/shard_map/ppermute | solution.py:285
  186.9 13.6 %collective-permute-start.15 = (bf16[512,512]{1,0:T(8,128)(2,1)}, bf16[512,512]{1,0:T(8,128)(2,1)S(1)}, u32[]{:S(2)}, u32[]{:S(2)}) collective-permute-start(bf16[512,512]{1,0:T(8,128)(2,1)} %shard_map.60), channel_id=1, source_target_pairs={{0,2},{2,0},{4,6},{6,4},{8,10},{10,8},{12,14},{14,12},{16,18},{18,... | collective-permute-start | bytes 1572872 | tf_op jit(solution)/shard_map/ppermute | solution.py:285
  198.3 3.6 %copy-start.20 = (bf16[512,512]{1,0:T(8,128)(2,1)S(1)}, bf16[512,512]{1,0:T(8,128)(2,1)}, u32[]{:S(2)}) copy-start(bf16[512,512]{1,0:T(8,128)(2,1)} %shard_map.61) | copy-start | bytes 1572868
  (11 other events, 16.8 us)
Sparse Core Ops, SparseCore 0:
  9.0 44.8 all-gather.2
  55.4 70.9 all-gather.4

commit v6 on v4

--- a/solution.py
+++ b/solution.py
@@ -17,7 +17,7 @@
 TILE = 256
 UNIT = 128
 PUT_BYTES = 20 * 1024 * 1024
-PROJECT_BYTES = 30 * 1024 * 1024
+PROJECT_BYTES = 58 * 1024 * 1024
 VMEM_BYTES = 58 * 1024 * 1024
 
 
@@ -130,13 +130,22 @@
     )(place, *arrays)
 
 
-def attend_kernel(kv_heads, share, halo_rows, first, bounds, ends, q_ref, halo_ref, kv_ref, out_ref, kv_all, q_all, sums, totals):
+def attend_kernel(kv_heads, share, halo_rows, first, bounds, ends, q_ref, halo_ref, kv_ref, out_ref, k_all, v_all, q_all, sums, begins):
     tile_index = pl.program_id(0)
+    wide = 2 * HEAD_DIM
 
     @pl.when(tile_index == 0)
     def _():
-        kv_all[:halo_rows, :] = halo_ref[...]
-        kv_all[halo_rows:, :] = kv_ref[...]
+        for source, start in ((halo_ref, 0), (kv_ref, halo_rows)):
+            rows = slice(start, start + source.shape[0])
+            for head in range(kv_heads):
+                columns = slice(head * HEAD_DIM, (head + 1) * HEAD_DIM)
+                at = (kv_heads + head) * HEAD_DIM
+                k_all[rows, columns] = source[:, columns]
+                v_all[rows, head * wide : head * wide + HEAD_DIM] = source[:, at : at + HEAD_DIM]
+                v_all[rows, head * wide + HEAD_DIM : (head + 1) * wide] = jnp.ones(
+                    (source.shape[0], HEAD_DIM), v_all.dtype
+                )
 
     tile = q_ref.shape[0]
     for head in range(kv_heads * share):
@@ -148,23 +157,26 @@
     lowest = first_start // UNIT * UNIT
     units = (q_first - lowest) // UNIT
     sums[...] = jnp.zeros_like(sums)
-    totals[...] = jnp.zeros_like(totals)
     inner = 1.0 / (math.sqrt(HEAD_DIM) * LOGIT_CAP)
     outer = LOGIT_CAP * math.log2(math.e)
+    rows_at = q_first + lax.broadcasted_iota(jnp.int32, (tile, UNIT), 0)
+    starts = jnp.zeros((tile, UNIT), jnp.int32)
+    for number in range(ends.shape[0]):
+        starts = jnp.where(rows_at >= ends[number], jnp.maximum(starts, ends[number]), starts)
+    begins[...] = starts
 
     def block_step(begin, size, masked):
         rows = pl.ds(pl.multiple_of(begin, UNIT), size)
         if masked:
-            k_ids = begin + lax.broadcasted_iota(jnp.int32, (tile, size), 1)
-            q_ids = q_first + lax.broadcasted_iota(jnp.int32, (tile, size), 0)
-            begins = jnp.zeros((tile, 1), jnp.int32)
-            for number in range(ends.shape[0]):
-                begins = jnp.where(q_ids[:, :1] >= ends[number], jnp.maximum(begins, ends[number]), begins)
-            allowed = (k_ids <= q_ids) & (k_ids >= begins)
+            parts = []
+            for part in range(size // UNIT):
+                k_ids = begin + part * UNIT + lax.broadcasted_iota(jnp.int32, (tile, UNIT), 1)
+                q_ids = q_first + lax.broadcasted_iota(jnp.int32, (tile, UNIT), 0)
+                parts.append((k_ids <= q_ids) & (k_ids >= begins[...]))
+            allowed = parts[0] if len(parts) == 1 else jnp.concatenate(parts, axis=1)
         for kv_head in range(kv_heads):
-            keys = kv_all[rows, kv_head * HEAD_DIM : (kv_head + 1) * HEAD_DIM]
-            at = (kv_heads + kv_head) * HEAD_DIM
-            values = kv_all[rows, at : at + HEAD_DIM]
+            keys = k_all[rows, kv_head * HEAD_DIM : (kv_head + 1) * HEAD_DIM]
+            values = v_all[rows, kv_head * wide : (kv_head + 1) * wide]
             members = slice(kv_head * share * tile, (kv_head + 1) * share * tile)
             raw = lax.dot_general(
                 q_all[members, :], keys, (((1,), (1,)), ((), ())), preferred_element_type=jnp.float32
@@ -173,10 +185,6 @@
             if masked:
                 weights = weights.reshape(share, tile, size)
                 weights = jnp.where(allowed[None], weights, 0.0).reshape(share * tile, size)
-            partial = weights[:, :HEAD_DIM]
-            for part in range(1, size // HEAD_DIM):
-                partial = partial + weights[:, part * HEAD_DIM : (part + 1) * HEAD_DIM]
-            totals[members, :] += partial
             sums[members, :] += jnp.dot(weights.astype(jnp.bfloat16), values, preferred_element_type=jnp.float32)
 
     def either(begin, size):
@@ -208,8 +216,8 @@
 
     for head in range(kv_heads * share):
         rows = slice(head * tile, (head + 1) * tile)
-        denominator = jnp.sum(totals[rows, :], axis=1, keepdims=True)
-        out_ref[:, head * HEAD_DIM : (head + 1) * HEAD_DIM] = (sums[rows, :] / denominator).astype(out_ref.dtype)
+        mixed = sums[rows, :HEAD_DIM] / sums[rows, HEAD_DIM:]
+        out_ref[:, head * HEAD_DIM : (head + 1) * HEAD_DIM] = mixed.astype(out_ref.dtype)
 
 
 def attend(chunk, chunk_rows, query, ends, bounds, halo, kv, kv_heads):
@@ -232,10 +240,11 @@
             ],
             out_specs=pl.BlockSpec((TILE, width), lambda i, c, s, e: (i, 0)),
             scratch_shapes=[
-                pltpu.VMEM((halo_rows + kv.shape[0], kv.shape[1]), jnp.bfloat16),
+                pltpu.VMEM((halo_rows + kv.shape[0], kv_heads * HEAD_DIM), jnp.bfloat16),
+                pltpu.VMEM((halo_rows + kv.shape[0], kv_heads * 2 * HEAD_DIM), jnp.bfloat16),
                 pltpu.VMEM((heads * TILE, HEAD_DIM), jnp.bfloat16),
-                pltpu.VMEM((heads * TILE, HEAD_DIM), jnp.float32),
-                pltpu.VMEM((heads * TILE, HEAD_DIM), jnp.float32),
+                pltpu.VMEM((heads * TILE, 2 * HEAD_DIM), jnp.float32),
+                pltpu.VMEM((TILE, UNIT), jnp.int32),
             ],
         ),
         compiler_params=pltpu.CompilerParams(vmem_limit_bytes=VMEM_BYTES),

time: 209 us -> 205 us (0.981)
  local copies, waits for them, and re-layouts: 21.4 us -> 15.9 us
  starting transfers between devices: 23 us -> 25.6 us
    unnamed x36 -> x22, local copies, waits for them, and re-layouts: 13.1 us -> 4.48 us
    pallas_call x2, Pallas kernels: 22.6 us -> 26.8 us  [project(): pl.pallas_call(functools.partial(project_kernel, rope_heads, layout, len(...]
    ppermute x6, waiting for transfers between devices: 21.6 us -> 17.9 us  [to_partner(): return lax.ppermute(block, 'ca', [(i, i ^ step) for i in devices])]
    pallas_call x4, Pallas kernels: 34.2 us -> 30.9 us  [attend(): pl.pallas_call(kernel, out_shape=jax.ShapeDtypeStruct((chunk_rows, width)...]
    cond x0 -> x4, local copies, waits for them, and re-layouts: none -> 2.91 us
    ppermute x6, starting transfers between devices: 9.68 us -> 12.3 us  [to_partner(): return lax.ppermute(block, 'ca', [(i, i ^ step) for i in devices])]
  transfers between devices with their start and end apart: 18 -> 18, of which waited for: 11 -> 11; matrix products, arithmetic and copies ran while one was open for 8% -> 7% of each run, Pallas kernels for 29% -> 30%
where the time goes in v6:
time: 205 us
  waiting for transfers between devices  69.9 us (34%)
  Pallas kernels  68.4 us (33%)
  starting transfers between devices  25.6 us (12%)
  local copies, waits for them, and re-layouts  15.9 us (8%)
  between operations  15 us (7%)
  other arithmetic  9.67 us (5%)
    pallas_call x4, Pallas kernels, attend(): pl.pallas_call(kernel, out_shape=jax.ShapeDtypeStruct((chunk_rows, width)...  30.9 us
    pallas_call x2, Pallas kernels, project(): pl.pallas_call(functools.partial(project_kernel, rope_heads, layout, len(...  26.8 us
    ppermute x3, waiting for transfers between devices, cross(): return lax.ppermute(block, both, pairs)  21.5 us
    ppermute x3, waiting for transfers between devices, forwarded(): lax.ppermute(block, 'ca', [(i, (i + group) % (group * lines)) for i in de...  18.7 us
    ppermute x6, waiting for transfers between devices, to_partner(): return lax.ppermute(block, 'ca', [(i, i ^ step) for i in devices])  17.9 us
    ppermute x6, starting transfers between devices, to_partner(): return lax.ppermute(block, 'ca', [(i, i ^ step) for i in devices])  12.3 us
    pallas_call x3, Pallas kernels, put(): pl.pallas_call(functools.partial(put_kernel, targets), out_shape=jax.Shap...  10.6 us
    ppermute x3, waiting for transfers between devices, swap(): lax.ppermute(block, both, [(i * 2 + c, i * 2 + 1 - c) for i in devices fo...  9.62 us
  transfers between devices with their start and end apart: 18, of which 11 were waited for; matrix products, arithmetic and copies ran while one was open for 7% of the time, Pallas kernels for 30%

profile of v6, /device:TPU:16, one launch (start us, length us, event | category | flops | bytes accessed | tf_op | source)
XLA Modules:
  0.0 204.5 jit_solution(9129792067948481129)
XLA Ops:
  12.7 8.3 %collective-permute-done.5 = bf16[256,768]{1,0:T(8,128)(2,1)S(1)} collective-permute-done((bf16[256,768]{1,0:T(8,128)(2,1)S(1)}, bf16[256,768]{1,0:T(8,128)(2,1)S(1)}, u32[]{:S(2)}, u32[]{:S(2)}) %collective-permute-start.5) | collective-permute-done | bytes 393248 | tf_op jit(solution)/shard_map/ppermute | solution.py:294
  21.0 8.6 %collective-permute-done.6 = bf16[256,768]{1,0:T(8,128)(2,1)S(1)} collective-permute-done((bf16[256,768]{1,0:T(8,128)(2,1)S(1)}, bf16[256,768]{1,0:T(8,128)(2,1)S(1)}, u32[]{:S(2)}, u32[]{:S(2)}) %collective-permute-start.6) | collective-permute-done | bytes 393248 | tf_op jit(solution)/shard_map/ppermute | solution.py:294
  30.6 3.1 %constant_dynamic-slice_fusion.12 = bf16[256,4096]{1,0:T(8,128)(2,1)} fusion(bf16[512,4096]{1,0:T(8,128)(2,1)} %refs_0_.1, s32[]{:T(128)S(6)} %select_n.53), kind=kLoop, calls=%fused_computation.30 | loop fusion | bytes 4194308 | tf_op jit(solution)/shard_map/dynamic_slice | solution.py:359
  36.3 1.6 collective-permute-start.8
  39.3 13.6 %collective-permute-done.8.refs_2_ = bf16[768,256]{1,0:T(8,128)(2,1)S(1)} collective-permute-done((bf16[768,256]{1,0:T(8,128)(2,1)S(1)}, bf16[768,256]{1,0:T(8,128)(2,1)S(1)}, u32[]{:S(2)}, u32[]{:S(2)}) %collective-permute-start.8) | collective-permute-done | bytes 393248 | tf_op jit(solution)/shard_map/ppermute | solution.py:301
  52.9 1.7 collective-permute-start.9
  54.6 3.7 %fusion = (f32[2048,64]{1,0:T(8,128)S(1)}, f32[2048,64]{1,0:T(8,128)S(1)}, f32[2048,64]{1,0:T(8,128)S(1)}) fusion(f32[64]{0:T(128)S(1)} %multiply_power_fusion, f32[2048]{0:T(1024)S(1)} %get-tuple-element.37), kind=kLoop, calls=%fused_computation.10 | loop fusion | flops 262144 | bytes 1581312 | tf_op jit(solution)/shard_map/neg | solution.py:35
  58.4 5.1 %collective-permute-done.9.refs_1_.refs_3_ = bf16[768,256]{1,0:T(8,128)(2,1)S(1)} collective-permute-done((bf16[768,256]{1,0:T(8,128)(2,1)S(1)}, bf16[768,256]{1,0:T(8,128)(2,1)S(1)}, u32[]{:S(2)}, u32[]{:S(2)}) %collective-permute-start.9) | collective-permute-done | bytes 393248 | tf_op jit(solution)/shard_map/ppermute | solution.py:301
  63.5 1.9 collective-permute-start.11
  65.5 2.2 %copy-done = bf16[512,4096]{1,0:T(8,128)(2,1)S(1)} copy-done((bf16[512,4096]{1,0:T(8,128)(2,1)S(1)}, bf16[512,4096]{1,0:T(8,128)(2,1)}, u32[]{:S(2)}) %copy-start) | copy-done | bytes 4194328
  67.7 2.5 %shard_map.56 = bf16[2048,4096]{1,0:T(8,128)(2,1)} custom-call(s32[3]{0:T(128)S(1)} %pad_add_fusion.1.place, bf16[512,4096]{1,0:T(8,128)(2,1)S(1)} %copy-done), custom_call_target="tpu_custom_call" | custom-call | tf_op jit(solution)/shard_map/pallas_call | solution.py:122
  70.8 1.9 pad_maximum_fusion
  72.7 7.8 %collective-permute-done.4.refs_0_ = bf16[256,4096]{1,0:T(8,128)(2,1)} collective-permute-done((bf16[256,4096]{1,0:T(8,128)(2,1)}, bf16[256,4096]{1,0:T(8,128)(2,1)}, u32[]{:S(2)}, u32[]{:S(2)}) %collective-permute-start.4) | collective-permute-done | bytes 2097184 | tf_op jit(solution)/shard_map/ppermute | solution.py:352
  83.0 36.6 %conditional.1 = (bf16[2048,4096]{1,0:T(8,128)(2,1)}) conditional(s32[]{:T(128)} %bitcast.6, () %tuple.11, (bf16[256,4096]{1,0:T(8,128)(2,1)}, bf16[256,4096]{1,0:T(8,128)(2,1)}, s32[3]{0:T(128)S(1)}, bf16[2048,4096]{1,0:T(8,128)(2,1)}) %tuple.12), branch_computations={%region_2.3_spmd, %region_3.4_spmd} | conditional | bytes 50331872 | solution.py:393
  83.6 1.6 collective-permute-start
  85.2 2.3 %collective-permute-done.1.refs_1_ = bf16[256,4096]{1,0:T(8,128)(2,1)S(1)} collective-permute-done((bf16[256,4096]{1,0:T(8,128)(2,1)}, bf16[256,4096]{1,0:T(8,128)(2,1)S(1)}, u32[]{:S(2)}, u32[]{:S(2)}) %collective-permute-start.1) | collective-permute-done | bytes 2097184 | tf_op jit(solution)/shard_map/cond/branch_1_fun/ppermute | solution.py:355
  87.5 3.0 %collective-permute-done.2.refs_3_ = bf16[256,4096]{1,0:T(8,128)(2,1)S(1)} collective-permute-done((bf16[256,4096]{1,0:T(8,128)(2,1)}, bf16[256,4096]{1,0:T(8,128)(2,1)S(1)}, u32[]{:S(2)}, u32[]{:S(2)}) %collective-permute-start.2) | collective-permute-done | bytes 2097184 | tf_op jit(solution)/shard_map/cond/branch_1_fun/ppermute | solution.py:355
  90.5 5.6 %branch_1_fun.3.refs_1_.refs_2_ = bf16[2048,4096]{1,0:T(8,128)(2,1)} custom-call(s32[3]{0:T(128)S(1)} %get-tuple-element.16.place, bf16[256,4096]{1,0:T(8,128)(2,1)} %get-tuple-element.17.refs_0_, bf16[256,4096]{1,0:T(8,128)(2,1)S(1)} %collective-permute-done.1.refs_1_, bf16[256,4096]{1,0:T(8,128)(2,1)} %get-tuple-element.18.refs_2_, ...), custom_call_target="tpu_custom_call", output_to_operand_aliasing={{}: (5, {})} | custom-call | tf_op jit(solution)/shard_map/cond/branch_1_fun/pallas_call | solution.py:122
  96.1 13.8 %collective-permute-done.refs_0_ = bf16[256,4096]{1,0:T(8,128)(2,1)S(1)} collective-permute-done((bf16[256,4096]{1,0:T(8,128)(2,1)}, bf16[256,4096]{1,0:T(8,128)(2,1)S(1)}, u32[]{:S(2)}, u32[]{:S(2)}) %collective-permute-start) | collective-permute-done | bytes 2097184 | tf_op jit(solution)/shard_map/cond/branch_1_fun/ppermute | solution.py:352
  111.2 4.4 %collective-permute-done.3.refs_1_ = bf16[256,4096]{1,0:T(8,128)(2,1)S(1)} collective-permute-done((bf16[256,4096]{1,0:T(8,128)(2,1)}, bf16[256,4096]{1,0:T(8,128)(2,1)S(1)}, u32[]{:S(2)}, u32[]{:S(2)}) %collective-permute-start.3) | collective-permute-done | bytes 2097184 | tf_op jit(solution)/shard_map/cond/branch_1_fun/ppermute | solution.py:355
  115.5 1.6 copy-done.2
  117.1 2.5 %branch_1_fun.5 = bf16[2048,4096]{1,0:T(8,128)(2,1)} custom-call(s32[3]{0:T(128)S(1)} %get-tuple-element.16.place, bf16[256,4096]{1,0:T(8,128)(2,1)S(1)} %copy-done.2, bf16[256,4096]{1,0:T(8,128)(2,1)S(1)} %collective-permute-done.3.refs_1_, bf16[2048,4096]{1,0:T(8,128)(2,1)} %branch_1_fun.3.refs_1_.refs_2_), custom_call_target="tpu_custom_call", output_to_operand_aliasing={{}: (3, {})} | custom-call | tf_op jit(solution)/shard_map/cond/branch_1_fun/pallas_call | solution.py:122
  119.7 11.2 %shard_map.58.kv_ref = bf16[2048,256]{1,0:T(8,128)(2,1)} custom-call(s32[3]{0:T(128)S(1)} %pad_add_fusion.1.place, bf16[2048,4096]{1,0:T(8,128)(2,1)} %get-tuple-element.45.x_ref, bf16[1024,768]{1,0:T(8,128)(2,1)} %all-gather.3.cloned.1.call-done.refs_0_, bf16[768,256]{1,0:T(8,128)(2,1)} %copy-done.5, bf16[768,256]{1,0:T(8,128)(2,1)} %copy-done.7, ...), custom_call_target="tpu_custom_call" | custom-call | flops 4294967296 | bytes 18874368 | tf_op jit(solution)/shard_map/pallas_call | solution.py:79
  132.1 3.8 %collective-permute-start.12 = (bf16[1536,256]{1,0:T(8,128)(2,1)S(1)}, bf16[1536,256]{1,0:T(8,128)(2,1)S(1)}, u32[]{:S(2)}, u32[]{:S(2)}) collective-permute-start(bf16[1536,256]{1,0:T(8,128)(2,1)S(1)} %slice.49), channel_id=1, source_target_pairs={{0,8},{2,10},{4,12},{6,14},{8,16},{10,18},{12,20},{14,22},{16,24},... | collective-permute-start | bytes 2359304 | tf_op jit(solution)/shard_map/ppermute | solution.py:416
  135.9 15.6 %shard_map.57.q_ref = bf16[2048,512]{1,0:T(8,128)(2,1)} custom-call(s32[3]{0:T(128)S(1)} %pad_add_fusion.1.place, bf16[2048,4096]{1,0:T(8,128)(2,1)} %get-tuple-element.45.x_ref, bf16[1024,768]{1,0:T(8,128)(2,1)} %all-gather.3.cloned.1.call-done.refs_0_, bf16[3072,512]{1,0:T(8,128)(2,1)} %all-gather.5.cloned.1.call-done.refs_1_, ...), custom_call_target="tpu_custom_call" | custom-call | flops 8589934592 | bytes 20971520 | tf_op jit(solution)/shard_map/pallas_call | solution.py:79
  151.5 2.1 %collective-permute-done.12.halo_ref = bf16[1536,256]{1,0:T(8,128)(2,1)S(1)} collective-permute-done((bf16[1536,256]{1,0:T(8,128)(2,1)S(1)}, bf16[1536,256]{1,0:T(8,128)(2,1)S(1)}, u32[]{:S(2)}, u32[]{:S(2)}) %collective-permute-start.12) | collective-permute-done | bytes 786464 | tf_op jit(solution)/shard_map/ppermute | solution.py:416
  154.5 7.4 %shard_map.59 = bf16[512,512]{1,0:T(8,128)(2,1)} custom-call(s32[1]{0:T(128)} %bitcast.first, s32[3,8]{1,0:T(4,128)} %pad_add_fusion.refs_5_.bounds, s32[8]{0:T(128)} %broadcast_subtract_fusion.1.refs_4_.ends, bf16[2048,512]{1,0:T(8,128)(2,1)} %shard_map.57.q_ref, bf16[1536,256]{1,0:T(8,128)(2,1)} %copy-done.11, bf16[2048,256]{1,0:T(8,128)(2,1)} %shard_map.58.kv_ref), custom_call_target="tpu_custom_call" | custom-call | flops 1073741824 | bytes 1048576 | tf_op jit(solution)/shard_map/pallas_call | solution.py:230
  161.8 5.0 %collective-permute-start.13 = (bf16[512,512]{1,0:T(8,128)(2,1)}, bf16[512,512]{1,0:T(8,128)(2,1)S(1)}, u32[]{:S(2)}, u32[]{:S(2)}) collective-permute-start(bf16[512,512]{1,0:T(8,128)(2,1)} %shard_map.59), channel_id=1, source_target_pairs={{0,6},{2,4},{4,2},{6,0},{8,14},{10,12},{12,10},{14,8},{16,22},{18,... | collective-permute-start | bytes 1572872 | tf_op jit(solution)/shard_map/ppermute | solution.py:294
  166.8 6.9 %shard_map.60 = bf16[512,512]{1,0:T(8,128)(2,1)} custom-call(s32[1]{0:T(128)} %bitcast.7.first, s32[3,8]{1,0:T(4,128)} %pad_add_fusion.refs_5_.bounds, s32[8]{0:T(128)} %broadcast_subtract_fusion.1.refs_4_.ends, bf16[2048,512]{1,0:T(8,128)(2,1)} %shard_map.57.q_ref, bf16[1536,256]{1,0:T(8,128)(2,1)} %copy-done.11, bf16[2048,256]{1,0:T(8,128)(2,1)} %shard_map.58.kv_ref), custom_call_target="tpu_custom_call" | custom-call | flops 1073741824 | bytes 1048576 | tf_op jit(solution)/shard_map/pallas_call | solution.py:230
  174.2 6.8 %shard_map.61 = bf16[512,512]{1,0:T(8,128)(2,1)} custom-call(s32[1]{0:T(128)} %bitcast.8.first, s32[3,8]{1,0:T(4,128)} %pad_add_fusion.refs_5_.bounds, s32[8]{0:T(128)} %broadcast_subtract_fusion.1.refs_4_.ends, bf16[2048,512]{1,0:T(8,128)(2,1)} %shard_map.57.q_ref, bf16[1536,256]{1,0:T(8,128)(2,1)} %copy-done.11, bf16[2048,256]{1,0:T(8,128)(2,1)} %shard_map.58.kv_ref), custom_call_target="tpu_custom_call" | custom-call | flops 1073741824 | bytes 1048576 | tf_op jit(solution)/shard_map/pallas_call | solution.py:230
  181.0 3.1 %collective-permute-start.15 = (bf16[512,512]{1,0:T(8,128)(2,1)}, bf16[512,512]{1,0:T(8,128)(2,1)S(1)}, u32[]{:S(2)}, u32[]{:S(2)}) collective-permute-start(bf16[512,512]{1,0:T(8,128)(2,1)} %shard_map.61), channel_id=1, source_target_pairs={{0,2},{2,0},{4,6},{6,4},{8,10},{10,8},{12,14},{14,12},{16,18},{18,... | collective-permute-start | bytes 1572872 | tf_op jit(solution)/shard_map/ppermute | solution.py:294
  184.1 9.9 %shard_map.62 = bf16[512,512]{1,0:T(8,128)(2,1)} custom-call(s32[1]{0:T(128)} %bitcast.9.first, s32[3,8]{1,0:T(4,128)} %pad_add_fusion.refs_5_.bounds, s32[8]{0:T(128)} %broadcast_subtract_fusion.1.refs_4_.ends, bf16[2048,512]{1,0:T(8,128)(2,1)} %shard_map.57.q_ref, bf16[1536,256]{1,0:T(8,128)(2,1)} %copy-done.11, bf16[2048,256]{1,0:T(8,128)(2,1)} %shard_map.58.kv_ref), custom_call_target="tpu_custom_call" | custom-call | flops 1073741824 | bytes 1048576 | tf_op jit(solution)/shard_map/pallas_call | solution.py:230
  (79 shorter events, 20.9 us)
Async XLA Ops:
  6.5 1.4 copy-start.9
  6.5 1.4 copy-start.8
  6.5 113.1 %all-gather.3.cloned.1.call-start = ((), (), s32[]{:S(2)}) async-start(), calls=%async_computation | async-start | bytes 1966080 | tf_op jit(solution)/shard_map/all_gather | solution.py:298
  8.8 127.0 %all-gather.5.cloned.1.call-start = ((), (), s32[]{:S(2)}) async-start(), calls=%async_computation.1 | async-start | bytes 3932160 | tf_op jit(solution)/shard_map/all_gather | solution.py:298
  8.9 12.1 %collective-permute-start.5 = (bf16[256,768]{1,0:T(8,128)(2,1)S(1)}, bf16[256,768]{1,0:T(8,128)(2,1)S(1)}, u32[]{:S(2)}, u32[]{:S(2)}) collective-permute-start(bf16[256,768]{1,0:T(8,128)(2,1)S(1)} %pad_maximum_fusion.3), channel_id=1, source_target_pairs={{0,2},{2,0},{4,6},{6,4},{8,10},{10,8},{12,14},{14,12},{16,18},{18,... | collective-permute-start | bytes 1179656 | tf_op jit(solution)/shard_map/ppermute | solution.py:294
  10.5 19.1 %collective-permute-start.6 = (bf16[256,768]{1,0:T(8,128)(2,1)S(1)}, bf16[256,768]{1,0:T(8,128)(2,1)S(1)}, u32[]{:S(2)}, u32[]{:S(2)}) collective-permute-start(bf16[256,768]{1,0:T(8,128)(2,1)S(1)} %pad_maximum_fusion.4), channel_id=1, source_target_pairs={{0,4},{2,6},{4,0},{6,2},{8,12},{10,14},{12,8},{14,10},{16,20},{18,... | collective-permute-start | bytes 1179656 | tf_op jit(solution)/shard_map/ppermute | solution.py:294
  12.2 17.5 %collective-permute-start.7 = (bf16[256,768]{1,0:T(8,128)(2,1)S(1)}, bf16[256,768]{1,0:T(8,128)(2,1)S(1)}, u32[]{:S(2)}, u32[]{:S(2)}) collective-permute-start(bf16[256,768]{1,0:T(8,128)(2,1)S(1)} %pad_maximum_fusion.5), channel_id=1, source_target_pairs={{0,6},{2,4},{4,2},{6,0},{8,14},{10,12},{12,10},{14,8},{16,22},{18,... | collective-permute-start | bytes 1179656 | tf_op jit(solution)/shard_map/ppermute | solution.py:294
  30.6 5.2 %copy-start.12 = (s32[8]{0:T(128)S(1)}, s32[8]{0:T(128)}, u32[]{:S(2)}) copy-start(s32[8]{0:T(128)} %param.8) | copy-start | bytes 100
  33.8 46.7 %collective-permute-start.4 = (bf16[256,4096]{1,0:T(8,128)(2,1)}, bf16[256,4096]{1,0:T(8,128)(2,1)}, u32[]{:S(2)}, u32[]{:S(2)}) collective-permute-start(bf16[256,4096]{1,0:T(8,128)(2,1)} %constant_dynamic-slice_fusion.12), channel_id=1, source_target_pairs={{0,2},{1,5},{2,0},{3,7},{4,6},{5,1},{6,4},{7,3},{8,10},{9,13},{10,... | collective-permute-start | bytes 6291464 | tf_op jit(solution)/shard_map/ppermute | solution.py:352
  34.9 48.1 %collective-permute-start.10 = (bf16[256,4096]{1,0:T(8,128)(2,1)}, bf16[256,4096]{1,0:T(8,128)(2,1)}, u32[]{:S(2)}, u32[]{:S(2)}) collective-permute-start(bf16[256,4096]{1,0:T(8,128)(2,1)} %constant_dynamic-slice_fusion.12), channel_id=1, source_target_pairs={{0,4},{1,3},{2,6},{3,1},{4,0},{5,7},{6,2},{7,5},{8,12},{9,11},{10,... | collective-permute-start | bytes 6291464 | tf_op jit(solution)/shard_map/ppermute | solution.py:352
  36.3 27.2 %copy-start.5 = (bf16[768,256]{1,0:T(8,128)(2,1)}, bf16[768,256]{1,0:T(8,128)(2,1)S(1)}, u32[]{:S(2)}) copy-start(bf16[768,256]{1,0:T(8,128)(2,1)S(1)} %pad_maximum_fusion.6.refs_1_) | copy-start | bytes 1179652
  36.3 16.6 %collective-permute-start.8 = (bf16[768,256]{1,0:T(8,128)(2,1)S(1)}, bf16[768,256]{1,0:T(8,128)(2,1)S(1)}, u32[]{:S(2)}, u32[]{:S(2)}) collective-permute-start(bf16[768,256]{1,0:T(8,128)(2,1)S(1)} %pad_maximum_fusion.6.refs_1_), channel_id=1, source_target_pairs={{0,8},{2,10},{4,12},{6,14},{8,16},{10,18},{12,20},{14,22},{16,24},... | collective-permute-start | bytes 1179656 | tf_op jit(solution)/shard_map/ppermute | solution.py:301
  52.9 12.5 %copy-start.7 = (bf16[768,256]{1,0:T(8,128)(2,1)}, bf16[768,256]{1,0:T(8,128)(2,1)S(1)}, u32[]{:S(2)}) copy-start(bf16[768,256]{1,0:T(8,128)(2,1)S(1)} %collective-permute-done.8.refs_2_) | copy-start | bytes 1179652
  52.9 10.6 %collective-permute-start.9 = (bf16[768,256]{1,0:T(8,128)(2,1)S(1)}, bf16[768,256]{1,0:T(8,128)(2,1)S(1)}, u32[]{:S(2)}, u32[]{:S(2)}) collective-permute-start(bf16[768,256]{1,0:T(8,128)(2,1)S(1)} %collective-permute-done.8.refs_2_), channel_id=1, source_target_pairs={{0,8},{2,10},{4,12},{6,14},{8,16},{10,18},{12,20},{14,22},{16,24},... | collective-permute-start | bytes 1179656 | tf_op jit(solution)/shard_map/ppermute | solution.py:301
  63.5 6.8 %copy-start.4 = (bf16[768,256]{1,0:T(8,128)(2,1)}, bf16[768,256]{1,0:T(8,128)(2,1)S(1)}, u32[]{:S(2)}) copy-start(bf16[768,256]{1,0:T(8,128)(2,1)S(1)} %collective-permute-done.9.refs_1_.refs_3_) | copy-start | bytes 1179652
  63.5 56.2 %collective-permute-start.11 = (bf16[768,256]{1,0:T(8,128)(2,1)S(1)}, bf16[768,256]{1,0:T(8,128)(2,1)}, u32[]{:S(2)}, u32[]{:S(2)}) collective-permute-start(bf16[768,256]{1,0:T(8,128)(2,1)S(1)} %collective-permute-done.9.refs_1_.refs_3_), channel_id=1, source_target_pairs={{0,8},{2,10},{4,12},{6,14},{8,16},{10,18},{12,20},{14,22},{16,24},... | collective-permute-start | bytes 1179656 | tf_op jit(solution)/shard_map/ppermute | solution.py:301
  65.5 2.2 %copy-start = (bf16[512,4096]{1,0:T(8,128)(2,1)S(1)}, bf16[512,4096]{1,0:T(8,128)(2,1)}, u32[]{:S(2)}) copy-start(bf16[512,4096]{1,0:T(8,128)(2,1)} %refs_0_.1) | copy-start | bytes 12582916
  67.7 2.5 %copy-start.10 = (s32[1,8]{1,0:T(1,128)S(1)}, s32[1,8]{1,0:T(1,128)}, u32[]{:S(2)}) copy-start(s32[1,8]{1,0:T(1,128)} %iota_multiply_fusion) | copy-start | bytes 100
  83.0 4.4 %collective-permute-start.1 = (bf16[256,4096]{1,0:T(8,128)(2,1)}, bf16[256,4096]{1,0:T(8,128)(2,1)S(1)}, u32[]{:S(2)}, u32[]{:S(2)}) collective-permute-start(bf16[256,4096]{1,0:T(8,128)(2,1)} %get-tuple-element.17.refs_0_), channel_id=1, source_target_pairs={{0,1},{1,0},{2,3},{3,2},{4,5},{5,4},{6,7},{7,6},{8,9},{9,8},{10,11... | collective-permute-start | bytes 6291464 | tf_op jit(solution)/shard_map/cond/branch_1_fun/ppermute | solution.py:355
  83.1 7.4 %collective-permute-start.2 = (bf16[256,4096]{1,0:T(8,128)(2,1)}, bf16[256,4096]{1,0:T(8,128)(2,1)S(1)}, u32[]{:S(2)}, u32[]{:S(2)}) collective-permute-start(bf16[256,4096]{1,0:T(8,128)(2,1)} %get-tuple-element.18.refs_2_), channel_id=1, source_target_pairs={{0,1},{1,0},{2,3},{3,2},{4,5},{5,4},{6,7},{7,6},{8,9},{9,8},{10,11... | collective-permute-start | bytes 6291464 | tf_op jit(solution)/shard_map/cond/branch_1_fun/ppermute | solution.py:355
  83.6 26.2 %collective-permute-start = (bf16[256,4096]{1,0:T(8,128)(2,1)}, bf16[256,4096]{1,0:T(8,128)(2,1)S(1)}, u32[]{:S(2)}, u32[]{:S(2)}) collective-permute-start(bf16[256,4096]{1,0:T(8,128)(2,1)} %get-tuple-element.17.refs_0_), channel_id=1, source_target_pairs={{0,4},{1,3},{2,6},{3,1},{4,0},{5,7},{6,2},{7,5},{8,12},{9,11},{10,... | collective-permute-start | bytes 6291464 | tf_op jit(solution)/shard_map/cond/branch_1_fun/ppermute | solution.py:352
  109.8 1.3 copy-start.1
  111.2 4.4 %collective-permute-start.3 = (bf16[256,4096]{1,0:T(8,128)(2,1)}, bf16[256,4096]{1,0:T(8,128)(2,1)S(1)}, u32[]{:S(2)}, u32[]{:S(2)}) collective-permute-start(bf16[256,4096]{1,0:T(8,128)(2,1)} %branch_1_fun.4.refs_0_), channel_id=1, source_target_pairs={{0,1},{1,0},{2,3},{3,2},{4,5},{5,4},{6,7},{7,6},{8,9},{9,8},{10,11... | collective-permute-start | bytes 6291464 | tf_op jit(solution)/shard_map/cond/branch_1_fun/ppermute | solution.py:355
  115.5 1.6 copy-start.2
  132.1 21.5 %collective-permute-start.12 = (bf16[1536,256]{1,0:T(8,128)(2,1)S(1)}, bf16[1536,256]{1,0:T(8,128)(2,1)S(1)}, u32[]{:S(2)}, u32[]{:S(2)}) collective-permute-start(bf16[1536,256]{1,0:T(8,128)(2,1)S(1)} %slice.49), channel_id=1, source_target_pairs={{0,8},{2,10},{4,12},{6,14},{8,16},{10,18},{12,20},{14,22},{16,24},... | collective-permute-start | bytes 2359304 | tf_op jit(solution)/shard_map/ppermute | solution.py:416
  153.6 0.9 copy-start.11
  161.8 32.2 %collective-permute-start.13 = (bf16[512,512]{1,0:T(8,128)(2,1)}, bf16[512,512]{1,0:T(8,128)(2,1)S(1)}, u32[]{:S(2)}, u32[]{:S(2)}) collective-permute-start(bf16[512,512]{1,0:T(8,128)(2,1)} %shard_map.59), channel_id=1, source_target_pairs={{0,6},{2,4},{4,2},{6,0},{8,14},{10,12},{12,10},{14,8},{16,22},{18,... | collective-permute-start | bytes 1572872 | tf_op jit(solution)/shard_map/ppermute | solution.py:294
  173.7 20.7 %collective-permute-start.14 = (bf16[512,512]{1,0:T(8,128)(2,1)}, bf16[512,512]{1,0:T(8,128)(2,1)S(1)}, u32[]{:S(2)}, u32[]{:S(2)}) collective-permute-start(bf16[512,512]{1,0:T(8,128)(2,1)} %shard_map.60), channel_id=1, source_target_pairs={{0,4},{2,6},{4,0},{6,2},{8,12},{10,14},{12,8},{14,10},{16,20},{18,... | collective-permute-start | bytes 1572872 | tf_op jit(solution)/shard_map/ppermute | solution.py:294
  181.0 14.5 %collective-permute-start.15 = (bf16[512,512]{1,0:T(8,128)(2,1)}, bf16[512,512]{1,0:T(8,128)(2,1)S(1)}, u32[]{:S(2)}, u32[]{:S(2)}) collective-permute-start(bf16[512,512]{1,0:T(8,128)(2,1)} %shard_map.61), channel_id=1, source_target_pairs={{0,2},{2,0},{4,6},{6,4},{8,10},{10,8},{12,14},{14,12},{16,18},{18,... | collective-permute-start | bytes 1572872 | tf_op jit(solution)/shard_map/ppermute | solution.py:294
  194.3 2.5 %copy-start.6 = (bf16[512,512]{1,0:T(8,128)(2,1)S(1)}, bf16[512,512]{1,0:T(8,128)(2,1)}, u32[]{:S(2)}) copy-start(bf16[512,512]{1,0:T(8,128)(2,1)} %shard_map.62) | copy-start | bytes 1572868
  195.5 1.3 copy-start.3
Sparse Core Ops, SparseCore 0:
  9.0 44.8 all-gather.2
  55.4 70.9 all-gather.4

commit v7 on v6

--- a/solution.py
+++ b/solution.py
@@ -127,25 +127,34 @@
         scratch_shapes=[pltpu.SemaphoreType.DMA((len(targets),))],
         input_output_aliases=aliases,
         compiler_params=pltpu.CompilerParams(vmem_limit_bytes=PUT_BYTES),
+        cost_estimate=pl.CostEstimate(
+            flops=0, bytes_accessed=sum(4 * block.size for block, _ in blocks), transcendentals=0
+        ),
     )(place, *arrays)
 
 
-def attend_kernel(kv_heads, share, halo_rows, first, bounds, ends, q_ref, halo_ref, kv_ref, out_ref, k_all, v_all, q_all, sums, begins):
+def attend_kernel(kv_heads, share, halo_rows, chunk, first, bounds, ends, q_ref, halo_ref, kv_ref, out_ref, k_all, v_all, q_all, sums, begins):
     tile_index = pl.program_id(0)
     wide = 2 * HEAD_DIM
 
     @pl.when(tile_index == 0)
     def _():
         for source, start in ((halo_ref, 0), (kv_ref, halo_rows)):
-            rows = slice(start, start + source.shape[0])
-            for head in range(kv_heads):
-                columns = slice(head * HEAD_DIM, (head + 1) * HEAD_DIM)
-                at = (kv_heads + head) * HEAD_DIM
-                k_all[rows, columns] = source[:, columns]
-                v_all[rows, head * wide : head * wide + HEAD_DIM] = source[:, at : at + HEAD_DIM]
-                v_all[rows, head * wide + HEAD_DIM : (head + 1) * wide] = jnp.ones(
-                    (source.shape[0], HEAD_DIM), v_all.dtype
-                )
+            for number in range(source.shape[0] // chunk):
+                here = slice(number * chunk, (number + 1) * chunk)
+                rows = slice(start + number * chunk, start + (number + 1) * chunk)
+                back = halo_rows + bounds[0, first[0]] - rows.start
+
+                @pl.when((back >= 0) & (back <= halo_rows))
+                def _(source=source, here=here, rows=rows):
+                    for head in range(kv_heads):
+                        columns = slice(head * HEAD_DIM, (head + 1) * HEAD_DIM)
+                        at = (kv_heads + head) * HEAD_DIM
+                        k_all[rows, columns] = source[here, columns]
+                        v_all[rows, head * wide : head * wide + HEAD_DIM] = source[here, at : at + HEAD_DIM]
+                        v_all[rows, head * wide + HEAD_DIM : (head + 1) * wide] = jnp.ones(
+                            (chunk, HEAD_DIM), v_all.dtype
+                        )
 
     tile = q_ref.shape[0]
     for head in range(kv_heads * share):
@@ -226,7 +235,7 @@
     halo_rows = halo.shape[0]
     tiles = chunk_rows // TILE
     first = (chunk * tiles).reshape(1).astype(jnp.int32)
-    kernel = functools.partial(attend_kernel, kv_heads, heads // kv_heads, halo_rows)
+    kernel = functools.partial(attend_kernel, kv_heads, heads // kv_heads, halo_rows, chunk_rows)
     return pl.pallas_call(
         kernel,
         out_shape=jax.ShapeDtypeStruct((chunk_rows, width), jnp.bfloat16),
@@ -256,6 +265,37 @@
     )(first, bounds, ends, query, halo, kv)
 
 
+def copied_kernel(block_ref, other_ref, out_ref):
+    out_ref[...] = block_ref[...]
+
+
+def copied_after(block, other):
+    return pl.pallas_call(
+        copied_kernel,
+        out_shape=jax.ShapeDtypeStruct(block.shape, block.dtype),
+        in_specs=[pl.BlockSpec(memory_space=pltpu.VMEM), pl.BlockSpec(memory_space=pl.ANY)],
+        out_specs=pl.BlockSpec(memory_space=pltpu.VMEM),
+        compiler_params=pltpu.CompilerParams(vmem_limit_bytes=PUT_BYTES),
+    )(block, other)
+
+
+def pick_kernel(which, block_ref, out_ref):
+    out_ref[...] = block_ref[...]
+
+
+def pick(which, rows, array):
+    return pl.pallas_call(
+        pick_kernel,
+        out_shape=jax.ShapeDtypeStruct((rows, array.shape[1]), array.dtype),
+        grid_spec=pltpu.PrefetchScalarGridSpec(
+            num_scalar_prefetch=1,
+            grid=(4,),
+            in_specs=[pl.BlockSpec((rows // 4, array.shape[1]), lambda i, s: (4 * s[0] + i, 0))],
+            out_specs=pl.BlockSpec((rows // 4, array.shape[1]), lambda i, s: (i, 0)),
+        ),
+    )(which.reshape(1).astype(jnp.int32), array)
+
+
 def after(block, *others):
     space = pl.BlockSpec(memory_space=pl.ANY)
     return pl.pallas_call(
@@ -354,9 +394,8 @@
         def swap(block):
             return lax.ppermute(block, both, [(i * 2 + c, i * 2 + 1 - c) for i in devices for c in range(2)])
 
-        begin = core * half
-
-        own_half = lax.dynamic_slice_in_dim(tokens, begin, half, 0)
+
+        own_half = pick(core, half, tokens)
 
         def home(step_even, step_odd, mate):
             def target(s):
@@ -380,7 +419,7 @@
             mates = [swap(block) for block in (near, other)]
             first = [(near, home(1, 2, 0)), (mates[0], home(1, 2, 1)), (other, home(2, 1, 0)), (mates[1], home(2, 1, 1))]
             everything = put(place, group_rows, first, everything)
-            far = after(far, everything)
+            far = copied_after(far, everything)
             last = [(far, home(3, 3, 0)), (swap(far), home(3, 3, 1))]
             return put(place, group_rows, last, everything)
 
@@ -395,7 +434,7 @@
         all_tokens, known_tables, held = prepare(tokens, rest_kv)
         held = (*held, forwarded(held[-1]))
         near = after(near, held[1], *known_tables)
-        all_tokens = region(share, near[:1, :1], all_tokens, near, other)
+        all_tokens = region(share, rest_kv[:1, :1], all_tokens, near, other)
         others = range(1, group)
         kv_weights = [gathered(own_slices, (q_width // kv_width, kv_width), 0, [0])]
         kv_weights += from_lines((rest_kv, *held), 0, others)

time: 205 us -> 202 us (0.985); the launches traced: 205 us -> 198 us
  local copies, waits for them, and re-layouts: 15.9 us -> 9.84 us
  starting transfers between devices: 25.6 us -> 21.4 us
    ppermute x6, starting transfers between devices: 12.3 us -> 8.04 us  [to_partner(): return lax.ppermute(block, 'ca', [(i, i ^ step) for i in devices])]
    ppermute x6, waiting for transfers between devices: 17.9 us -> 22 us  [to_partner(): return lax.ppermute(block, 'ca', [(i, i ^ step) for i in devices])]
    pallas_call x0 -> x2, Pallas kernels: none -> 3.93 us  [the longest x1 3.79 us: pick(): pl.pallas_call(pick_kernel, out_shape=jax.ShapeDtypeStruct((rows, array.s...]
    ppermute x3, waiting for transfers between devices: 18.7 us -> 15.3 us  [forwarded(): lax.ppermute(block, 'ca', [(i, (i + group) % (group * lines)) for i in de...]
    dynamic_slice x1 -> x0, local copies, waits for them, and re-layouts: 3.13 us -> none  [per_device(): own_half = lax.dynamic_slice_in_dim(tokens, begin, half, 0)]
    cond x4 -> x0, local copies, waits for them, and re-layouts: 2.91 us -> none
    pallas_call x4, Pallas kernels: 30.9 us -> 28.7 us  [attend(): pl.pallas_call(kernel, out_shape=jax.ShapeDtypeStruct((chunk_rows, width)...]
    unnamed x22 -> x28, local copies, waits for them, and re-layouts: 4.48 us -> 4.45 us
  transfers between devices with their start and end apart: 18 -> 18, of which waited for: 11 -> 11; matrix products, arithmetic and copies ran while one was open for 7% -> 7% of each run, Pallas kernels for 30% -> 32%
where the time goes in v7:
time: 202 us; the launch traced here: 198 us
  waiting for transfers between devices  70.8 us (35%)
  Pallas kernels  69.5 us (34%)
  starting transfers between devices  21.4 us (11%)
  between operations  14.9 us (7%)
  other arithmetic  11.6 us (6%)
  local copies, waits for them, and re-layouts  9.84 us (5%)
    pallas_call x4, Pallas kernels, attend(): pl.pallas_call(kernel, out_shape=jax.ShapeDtypeStruct((chunk_rows, width)...  28.7 us
    pallas_call x2, Pallas kernels, project(): pl.pallas_call(functools.partial(project_kernel, rope_heads, layout, len(...  26.8 us
    ppermute x6, waiting for transfers between devices, to_partner(): return lax.ppermute(block, 'ca', [(i, i ^ step) for i in devices])  22 us
    ppermute x3, waiting for transfers between devices, cross(): return lax.ppermute(block, both, pairs)  20.9 us
    ppermute x3, waiting for transfers between devices, forwarded(): lax.ppermute(block, 'ca', [(i, (i + group) % (group * lines)) for i in de...  15.3 us
    ppermute x3, waiting for transfers between devices, swap(): lax.ppermute(block, both, [(i * 2 + c, i * 2 + 1 - c) for i in devices fo...  10.5 us
    pallas_call x3, Pallas kernels, put(): pl.pallas_call(functools.partial(put_kernel, targets), out_shape=jax.Shap...  9.99 us
    ppermute x6, starting transfers between devices, to_partner(): return lax.ppermute(block, 'ca', [(i, i ^ step) for i in devices])  8.04 us
  transfers between devices with their start and end apart: 18, of which 11 were waited for; matrix products, arithmetic and copies ran while one was open for 7% of the time, Pallas kernels for 32%

profile of v7, /device:TPU:16, one launch (start us, length us, event | category | flops | bytes accessed | tf_op | source)
XLA Modules:
  0.0 198.1 jit_solution(4824070519426722211)
XLA Ops:
  8.9 1.6 collective-permute-start.6
  10.5 1.5 collective-permute-start.7
  12.7 15.6 %collective-permute-done.6 = bf16[256,768]{1,0:T(8,128)(2,1)S(1)} collective-permute-done((bf16[256,768]{1,0:T(8,128)(2,1)S(1)}, bf16[256,768]{1,0:T(8,128)(2,1)S(1)}, u32[]{:S(2)}, u32[]{:S(2)}) %collective-permute-start.6) | collective-permute-done | bytes 393248 | tf_op jit(solution)/shard_map/ppermute | solution.py:334
  30.7 3.8 %shard_map.55 = bf16[256,4096]{1,0:T(8,128)(2,1)} custom-call(s32[1]{0:T(128)} %bitcast.5.which, bf16[512,4096]{1,0:T(8,128)(2,1)} %refs_0_.1), custom_call_target="tpu_custom_call" | custom-call | tf_op jit(solution)/shard_map/pallas_call | solution.py:287
  36.0 1.5 collective-permute-start.10
  37.9 1.6 collective-permute-start.8
  40.9 12.0 %collective-permute-done.8.refs_2_ = bf16[768,256]{1,0:T(8,128)(2,1)S(1)} collective-permute-done((bf16[768,256]{1,0:T(8,128)(2,1)S(1)}, bf16[768,256]{1,0:T(8,128)(2,1)S(1)}, u32[]{:S(2)}, u32[]{:S(2)}) %collective-permute-start.8) | collective-permute-done | bytes 393248 | tf_op jit(solution)/shard_map/ppermute | solution.py:341
  52.9 1.7 collective-permute-start.9
  54.6 5.6 %fusion = (f32[2048,64]{1,0:T(8,128)S(1)}, f32[2048,64]{1,0:T(8,128)}, f32[2048,64]{1,0:T(8,128)}) fusion(f32[64]{0:T(128)S(1)} %multiply_power_fusion, f32[2048]{0:T(1024)S(1)} %get-tuple-element.37), kind=kLoop, calls=%fused_computation.10 | loop fusion | flops 262144 | bytes 1581312 | tf_op jit(solution)/shard_map/neg | solution.py:35
  60.2 3.2 %collective-permute-done.9.refs_1_.refs_3_ = bf16[768,256]{1,0:T(8,128)(2,1)S(1)} collective-permute-done((bf16[768,256]{1,0:T(8,128)(2,1)S(1)}, bf16[768,256]{1,0:T(8,128)(2,1)S(1)}, u32[]{:S(2)}, u32[]{:S(2)}) %collective-permute-start.9) | collective-permute-done | bytes 393248 | tf_op jit(solution)/shard_map/ppermute | solution.py:341
  63.5 2.2 %collective-permute-start.11 = (bf16[768,256]{1,0:T(8,128)(2,1)S(1)}, bf16[768,256]{1,0:T(8,128)(2,1)}, u32[]{:S(2)}, u32[]{:S(2)}) collective-permute-start(bf16[768,256]{1,0:T(8,128)(2,1)S(1)} %collective-permute-done.9.refs_1_.refs_3_), channel_id=1, source_target_pairs={{0,8},{2,10},{4,12},{6,14},{8,16},{10,18},{12,20},{14,22},{16,24},... | collective-permute-start | bytes 1179656 | tf_op jit(solution)/shard_map/ppermute | solution.py:341
  65.8 2.2 %copy-done = bf16[512,4096]{1,0:T(8,128)(2,1)S(1)} copy-done((bf16[512,4096]{1,0:T(8,128)(2,1)S(1)}, bf16[512,4096]{1,0:T(8,128)(2,1)}, u32[]{:S(2)}) %copy-start) | copy-done | bytes 4194328
  67.9 2.5 %shard_map.57 = bf16[2048,4096]{1,0:T(8,128)(2,1)} custom-call(s32[3]{0:T(128)S(1)} %pad_add_fusion.1.place, bf16[512,4096]{1,0:T(8,128)(2,1)S(1)} %copy-done), custom_call_target="tpu_custom_call" | custom-call | bytes 8388608 | tf_op jit(solution)/shard_map/pallas_call | solution.py:122
  71.1 2.0 %pad_maximum_fusion = (f32[2048,128]{1,0:T(8,128)}, f32[2048,128]{1,0:T(8,128)}) fusion(f32[2048,64]{1,0:T(8,128)S(1)} %copy-done.2, f32[2048,64]{1,0:T(8,128)S(1)} %copy-done.1, f32[2048,64]{1,0:T(8,128)S(1)} %get-tuple-element.34), kind=kLoop, calls=%fused_computation.2 | loop fusion | flops 524288 | bytes 3670016 | tf_op jit(solution)/shard_map/concatenate | solution.py:35
  75.6 6.7 %collective-permute-done.5.refs_0_ = bf16[256,4096]{1,0:T(8,128)(2,1)S(1)} collective-permute-done((bf16[256,4096]{1,0:T(8,128)(2,1)}, bf16[256,4096]{1,0:T(8,128)(2,1)S(1)}, u32[]{:S(2)}, u32[]{:S(2)}) %collective-permute-start.5) | collective-permute-done | bytes 2097184 | tf_op jit(solution)/shard_map/ppermute | solution.py:392
  82.3 33.4 %conditional.1 = (bf16[2048,4096]{1,0:T(8,128)(2,1)}) conditional(s32[]{:T(128)} %bitcast.6, () %tuple.11, (bf16[256,4096]{1,0:T(8,128)(2,1)S(1)}, bf16[256,4096]{1,0:T(8,128)(2,1)}, s32[3]{0:T(128)S(1)}, bf16[2048,4096]{1,0:T(8,128)(2,1)}) %tuple.12), branch_computations={%region_2.3_spmd, %region_3.4_spmd} | conditional | bytes 58720424 | solution.py:432
  83.3 5.4 %collective-permute-done.1.refs_1_ = bf16[256,4096]{1,0:T(8,128)(2,1)S(1)} collective-permute-done((bf16[256,4096]{1,0:T(8,128)(2,1)S(1)}, bf16[256,4096]{1,0:T(8,128)(2,1)S(1)}, u32[]{:S(2)}, u32[]{:S(2)}) %collective-permute-start.1) | collective-permute-done | bytes 2097184 | tf_op jit(solution)/shard_map/cond/branch_1_fun/ppermute | solution.py:395
  89.6 5.0 %branch_1_fun.3.other_ref.refs_2_ = bf16[2048,4096]{1,0:T(8,128)(2,1)} custom-call(s32[3]{0:T(128)S(1)} %get-tuple-element.16.place, bf16[256,4096]{1,0:T(8,128)(2,1)S(1)} %get-tuple-element.17.refs_0_, bf16[256,4096]{1,0:T(8,128)(2,1)S(1)} %collective-permute-done.1.refs_1_, ...), custom_call_target="tpu_custom_call", output_to_operand_aliasing={{}: (5, {})} | custom-call | bytes 16777216 | tf_op jit(solution)/shard_map/cond/branch_1_fun/pallas_call | solution.py:122
  94.6 14.2 %collective-permute-done.block_ref = bf16[256,4096]{1,0:T(8,128)(2,1)S(1)} collective-permute-done((bf16[256,4096]{1,0:T(8,128)(2,1)S(1)}, bf16[256,4096]{1,0:T(8,128)(2,1)S(1)}, u32[]{:S(2)}, u32[]{:S(2)}) %collective-permute-start) | collective-permute-done | bytes 2097184 | tf_op jit(solution)/shard_map/cond/branch_1_fun/ppermute | solution.py:392
  109.0 4.1 %collective-permute-done.3.refs_1_ = bf16[256,4096]{1,0:T(8,128)(2,1)S(1)} collective-permute-done((bf16[256,4096]{1,0:T(8,128)(2,1)S(1)}, bf16[256,4096]{1,0:T(8,128)(2,1)S(1)}, u32[]{:S(2)}, u32[]{:S(2)}) %collective-permute-start.3) | collective-permute-done | bytes 2097184 | tf_op jit(solution)/shard_map/cond/branch_1_fun/ppermute | solution.py:395
  113.2 2.5 %branch_1_fun.5 = bf16[2048,4096]{1,0:T(8,128)(2,1)} custom-call(s32[3]{0:T(128)S(1)} %get-tuple-element.16.place, bf16[256,4096]{1,0:T(8,128)(2,1)S(1)} %branch_1_fun.4.refs_0_, bf16[256,4096]{1,0:T(8,128)(2,1)S(1)} %collective-permute-done.3.refs_1_, bf16[2048,4096]{1,0:T(8,128)(2,1)} %branch_1_fun.3.other_ref.refs_2_), custom_call_target="tpu_custom_call", output_to_operand_aliasing={{}: (3, {})} | custom-call | bytes 8388608 | tf_op jit(solution)/shard_map/cond/branch_1_fun/pallas_call | solution.py:122
  115.7 11.2 %shard_map.59.kv_ref = bf16[2048,256]{1,0:T(8,128)(2,1)} custom-call(s32[3]{0:T(128)S(1)} %pad_add_fusion.1.place, bf16[2048,4096]{1,0:T(8,128)(2,1)} %get-tuple-element.45.x_ref, bf16[1024,768]{1,0:T(8,128)(2,1)} %all-gather.3.cloned.1.call-done.refs_0_, bf16[768,256]{1,0:T(8,128)(2,1)} %copy-done.5, bf16[768,256]{1,0:T(8,128)(2,1)} %copy-done.8, ...), custom_call_target="tpu_custom_call" | custom-call | flops 4294967296 | bytes 18874368 | tf_op jit(solution)/shard_map/pallas_call | solution.py:79
  128.1 3.7 %collective-permute-start.12 = (bf16[1536,256]{1,0:T(8,128)(2,1)S(1)}, bf16[1536,256]{1,0:T(8,128)(2,1)S(1)}, u32[]{:S(2)}, u32[]{:S(2)}) collective-permute-start(bf16[1536,256]{1,0:T(8,128)(2,1)S(1)} %slice.50), channel_id=1, source_target_pairs={{0,8},{2,10},{4,12},{6,14},{8,16},{10,18},{12,20},{14,22},{16,24},... | collective-permute-start | bytes 2359304 | tf_op jit(solution)/shard_map/ppermute | solution.py:455
  131.8 15.6 %shard_map.58.q_ref = bf16[2048,512]{1,0:T(8,128)(2,1)} custom-call(s32[3]{0:T(128)S(1)} %pad_add_fusion.1.place, bf16[2048,4096]{1,0:T(8,128)(2,1)} %get-tuple-element.45.x_ref, bf16[1024,768]{1,0:T(8,128)(2,1)} %all-gather.3.cloned.1.call-done.refs_0_, bf16[3072,512]{1,0:T(8,128)(2,1)} %all-gather.5.cloned.1.call-done.refs_1_, ...), custom_call_target="tpu_custom_call" | custom-call | flops 8589934592 | bytes 20971520 | tf_op jit(solution)/shard_map/pallas_call | solution.py:79
  147.5 2.2 %collective-permute-done.12.halo_ref = bf16[1536,256]{1,0:T(8,128)(2,1)S(1)} collective-permute-done((bf16[1536,256]{1,0:T(8,128)(2,1)S(1)}, bf16[1536,256]{1,0:T(8,128)(2,1)S(1)}, u32[]{:S(2)}, u32[]{:S(2)}) %collective-permute-start.12) | collective-permute-done | bytes 786464 | tf_op jit(solution)/shard_map/ppermute | solution.py:455
  150.5 6.4 %shard_map.60 = bf16[512,512]{1,0:T(8,128)(2,1)} custom-call(s32[1]{0:T(128)} %bitcast.first, s32[3,8]{1,0:T(4,128)} %pad_add_fusion.refs_5_.bounds, s32[8]{0:T(128)} %broadcast_subtract_fusion.1.refs_4_.ends, bf16[2048,512]{1,0:T(8,128)(2,1)} %shard_map.58.q_ref, bf16[1536,256]{1,0:T(8,128)(2,1)} %copy-done.12, bf16[2048,256]{1,0:T(8,128)(2,1)} %shard_map.59.kv_ref), custom_call_target="tpu_custom_call" | custom-call | flops 1073741824 | bytes 1048576 | tf_op jit(solution)/shard_map/pallas_call | solution.py:239
  156.9 2.1 %collective-permute-start.13 = (bf16[512,512]{1,0:T(8,128)(2,1)}, bf16[512,512]{1,0:T(8,128)(2,1)S(1)}, u32[]{:S(2)}, u32[]{:S(2)}) collective-permute-start(bf16[512,512]{1,0:T(8,128)(2,1)} %shard_map.60), channel_id=1, source_target_pairs={{0,6},{2,4},{4,2},{6,0},{8,14},{10,12},{12,10},{14,8},{16,22},{18,... | collective-permute-start | bytes 1572872 | tf_op jit(solution)/shard_map/ppermute | solution.py:334
  159.0 6.2 %shard_map.61 = bf16[512,512]{1,0:T(8,128)(2,1)} custom-call(s32[1]{0:T(128)} %bitcast.7.first, s32[3,8]{1,0:T(4,128)} %pad_add_fusion.refs_5_.bounds, s32[8]{0:T(128)} %broadcast_subtract_fusion.1.refs_4_.ends, bf16[2048,512]{1,0:T(8,128)(2,1)} %shard_map.58.q_ref, bf16[1536,256]{1,0:T(8,128)(2,1)} %copy-done.12, bf16[2048,256]{1,0:T(8,128)(2,1)} %shard_map.59.kv_ref), custom_call_target="tpu_custom_call" | custom-call | flops 1073741824 | bytes 1048576 | tf_op jit(solution)/shard_map/pallas_call | solution.py:239
  165.3 1.7 collective-permute-start.14
  167.0 9.0 %shard_map.62 = bf16[512,512]{1,0:T(8,128)(2,1)} custom-call(s32[1]{0:T(128)} %bitcast.8.first, s32[3,8]{1,0:T(4,128)} %pad_add_fusion.refs_5_.bounds, s32[8]{0:T(128)} %broadcast_subtract_fusion.1.refs_4_.ends, bf16[2048,512]{1,0:T(8,128)(2,1)} %shard_map.58.q_ref, bf16[1536,256]{1,0:T(8,128)(2,1)} %copy-done.12, bf16[2048,256]{1,0:T(8,128)(2,1)} %shard_map.59.kv_ref), custom_call_target="tpu_custom_call" | custom-call | flops 1073741824 | bytes 1048576 | tf_op jit(solution)/shard_map/pallas_call | solution.py:239
  176.5 7.1 %shard_map.63 = bf16[512,512]{1,0:T(8,128)(2,1)} custom-call(s32[1]{0:T(128)} %bitcast.9.first, s32[3,8]{1,0:T(4,128)} %pad_add_fusion.refs_5_.bounds, s32[8]{0:T(128)} %broadcast_subtract_fusion.1.refs_4_.ends, bf16[2048,512]{1,0:T(8,128)(2,1)} %shard_map.58.q_ref, bf16[1536,256]{1,0:T(8,128)(2,1)} %copy-done.12, bf16[2048,256]{1,0:T(8,128)(2,1)} %shard_map.59.kv_ref), custom_call_target="tpu_custom_call" | custom-call | flops 1073741824 | bytes 1048576 | tf_op jit(solution)/shard_map/pallas_call | solution.py:239
  184.0 5.1 %collective-permute-done.15 = bf16[512,512]{1,0:T(8,128)(2,1)S(1)} collective-permute-done((bf16[512,512]{1,0:T(8,128)(2,1)}, bf16[512,512]{1,0:T(8,128)(2,1)S(1)}, u32[]{:S(2)}, u32[]{:S(2)}) %collective-permute-start.15) | collective-permute-done | bytes 524320 | tf_op jit(solution)/shard_map/ppermute | solution.py:334
  (81 shorter events, 17.8 us)
Async XLA Ops:
  6.5 1.4 copy-start.10
  6.5 1.4 copy-start.9
  6.5 109.2 %all-gather.3.cloned.1.call-start = ((), (), s32[]{:S(2)}) async-start(), calls=%async_computation | async-start | bytes 1966080 | tf_op jit(solution)/shard_map/all_gather | solution.py:338
  8.8 123.0 %all-gather.5.cloned.1.call-start = ((), (), s32[]{:S(2)}) async-start(), calls=%async_computation.1 | async-start | bytes 3932160 | tf_op jit(solution)/shard_map/all_gather | solution.py:338
  8.9 19.3 %collective-permute-start.6 = (bf16[256,768]{1,0:T(8,128)(2,1)S(1)}, bf16[256,768]{1,0:T(8,128)(2,1)S(1)}, u32[]{:S(2)}, u32[]{:S(2)}) collective-permute-start(bf16[256,768]{1,0:T(8,128)(2,1)S(1)} %pad_maximum_fusion.4), channel_id=1, source_target_pairs={{0,4},{2,6},{4,0},{6,2},{8,12},{10,14},{12,8},{14,10},{16,20},{18,... | collective-permute-start | bytes 1179656 | tf_op jit(solution)/shard_map/ppermute | solution.py:334
  10.5 17.8 %collective-permute-start.7 = (bf16[256,768]{1,0:T(8,128)(2,1)S(1)}, bf16[256,768]{1,0:T(8,128)(2,1)S(1)}, u32[]{:S(2)}, u32[]{:S(2)}) collective-permute-start(bf16[256,768]{1,0:T(8,128)(2,1)S(1)} %pad_maximum_fusion.5), channel_id=1, source_target_pairs={{0,6},{2,4},{4,2},{6,0},{8,14},{10,12},{12,10},{14,8},{16,22},{18,... | collective-permute-start | bytes 1179656 | tf_op jit(solution)/shard_map/ppermute | solution.py:334
  12.1 17.5 %collective-permute-start.4 = (bf16[256,768]{1,0:T(8,128)(2,1)S(1)}, bf16[256,768]{1,0:T(8,128)(2,1)S(1)}, u32[]{:S(2)}, u32[]{:S(2)}) collective-permute-start(bf16[256,768]{1,0:T(8,128)(2,1)S(1)} %pad_maximum_fusion.3), channel_id=1, source_target_pairs={{0,2},{2,0},{4,6},{6,4},{8,10},{10,8},{12,14},{14,12},{16,18},{18,... | collective-permute-start | bytes 1179656 | tf_op jit(solution)/shard_map/ppermute | solution.py:334
  29.6 8.2 %copy-start.7 = (bf16[256,768]{1,0:T(8,128)(2,1)}, bf16[256,768]{1,0:T(8,128)(2,1)S(1)}, u32[]{:S(2)}) copy-start(bf16[256,768]{1,0:T(8,128)(2,1)S(1)} %collective-permute-done.4) | copy-start | bytes 1179652
  30.7 6.8 %copy-start.13 = (s32[8]{0:T(128)S(1)}, s32[8]{0:T(128)}, u32[]{:S(2)}) copy-start(s32[8]{0:T(128)} %param.8) | copy-start | bytes 100
  34.5 47.8 %collective-permute-start.5 = (bf16[256,4096]{1,0:T(8,128)(2,1)}, bf16[256,4096]{1,0:T(8,128)(2,1)S(1)}, u32[]{:S(2)}, u32[]{:S(2)}) collective-permute-start(bf16[256,4096]{1,0:T(8,128)(2,1)} %shard_map.55), channel_id=1, source_target_pairs={{0,2},{1,5},{2,0},{3,7},{4,6},{5,1},{6,4},{7,3},{8,10},{9,13},{10,... | collective-permute-start | bytes 6291464 | tf_op jit(solution)/shard_map/ppermute | solution.py:392
  36.0 46.3 %collective-permute-start.10 = (bf16[256,4096]{1,0:T(8,128)(2,1)}, bf16[256,4096]{1,0:T(8,128)(2,1)}, u32[]{:S(2)}, u32[]{:S(2)}) collective-permute-start(bf16[256,4096]{1,0:T(8,128)(2,1)} %shard_map.55), channel_id=1, source_target_pairs={{0,4},{1,3},{2,6},{3,1},{4,0},{5,7},{6,2},{7,5},{8,12},{9,11},{10,... | collective-permute-start | bytes 6291464 | tf_op jit(solution)/shard_map/ppermute | solution.py:392
  37.9 25.6 %copy-start.5 = (bf16[768,256]{1,0:T(8,128)(2,1)}, bf16[768,256]{1,0:T(8,128)(2,1)S(1)}, u32[]{:S(2)}) copy-start(bf16[768,256]{1,0:T(8,128)(2,1)S(1)} %pad_maximum_fusion.6.refs_1_) | copy-start | bytes 1179652
  37.9 15.0 %collective-permute-start.8 = (bf16[768,256]{1,0:T(8,128)(2,1)S(1)}, bf16[768,256]{1,0:T(8,128)(2,1)S(1)}, u32[]{:S(2)}, u32[]{:S(2)}) collective-permute-start(bf16[768,256]{1,0:T(8,128)(2,1)S(1)} %pad_maximum_fusion.6.refs_1_), channel_id=1, source_target_pairs={{0,8},{2,10},{4,12},{6,14},{8,16},{10,18},{12,20},{14,22},{16,24},... | collective-permute-start | bytes 1179656 | tf_op jit(solution)/shard_map/ppermute | solution.py:341
  52.9 12.8 %copy-start.8 = (bf16[768,256]{1,0:T(8,128)(2,1)}, bf16[768,256]{1,0:T(8,128)(2,1)S(1)}, u32[]{:S(2)}) copy-start(bf16[768,256]{1,0:T(8,128)(2,1)S(1)} %collective-permute-done.8.refs_2_) | copy-start | bytes 1179652
  52.9 10.6 %collective-permute-start.9 = (bf16[768,256]{1,0:T(8,128)(2,1)S(1)}, bf16[768,256]{1,0:T(8,128)(2,1)S(1)}, u32[]{:S(2)}, u32[]{:S(2)}) collective-permute-start(bf16[768,256]{1,0:T(8,128)(2,1)S(1)} %collective-permute-done.8.refs_2_), channel_id=1, source_target_pairs={{0,8},{2,10},{4,12},{6,14},{8,16},{10,18},{12,20},{14,22},{16,24},... | collective-permute-start | bytes 1179656 | tf_op jit(solution)/shard_map/ppermute | solution.py:341
  63.5 7.0 %copy-start.4 = (bf16[768,256]{1,0:T(8,128)(2,1)}, bf16[768,256]{1,0:T(8,128)(2,1)S(1)}, u32[]{:S(2)}) copy-start(bf16[768,256]{1,0:T(8,128)(2,1)S(1)} %collective-permute-done.9.refs_1_.refs_3_) | copy-start | bytes 1179652
  63.5 52.2 %collective-permute-start.11 = (bf16[768,256]{1,0:T(8,128)(2,1)S(1)}, bf16[768,256]{1,0:T(8,128)(2,1)}, u32[]{:S(2)}, u32[]{:S(2)}) collective-permute-start(bf16[768,256]{1,0:T(8,128)(2,1)S(1)} %collective-permute-done.9.refs_1_.refs_3_), channel_id=1, source_target_pairs={{0,8},{2,10},{4,12},{6,14},{8,16},{10,18},{12,20},{14,22},{16,24},... | collective-permute-start | bytes 1179656 | tf_op jit(solution)/shard_map/ppermute | solution.py:341
  65.8 2.2 %copy-start = (bf16[512,4096]{1,0:T(8,128)(2,1)S(1)}, bf16[512,4096]{1,0:T(8,128)(2,1)}, u32[]{:S(2)}) copy-start(bf16[512,4096]{1,0:T(8,128)(2,1)} %refs_0_.1) | copy-start | bytes 12582916
  67.9 2.5 %copy-start.11 = (s32[1,8]{1,0:T(1,128)S(1)}, s32[1,8]{1,0:T(1,128)}, u32[]{:S(2)}) copy-start(s32[1,8]{1,0:T(1,128)} %iota_multiply_fusion) | copy-start | bytes 100
  67.9 3.1 %copy-start.1 = (f32[2048,64]{1,0:T(8,128)S(1)}, f32[2048,64]{1,0:T(8,128)}, u32[]{:S(2)}) copy-start(f32[2048,64]{1,0:T(8,128)} %get-tuple-element.35) | copy-start | bytes 1572868
  67.9 3.1 %copy-start.2 = (f32[2048,64]{1,0:T(8,128)S(1)}, f32[2048,64]{1,0:T(8,128)}, u32[]{:S(2)}) copy-start(f32[2048,64]{1,0:T(8,128)} %get-tuple-element.36) | copy-start | bytes 1572868
  82.3 6.4 %collective-permute-start.1 = (bf16[256,4096]{1,0:T(8,128)(2,1)S(1)}, bf16[256,4096]{1,0:T(8,128)(2,1)S(1)}, u32[]{:S(2)}, u32[]{:S(2)}) collective-permute-start(bf16[256,4096]{1,0:T(8,128)(2,1)S(1)} %get-tuple-element.17.refs_0_), channel_id=1, source_target_pairs={{0,1},{1,0},{2,3},{3,2},{4,5},{5,4},{6,7},{7,6},{8,9},{9,8},{10,11... | collective-permute-start | bytes 6291464 | tf_op jit(solution)/shard_map/cond/branch_1_fun/ppermute | solution.py:395
  82.3 7.4 %collective-permute-start.2 = (bf16[256,4096]{1,0:T(8,128)(2,1)}, bf16[256,4096]{1,0:T(8,128)(2,1)S(1)}, u32[]{:S(2)}, u32[]{:S(2)}) collective-permute-start(bf16[256,4096]{1,0:T(8,128)(2,1)} %get-tuple-element.18.refs_2_), channel_id=1, source_target_pairs={{0,1},{1,0},{2,3},{3,2},{4,5},{5,4},{6,7},{7,6},{8,9},{9,8},{10,11... | collective-permute-start | bytes 6291464 | tf_op jit(solution)/shard_map/cond/branch_1_fun/ppermute | solution.py:395
  82.8 26.0 %collective-permute-start = (bf16[256,4096]{1,0:T(8,128)(2,1)S(1)}, bf16[256,4096]{1,0:T(8,128)(2,1)S(1)}, u32[]{:S(2)}, u32[]{:S(2)}) collective-permute-start(bf16[256,4096]{1,0:T(8,128)(2,1)S(1)} %get-tuple-element.17.refs_0_), channel_id=1, source_target_pairs={{0,4},{1,3},{2,6},{3,1},{4,0},{5,7},{6,2},{7,5},{8,12},{9,11},{10,... | collective-permute-start | bytes 6291464 | tf_op jit(solution)/shard_map/cond/branch_1_fun/ppermute | solution.py:392
  108.9 4.2 %collective-permute-start.3 = (bf16[256,4096]{1,0:T(8,128)(2,1)S(1)}, bf16[256,4096]{1,0:T(8,128)(2,1)S(1)}, u32[]{:S(2)}, u32[]{:S(2)}) collective-permute-start(bf16[256,4096]{1,0:T(8,128)(2,1)S(1)} %branch_1_fun.4.refs_0_), channel_id=1, source_target_pairs={{0,1},{1,0},{2,3},{3,2},{4,5},{5,4},{6,7},{7,6},{8,9},{9,8},{10,11... | collective-permute-start | bytes 6291464 | tf_op jit(solution)/shard_map/cond/branch_1_fun/ppermute | solution.py:395
  128.1 21.5 %collective-permute-start.12 = (bf16[1536,256]{1,0:T(8,128)(2,1)S(1)}, bf16[1536,256]{1,0:T(8,128)(2,1)S(1)}, u32[]{:S(2)}, u32[]{:S(2)}) collective-permute-start(bf16[1536,256]{1,0:T(8,128)(2,1)S(1)} %slice.50), channel_id=1, source_target_pairs={{0,8},{2,10},{4,12},{6,14},{8,16},{10,18},{12,20},{14,22},{16,24},... | collective-permute-start | bytes 2359304 | tf_op jit(solution)/shard_map/ppermute | solution.py:455
  149.6 0.9 copy-start.12
  156.9 26.7 %collective-permute-start.13 = (bf16[512,512]{1,0:T(8,128)(2,1)}, bf16[512,512]{1,0:T(8,128)(2,1)S(1)}, u32[]{:S(2)}, u32[]{:S(2)}) collective-permute-start(bf16[512,512]{1,0:T(8,128)(2,1)} %shard_map.60), channel_id=1, source_target_pairs={{0,6},{2,4},{4,2},{6,0},{8,14},{10,12},{12,10},{14,8},{16,22},{18,... | collective-permute-start | bytes 1572872 | tf_op jit(solution)/shard_map/ppermute | solution.py:334
  165.3 18.6 %collective-permute-start.14 = (bf16[512,512]{1,0:T(8,128)(2,1)}, bf16[512,512]{1,0:T(8,128)(2,1)S(1)}, u32[]{:S(2)}, u32[]{:S(2)}) collective-permute-start(bf16[512,512]{1,0:T(8,128)(2,1)} %shard_map.61), channel_id=1, source_target_pairs={{0,4},{2,6},{4,0},{6,2},{8,12},{10,14},{12,8},{14,10},{16,20},{18,... | collective-permute-start | bytes 1572872 | tf_op jit(solution)/shard_map/ppermute | solution.py:334
  176.0 13.1 %collective-permute-start.15 = (bf16[512,512]{1,0:T(8,128)(2,1)}, bf16[512,512]{1,0:T(8,128)(2,1)S(1)}, u32[]{:S(2)}, u32[]{:S(2)}) collective-permute-start(bf16[512,512]{1,0:T(8,128)(2,1)} %shard_map.62), channel_id=1, source_target_pairs={{0,2},{2,0},{4,6},{6,4},{8,10},{10,8},{12,14},{14,12},{16,18},{18,... | collective-permute-start | bytes 1572872 | tf_op jit(solution)/shard_map/ppermute | solution.py:334
  183.8 6.6 %copy-start.6 = (bf16[512,512]{1,0:T(8,128)(2,1)S(1)}, bf16[512,512]{1,0:T(8,128)(2,1)}, u32[]{:S(2)}) copy-start(bf16[512,512]{1,0:T(8,128)(2,1)} %shard_map.63) | copy-start | bytes 1572868
  189.1 1.3 copy-start.3
Sparse Core Ops, SparseCore 0:
  9.0 43.3 all-gather.2
  54.0 71.9 all-gather.4

commit v8 on v7

--- a/solution.py
+++ b/solution.py
@@ -279,23 +279,6 @@
     )(block, other)
 
 
-def pick_kernel(which, block_ref, out_ref):
-    out_ref[...] = block_ref[...]
-
-
-def pick(which, rows, array):
-    return pl.pallas_call(
-        pick_kernel,
-        out_shape=jax.ShapeDtypeStruct((rows, array.shape[1]), array.dtype),
-        grid_spec=pltpu.PrefetchScalarGridSpec(
-            num_scalar_prefetch=1,
-            grid=(4,),
-            in_specs=[pl.BlockSpec((rows // 4, array.shape[1]), lambda i, s: (4 * s[0] + i, 0))],
-            out_specs=pl.BlockSpec((rows // 4, array.shape[1]), lambda i, s: (i, 0)),
-        ),
-    )(which.reshape(1).astype(jnp.int32), array)
-
-
 def after(block, *others):
     space = pl.BlockSpec(memory_space=pl.ANY)
     return pl.pallas_call(
@@ -381,7 +364,10 @@
 
     place = jnp.stack([mine, line, core]).astype(jnp.int32)
     if group > 1:
-        slices = [slice_for(mine)] + [to_partner(slice_for(mine ^ step), step) for step in range(1, group)]
+        own_half = lax.dynamic_slice_in_dim(tokens, core * half, half, 0)
+        leaving = [slice_for(mine ^ step) for step in range(1, group)]
+        leaving[-1] = after(leaving[-1], own_half)
+        slices = [slice_for(mine)] + [to_partner(block, step) for step, block in enumerate(leaving, 1)]
         own_slices = along_lines(slices[0])
         rest_q = along_lines(jnp.concatenate([a[:, :q_width] for a in slices[1:]]))
         rest_kv = jnp.concatenate([a[:, q_width:] for a in slices[1:]])
@@ -394,8 +380,6 @@
         def swap(block):
             return lax.ppermute(block, both, [(i * 2 + c, i * 2 + 1 - c) for i in devices for c in range(2)])
 
-
-        own_half = pick(core, half, tokens)
 
         def home(step_even, step_odd, mate):
             def target(s):

time: 202 us -> 201 us (level); the launches traced: 198 us -> 200 us
  local copies, waits for them, and re-layouts: 9.84 us -> 13 us
    pallas_call x1 -> x0, Pallas kernels: 3.79 us -> none  [pick(): pl.pallas_call(pick_kernel, out_shape=jax.ShapeDtypeStruct((rows, array.s...]
    dynamic_slice x0 -> x1, local copies, waits for them, and re-layouts: none -> 3.13 us  [per_device(): own_half = lax.dynamic_slice_in_dim(tokens, core * half, half, 0)]
    pallas_call x4, Pallas kernels: 28.7 us -> 31 us  [attend(): pl.pallas_call(kernel, out_shape=jax.ShapeDtypeStruct((chunk_rows, width)...]
  transfers between devices with their start and end apart: 18 -> 18, of which waited for: 11 -> 12; matrix products, arithmetic and copies ran while one was open for 7% -> 9% of each run, Pallas kernels for 32% -> 31%
where the time goes in v8:
time: 201 us; the launch traced here: 200 us
  waiting for transfers between devices  70.8 us (35%)
  Pallas kernels  67.9 us (34%)
  starting transfers between devices  20.9 us (10%)
  between operations  14.9 us (7%)
  local copies, waits for them, and re-layouts  13 us (6%)
  other arithmetic  12.4 us (6%)
    pallas_call x4, Pallas kernels, attend(): pl.pallas_call(kernel, out_shape=jax.ShapeDtypeStruct((chunk_rows, width)...  31 us
    pallas_call x2, Pallas kernels, project(): pl.pallas_call(functools.partial(project_kernel, rope_heads, layout, len(...  26.8 us
    ppermute x6, waiting for transfers between devices, to_partner(): return lax.ppermute(block, 'ca', [(i, i ^ step) for i in devices])  22.7 us
    ppermute x3, waiting for transfers between devices, cross(): return lax.ppermute(block, both, pairs)  19.5 us
    ppermute x3, waiting for transfers between devices, forwarded(): lax.ppermute(block, 'ca', [(i, (i + group) % (group * lines)) for i in de...  16.4 us
    ppermute x3, waiting for transfers between devices, swap(): lax.ppermute(block, both, [(i * 2 + c, i * 2 + 1 - c) for i in devices fo...  10 us
    pallas_call x3, Pallas kernels, put(): pl.pallas_call(functools.partial(put_kernel, targets), out_shape=jax.Shap...  9.99 us
    ppermute x3, starting transfers between devices, forwarded(): lax.ppermute(block, 'ca', [(i, (i + group) % (group * lines)) for i in de...  7.08 us
  transfers between devices with their start and end apart: 18, of which 12 were waited for; matrix products, arithmetic and copies ran while one was open for 9% of the time, Pallas kernels for 31%

profile of v8, /device:TPU:16, one launch (start us, length us, event | category | flops | bytes accessed | tf_op | source)
XLA Modules:
  0.0 200.0 jit_solution(8847341096328990370)
XLA Ops:
  6.5 1.3 constant_dynamic-slice_fusion.2
  9.7 3.1 %constant_dynamic-slice_fusion.9.refs_1_ = bf16[256,4096]{1,0:T(8,128)(2,1)} fusion(bf16[512,4096]{1,0:T(8,128)(2,1)} %refs_0_.1, s32[]{:T(128)S(6)} %select_n.55), kind=kLoop, calls=%fused_computation.27 | loop fusion | bytes 4194308 | tf_op jit(solution)/shard_map/dynamic_slice | solution.py:367
  12.8 2.4 %collective-permute-start.7 = (bf16[256,768]{1,0:T(8,128)(2,1)}, bf16[256,768]{1,0:T(8,128)(2,1)S(1)}, u32[]{:S(2)}, u32[]{:S(2)}) collective-permute-start(bf16[256,768]{1,0:T(8,128)(2,1)} %shard_map.55), channel_id=1, source_target_pairs={{0,6},{2,4},{4,2},{6,0},{8,14},{10,12},{12,10},{14,8},{16,22},{18,... | collective-permute-start | bytes 1179656 | tf_op jit(solution)/shard_map/ppermute | solution.py:317
  16.5 9.5 %collective-permute-done.7 = bf16[256,768]{1,0:T(8,128)(2,1)S(1)} collective-permute-done((bf16[256,768]{1,0:T(8,128)(2,1)}, bf16[256,768]{1,0:T(8,128)(2,1)S(1)}, u32[]{:S(2)}, u32[]{:S(2)}) %collective-permute-start.7) | collective-permute-done | bytes 393248 | tf_op jit(solution)/shard_map/ppermute | solution.py:317
  26.0 7.2 %collective-permute-done.6 = bf16[256,768]{1,0:T(8,128)(2,1)S(1)} collective-permute-done((bf16[256,768]{1,0:T(8,128)(2,1)S(1)}, bf16[256,768]{1,0:T(8,128)(2,1)S(1)}, u32[]{:S(2)}, u32[]{:S(2)}) %collective-permute-start.6) | collective-permute-done | bytes 393248 | tf_op jit(solution)/shard_map/ppermute | solution.py:317
  34.3 1.6 collective-permute-start.5
  37.0 1.6 collective-permute-start.8
  39.9 12.9 %collective-permute-done.8.refs_2_ = bf16[768,256]{1,0:T(8,128)(2,1)S(1)} collective-permute-done((bf16[768,256]{1,0:T(8,128)(2,1)S(1)}, bf16[768,256]{1,0:T(8,128)(2,1)S(1)}, u32[]{:S(2)}, u32[]{:S(2)}) %collective-permute-start.8) | collective-permute-done | bytes 393248 | tf_op jit(solution)/shard_map/ppermute | solution.py:324
  52.9 1.7 collective-permute-start.9
  54.6 5.6 %fusion = (f32[2048,64]{1,0:T(8,128)S(1)}, f32[2048,64]{1,0:T(8,128)}, f32[2048,64]{1,0:T(8,128)}) fusion(f32[64]{0:T(128)S(1)} %multiply_power_fusion, f32[2048]{0:T(1024)S(1)} %get-tuple-element.37), kind=kLoop, calls=%fused_computation.10 | loop fusion | flops 262144 | bytes 1581312 | tf_op jit(solution)/shard_map/neg | solution.py:35
  60.2 3.5 %collective-permute-done.9.refs_1_.refs_3_ = bf16[768,256]{1,0:T(8,128)(2,1)S(1)} collective-permute-done((bf16[768,256]{1,0:T(8,128)(2,1)S(1)}, bf16[768,256]{1,0:T(8,128)(2,1)S(1)}, u32[]{:S(2)}, u32[]{:S(2)}) %collective-permute-start.9) | collective-permute-done | bytes 393248 | tf_op jit(solution)/shard_map/ppermute | solution.py:324
  63.7 3.7 %collective-permute-start.11 = (bf16[768,256]{1,0:T(8,128)(2,1)S(1)}, bf16[768,256]{1,0:T(8,128)(2,1)}, u32[]{:S(2)}, u32[]{:S(2)}) collective-permute-start(bf16[768,256]{1,0:T(8,128)(2,1)S(1)} %collective-permute-done.9.refs_1_.refs_3_), channel_id=1, source_target_pairs={{0,8},{2,10},{4,12},{6,14},{8,16},{10,18},{12,20},{14,22},{16,24},... | collective-permute-start | bytes 1179656 | tf_op jit(solution)/shard_map/ppermute | solution.py:324
  67.5 2.2 %copy-done = bf16[512,4096]{1,0:T(8,128)(2,1)S(1)} copy-done((bf16[512,4096]{1,0:T(8,128)(2,1)S(1)}, bf16[512,4096]{1,0:T(8,128)(2,1)}, u32[]{:S(2)}) %copy-start) | copy-done | bytes 4194328
  69.7 2.5 %shard_map.57 = bf16[2048,4096]{1,0:T(8,128)(2,1)} custom-call(s32[3]{0:T(128)S(1)} %pad_add_fusion.1.place, bf16[512,4096]{1,0:T(8,128)(2,1)S(1)} %copy-done), custom_call_target="tpu_custom_call" | custom-call | bytes 8388608 | tf_op jit(solution)/shard_map/pallas_call | solution.py:122
  72.9 2.0 pad_maximum_fusion
  77.3 5.4 %collective-permute-done.5.refs_0_ = bf16[256,4096]{1,0:T(8,128)(2,1)S(1)} collective-permute-done((bf16[256,4096]{1,0:T(8,128)(2,1)}, bf16[256,4096]{1,0:T(8,128)(2,1)S(1)}, u32[]{:S(2)}, u32[]{:S(2)}) %collective-permute-start.5) | collective-permute-done | bytes 2097184 | tf_op jit(solution)/shard_map/ppermute | solution.py:378
  82.8 33.5 %conditional.1 = (bf16[2048,4096]{1,0:T(8,128)(2,1)}) conditional(s32[]{:T(128)} %bitcast.6, () %tuple.11, (bf16[256,4096]{1,0:T(8,128)(2,1)S(1)}, bf16[256,4096]{1,0:T(8,128)(2,1)}, s32[3]{0:T(128)S(1)}, bf16[2048,4096]{1,0:T(8,128)(2,1)}) %tuple.12), branch_computations={%region_2.3_spmd, %region_3.4_spmd} | conditional | bytes 58720424 | solution.py:416
  84.5 5.6 %collective-permute-done.1.refs_1_ = bf16[256,4096]{1,0:T(8,128)(2,1)S(1)} collective-permute-done((bf16[256,4096]{1,0:T(8,128)(2,1)S(1)}, bf16[256,4096]{1,0:T(8,128)(2,1)S(1)}, u32[]{:S(2)}, u32[]{:S(2)}) %collective-permute-start.1) | collective-permute-done | bytes 2097184 | tf_op jit(solution)/shard_map/cond/branch_1_fun/ppermute | solution.py:381
  90.3 5.0 %branch_1_fun.3.other_ref.refs_2_ = bf16[2048,4096]{1,0:T(8,128)(2,1)} custom-call(s32[3]{0:T(128)S(1)} %get-tuple-element.16.place, bf16[256,4096]{1,0:T(8,128)(2,1)S(1)} %get-tuple-element.17.refs_0_, bf16[256,4096]{1,0:T(8,128)(2,1)S(1)} %collective-permute-done.1.refs_1_, ...), custom_call_target="tpu_custom_call", output_to_operand_aliasing={{}: (5, {})} | custom-call | bytes 16777216 | tf_op jit(solution)/shard_map/cond/branch_1_fun/pallas_call | solution.py:122
  95.3 14.1 %collective-permute-done.block_ref = bf16[256,4096]{1,0:T(8,128)(2,1)S(1)} collective-permute-done((bf16[256,4096]{1,0:T(8,128)(2,1)S(1)}, bf16[256,4096]{1,0:T(8,128)(2,1)S(1)}, u32[]{:S(2)}, u32[]{:S(2)}) %collective-permute-start) | collective-permute-done | bytes 2097184 | tf_op jit(solution)/shard_map/cond/branch_1_fun/ppermute | solution.py:378
  109.6 4.1 %collective-permute-done.3.refs_1_ = bf16[256,4096]{1,0:T(8,128)(2,1)S(1)} collective-permute-done((bf16[256,4096]{1,0:T(8,128)(2,1)S(1)}, bf16[256,4096]{1,0:T(8,128)(2,1)S(1)}, u32[]{:S(2)}, u32[]{:S(2)}) %collective-permute-start.3) | collective-permute-done | bytes 2097184 | tf_op jit(solution)/shard_map/cond/branch_1_fun/ppermute | solution.py:381
  113.7 2.5 %branch_1_fun.5 = bf16[2048,4096]{1,0:T(8,128)(2,1)} custom-call(s32[3]{0:T(128)S(1)} %get-tuple-element.16.place, bf16[256,4096]{1,0:T(8,128)(2,1)S(1)} %branch_1_fun.4.refs_0_, bf16[256,4096]{1,0:T(8,128)(2,1)S(1)} %collective-permute-done.3.refs_1_, bf16[2048,4096]{1,0:T(8,128)(2,1)} %branch_1_fun.3.other_ref.refs_2_), custom_call_target="tpu_custom_call", output_to_operand_aliasing={{}: (3, {})} | custom-call | bytes 8388608 | tf_op jit(solution)/shard_map/cond/branch_1_fun/pallas_call | solution.py:122
  116.3 11.2 %shard_map.59.kv_ref = bf16[2048,256]{1,0:T(8,128)(2,1)} custom-call(s32[3]{0:T(128)S(1)} %pad_add_fusion.1.place, bf16[2048,4096]{1,0:T(8,128)(2,1)} %get-tuple-element.45.x_ref, bf16[1024,768]{1,0:T(8,128)(2,1)} %all-gather.3.cloned.1.call-done.refs_0_, bf16[768,256]{1,0:T(8,128)(2,1)} %copy-done.5, bf16[768,256]{1,0:T(8,128)(2,1)} %copy-done.8, ...), custom_call_target="tpu_custom_call" | custom-call | flops 4294967296 | bytes 18874368 | tf_op jit(solution)/shard_map/pallas_call | solution.py:79
  128.7 3.7 %collective-permute-start.12 = (bf16[1536,256]{1,0:T(8,128)(2,1)S(1)}, bf16[1536,256]{1,0:T(8,128)(2,1)S(1)}, u32[]{:S(2)}, u32[]{:S(2)}) collective-permute-start(bf16[1536,256]{1,0:T(8,128)(2,1)S(1)} %slice.50), channel_id=1, source_target_pairs={{0,8},{2,10},{4,12},{6,14},{8,16},{10,18},{12,20},{14,22},{16,24},... | collective-permute-start | bytes 2359304 | tf_op jit(solution)/shard_map/ppermute | solution.py:439
  132.4 15.6 %shard_map.58.q_ref = bf16[2048,512]{1,0:T(8,128)(2,1)} custom-call(s32[3]{0:T(128)S(1)} %pad_add_fusion.1.place, bf16[2048,4096]{1,0:T(8,128)(2,1)} %get-tuple-element.45.x_ref, bf16[1024,768]{1,0:T(8,128)(2,1)} %all-gather.3.cloned.1.call-done.refs_0_, bf16[3072,512]{1,0:T(8,128)(2,1)} %all-gather.5.cloned.1.call-done.refs_1_, ...), custom_call_target="tpu_custom_call" | custom-call | flops 8589934592 | bytes 20971520 | tf_op jit(solution)/shard_map/pallas_call | solution.py:79
  148.0 2.2 %collective-permute-done.12.halo_ref = bf16[1536,256]{1,0:T(8,128)(2,1)S(1)} collective-permute-done((bf16[1536,256]{1,0:T(8,128)(2,1)S(1)}, bf16[1536,256]{1,0:T(8,128)(2,1)S(1)}, u32[]{:S(2)}, u32[]{:S(2)}) %collective-permute-start.12) | collective-permute-done | bytes 786464 | tf_op jit(solution)/shard_map/ppermute | solution.py:439
  151.1 6.4 %shard_map.60 = bf16[512,512]{1,0:T(8,128)(2,1)} custom-call(s32[1]{0:T(128)} %bitcast.first, s32[3,8]{1,0:T(4,128)} %pad_add_fusion.refs_5_.bounds, s32[8]{0:T(128)} %broadcast_subtract_fusion.1.refs_4_.ends, bf16[2048,512]{1,0:T(8,128)(2,1)} %shard_map.58.q_ref, bf16[1536,256]{1,0:T(8,128)(2,1)} %copy-done.12, bf16[2048,256]{1,0:T(8,128)(2,1)} %shard_map.59.kv_ref), custom_call_target="tpu_custom_call" | custom-call | flops 1073741824 | bytes 1048576 | tf_op jit(solution)/shard_map/pallas_call | solution.py:239
  157.5 1.7 collective-permute-start.13
  159.2 9.8 %shard_map.61 = bf16[512,512]{1,0:T(8,128)(2,1)} custom-call(s32[1]{0:T(128)} %bitcast.7.first, s32[3,8]{1,0:T(4,128)} %pad_add_fusion.refs_5_.bounds, s32[8]{0:T(128)} %broadcast_subtract_fusion.1.refs_4_.ends, bf16[2048,512]{1,0:T(8,128)(2,1)} %shard_map.58.q_ref, bf16[1536,256]{1,0:T(8,128)(2,1)} %copy-done.12, bf16[2048,256]{1,0:T(8,128)(2,1)} %shard_map.59.kv_ref), custom_call_target="tpu_custom_call" | custom-call | flops 1073741824 | bytes 1048576 | tf_op jit(solution)/shard_map/pallas_call | solution.py:239
  169.8 8.3 %shard_map.62 = bf16[512,512]{1,0:T(8,128)(2,1)} custom-call(s32[1]{0:T(128)} %bitcast.8.first, s32[3,8]{1,0:T(4,128)} %pad_add_fusion.refs_5_.bounds, s32[8]{0:T(128)} %broadcast_subtract_fusion.1.refs_4_.ends, bf16[2048,512]{1,0:T(8,128)(2,1)} %shard_map.58.q_ref, bf16[1536,256]{1,0:T(8,128)(2,1)} %copy-done.12, bf16[2048,256]{1,0:T(8,128)(2,1)} %shard_map.59.kv_ref), custom_call_target="tpu_custom_call" | custom-call | flops 1073741824 | bytes 1048576 | tf_op jit(solution)/shard_map/pallas_call | solution.py:239
  178.1 6.4 %shard_map.63 = bf16[512,512]{1,0:T(8,128)(2,1)} custom-call(s32[1]{0:T(128)} %bitcast.9.first, s32[3,8]{1,0:T(4,128)} %pad_add_fusion.refs_5_.bounds, s32[8]{0:T(128)} %broadcast_subtract_fusion.1.refs_4_.ends, bf16[2048,512]{1,0:T(8,128)(2,1)} %shard_map.58.q_ref, bf16[1536,256]{1,0:T(8,128)(2,1)} %copy-done.12, bf16[2048,256]{1,0:T(8,128)(2,1)} %shard_map.59.kv_ref), custom_call_target="tpu_custom_call" | custom-call | flops 1073741824 | bytes 1048576 | tf_op jit(solution)/shard_map/pallas_call | solution.py:239
  185.0 5.9 %collective-permute-done.15 = bf16[512,512]{1,0:T(8,128)(2,1)S(1)} collective-permute-done((bf16[512,512]{1,0:T(8,128)(2,1)}, bf16[512,512]{1,0:T(8,128)(2,1)S(1)}, u32[]{:S(2)}, u32[]{:S(2)}) %collective-permute-start.15) | collective-permute-done | bytes 524320 | tf_op jit(solution)/shard_map/ppermute | solution.py:317
  (82 shorter events, 16.0 us)
Async XLA Ops:
  6.5 1.4 copy-start.10
  6.5 1.4 copy-start.9
  6.5 109.7 %all-gather.3.cloned.1.call-start = ((), (), s32[]{:S(2)}) async-start(), calls=%async_computation | async-start | bytes 1966080 | tf_op jit(solution)/shard_map/all_gather | solution.py:321
  8.8 123.6 %all-gather.5.cloned.1.call-start = ((), (), s32[]{:S(2)}) async-start(), calls=%async_computation.1 | async-start | bytes 3932160 | tf_op jit(solution)/shard_map/all_gather | solution.py:321
  12.8 13.2 %collective-permute-start.7 = (bf16[256,768]{1,0:T(8,128)(2,1)}, bf16[256,768]{1,0:T(8,128)(2,1)S(1)}, u32[]{:S(2)}, u32[]{:S(2)}) collective-permute-start(bf16[256,768]{1,0:T(8,128)(2,1)} %shard_map.55), channel_id=1, source_target_pairs={{0,6},{2,4},{4,2},{6,0},{8,14},{10,12},{12,10},{14,8},{16,22},{18,... | collective-permute-start | bytes 1179656 | tf_op jit(solution)/shard_map/ppermute | solution.py:317
  15.3 17.9 %collective-permute-start.6 = (bf16[256,768]{1,0:T(8,128)(2,1)S(1)}, bf16[256,768]{1,0:T(8,128)(2,1)S(1)}, u32[]{:S(2)}, u32[]{:S(2)}) collective-permute-start(bf16[256,768]{1,0:T(8,128)(2,1)S(1)} %pad_maximum_fusion.4), channel_id=1, source_target_pairs={{0,4},{2,6},{4,0},{6,2},{8,12},{10,14},{12,8},{14,10},{16,20},{18,... | collective-permute-start | bytes 1179656 | tf_op jit(solution)/shard_map/ppermute | solution.py:317
  15.9 20.7 %copy-start.13 = (s32[8]{0:T(128)S(1)}, s32[8]{0:T(128)}, u32[]{:S(2)}) copy-start(s32[8]{0:T(128)} %param.8) | copy-start | bytes 100
  15.9 17.4 %collective-permute-start.4 = (bf16[256,768]{1,0:T(8,128)(2,1)S(1)}, bf16[256,768]{1,0:T(8,128)(2,1)S(1)}, u32[]{:S(2)}, u32[]{:S(2)}) collective-permute-start(bf16[256,768]{1,0:T(8,128)(2,1)S(1)} %pad_maximum_fusion.3), channel_id=1, source_target_pairs={{0,2},{2,0},{4,6},{6,4},{8,10},{10,8},{12,14},{14,12},{16,18},{18,... | collective-permute-start | bytes 1179656 | tf_op jit(solution)/shard_map/ppermute | solution.py:317
  33.3 3.7 %copy-start.7 = (bf16[256,768]{1,0:T(8,128)(2,1)}, bf16[256,768]{1,0:T(8,128)(2,1)S(1)}, u32[]{:S(2)}) copy-start(bf16[256,768]{1,0:T(8,128)(2,1)S(1)} %collective-permute-done.4) | copy-start | bytes 1179652
  34.3 48.5 %collective-permute-start.5 = (bf16[256,4096]{1,0:T(8,128)(2,1)}, bf16[256,4096]{1,0:T(8,128)(2,1)S(1)}, u32[]{:S(2)}, u32[]{:S(2)}) collective-permute-start(bf16[256,4096]{1,0:T(8,128)(2,1)} %constant_dynamic-slice_fusion.9.refs_1_), channel_id=1, source_target_pairs={{0,2},{1,5},{2,0},{3,7},{4,6},{5,1},{6,4},{7,3},{8,10},{9,13},{10,... | collective-permute-start | bytes 6291464 | tf_op jit(solution)/shard_map/ppermute | solution.py:378
  35.9 46.9 %collective-permute-start.10 = (bf16[256,4096]{1,0:T(8,128)(2,1)}, bf16[256,4096]{1,0:T(8,128)(2,1)}, u32[]{:S(2)}, u32[]{:S(2)}) collective-permute-start(bf16[256,4096]{1,0:T(8,128)(2,1)} %constant_dynamic-slice_fusion.9.refs_1_), channel_id=1, source_target_pairs={{0,4},{1,3},{2,6},{3,1},{4,0},{5,7},{6,2},{7,5},{8,12},{9,11},{10,... | collective-permute-start | bytes 6291464 | tf_op jit(solution)/shard_map/ppermute | solution.py:378
  37.0 26.7 %copy-start.5 = (bf16[768,256]{1,0:T(8,128)(2,1)}, bf16[768,256]{1,0:T(8,128)(2,1)S(1)}, u32[]{:S(2)}) copy-start(bf16[768,256]{1,0:T(8,128)(2,1)S(1)} %pad_maximum_fusion.6.refs_1_) | copy-start | bytes 1179652
  37.0 15.9 %collective-permute-start.8 = (bf16[768,256]{1,0:T(8,128)(2,1)S(1)}, bf16[768,256]{1,0:T(8,128)(2,1)S(1)}, u32[]{:S(2)}, u32[]{:S(2)}) collective-permute-start(bf16[768,256]{1,0:T(8,128)(2,1)S(1)} %pad_maximum_fusion.6.refs_1_), channel_id=1, source_target_pairs={{0,8},{2,10},{4,12},{6,14},{8,16},{10,18},{12,20},{14,22},{16,24},... | collective-permute-start | bytes 1179656 | tf_op jit(solution)/shard_map/ppermute | solution.py:324
  52.9 14.5 %copy-start.8 = (bf16[768,256]{1,0:T(8,128)(2,1)}, bf16[768,256]{1,0:T(8,128)(2,1)S(1)}, u32[]{:S(2)}) copy-start(bf16[768,256]{1,0:T(8,128)(2,1)S(1)} %collective-permute-done.8.refs_2_) | copy-start | bytes 1179652
  52.9 10.8 %collective-permute-start.9 = (bf16[768,256]{1,0:T(8,128)(2,1)S(1)}, bf16[768,256]{1,0:T(8,128)(2,1)S(1)}, u32[]{:S(2)}, u32[]{:S(2)}) collective-permute-start(bf16[768,256]{1,0:T(8,128)(2,1)S(1)} %collective-permute-done.8.refs_2_), channel_id=1, source_target_pairs={{0,8},{2,10},{4,12},{6,14},{8,16},{10,18},{12,20},{14,22},{16,24},... | collective-permute-start | bytes 1179656 | tf_op jit(solution)/shard_map/ppermute | solution.py:324
  63.7 8.5 %copy-start.4 = (bf16[768,256]{1,0:T(8,128)(2,1)}, bf16[768,256]{1,0:T(8,128)(2,1)S(1)}, u32[]{:S(2)}) copy-start(bf16[768,256]{1,0:T(8,128)(2,1)S(1)} %collective-permute-done.9.refs_1_.refs_3_) | copy-start | bytes 1179652
  63.7 52.6 %collective-permute-start.11 = (bf16[768,256]{1,0:T(8,128)(2,1)S(1)}, bf16[768,256]{1,0:T(8,128)(2,1)}, u32[]{:S(2)}, u32[]{:S(2)}) collective-permute-start(bf16[768,256]{1,0:T(8,128)(2,1)S(1)} %collective-permute-done.9.refs_1_.refs_3_), channel_id=1, source_target_pairs={{0,8},{2,10},{4,12},{6,14},{8,16},{10,18},{12,20},{14,22},{16,24},... | collective-permute-start | bytes 1179656 | tf_op jit(solution)/shard_map/ppermute | solution.py:324
  67.5 2.2 %copy-start = (bf16[512,4096]{1,0:T(8,128)(2,1)S(1)}, bf16[512,4096]{1,0:T(8,128)(2,1)}, u32[]{:S(2)}) copy-start(bf16[512,4096]{1,0:T(8,128)(2,1)} %refs_0_.1) | copy-start | bytes 12582916
  69.7 2.5 %copy-start.11 = (s32[1,8]{1,0:T(1,128)S(1)}, s32[1,8]{1,0:T(1,128)}, u32[]{:S(2)}) copy-start(s32[1,8]{1,0:T(1,128)} %iota_multiply_fusion) | copy-start | bytes 100
  69.7 3.1 %copy-start.1 = (f32[2048,64]{1,0:T(8,128)S(1)}, f32[2048,64]{1,0:T(8,128)}, u32[]{:S(2)}) copy-start(f32[2048,64]{1,0:T(8,128)} %get-tuple-element.35) | copy-start | bytes 1572868
  69.7 3.1 %copy-start.2 = (f32[2048,64]{1,0:T(8,128)S(1)}, f32[2048,64]{1,0:T(8,128)}, u32[]{:S(2)}) copy-start(f32[2048,64]{1,0:T(8,128)} %get-tuple-element.36) | copy-start | bytes 1572868
  82.8 7.3 %collective-permute-start.1 = (bf16[256,4096]{1,0:T(8,128)(2,1)S(1)}, bf16[256,4096]{1,0:T(8,128)(2,1)S(1)}, u32[]{:S(2)}, u32[]{:S(2)}) collective-permute-start(bf16[256,4096]{1,0:T(8,128)(2,1)S(1)} %get-tuple-element.17.refs_0_), channel_id=1, source_target_pairs={{0,1},{1,0},{2,3},{3,2},{4,5},{5,4},{6,7},{7,6},{8,9},{9,8},{10,11... | collective-permute-start | bytes 6291464 | tf_op jit(solution)/shard_map/cond/branch_1_fun/ppermute | solution.py:381
  83.3 7.0 %collective-permute-start.2 = (bf16[256,4096]{1,0:T(8,128)(2,1)}, bf16[256,4096]{1,0:T(8,128)(2,1)S(1)}, u32[]{:S(2)}, u32[]{:S(2)}) collective-permute-start(bf16[256,4096]{1,0:T(8,128)(2,1)} %get-tuple-element.18.refs_2_), channel_id=1, source_target_pairs={{0,1},{1,0},{2,3},{3,2},{4,5},{5,4},{6,7},{7,6},{8,9},{9,8},{10,11... | collective-permute-start | bytes 6291464 | tf_op jit(solution)/shard_map/cond/branch_1_fun/ppermute | solution.py:381
  83.3 26.0 %collective-permute-start = (bf16[256,4096]{1,0:T(8,128)(2,1)S(1)}, bf16[256,4096]{1,0:T(8,128)(2,1)S(1)}, u32[]{:S(2)}, u32[]{:S(2)}) collective-permute-start(bf16[256,4096]{1,0:T(8,128)(2,1)S(1)} %get-tuple-element.17.refs_0_), channel_id=1, source_target_pairs={{0,4},{1,3},{2,6},{3,1},{4,0},{5,7},{6,2},{7,5},{8,12},{9,11},{10,... | collective-permute-start | bytes 6291464 | tf_op jit(solution)/shard_map/cond/branch_1_fun/ppermute | solution.py:378
  109.5 4.2 %collective-permute-start.3 = (bf16[256,4096]{1,0:T(8,128)(2,1)S(1)}, bf16[256,4096]{1,0:T(8,128)(2,1)S(1)}, u32[]{:S(2)}, u32[]{:S(2)}) collective-permute-start(bf16[256,4096]{1,0:T(8,128)(2,1)S(1)} %branch_1_fun.4.refs_0_), channel_id=1, source_target_pairs={{0,1},{1,0},{2,3},{3,2},{4,5},{5,4},{6,7},{7,6},{8,9},{9,8},{10,11... | collective-permute-start | bytes 6291464 | tf_op jit(solution)/shard_map/cond/branch_1_fun/ppermute | solution.py:381
  128.7 21.5 %collective-permute-start.12 = (bf16[1536,256]{1,0:T(8,128)(2,1)S(1)}, bf16[1536,256]{1,0:T(8,128)(2,1)S(1)}, u32[]{:S(2)}, u32[]{:S(2)}) collective-permute-start(bf16[1536,256]{1,0:T(8,128)(2,1)S(1)} %slice.50), channel_id=1, source_target_pairs={{0,8},{2,10},{4,12},{6,14},{8,16},{10,18},{12,20},{14,22},{16,24},... | collective-permute-start | bytes 2359304 | tf_op jit(solution)/shard_map/ppermute | solution.py:439
  150.2 0.9 copy-start.12
  157.5 27.1 %collective-permute-start.13 = (bf16[512,512]{1,0:T(8,128)(2,1)}, bf16[512,512]{1,0:T(8,128)(2,1)S(1)}, u32[]{:S(2)}, u32[]{:S(2)}) collective-permute-start(bf16[512,512]{1,0:T(8,128)(2,1)} %shard_map.60), channel_id=1, source_target_pairs={{0,6},{2,4},{4,2},{6,0},{8,14},{10,12},{12,10},{14,8},{16,22},{18,... | collective-permute-start | bytes 1572872 | tf_op jit(solution)/shard_map/ppermute | solution.py:317
  169.0 15.9 %collective-permute-start.14 = (bf16[512,512]{1,0:T(8,128)(2,1)}, bf16[512,512]{1,0:T(8,128)(2,1)S(1)}, u32[]{:S(2)}, u32[]{:S(2)}) collective-permute-start(bf16[512,512]{1,0:T(8,128)(2,1)} %shard_map.61), channel_id=1, source_target_pairs={{0,4},{2,6},{4,0},{6,2},{8,12},{10,14},{12,8},{14,10},{16,20},{18,... | collective-permute-start | bytes 1572872 | tf_op jit(solution)/shard_map/ppermute | solution.py:317
  178.1 12.8 %collective-permute-start.15 = (bf16[512,512]{1,0:T(8,128)(2,1)}, bf16[512,512]{1,0:T(8,128)(2,1)S(1)}, u32[]{:S(2)}, u32[]{:S(2)}) collective-permute-start(bf16[512,512]{1,0:T(8,128)(2,1)} %shard_map.62), channel_id=1, source_target_pairs={{0,2},{2,0},{4,6},{6,4},{8,10},{10,8},{12,14},{14,12},{16,18},{18,... | collective-permute-start | bytes 1572872 | tf_op jit(solution)/shard_map/ppermute | solution.py:317
  184.8 7.5 %copy-start.6 = (bf16[512,512]{1,0:T(8,128)(2,1)S(1)}, bf16[512,512]{1,0:T(8,128)(2,1)}, u32[]{:S(2)}) copy-start(bf16[512,512]{1,0:T(8,128)(2,1)} %shard_map.63) | copy-start | bytes 1572868
  191.0 1.3 copy-start.3
Sparse Core Ops, SparseCore 0:
  9.0 43.7 all-gather.2
  54.3 71.9 all-gather.4

commit v9 on v7

--- a/solution.py
+++ b/solution.py
@@ -186,15 +186,19 @@
         for kv_head in range(kv_heads):
             keys = k_all[rows, kv_head * HEAD_DIM : (kv_head + 1) * HEAD_DIM]
             values = v_all[rows, kv_head * wide : (kv_head + 1) * wide]
-            members = slice(kv_head * share * tile, (kv_head + 1) * share * tile)
-            raw = lax.dot_general(
-                q_all[members, :], keys, (((1,), (1,)), ((), ())), preferred_element_type=jnp.float32
-            )
-            weights = jnp.exp2(outer * jnp.tanh(raw * inner))
-            if masked:
-                weights = weights.reshape(share, tile, size)
-                weights = jnp.where(allowed[None], weights, 0.0).reshape(share * tile, size)
-            sums[members, :] += jnp.dot(weights.astype(jnp.bfloat16), values, preferred_element_type=jnp.float32)
+            pairs = 2 if share % 2 == 0 else 1
+            count = share // pairs
+            for pair in range(pairs):
+                at = (kv_head * share + pair * count) * tile
+                members = slice(at, at + count * tile)
+                raw = lax.dot_general(
+                    q_all[members, :], keys, (((1,), (1,)), ((), ())), preferred_element_type=jnp.float32
+                )
+                weights = jnp.exp2(outer * jnp.tanh(raw * inner))
+                if masked:
+                    weights = weights.reshape(count, tile, size)
+                    weights = jnp.where(allowed[None], weights, 0.0).reshape(count * tile, size)
+                sums[members, :] += jnp.dot(weights.astype(jnp.bfloat16), values, preferred_element_type=jnp.float32)
 
     def either(begin, size):
         whole = (begin >= last_start) & (begin + size - 1 <= q_first)

time: 202 us -> 202 us (level)
  waiting for transfers between devices: 70.8 us -> 66.7 us
  starting transfers between devices: 21.4 us -> 25.2 us
    ppermute x6, waiting for transfers between devices: 22 us -> 17.8 us  [to_partner(): return lax.ppermute(block, 'ca', [(i, i ^ step) for i in devices])]
    ppermute x6, starting transfers between devices: 8.04 us -> 11.9 us  [to_partner(): return lax.ppermute(block, 'ca', [(i, i ^ step) for i in devices])]
    pallas_call x4, Pallas kernels: 28.7 us -> 30.7 us  [attend(): pl.pallas_call(kernel, out_shape=jax.ShapeDtypeStruct((chunk_rows, width)...]
where the time goes in v9:
time: 202 us; the launch traced here: 200 us
  Pallas kernels  71.5 us (35%)
  waiting for transfers between devices  66.7 us (33%)
  starting transfers between devices  25.2 us (12%)
  between operations  14.9 us (7%)
  other arithmetic  11.6 us (6%)
  local copies, waits for them, and re-layouts  9.84 us (5%)
    pallas_call x4, Pallas kernels, attend(): pl.pallas_call(kernel, out_shape=jax.ShapeDtypeStruct((chunk_rows, width)...  30.7 us
    pallas_call x2, Pallas kernels, project(): pl.pallas_call(functools.partial(project_kernel, rope_heads, layout, len(...  26.8 us
    ppermute x3, waiting for transfers between devices, cross(): return lax.ppermute(block, both, pairs)  20.9 us
    ppermute x6, waiting for transfers between devices, to_partner(): return lax.ppermute(block, 'ca', [(i, i ^ step) for i in devices])  17.8 us
    ppermute x3, waiting for transfers between devices, forwarded(): lax.ppermute(block, 'ca', [(i, (i + group) % (group * lines)) for i in de...  15.3 us
    ppermute x6, starting transfers between devices, to_partner(): return lax.ppermute(block, 'ca', [(i, i ^ step) for i in devices])  11.9 us
    ppermute x3, waiting for transfers between devices, swap(): lax.ppermute(block, both, [(i * 2 + c, i * 2 + 1 - c) for i in devices fo...  10.5 us
    pallas_call x3, Pallas kernels, put(): pl.pallas_call(functools.partial(put_kernel, targets), out_shape=jax.Shap...  9.99 us
  transfers between devices with their start and end apart: 18, of which 11 were waited for; matrix products, arithmetic and copies ran while one was open for 7% of the time, Pallas kernels for 32%

profile of v9, /device:TPU:16, one launch (start us, length us, event | category | flops | bytes accessed | tf_op | source)
XLA Modules:
  0.0 199.8 jit_solution(6174672888648092368)
XLA Ops:
  8.9 1.6 collective-permute-start.6
  10.5 1.5 collective-permute-start.7
  12.7 15.6 %collective-permute-done.6 = bf16[256,768]{1,0:T(8,128)(2,1)S(1)} collective-permute-done((bf16[256,768]{1,0:T(8,128)(2,1)S(1)}, bf16[256,768]{1,0:T(8,128)(2,1)S(1)}, u32[]{:S(2)}, u32[]{:S(2)}) %collective-permute-start.6) | collective-permute-done | bytes 393248 | tf_op jit(solution)/shard_map/ppermute | solution.py:338
  30.7 3.8 %shard_map.55 = bf16[256,4096]{1,0:T(8,128)(2,1)} custom-call(s32[1]{0:T(128)} %bitcast.5.which, bf16[512,4096]{1,0:T(8,128)(2,1)} %refs_0_.1), custom_call_target="tpu_custom_call" | custom-call | tf_op jit(solution)/shard_map/pallas_call | solution.py:291
  36.0 1.5 collective-permute-start.10
  37.9 1.6 collective-permute-start.8
  40.9 12.0 %collective-permute-done.8.refs_2_ = bf16[768,256]{1,0:T(8,128)(2,1)S(1)} collective-permute-done((bf16[768,256]{1,0:T(8,128)(2,1)S(1)}, bf16[768,256]{1,0:T(8,128)(2,1)S(1)}, u32[]{:S(2)}, u32[]{:S(2)}) %collective-permute-start.8) | collective-permute-done | bytes 393248 | tf_op jit(solution)/shard_map/ppermute | solution.py:345
  52.9 1.7 collective-permute-start.9
  54.6 5.6 %fusion = (f32[2048,64]{1,0:T(8,128)S(1)}, f32[2048,64]{1,0:T(8,128)}, f32[2048,64]{1,0:T(8,128)}) fusion(f32[64]{0:T(128)S(1)} %multiply_power_fusion, f32[2048]{0:T(1024)S(1)} %get-tuple-element.37), kind=kLoop, calls=%fused_computation.10 | loop fusion | flops 262144 | bytes 1581312 | tf_op jit(solution)/shard_map/neg | solution.py:35
  60.2 3.2 %collective-permute-done.9.refs_1_.refs_3_ = bf16[768,256]{1,0:T(8,128)(2,1)S(1)} collective-permute-done((bf16[768,256]{1,0:T(8,128)(2,1)S(1)}, bf16[768,256]{1,0:T(8,128)(2,1)S(1)}, u32[]{:S(2)}, u32[]{:S(2)}) %collective-permute-start.9) | collective-permute-done | bytes 393248 | tf_op jit(solution)/shard_map/ppermute | solution.py:345
  63.5 2.2 %collective-permute-start.11 = (bf16[768,256]{1,0:T(8,128)(2,1)S(1)}, bf16[768,256]{1,0:T(8,128)(2,1)}, u32[]{:S(2)}, u32[]{:S(2)}) collective-permute-start(bf16[768,256]{1,0:T(8,128)(2,1)S(1)} %collective-permute-done.9.refs_1_.refs_3_), channel_id=1, source_target_pairs={{0,8},{2,10},{4,12},{6,14},{8,16},{10,18},{12,20},{14,22},{16,24},... | collective-permute-start | bytes 1179656 | tf_op jit(solution)/shard_map/ppermute | solution.py:345
  65.8 2.2 %copy-done = bf16[512,4096]{1,0:T(8,128)(2,1)S(1)} copy-done((bf16[512,4096]{1,0:T(8,128)(2,1)S(1)}, bf16[512,4096]{1,0:T(8,128)(2,1)}, u32[]{:S(2)}) %copy-start) | copy-done | bytes 4194328
  67.9 2.5 %shard_map.57 = bf16[2048,4096]{1,0:T(8,128)(2,1)} custom-call(s32[3]{0:T(128)S(1)} %pad_add_fusion.1.place, bf16[512,4096]{1,0:T(8,128)(2,1)S(1)} %copy-done), custom_call_target="tpu_custom_call" | custom-call | bytes 8388608 | tf_op jit(solution)/shard_map/pallas_call | solution.py:122
  71.1 2.0 %pad_maximum_fusion = (f32[2048,128]{1,0:T(8,128)}, f32[2048,128]{1,0:T(8,128)}) fusion(f32[2048,64]{1,0:T(8,128)S(1)} %copy-done.2, f32[2048,64]{1,0:T(8,128)S(1)} %copy-done.1, f32[2048,64]{1,0:T(8,128)S(1)} %get-tuple-element.34), kind=kLoop, calls=%fused_computation.2 | loop fusion | flops 524288 | bytes 3670016 | tf_op jit(solution)/shard_map/concatenate | solution.py:35
  75.6 6.7 %collective-permute-done.5.refs_0_ = bf16[256,4096]{1,0:T(8,128)(2,1)S(1)} collective-permute-done((bf16[256,4096]{1,0:T(8,128)(2,1)}, bf16[256,4096]{1,0:T(8,128)(2,1)S(1)}, u32[]{:S(2)}, u32[]{:S(2)}) %collective-permute-start.5) | collective-permute-done | bytes 2097184 | tf_op jit(solution)/shard_map/ppermute | solution.py:396
  82.3 33.4 %conditional.1 = (bf16[2048,4096]{1,0:T(8,128)(2,1)}) conditional(s32[]{:T(128)} %bitcast.6, () %tuple.11, (bf16[256,4096]{1,0:T(8,128)(2,1)S(1)}, bf16[256,4096]{1,0:T(8,128)(2,1)}, s32[3]{0:T(128)S(1)}, bf16[2048,4096]{1,0:T(8,128)(2,1)}) %tuple.12), branch_computations={%region_2.3_spmd, %region_3.4_spmd} | conditional | bytes 58720424 | solution.py:436
  83.3 5.4 %collective-permute-done.1.refs_1_ = bf16[256,4096]{1,0:T(8,128)(2,1)S(1)} collective-permute-done((bf16[256,4096]{1,0:T(8,128)(2,1)S(1)}, bf16[256,4096]{1,0:T(8,128)(2,1)S(1)}, u32[]{:S(2)}, u32[]{:S(2)}) %collective-permute-start.1) | collective-permute-done | bytes 2097184 | tf_op jit(solution)/shard_map/cond/branch_1_fun/ppermute | solution.py:399
  89.6 5.0 %branch_1_fun.3.other_ref.refs_2_ = bf16[2048,4096]{1,0:T(8,128)(2,1)} custom-call(s32[3]{0:T(128)S(1)} %get-tuple-element.16.place, bf16[256,4096]{1,0:T(8,128)(2,1)S(1)} %get-tuple-element.17.refs_0_, bf16[256,4096]{1,0:T(8,128)(2,1)S(1)} %collective-permute-done.1.refs_1_, ...), custom_call_target="tpu_custom_call", output_to_operand_aliasing={{}: (5, {})} | custom-call | bytes 16777216 | tf_op jit(solution)/shard_map/cond/branch_1_fun/pallas_call | solution.py:122
  94.6 14.2 %collective-permute-done.block_ref = bf16[256,4096]{1,0:T(8,128)(2,1)S(1)} collective-permute-done((bf16[256,4096]{1,0:T(8,128)(2,1)S(1)}, bf16[256,4096]{1,0:T(8,128)(2,1)S(1)}, u32[]{:S(2)}, u32[]{:S(2)}) %collective-permute-start) | collective-permute-done | bytes 2097184 | tf_op jit(solution)/shard_map/cond/branch_1_fun/ppermute | solution.py:396
  109.0 4.1 %collective-permute-done.3.refs_1_ = bf16[256,4096]{1,0:T(8,128)(2,1)S(1)} collective-permute-done((bf16[256,4096]{1,0:T(8,128)(2,1)S(1)}, bf16[256,4096]{1,0:T(8,128)(2,1)S(1)}, u32[]{:S(2)}, u32[]{:S(2)}) %collective-permute-start.3) | collective-permute-done | bytes 2097184 | tf_op jit(solution)/shard_map/cond/branch_1_fun/ppermute | solution.py:399
  113.2 2.5 %branch_1_fun.5 = bf16[2048,4096]{1,0:T(8,128)(2,1)} custom-call(s32[3]{0:T(128)S(1)} %get-tuple-element.16.place, bf16[256,4096]{1,0:T(8,128)(2,1)S(1)} %branch_1_fun.4.refs_0_, bf16[256,4096]{1,0:T(8,128)(2,1)S(1)} %collective-permute-done.3.refs_1_, bf16[2048,4096]{1,0:T(8,128)(2,1)} %branch_1_fun.3.other_ref.refs_2_), custom_call_target="tpu_custom_call", output_to_operand_aliasing={{}: (3, {})} | custom-call | bytes 8388608 | tf_op jit(solution)/shard_map/cond/branch_1_fun/pallas_call | solution.py:122
  115.7 11.2 %shard_map.59.kv_ref = bf16[2048,256]{1,0:T(8,128)(2,1)} custom-call(s32[3]{0:T(128)S(1)} %pad_add_fusion.1.place, bf16[2048,4096]{1,0:T(8,128)(2,1)} %get-tuple-element.45.x_ref, bf16[1024,768]{1,0:T(8,128)(2,1)} %all-gather.3.cloned.1.call-done.refs_0_, bf16[768,256]{1,0:T(8,128)(2,1)} %copy-done.5, bf16[768,256]{1,0:T(8,128)(2,1)} %copy-done.8, ...), custom_call_target="tpu_custom_call" | custom-call | flops 4294967296 | bytes 18874368 | tf_op jit(solution)/shard_map/pallas_call | solution.py:79
  128.1 3.7 %collective-permute-start.12 = (bf16[1536,256]{1,0:T(8,128)(2,1)S(1)}, bf16[1536,256]{1,0:T(8,128)(2,1)S(1)}, u32[]{:S(2)}, u32[]{:S(2)}) collective-permute-start(bf16[1536,256]{1,0:T(8,128)(2,1)S(1)} %slice.50), channel_id=1, source_target_pairs={{0,8},{2,10},{4,12},{6,14},{8,16},{10,18},{12,20},{14,22},{16,24},... | collective-permute-start | bytes 2359304 | tf_op jit(solution)/shard_map/ppermute | solution.py:459
  131.8 15.6 %shard_map.58.q_ref = bf16[2048,512]{1,0:T(8,128)(2,1)} custom-call(s32[3]{0:T(128)S(1)} %pad_add_fusion.1.place, bf16[2048,4096]{1,0:T(8,128)(2,1)} %get-tuple-element.45.x_ref, bf16[1024,768]{1,0:T(8,128)(2,1)} %all-gather.3.cloned.1.call-done.refs_0_, bf16[3072,512]{1,0:T(8,128)(2,1)} %all-gather.5.cloned.1.call-done.refs_1_, ...), custom_call_target="tpu_custom_call" | custom-call | flops 8589934592 | bytes 20971520 | tf_op jit(solution)/shard_map/pallas_call | solution.py:79
  147.5 2.2 %collective-permute-done.12.halo_ref = bf16[1536,256]{1,0:T(8,128)(2,1)S(1)} collective-permute-done((bf16[1536,256]{1,0:T(8,128)(2,1)S(1)}, bf16[1536,256]{1,0:T(8,128)(2,1)S(1)}, u32[]{:S(2)}, u32[]{:S(2)}) %collective-permute-start.12) | collective-permute-done | bytes 786464 | tf_op jit(solution)/shard_map/ppermute | solution.py:459
  150.5 7.0 %shard_map.60 = bf16[512,512]{1,0:T(8,128)(2,1)} custom-call(s32[1]{0:T(128)} %bitcast.first, s32[3,8]{1,0:T(4,128)} %pad_add_fusion.refs_5_.bounds, s32[8]{0:T(128)} %broadcast_subtract_fusion.1.refs_4_.ends, bf16[2048,512]{1,0:T(8,128)(2,1)} %shard_map.58.q_ref, bf16[1536,256]{1,0:T(8,128)(2,1)} %copy-done.12, bf16[2048,256]{1,0:T(8,128)(2,1)} %shard_map.59.kv_ref), custom_call_target="tpu_custom_call" | custom-call | flops 1073741824 | bytes 1048576 | tf_op jit(solution)/shard_map/pallas_call | solution.py:243
  157.6 4.4 %collective-permute-start.13 = (bf16[512,512]{1,0:T(8,128)(2,1)}, bf16[512,512]{1,0:T(8,128)(2,1)S(1)}, u32[]{:S(2)}, u32[]{:S(2)}) collective-permute-start(bf16[512,512]{1,0:T(8,128)(2,1)} %shard_map.60), channel_id=1, source_target_pairs={{0,6},{2,4},{4,2},{6,0},{8,14},{10,12},{12,10},{14,8},{16,22},{18,... | collective-permute-start | bytes 1572872 | tf_op jit(solution)/shard_map/ppermute | solution.py:338
  162.0 6.9 %shard_map.61 = bf16[512,512]{1,0:T(8,128)(2,1)} custom-call(s32[1]{0:T(128)} %bitcast.7.first, s32[3,8]{1,0:T(4,128)} %pad_add_fusion.refs_5_.bounds, s32[8]{0:T(128)} %broadcast_subtract_fusion.1.refs_4_.ends, bf16[2048,512]{1,0:T(8,128)(2,1)} %shard_map.58.q_ref, bf16[1536,256]{1,0:T(8,128)(2,1)} %copy-done.12, bf16[2048,256]{1,0:T(8,128)(2,1)} %shard_map.59.kv_ref), custom_call_target="tpu_custom_call" | custom-call | flops 1073741824 | bytes 1048576 | tf_op jit(solution)/shard_map/pallas_call | solution.py:243
  168.8 1.5 collective-permute-start.14
  170.4 6.8 %shard_map.62 = bf16[512,512]{1,0:T(8,128)(2,1)} custom-call(s32[1]{0:T(128)} %bitcast.8.first, s32[3,8]{1,0:T(4,128)} %pad_add_fusion.refs_5_.bounds, s32[8]{0:T(128)} %broadcast_subtract_fusion.1.refs_4_.ends, bf16[2048,512]{1,0:T(8,128)(2,1)} %shard_map.58.q_ref, bf16[1536,256]{1,0:T(8,128)(2,1)} %copy-done.12, bf16[2048,256]{1,0:T(8,128)(2,1)} %shard_map.59.kv_ref), custom_call_target="tpu_custom_call" | custom-call | flops 1073741824 | bytes 1048576 | tf_op jit(solution)/shard_map/pallas_call | solution.py:243
  177.2 2.2 %collective-permute-start.15 = (bf16[512,512]{1,0:T(8,128)(2,1)}, bf16[512,512]{1,0:T(8,128)(2,1)S(1)}, u32[]{:S(2)}, u32[]{:S(2)}) collective-permute-start(bf16[512,512]{1,0:T(8,128)(2,1)} %shard_map.62), channel_id=1, source_target_pairs={{0,2},{2,0},{4,6},{6,4},{8,10},{10,8},{12,14},{14,12},{16,18},{18,... | collective-permute-start | bytes 1572872 | tf_op jit(solution)/shard_map/ppermute | solution.py:338
  179.4 10.0 %shard_map.63 = bf16[512,512]{1,0:T(8,128)(2,1)} custom-call(s32[1]{0:T(128)} %bitcast.9.first, s32[3,8]{1,0:T(4,128)} %pad_add_fusion.refs_5_.bounds, s32[8]{0:T(128)} %broadcast_subtract_fusion.1.refs_4_.ends, bf16[2048,512]{1,0:T(8,128)(2,1)} %shard_map.58.q_ref, bf16[1536,256]{1,0:T(8,128)(2,1)} %copy-done.12, bf16[2048,256]{1,0:T(8,128)(2,1)} %shard_map.59.kv_ref), custom_call_target="tpu_custom_call" | custom-call | flops 1073741824 | bytes 1048576 | tf_op jit(solution)/shard_map/pallas_call | solution.py:243
  (81 shorter events, 18.3 us)
Async XLA Ops:
  6.5 1.4 copy-start.10
  6.5 1.4 copy-start.9
  6.5 109.2 %all-gather.3.cloned.1.call-start = ((), (), s32[]{:S(2)}) async-start(), calls=%async_computation | async-start | bytes 1966080 | tf_op jit(solution)/shard_map/all_gather | solution.py:342
  8.8 123.0 %all-gather.5.cloned.1.call-start = ((), (), s32[]{:S(2)}) async-start(), calls=%async_computation.1 | async-start | bytes 3932160 | tf_op jit(solution)/shard_map/all_gather | solution.py:342
  8.9 19.3 %collective-permute-start.6 = (bf16[256,768]{1,0:T(8,128)(2,1)S(1)}, bf16[256,768]{1,0:T(8,128)(2,1)S(1)}, u32[]{:S(2)}, u32[]{:S(2)}) collective-permute-start(bf16[256,768]{1,0:T(8,128)(2,1)S(1)} %pad_maximum_fusion.4), channel_id=1, source_target_pairs={{0,4},{2,6},{4,0},{6,2},{8,12},{10,14},{12,8},{14,10},{16,20},{18,... | collective-permute-start | bytes 1179656 | tf_op jit(solution)/shard_map/ppermute | solution.py:338
  10.5 17.8 %collective-permute-start.7 = (bf16[256,768]{1,0:T(8,128)(2,1)S(1)}, bf16[256,768]{1,0:T(8,128)(2,1)S(1)}, u32[]{:S(2)}, u32[]{:S(2)}) collective-permute-start(bf16[256,768]{1,0:T(8,128)(2,1)S(1)} %pad_maximum_fusion.5), channel_id=1, source_target_pairs={{0,6},{2,4},{4,2},{6,0},{8,14},{10,12},{12,10},{14,8},{16,22},{18,... | collective-permute-start | bytes 1179656 | tf_op jit(solution)/shard_map/ppermute | solution.py:338
  12.1 17.5 %collective-permute-start.4 = (bf16[256,768]{1,0:T(8,128)(2,1)S(1)}, bf16[256,768]{1,0:T(8,128)(2,1)S(1)}, u32[]{:S(2)}, u32[]{:S(2)}) collective-permute-start(bf16[256,768]{1,0:T(8,128)(2,1)S(1)} %pad_maximum_fusion.3), channel_id=1, source_target_pairs={{0,2},{2,0},{4,6},{6,4},{8,10},{10,8},{12,14},{14,12},{16,18},{18,... | collective-permute-start | bytes 1179656 | tf_op jit(solution)/shard_map/ppermute | solution.py:338
  29.6 8.2 %copy-start.7 = (bf16[256,768]{1,0:T(8,128)(2,1)}, bf16[256,768]{1,0:T(8,128)(2,1)S(1)}, u32[]{:S(2)}) copy-start(bf16[256,768]{1,0:T(8,128)(2,1)S(1)} %collective-permute-done.4) | copy-start | bytes 1179652
  30.7 6.8 %copy-start.13 = (s32[8]{0:T(128)S(1)}, s32[8]{0:T(128)}, u32[]{:S(2)}) copy-start(s32[8]{0:T(128)} %param.8) | copy-start | bytes 100
  34.5 47.8 %collective-permute-start.5 = (bf16[256,4096]{1,0:T(8,128)(2,1)}, bf16[256,4096]{1,0:T(8,128)(2,1)S(1)}, u32[]{:S(2)}, u32[]{:S(2)}) collective-permute-start(bf16[256,4096]{1,0:T(8,128)(2,1)} %shard_map.55), channel_id=1, source_target_pairs={{0,2},{1,5},{2,0},{3,7},{4,6},{5,1},{6,4},{7,3},{8,10},{9,13},{10,... | collective-permute-start | bytes 6291464 | tf_op jit(solution)/shard_map/ppermute | solution.py:396
  36.0 46.3 %collective-permute-start.10 = (bf16[256,4096]{1,0:T(8,128)(2,1)}, bf16[256,4096]{1,0:T(8,128)(2,1)}, u32[]{:S(2)}, u32[]{:S(2)}) collective-permute-start(bf16[256,4096]{1,0:T(8,128)(2,1)} %shard_map.55), channel_id=1, source_target_pairs={{0,4},{1,3},{2,6},{3,1},{4,0},{5,7},{6,2},{7,5},{8,12},{9,11},{10,... | collective-permute-start | bytes 6291464 | tf_op jit(solution)/shard_map/ppermute | solution.py:396
  37.9 25.6 %copy-start.5 = (bf16[768,256]{1,0:T(8,128)(2,1)}, bf16[768,256]{1,0:T(8,128)(2,1)S(1)}, u32[]{:S(2)}) copy-start(bf16[768,256]{1,0:T(8,128)(2,1)S(1)} %pad_maximum_fusion.6.refs_1_) | copy-start | bytes 1179652
  37.9 15.0 %collective-permute-start.8 = (bf16[768,256]{1,0:T(8,128)(2,1)S(1)}, bf16[768,256]{1,0:T(8,128)(2,1)S(1)}, u32[]{:S(2)}, u32[]{:S(2)}) collective-permute-start(bf16[768,256]{1,0:T(8,128)(2,1)S(1)} %pad_maximum_fusion.6.refs_1_), channel_id=1, source_target_pairs={{0,8},{2,10},{4,12},{6,14},{8,16},{10,18},{12,20},{14,22},{16,24},... | collective-permute-start | bytes 1179656 | tf_op jit(solution)/shard_map/ppermute | solution.py:345
  52.9 12.8 %copy-start.8 = (bf16[768,256]{1,0:T(8,128)(2,1)}, bf16[768,256]{1,0:T(8,128)(2,1)S(1)}, u32[]{:S(2)}) copy-start(bf16[768,256]{1,0:T(8,128)(2,1)S(1)} %collective-permute-done.8.refs_2_) | copy-start | bytes 1179652
  52.9 10.6 %collective-permute-start.9 = (bf16[768,256]{1,0:T(8,128)(2,1)S(1)}, bf16[768,256]{1,0:T(8,128)(2,1)S(1)}, u32[]{:S(2)}, u32[]{:S(2)}) collective-permute-start(bf16[768,256]{1,0:T(8,128)(2,1)S(1)} %collective-permute-done.8.refs_2_), channel_id=1, source_target_pairs={{0,8},{2,10},{4,12},{6,14},{8,16},{10,18},{12,20},{14,22},{16,24},... | collective-permute-start | bytes 1179656 | tf_op jit(solution)/shard_map/ppermute | solution.py:345
  63.5 7.0 %copy-start.4 = (bf16[768,256]{1,0:T(8,128)(2,1)}, bf16[768,256]{1,0:T(8,128)(2,1)S(1)}, u32[]{:S(2)}) copy-start(bf16[768,256]{1,0:T(8,128)(2,1)S(1)} %collective-permute-done.9.refs_1_.refs_3_) | copy-start | bytes 1179652
  63.5 52.2 %collective-permute-start.11 = (bf16[768,256]{1,0:T(8,128)(2,1)S(1)}, bf16[768,256]{1,0:T(8,128)(2,1)}, u32[]{:S(2)}, u32[]{:S(2)}) collective-permute-start(bf16[768,256]{1,0:T(8,128)(2,1)S(1)} %collective-permute-done.9.refs_1_.refs_3_), channel_id=1, source_target_pairs={{0,8},{2,10},{4,12},{6,14},{8,16},{10,18},{12,20},{14,22},{16,24},... | collective-permute-start | bytes 1179656 | tf_op jit(solution)/shard_map/ppermute | solution.py:345
  65.8 2.2 %copy-start = (bf16[512,4096]{1,0:T(8,128)(2,1)S(1)}, bf16[512,4096]{1,0:T(8,128)(2,1)}, u32[]{:S(2)}) copy-start(bf16[512,4096]{1,0:T(8,128)(2,1)} %refs_0_.1) | copy-start | bytes 12582916
  67.9 2.5 %copy-start.11 = (s32[1,8]{1,0:T(1,128)S(1)}, s32[1,8]{1,0:T(1,128)}, u32[]{:S(2)}) copy-start(s32[1,8]{1,0:T(1,128)} %iota_multiply_fusion) | copy-start | bytes 100
  67.9 3.1 %copy-start.1 = (f32[2048,64]{1,0:T(8,128)S(1)}, f32[2048,64]{1,0:T(8,128)}, u32[]{:S(2)}) copy-start(f32[2048,64]{1,0:T(8,128)} %get-tuple-element.35) | copy-start | bytes 1572868
  67.9 3.1 %copy-start.2 = (f32[2048,64]{1,0:T(8,128)S(1)}, f32[2048,64]{1,0:T(8,128)}, u32[]{:S(2)}) copy-start(f32[2048,64]{1,0:T(8,128)} %get-tuple-element.36) | copy-start | bytes 1572868
  82.3 6.4 %collective-permute-start.1 = (bf16[256,4096]{1,0:T(8,128)(2,1)S(1)}, bf16[256,4096]{1,0:T(8,128)(2,1)S(1)}, u32[]{:S(2)}, u32[]{:S(2)}) collective-permute-start(bf16[256,4096]{1,0:T(8,128)(2,1)S(1)} %get-tuple-element.17.refs_0_), channel_id=1, source_target_pairs={{0,1},{1,0},{2,3},{3,2},{4,5},{5,4},{6,7},{7,6},{8,9},{9,8},{10,11... | collective-permute-start | bytes 6291464 | tf_op jit(solution)/shard_map/cond/branch_1_fun/ppermute | solution.py:399
  82.3 7.4 %collective-permute-start.2 = (bf16[256,4096]{1,0:T(8,128)(2,1)}, bf16[256,4096]{1,0:T(8,128)(2,1)S(1)}, u32[]{:S(2)}, u32[]{:S(2)}) collective-permute-start(bf16[256,4096]{1,0:T(8,128)(2,1)} %get-tuple-element.18.refs_2_), channel_id=1, source_target_pairs={{0,1},{1,0},{2,3},{3,2},{4,5},{5,4},{6,7},{7,6},{8,9},{9,8},{10,11... | collective-permute-start | bytes 6291464 | tf_op jit(solution)/shard_map/cond/branch_1_fun/ppermute | solution.py:399
  82.8 26.0 %collective-permute-start = (bf16[256,4096]{1,0:T(8,128)(2,1)S(1)}, bf16[256,4096]{1,0:T(8,128)(2,1)S(1)}, u32[]{:S(2)}, u32[]{:S(2)}) collective-permute-start(bf16[256,4096]{1,0:T(8,128)(2,1)S(1)} %get-tuple-element.17.refs_0_), channel_id=1, source_target_pairs={{0,4},{1,3},{2,6},{3,1},{4,0},{5,7},{6,2},{7,5},{8,12},{9,11},{10,... | collective-permute-start | bytes 6291464 | tf_op jit(solution)/shard_map/cond/branch_1_fun/ppermute | solution.py:396
  108.9 4.2 %collective-permute-start.3 = (bf16[256,4096]{1,0:T(8,128)(2,1)S(1)}, bf16[256,4096]{1,0:T(8,128)(2,1)S(1)}, u32[]{:S(2)}, u32[]{:S(2)}) collective-permute-start(bf16[256,4096]{1,0:T(8,128)(2,1)S(1)} %branch_1_fun.4.refs_0_), channel_id=1, source_target_pairs={{0,1},{1,0},{2,3},{3,2},{4,5},{5,4},{6,7},{7,6},{8,9},{9,8},{10,11... | collective-permute-start | bytes 6291464 | tf_op jit(solution)/shard_map/cond/branch_1_fun/ppermute | solution.py:399
  128.1 21.5 %collective-permute-start.12 = (bf16[1536,256]{1,0:T(8,128)(2,1)S(1)}, bf16[1536,256]{1,0:T(8,128)(2,1)S(1)}, u32[]{:S(2)}, u32[]{:S(2)}) collective-permute-start(bf16[1536,256]{1,0:T(8,128)(2,1)S(1)} %slice.50), channel_id=1, source_target_pairs={{0,8},{2,10},{4,12},{6,14},{8,16},{10,18},{12,20},{14,22},{16,24},... | collective-permute-start | bytes 2359304 | tf_op jit(solution)/shard_map/ppermute | solution.py:459
  149.6 0.9 copy-start.12
  157.6 31.9 %collective-permute-start.13 = (bf16[512,512]{1,0:T(8,128)(2,1)}, bf16[512,512]{1,0:T(8,128)(2,1)S(1)}, u32[]{:S(2)}, u32[]{:S(2)}) collective-permute-start(bf16[512,512]{1,0:T(8,128)(2,1)} %shard_map.60), channel_id=1, source_target_pairs={{0,6},{2,4},{4,2},{6,0},{8,14},{10,12},{12,10},{14,8},{16,22},{18,... | collective-permute-start | bytes 1572872 | tf_op jit(solution)/shard_map/ppermute | solution.py:338
  168.8 20.9 %collective-permute-start.14 = (bf16[512,512]{1,0:T(8,128)(2,1)}, bf16[512,512]{1,0:T(8,128)(2,1)S(1)}, u32[]{:S(2)}, u32[]{:S(2)}) collective-permute-start(bf16[512,512]{1,0:T(8,128)(2,1)} %shard_map.61), channel_id=1, source_target_pairs={{0,4},{2,6},{4,0},{6,2},{8,12},{10,14},{12,8},{14,10},{16,20},{18,... | collective-permute-start | bytes 1572872 | tf_op jit(solution)/shard_map/ppermute | solution.py:338
  177.2 13.6 %collective-permute-start.15 = (bf16[512,512]{1,0:T(8,128)(2,1)}, bf16[512,512]{1,0:T(8,128)(2,1)S(1)}, u32[]{:S(2)}, u32[]{:S(2)}) collective-permute-start(bf16[512,512]{1,0:T(8,128)(2,1)} %shard_map.62), channel_id=1, source_target_pairs={{0,2},{2,0},{4,6},{6,4},{8,10},{10,8},{12,14},{14,12},{16,18},{18,... | collective-permute-start | bytes 1572872 | tf_op jit(solution)/shard_map/ppermute | solution.py:338
  189.7 2.5 %copy-start.6 = (bf16[512,512]{1,0:T(8,128)(2,1)S(1)}, bf16[512,512]{1,0:T(8,128)(2,1)}, u32[]{:S(2)}) copy-start(bf16[512,512]{1,0:T(8,128)(2,1)} %shard_map.63) | copy-start | bytes 1572868
  190.8 1.3 copy-start.3
Sparse Core Ops, SparseCore 0:
  9.0 43.3 all-gather.2
  54.0 71.9 all-gather.4

commit v10 on v7

--- a/solution.py
+++ b/solution.py
@@ -190,7 +190,8 @@
             raw = lax.dot_general(
                 q_all[members, :], keys, (((1,), (1,)), ((), ())), preferred_element_type=jnp.float32
             )
-            weights = jnp.exp2(outer * jnp.tanh(raw * inner))
+            growth = jnp.exp2(jnp.minimum(raw * (2.0 * inner * math.log2(math.e)), 126.0))
+            weights = jnp.exp2(outer - (2.0 * outer) / (1.0 + growth))
             if masked:
                 weights = weights.reshape(share, tile, size)
                 weights = jnp.where(allowed[None], weights, 0.0).reshape(share * tile, size)

time: 202 us -> 205 us (1.015)
  Pallas kernels: 69.5 us -> 75.7 us
    pallas_call x4, Pallas kernels: 28.7 us -> 34.9 us  [attend(): pl.pallas_call(kernel, out_shape=jax.ShapeDtypeStruct((chunk_rows, width)...]
  transfers between devices with their start and end apart: 18 -> 18, of which waited for: 11 -> 11; matrix products, arithmetic and copies ran while one was open for 7% -> 7% of each run, Pallas kernels for 32% -> 34%
where the time goes in v10:
time: 205 us; the launch traced here: 203 us
  Pallas kernels  75.7 us (37%)
  waiting for transfers between devices  70.9 us (35%)
  starting transfers between devices  20.1 us (10%)
  between operations  14.9 us (7%)
  other arithmetic  11.6 us (6%)
  local copies, waits for them, and re-layouts  9.84 us (5%)
    pallas_call x4, Pallas kernels, attend(): pl.pallas_call(kernel, out_shape=jax.ShapeDtypeStruct((chunk_rows, width)...  34.9 us
    pallas_call x2, Pallas kernels, project(): pl.pallas_call(functools.partial(project_kernel, rope_heads, layout, len(...  26.8 us
    ppermute x6, waiting for transfers between devices, to_partner(): return lax.ppermute(block, 'ca', [(i, i ^ step) for i in devices])  22 us
    ppermute x3, waiting for transfers between devices, cross(): return lax.ppermute(block, both, pairs)  20.9 us
    ppermute x3, waiting for transfers between devices, forwarded(): lax.ppermute(block, 'ca', [(i, (i + group) % (group * lines)) for i in de...  15.3 us
    ppermute x3, waiting for transfers between devices, swap(): lax.ppermute(block, both, [(i * 2 + c, i * 2 + 1 - c) for i in devices fo...  10.5 us
    pallas_call x3, Pallas kernels, put(): pl.pallas_call(functools.partial(put_kernel, targets), out_shape=jax.Shap...  9.99 us
    ppermute x6, starting transfers between devices, to_partner(): return lax.ppermute(block, 'ca', [(i, i ^ step) for i in devices])  6.72 us
  transfers between devices with their start and end apart: 18, of which 11 were waited for; matrix products, arithmetic and copies ran while one was open for 7% of the time, Pallas kernels for 34%

profile of v10, /device:TPU:16, one launch (start us, length us, event | category | flops | bytes accessed | tf_op | source)
XLA Modules:
  0.0 203.1 jit_solution(7652448097914673788)
XLA Ops:
  8.9 1.6 collective-permute-start.6
  10.5 1.5 collective-permute-start.7
  12.7 15.6 %collective-permute-done.6 = bf16[256,768]{1,0:T(8,128)(2,1)S(1)} collective-permute-done((bf16[256,768]{1,0:T(8,128)(2,1)S(1)}, bf16[256,768]{1,0:T(8,128)(2,1)S(1)}, u32[]{:S(2)}, u32[]{:S(2)}) %collective-permute-start.6) | collective-permute-done | bytes 393248 | tf_op jit(solution)/shard_map/ppermute | solution.py:335
  30.7 3.8 %shard_map.55 = bf16[256,4096]{1,0:T(8,128)(2,1)} custom-call(s32[1]{0:T(128)} %bitcast.5.which, bf16[512,4096]{1,0:T(8,128)(2,1)} %refs_0_.1), custom_call_target="tpu_custom_call" | custom-call | tf_op jit(solution)/shard_map/pallas_call | solution.py:288
  36.0 1.5 collective-permute-start.10
  37.9 1.6 collective-permute-start.8
  40.9 12.0 %collective-permute-done.8.refs_2_ = bf16[768,256]{1,0:T(8,128)(2,1)S(1)} collective-permute-done((bf16[768,256]{1,0:T(8,128)(2,1)S(1)}, bf16[768,256]{1,0:T(8,128)(2,1)S(1)}, u32[]{:S(2)}, u32[]{:S(2)}) %collective-permute-start.8) | collective-permute-done | bytes 393248 | tf_op jit(solution)/shard_map/ppermute | solution.py:342
  52.9 1.7 collective-permute-start.9
  54.6 5.6 %fusion = (f32[2048,64]{1,0:T(8,128)S(1)}, f32[2048,64]{1,0:T(8,128)}, f32[2048,64]{1,0:T(8,128)}) fusion(f32[64]{0:T(128)S(1)} %multiply_power_fusion, f32[2048]{0:T(1024)S(1)} %get-tuple-element.37), kind=kLoop, calls=%fused_computation.10 | loop fusion | flops 262144 | bytes 1581312 | tf_op jit(solution)/shard_map/neg | solution.py:35
  60.2 3.2 %collective-permute-done.9.refs_1_.refs_3_ = bf16[768,256]{1,0:T(8,128)(2,1)S(1)} collective-permute-done((bf16[768,256]{1,0:T(8,128)(2,1)S(1)}, bf16[768,256]{1,0:T(8,128)(2,1)S(1)}, u32[]{:S(2)}, u32[]{:S(2)}) %collective-permute-start.9) | collective-permute-done | bytes 393248 | tf_op jit(solution)/shard_map/ppermute | solution.py:342
  63.5 2.2 %collective-permute-start.11 = (bf16[768,256]{1,0:T(8,128)(2,1)S(1)}, bf16[768,256]{1,0:T(8,128)(2,1)}, u32[]{:S(2)}, u32[]{:S(2)}) collective-permute-start(bf16[768,256]{1,0:T(8,128)(2,1)S(1)} %collective-permute-done.9.refs_1_.refs_3_), channel_id=1, source_target_pairs={{0,8},{2,10},{4,12},{6,14},{8,16},{10,18},{12,20},{14,22},{16,24},... | collective-permute-start | bytes 1179656 | tf_op jit(solution)/shard_map/ppermute | solution.py:342
  65.8 2.2 %copy-done = bf16[512,4096]{1,0:T(8,128)(2,1)S(1)} copy-done((bf16[512,4096]{1,0:T(8,128)(2,1)S(1)}, bf16[512,4096]{1,0:T(8,128)(2,1)}, u32[]{:S(2)}) %copy-start) | copy-done | bytes 4194328
  67.9 2.5 %shard_map.57 = bf16[2048,4096]{1,0:T(8,128)(2,1)} custom-call(s32[3]{0:T(128)S(1)} %pad_add_fusion.1.place, bf16[512,4096]{1,0:T(8,128)(2,1)S(1)} %copy-done), custom_call_target="tpu_custom_call" | custom-call | bytes 8388608 | tf_op jit(solution)/shard_map/pallas_call | solution.py:122
  71.1 2.0 pad_maximum_fusion
  75.6 6.7 %collective-permute-done.5.refs_0_ = bf16[256,4096]{1,0:T(8,128)(2,1)S(1)} collective-permute-done((bf16[256,4096]{1,0:T(8,128)(2,1)}, bf16[256,4096]{1,0:T(8,128)(2,1)S(1)}, u32[]{:S(2)}, u32[]{:S(2)}) %collective-permute-start.5) | collective-permute-done | bytes 2097184 | tf_op jit(solution)/shard_map/ppermute | solution.py:393
  82.3 33.4 %conditional.1 = (bf16[2048,4096]{1,0:T(8,128)(2,1)}) conditional(s32[]{:T(128)} %bitcast.6, () %tuple.11, (bf16[256,4096]{1,0:T(8,128)(2,1)S(1)}, bf16[256,4096]{1,0:T(8,128)(2,1)}, s32[3]{0:T(128)S(1)}, bf16[2048,4096]{1,0:T(8,128)(2,1)}) %tuple.12), branch_computations={%region_2.3_spmd, %region_3.4_spmd} | conditional | bytes 58720424 | solution.py:433
  83.3 5.4 %collective-permute-done.1.refs_1_ = bf16[256,4096]{1,0:T(8,128)(2,1)S(1)} collective-permute-done((bf16[256,4096]{1,0:T(8,128)(2,1)S(1)}, bf16[256,4096]{1,0:T(8,128)(2,1)S(1)}, u32[]{:S(2)}, u32[]{:S(2)}) %collective-permute-start.1) | collective-permute-done | bytes 2097184 | tf_op jit(solution)/shard_map/cond/branch_1_fun/ppermute | solution.py:396
  89.6 5.0 %branch_1_fun.3.other_ref.refs_2_ = bf16[2048,4096]{1,0:T(8,128)(2,1)} custom-call(s32[3]{0:T(128)S(1)} %get-tuple-element.16.place, bf16[256,4096]{1,0:T(8,128)(2,1)S(1)} %get-tuple-element.17.refs_0_, bf16[256,4096]{1,0:T(8,128)(2,1)S(1)} %collective-permute-done.1.refs_1_, ...), custom_call_target="tpu_custom_call", output_to_operand_aliasing={{}: (5, {})} | custom-call | bytes 16777216 | tf_op jit(solution)/shard_map/cond/branch_1_fun/pallas_call | solution.py:122
  94.6 14.2 %collective-permute-done.block_ref = bf16[256,4096]{1,0:T(8,128)(2,1)S(1)} collective-permute-done((bf16[256,4096]{1,0:T(8,128)(2,1)S(1)}, bf16[256,4096]{1,0:T(8,128)(2,1)S(1)}, u32[]{:S(2)}, u32[]{:S(2)}) %collective-permute-start) | collective-permute-done | bytes 2097184 | tf_op jit(solution)/shard_map/cond/branch_1_fun/ppermute | solution.py:393
  109.0 4.1 %collective-permute-done.3.refs_1_ = bf16[256,4096]{1,0:T(8,128)(2,1)S(1)} collective-permute-done((bf16[256,4096]{1,0:T(8,128)(2,1)S(1)}, bf16[256,4096]{1,0:T(8,128)(2,1)S(1)}, u32[]{:S(2)}, u32[]{:S(2)}) %collective-permute-start.3) | collective-permute-done | bytes 2097184 | tf_op jit(solution)/shard_map/cond/branch_1_fun/ppermute | solution.py:396
  113.2 2.5 %branch_1_fun.5 = bf16[2048,4096]{1,0:T(8,128)(2,1)} custom-call(s32[3]{0:T(128)S(1)} %get-tuple-element.16.place, bf16[256,4096]{1,0:T(8,128)(2,1)S(1)} %branch_1_fun.4.refs_0_, bf16[256,4096]{1,0:T(8,128)(2,1)S(1)} %collective-permute-done.3.refs_1_, bf16[2048,4096]{1,0:T(8,128)(2,1)} %branch_1_fun.3.other_ref.refs_2_), custom_call_target="tpu_custom_call", output_to_operand_aliasing={{}: (3, {})} | custom-call | bytes 8388608 | tf_op jit(solution)/shard_map/cond/branch_1_fun/pallas_call | solution.py:122
  115.7 11.2 %shard_map.59.kv_ref = bf16[2048,256]{1,0:T(8,128)(2,1)} custom-call(s32[3]{0:T(128)S(1)} %pad_add_fusion.1.place, bf16[2048,4096]{1,0:T(8,128)(2,1)} %get-tuple-element.45.x_ref, bf16[1024,768]{1,0:T(8,128)(2,1)} %all-gather.3.cloned.1.call-done.refs_0_, bf16[768,256]{1,0:T(8,128)(2,1)} %copy-done.5, bf16[768,256]{1,0:T(8,128)(2,1)} %copy-done.8, ...), custom_call_target="tpu_custom_call" | custom-call | flops 4294967296 | bytes 18874368 | tf_op jit(solution)/shard_map/pallas_call | solution.py:79
  128.1 3.7 %collective-permute-start.12 = (bf16[1536,256]{1,0:T(8,128)(2,1)S(1)}, bf16[1536,256]{1,0:T(8,128)(2,1)S(1)}, u32[]{:S(2)}, u32[]{:S(2)}) collective-permute-start(bf16[1536,256]{1,0:T(8,128)(2,1)S(1)} %slice.50), channel_id=1, source_target_pairs={{0,8},{2,10},{4,12},{6,14},{8,16},{10,18},{12,20},{14,22},{16,24},... | collective-permute-start | bytes 2359304 | tf_op jit(solution)/shard_map/ppermute | solution.py:456
  131.8 15.6 %shard_map.58.q_ref = bf16[2048,512]{1,0:T(8,128)(2,1)} custom-call(s32[3]{0:T(128)S(1)} %pad_add_fusion.1.place, bf16[2048,4096]{1,0:T(8,128)(2,1)} %get-tuple-element.45.x_ref, bf16[1024,768]{1,0:T(8,128)(2,1)} %all-gather.3.cloned.1.call-done.refs_0_, bf16[3072,512]{1,0:T(8,128)(2,1)} %all-gather.5.cloned.1.call-done.refs_1_, ...), custom_call_target="tpu_custom_call" | custom-call | flops 8589934592 | bytes 20971520 | tf_op jit(solution)/shard_map/pallas_call | solution.py:79
  147.5 2.2 %collective-permute-done.12.halo_ref = bf16[1536,256]{1,0:T(8,128)(2,1)S(1)} collective-permute-done((bf16[1536,256]{1,0:T(8,128)(2,1)S(1)}, bf16[1536,256]{1,0:T(8,128)(2,1)S(1)}, u32[]{:S(2)}, u32[]{:S(2)}) %collective-permute-start.12) | collective-permute-done | bytes 786464 | tf_op jit(solution)/shard_map/ppermute | solution.py:456
  150.5 6.9 %shard_map.60 = bf16[512,512]{1,0:T(8,128)(2,1)} custom-call(s32[1]{0:T(128)} %bitcast.first, s32[3,8]{1,0:T(4,128)} %pad_add_fusion.refs_5_.bounds, s32[8]{0:T(128)} %broadcast_subtract_fusion.1.refs_4_.ends, bf16[2048,512]{1,0:T(8,128)(2,1)} %shard_map.58.q_ref, bf16[1536,256]{1,0:T(8,128)(2,1)} %copy-done.12, bf16[2048,256]{1,0:T(8,128)(2,1)} %shard_map.59.kv_ref), custom_call_target="tpu_custom_call" | custom-call | flops 1073741824 | bytes 1048576 | tf_op jit(solution)/shard_map/pallas_call | solution.py:240
  157.4 1.5 collective-permute-start.13
  158.9 11.7 %shard_map.61 = bf16[512,512]{1,0:T(8,128)(2,1)} custom-call(s32[1]{0:T(128)} %bitcast.7.first, s32[3,8]{1,0:T(4,128)} %pad_add_fusion.refs_5_.bounds, s32[8]{0:T(128)} %broadcast_subtract_fusion.1.refs_4_.ends, bf16[2048,512]{1,0:T(8,128)(2,1)} %shard_map.58.q_ref, bf16[1536,256]{1,0:T(8,128)(2,1)} %copy-done.12, bf16[2048,256]{1,0:T(8,128)(2,1)} %shard_map.59.kv_ref), custom_call_target="tpu_custom_call" | custom-call | flops 1073741824 | bytes 1048576 | tf_op jit(solution)/shard_map/pallas_call | solution.py:240
  170.6 1.5 collective-permute-start.14
  172.1 9.1 %shard_map.62 = bf16[512,512]{1,0:T(8,128)(2,1)} custom-call(s32[1]{0:T(128)} %bitcast.8.first, s32[3,8]{1,0:T(4,128)} %pad_add_fusion.refs_5_.bounds, s32[8]{0:T(128)} %broadcast_subtract_fusion.1.refs_4_.ends, bf16[2048,512]{1,0:T(8,128)(2,1)} %shard_map.58.q_ref, bf16[1536,256]{1,0:T(8,128)(2,1)} %copy-done.12, bf16[2048,256]{1,0:T(8,128)(2,1)} %shard_map.59.kv_ref), custom_call_target="tpu_custom_call" | custom-call | flops 1073741824 | bytes 1048576 | tf_op jit(solution)/shard_map/pallas_call | solution.py:240
  181.2 7.2 %shard_map.63 = bf16[512,512]{1,0:T(8,128)(2,1)} custom-call(s32[1]{0:T(128)} %bitcast.9.first, s32[3,8]{1,0:T(4,128)} %pad_add_fusion.refs_5_.bounds, s32[8]{0:T(128)} %broadcast_subtract_fusion.1.refs_4_.ends, bf16[2048,512]{1,0:T(8,128)(2,1)} %shard_map.58.q_ref, bf16[1536,256]{1,0:T(8,128)(2,1)} %copy-done.12, bf16[2048,256]{1,0:T(8,128)(2,1)} %shard_map.59.kv_ref), custom_call_target="tpu_custom_call" | custom-call | flops 1073741824 | bytes 1048576 | tf_op jit(solution)/shard_map/pallas_call | solution.py:240
  188.9 5.2 %collective-permute-done.15 = bf16[512,512]{1,0:T(8,128)(2,1)S(1)} collective-permute-done((bf16[512,512]{1,0:T(8,128)(2,1)}, bf16[512,512]{1,0:T(8,128)(2,1)S(1)}, u32[]{:S(2)}, u32[]{:S(2)}) %collective-permute-start.15) | collective-permute-done | bytes 524320 | tf_op jit(solution)/shard_map/ppermute | solution.py:335
  (81 shorter events, 17.3 us)
Async XLA Ops:
  6.5 1.4 copy-start.10
  6.5 1.4 copy-start.9
  6.5 109.2 %all-gather.3.cloned.1.call-start = ((), (), s32[]{:S(2)}) async-start(), calls=%async_computation | async-start | bytes 1966080 | tf_op jit(solution)/shard_map/all_gather | solution.py:339
  8.8 123.0 %all-gather.5.cloned.1.call-start = ((), (), s32[]{:S(2)}) async-start(), calls=%async_computation.1 | async-start | bytes 3932160 | tf_op jit(solution)/shard_map/all_gather | solution.py:339
  8.9 19.3 %collective-permute-start.6 = (bf16[256,768]{1,0:T(8,128)(2,1)S(1)}, bf16[256,768]{1,0:T(8,128)(2,1)S(1)}, u32[]{:S(2)}, u32[]{:S(2)}) collective-permute-start(bf16[256,768]{1,0:T(8,128)(2,1)S(1)} %pad_maximum_fusion.4), channel_id=1, source_target_pairs={{0,4},{2,6},{4,0},{6,2},{8,12},{10,14},{12,8},{14,10},{16,20},{18,... | collective-permute-start | bytes 1179656 | tf_op jit(solution)/shard_map/ppermute | solution.py:335
  10.5 17.8 %collective-permute-start.7 = (bf16[256,768]{1,0:T(8,128)(2,1)S(1)}, bf16[256,768]{1,0:T(8,128)(2,1)S(1)}, u32[]{:S(2)}, u32[]{:S(2)}) collective-permute-start(bf16[256,768]{1,0:T(8,128)(2,1)S(1)} %pad_maximum_fusion.5), channel_id=1, source_target_pairs={{0,6},{2,4},{4,2},{6,0},{8,14},{10,12},{12,10},{14,8},{16,22},{18,... | collective-permute-start | bytes 1179656 | tf_op jit(solution)/shard_map/ppermute | solution.py:335
  12.1 17.5 %collective-permute-start.4 = (bf16[256,768]{1,0:T(8,128)(2,1)S(1)}, bf16[256,768]{1,0:T(8,128)(2,1)S(1)}, u32[]{:S(2)}, u32[]{:S(2)}) collective-permute-start(bf16[256,768]{1,0:T(8,128)(2,1)S(1)} %pad_maximum_fusion.3), channel_id=1, source_target_pairs={{0,2},{2,0},{4,6},{6,4},{8,10},{10,8},{12,14},{14,12},{16,18},{18,... | collective-permute-start | bytes 1179656 | tf_op jit(solution)/shard_map/ppermute | solution.py:335
  29.6 8.2 %copy-start.7 = (bf16[256,768]{1,0:T(8,128)(2,1)}, bf16[256,768]{1,0:T(8,128)(2,1)S(1)}, u32[]{:S(2)}) copy-start(bf16[256,768]{1,0:T(8,128)(2,1)S(1)} %collective-permute-done.4) | copy-start | bytes 1179652
  30.7 6.8 %copy-start.13 = (s32[8]{0:T(128)S(1)}, s32[8]{0:T(128)}, u32[]{:S(2)}) copy-start(s32[8]{0:T(128)} %param.8) | copy-start | bytes 100
  34.5 47.8 %collective-permute-start.5 = (bf16[256,4096]{1,0:T(8,128)(2,1)}, bf16[256,4096]{1,0:T(8,128)(2,1)S(1)}, u32[]{:S(2)}, u32[]{:S(2)}) collective-permute-start(bf16[256,4096]{1,0:T(8,128)(2,1)} %shard_map.55), channel_id=1, source_target_pairs={{0,2},{1,5},{2,0},{3,7},{4,6},{5,1},{6,4},{7,3},{8,10},{9,13},{10,... | collective-permute-start | bytes 6291464 | tf_op jit(solution)/shard_map/ppermute | solution.py:393
  36.0 46.3 %collective-permute-start.10 = (bf16[256,4096]{1,0:T(8,128)(2,1)}, bf16[256,4096]{1,0:T(8,128)(2,1)}, u32[]{:S(2)}, u32[]{:S(2)}) collective-permute-start(bf16[256,4096]{1,0:T(8,128)(2,1)} %shard_map.55), channel_id=1, source_target_pairs={{0,4},{1,3},{2,6},{3,1},{4,0},{5,7},{6,2},{7,5},{8,12},{9,11},{10,... | collective-permute-start | bytes 6291464 | tf_op jit(solution)/shard_map/ppermute | solution.py:393
  37.9 25.6 %copy-start.5 = (bf16[768,256]{1,0:T(8,128)(2,1)}, bf16[768,256]{1,0:T(8,128)(2,1)S(1)}, u32[]{:S(2)}) copy-start(bf16[768,256]{1,0:T(8,128)(2,1)S(1)} %pad_maximum_fusion.6.refs_1_) | copy-start | bytes 1179652
  37.9 15.0 %collective-permute-start.8 = (bf16[768,256]{1,0:T(8,128)(2,1)S(1)}, bf16[768,256]{1,0:T(8,128)(2,1)S(1)}, u32[]{:S(2)}, u32[]{:S(2)}) collective-permute-start(bf16[768,256]{1,0:T(8,128)(2,1)S(1)} %pad_maximum_fusion.6.refs_1_), channel_id=1, source_target_pairs={{0,8},{2,10},{4,12},{6,14},{8,16},{10,18},{12,20},{14,22},{16,24},... | collective-permute-start | bytes 1179656 | tf_op jit(solution)/shard_map/ppermute | solution.py:342
  52.9 12.8 %copy-start.8 = (bf16[768,256]{1,0:T(8,128)(2,1)}, bf16[768,256]{1,0:T(8,128)(2,1)S(1)}, u32[]{:S(2)}) copy-start(bf16[768,256]{1,0:T(8,128)(2,1)S(1)} %collective-permute-done.8.refs_2_) | copy-start | bytes 1179652
  52.9 10.6 %collective-permute-start.9 = (bf16[768,256]{1,0:T(8,128)(2,1)S(1)}, bf16[768,256]{1,0:T(8,128)(2,1)S(1)}, u32[]{:S(2)}, u32[]{:S(2)}) collective-permute-start(bf16[768,256]{1,0:T(8,128)(2,1)S(1)} %collective-permute-done.8.refs_2_), channel_id=1, source_target_pairs={{0,8},{2,10},{4,12},{6,14},{8,16},{10,18},{12,20},{14,22},{16,24},... | collective-permute-start | bytes 1179656 | tf_op jit(solution)/shard_map/ppermute | solution.py:342
  63.5 7.0 %copy-start.4 = (bf16[768,256]{1,0:T(8,128)(2,1)}, bf16[768,256]{1,0:T(8,128)(2,1)S(1)}, u32[]{:S(2)}) copy-start(bf16[768,256]{1,0:T(8,128)(2,1)S(1)} %collective-permute-done.9.refs_1_.refs_3_) | copy-start | bytes 1179652
  63.5 52.2 %collective-permute-start.11 = (bf16[768,256]{1,0:T(8,128)(2,1)S(1)}, bf16[768,256]{1,0:T(8,128)(2,1)}, u32[]{:S(2)}, u32[]{:S(2)}) collective-permute-start(bf16[768,256]{1,0:T(8,128)(2,1)S(1)} %collective-permute-done.9.refs_1_.refs_3_), channel_id=1, source_target_pairs={{0,8},{2,10},{4,12},{6,14},{8,16},{10,18},{12,20},{14,22},{16,24},... | collective-permute-start | bytes 1179656 | tf_op jit(solution)/shard_map/ppermute | solution.py:342
  65.8 2.2 %copy-start = (bf16[512,4096]{1,0:T(8,128)(2,1)S(1)}, bf16[512,4096]{1,0:T(8,128)(2,1)}, u32[]{:S(2)}) copy-start(bf16[512,4096]{1,0:T(8,128)(2,1)} %refs_0_.1) | copy-start | bytes 12582916
  67.9 2.5 %copy-start.11 = (s32[1,8]{1,0:T(1,128)S(1)}, s32[1,8]{1,0:T(1,128)}, u32[]{:S(2)}) copy-start(s32[1,8]{1,0:T(1,128)} %iota_multiply_fusion) | copy-start | bytes 100
  67.9 3.1 %copy-start.1 = (f32[2048,64]{1,0:T(8,128)S(1)}, f32[2048,64]{1,0:T(8,128)}, u32[]{:S(2)}) copy-start(f32[2048,64]{1,0:T(8,128)} %get-tuple-element.35) | copy-start | bytes 1572868
  67.9 3.1 %copy-start.2 = (f32[2048,64]{1,0:T(8,128)S(1)}, f32[2048,64]{1,0:T(8,128)}, u32[]{:S(2)}) copy-start(f32[2048,64]{1,0:T(8,128)} %get-tuple-element.36) | copy-start | bytes 1572868
  82.3 6.4 %collective-permute-start.1 = (bf16[256,4096]{1,0:T(8,128)(2,1)S(1)}, bf16[256,4096]{1,0:T(8,128)(2,1)S(1)}, u32[]{:S(2)}, u32[]{:S(2)}) collective-permute-start(bf16[256,4096]{1,0:T(8,128)(2,1)S(1)} %get-tuple-element.17.refs_0_), channel_id=1, source_target_pairs={{0,1},{1,0},{2,3},{3,2},{4,5},{5,4},{6,7},{7,6},{8,9},{9,8},{10,11... | collective-permute-start | bytes 6291464 | tf_op jit(solution)/shard_map/cond/branch_1_fun/ppermute | solution.py:396
  82.3 7.4 %collective-permute-start.2 = (bf16[256,4096]{1,0:T(8,128)(2,1)}, bf16[256,4096]{1,0:T(8,128)(2,1)S(1)}, u32[]{:S(2)}, u32[]{:S(2)}) collective-permute-start(bf16[256,4096]{1,0:T(8,128)(2,1)} %get-tuple-element.18.refs_2_), channel_id=1, source_target_pairs={{0,1},{1,0},{2,3},{3,2},{4,5},{5,4},{6,7},{7,6},{8,9},{9,8},{10,11... | collective-permute-start | bytes 6291464 | tf_op jit(solution)/shard_map/cond/branch_1_fun/ppermute | solution.py:396
  82.8 26.0 %collective-permute-start = (bf16[256,4096]{1,0:T(8,128)(2,1)S(1)}, bf16[256,4096]{1,0:T(8,128)(2,1)S(1)}, u32[]{:S(2)}, u32[]{:S(2)}) collective-permute-start(bf16[256,4096]{1,0:T(8,128)(2,1)S(1)} %get-tuple-element.17.refs_0_), channel_id=1, source_target_pairs={{0,4},{1,3},{2,6},{3,1},{4,0},{5,7},{6,2},{7,5},{8,12},{9,11},{10,... | collective-permute-start | bytes 6291464 | tf_op jit(solution)/shard_map/cond/branch_1_fun/ppermute | solution.py:393
  108.9 4.2 %collective-permute-start.3 = (bf16[256,4096]{1,0:T(8,128)(2,1)S(1)}, bf16[256,4096]{1,0:T(8,128)(2,1)S(1)}, u32[]{:S(2)}, u32[]{:S(2)}) collective-permute-start(bf16[256,4096]{1,0:T(8,128)(2,1)S(1)} %branch_1_fun.4.refs_0_), channel_id=1, source_target_pairs={{0,1},{1,0},{2,3},{3,2},{4,5},{5,4},{6,7},{7,6},{8,9},{9,8},{10,11... | collective-permute-start | bytes 6291464 | tf_op jit(solution)/shard_map/cond/branch_1_fun/ppermute | solution.py:396
  128.1 21.5 %collective-permute-start.12 = (bf16[1536,256]{1,0:T(8,128)(2,1)S(1)}, bf16[1536,256]{1,0:T(8,128)(2,1)S(1)}, u32[]{:S(2)}, u32[]{:S(2)}) collective-permute-start(bf16[1536,256]{1,0:T(8,128)(2,1)S(1)} %slice.50), channel_id=1, source_target_pairs={{0,8},{2,10},{4,12},{6,14},{8,16},{10,18},{12,20},{14,22},{16,24},... | collective-permute-start | bytes 2359304 | tf_op jit(solution)/shard_map/ppermute | solution.py:456
  149.6 0.9 copy-start.12
  157.4 31.0 %collective-permute-start.13 = (bf16[512,512]{1,0:T(8,128)(2,1)}, bf16[512,512]{1,0:T(8,128)(2,1)S(1)}, u32[]{:S(2)}, u32[]{:S(2)}) collective-permute-start(bf16[512,512]{1,0:T(8,128)(2,1)} %shard_map.60), channel_id=1, source_target_pairs={{0,6},{2,4},{4,2},{6,0},{8,14},{10,12},{12,10},{14,8},{16,22},{18,... | collective-permute-start | bytes 1572872 | tf_op jit(solution)/shard_map/ppermute | solution.py:335
  170.6 18.2 %collective-permute-start.14 = (bf16[512,512]{1,0:T(8,128)(2,1)}, bf16[512,512]{1,0:T(8,128)(2,1)S(1)}, u32[]{:S(2)}, u32[]{:S(2)}) collective-permute-start(bf16[512,512]{1,0:T(8,128)(2,1)} %shard_map.61), channel_id=1, source_target_pairs={{0,4},{2,6},{4,0},{6,2},{8,12},{10,14},{12,8},{14,10},{16,20},{18,... | collective-permute-start | bytes 1572872 | tf_op jit(solution)/shard_map/ppermute | solution.py:335
  181.2 12.8 %collective-permute-start.15 = (bf16[512,512]{1,0:T(8,128)(2,1)}, bf16[512,512]{1,0:T(8,128)(2,1)S(1)}, u32[]{:S(2)}, u32[]{:S(2)}) collective-permute-start(bf16[512,512]{1,0:T(8,128)(2,1)} %shard_map.62), channel_id=1, source_target_pairs={{0,2},{2,0},{4,6},{6,4},{8,10},{10,8},{12,14},{14,12},{16,18},{18,... | collective-permute-start | bytes 1572872 | tf_op jit(solution)/shard_map/ppermute | solution.py:335
  188.7 6.7 %copy-start.6 = (bf16[512,512]{1,0:T(8,128)(2,1)S(1)}, bf16[512,512]{1,0:T(8,128)(2,1)}, u32[]{:S(2)}) copy-start(bf16[512,512]{1,0:T(8,128)(2,1)} %shard_map.63) | copy-start | bytes 1572868
  194.1 1.3 copy-start.3
Sparse Core Ops, SparseCore 0:
  9.0 43.3 all-gather.2
  54.0 71.9 all-gather.4
